TPU v7x, 32 devices: a whole 2x2x4 slice. The times are simulated.
32 devices in a mesh: batch: 4 (over y, core), blk: 8 (over z, x).
Axes of the slice: x: 2, y: 2, z: 4, core: 2. Of those that a mesh axis runs over, the one named last changes fastest.
Arguments:
- tokens: bfloat16 [8, 2048, 1536], P('batch', 'blk'), may hold values from -6 to 6
- cotangent: bfloat16 [8, 2048, 1536], P('batch', 'blk'), may hold values from -6 to 6
- lengths: int32 [8, 6], P('batch'), may hold values from 1 to 1024, 2048 in all within a row
- unit_owner: int32 [36], replicated, may hold values from 0 to 35, each once
- step_count: int32 [1], replicated, may hold values from 1 to 20
- master: float32 [1536, 36, 512], P('blk', 'batch'), may hold values from -0.15625 to 0.15625
- first: float32 [1536, 36, 512], P('blk', 'batch'), may hold values from -80 to 80
- second: float32 [1536, 36, 512], P('blk', 'batch'), may hold values from 861.7984 to 3440.64
- bases: float32 [1536, 36, 1536], P('blk', 'batch'), may hold values from -0.0612372436 to 0.8612372
- small: float32 [3456], replicated, may hold values from -0.4 to 1.5
- small_first: float32 [3456], replicated, may hold values from -80 to 80
- small_second: float32 [3456], replicated, may hold values from 861.7984 to 3440.64
Outputs:
- block_out: bfloat16 [8, 2048, 1536], P('batch', 'blk')
- input_grad: bfloat16 [8, 2048, 1536], P('batch', 'blk')
- new_master: float32 [1536, 36, 512], P('blk', 'batch')
- new_first: float32 [1536, 36, 512], P('blk', 'batch')
- new_second: float32 [1536, 36, 512], P('blk', 'batch')
- small_grads: float32 [3456], replicated
- new_small: float32 [3456], replicated
- new_small_first: float32 [3456], replicated
- new_small_second: float32 [3456], replicated
Inputs may be any that keep to these rules, and one draw needn't show every extreme that they name: `lengths`: each row's entries sum to 2048; the last entry counts the padding positions at the row's end, the others are documents. Each slot holds exactly one unit: unit u lies in slot unit_owner[u], and slot s lies with batch index s // 9.
All inputs are finite; a program needn't handle non-finite values.
Results may differ from a plain program's by a relative error of at most 0.029.
Values may be sent and summed in bfloat16 or wider, within the bound.
A program may use at most 448 MiB of HBM per device.

v0:
```python
import jax
import jax.numpy as jnp
from jax import lax
from jax.sharding import PartitionSpec as P

D = 1536
H = 12
HD = 64
VD = 128
FF = 4096
UW = 512
NDOC = 6
UNITS = 36


norm_epsilon = 1e-05
lambda_start = 0.2
rope_base = 10000.0
masked_fill = -1000000000.0
beta_one = 0.9
beta_two = 0.95
adam_epsilon = 1e-08
weight_decay = 0.01
small_rate = 1.0


def from_behind(shard, axis, by):
    count = lax.axis_size(axis)
    return lax.ppermute(shard, axis, [(i, (i + by) % count) for i in range(count)])


def root_norm(values, gain):
    return (
        values * lax.rsqrt(jnp.mean(values * values, axis=-1, keepdims=True) + norm_epsilon) * gain
    )


def mix_value(mixers):
    return (
        jnp.exp(jnp.sum(mixers[0] * mixers[1]))
        - jnp.exp(jnp.sum(mixers[2] * mixers[3]))
        + lambda_start
    )


def head_mix(maps_out, head_gain, mixer):
    combined = maps_out[:, :, 0] - mixer * maps_out[:, :, 1]
    normed = (
        combined
        * lax.rsqrt(jnp.mean(combined * combined, axis=-1, keepdims=True) + norm_epsilon)
        * head_gain
        * (1.0 - lambda_start)
    )
    rows_count, heads, positions, width = normed.shape
    return jnp.transpose(normed, (0, 2, 1, 3)).reshape(rows_count, positions, heads * width)


def gated_unit(gate, up):
    return jax.nn.silu(gate) * up


def document_places(lengths, places):
    ends = jnp.cumsum(lengths, axis=1)
    starts = ends - lengths
    segment = jnp.sum((places[None, :, None] >= ends[:, None, :]).astype(jnp.int32), axis=2)
    chosen = segment[:, :, None] == jnp.arange(lengths.shape[1], dtype=jnp.int32)[None, None, :]
    offset = jnp.sum(jnp.where(chosen, starts[:, None, :], 0), axis=2)
    return (segment, places[None, :] - offset)


def allowed(seg_query, place_query, seg_key, place_key, last):
    same = seg_query[:, :, None] == seg_key[:, None, :]
    causal = place_key[None, None, :] <= place_query[None, :, None]
    itself = place_key[None, None, :] == place_query[None, :, None]
    return same & causal & ((seg_query[:, :, None] < last) | itself)


def turn_tables(position):
    rates = rope_base ** (-2.0 * jnp.arange(HD // 2, dtype=jnp.float32) / HD)
    angle = position.astype(jnp.float32)[..., None] * rates
    return (jnp.cos(angle), jnp.sin(angle))


def rotate(values, cosine, sine):
    half = values.shape[-1] // 2
    front = values[..., :half]
    back = values[..., half:]
    return jnp.concatenate([front * cosine - back * sine, back * cosine + front * sine], axis=-1)


def adam_step(first_new, second_new, steps_done):
    return (
        first_new
        / (1.0 - beta_one**steps_done)
        / (jnp.sqrt(second_new / (1.0 - beta_two**steps_done)) + adam_epsilon)
    )


def contract_rows(left, right):
    return lax.dot_general(
        left, right, (((1,), (1,)), ((), ())), preferred_element_type=jnp.float32
    )


def local(
    tokens,
    cotangent,
    lengths,
    unit_owner,
    step_count,
    master,
    first,
    second,
    bases,
    small,
    small_first,
    small_second,
):
    rows_count, seq_part, width = tokens.shape
    token_count = rows_count * seq_part
    axis_count = lax.axis_size("blk")
    axis_place = lax.axis_index("blk")
    rows_part = master.shape[0]
    scale = HD ** (-0.5)
    highest = lax.Precision.HIGHEST
    learn_rate = 2.0 / D**0.5
    every_slot = lax.all_gather(master.astype(jnp.bfloat16), "batch", axis=1, tiled=True)
    by_unit = jnp.take(every_slot, unit_owner, axis=1).reshape(rows_part, UNITS * UW)
    attention_whole = lax.all_gather(by_unit[:, : 4 * D], "blk", axis=0, tiled=True)
    gate_whole = lax.all_gather(by_unit[:, 4 * D : 4 * D + 2 * FF], "blk", axis=0, tiled=True)
    down_whole = lax.all_gather(by_unit[:, 4 * D + 2 * FF :], "blk", axis=0, tiled=True)
    places = axis_place * seq_part + jnp.arange(seq_part, dtype=jnp.int32)
    segment, position = document_places(lengths, places)
    cosine, sine = turn_tables(position)
    cosine = cosine[:, :, None, None, :]
    sine = sine[:, :, None, None, :]
    residual = tokens.astype(jnp.float32)
    gain_one = small[:D]
    gain_two = small[D : 2 * D]
    head_gain = small[2 * D : 2 * D + VD]
    mixer, mixer_back = jax.vjp(mix_value, small[2 * D + VD :].reshape(4, HD))
    normed_exact, norm_one_back = jax.vjp(root_norm, residual, gain_one)
    normed_one = normed_exact.astype(jnp.bfloat16).reshape(token_count, D)
    projected = jnp.dot(normed_one, attention_whole[:, : 3 * D], preferred_element_type=jnp.float32)
    query = rotate(projected[:, :D].reshape(rows_count, seq_part, H, 2, HD), cosine, sine).astype(
        jnp.bfloat16
    )
    key_own = (
        rotate(projected[:, D : 2 * D].reshape(rows_count, seq_part, H, 2, HD), cosine, sine)
        .astype(jnp.bfloat16)
        .reshape(rows_count, seq_part, D)
    )
    value_own = projected[:, 2 * D :].astype(jnp.bfloat16).reshape(rows_count, seq_part, D)
    best = jnp.full((rows_count, H, 2, seq_part), masked_fill, jnp.float32)
    key_piece = lax.all_gather(key_own, "blk", axis=1, tiled=True)
    value_piece = lax.all_gather(value_own, "blk", axis=1, tiled=True)
    count = key_piece.shape[1]
    key_places = jnp.arange(count, dtype=jnp.int32)
    key_segment, unused = document_places(lengths, key_places)
    mask = allowed(segment, places, key_segment, key_places, NDOC - 1)[:, None, None]
    keys = key_piece.reshape(rows_count, count, H, 2, HD)
    values = value_piece.reshape(rows_count, count, H, VD)
    scores = (
        jnp.einsum("rqhcd,rkhcd->rhcqk", query, keys, preferred_element_type=jnp.float32) * scale
    )
    scores = jnp.where(mask, scores, masked_fill)
    top = jnp.maximum(best, jnp.max(scores, axis=-1))
    shares = jnp.where(mask, jnp.exp(scores - top[..., None]), 0.0)
    mass = jnp.sum(shares, axis=-1)
    summed = jnp.einsum(
        "rhcqk,rkhe->rhcqe", shares.astype(jnp.bfloat16), values, preferred_element_type=jnp.float32
    )
    best, mass, summed = (top, mass, summed)
    maps_out = summed / mass[..., None]
    log_mass = best + jnp.log(mass)
    mixed_exact, mix_back = jax.vjp(head_mix, maps_out, head_gain, mixer)
    mixed = mixed_exact.astype(jnp.bfloat16).reshape(token_count, D)
    middle = residual.reshape(token_count, D) + contract_rows(mixed, attention_whole[:, 3 * D :])
    normed_two_exact, norm_two_back = jax.vjp(root_norm, middle, gain_two)
    normed_two = normed_two_exact.astype(jnp.bfloat16)
    gate_up = jnp.dot(normed_two, gate_whole, preferred_element_type=jnp.float32)
    hidden_exact, gated_back = jax.vjp(gated_unit, gate_up[:, :FF], gate_up[:, FF:])
    hidden = hidden_exact.astype(jnp.bfloat16)
    result = middle + contract_rows(hidden, down_whole)
    block_out = result.astype(jnp.bfloat16).reshape(rows_count, seq_part, D)
    output_grad = cotangent.reshape(token_count, D)
    hidden_grad = jnp.dot(output_grad, down_whole, preferred_element_type=jnp.float32)
    gate_grad, up_grad = gated_back(hidden_grad)
    gate_up_grad = jnp.concatenate([gate_grad, up_grad], axis=1).astype(jnp.bfloat16)
    normed_two_grad = contract_rows(gate_up_grad, gate_whole)
    middle_part, gain_two_grad = norm_two_back(normed_two_grad)
    middle_grad = output_grad.astype(jnp.float32) + middle_part
    middle_low = middle_grad.astype(jnp.bfloat16)
    mixed_grad = jnp.dot(
        middle_low, attention_whole[:, 3 * D :], preferred_element_type=jnp.float32
    )
    maps_grad, head_gain_grad, mixer_grad = mix_back(mixed_grad.reshape(rows_count, seq_part, D))
    maps_low = maps_grad.astype(jnp.bfloat16)
    offset_term = jnp.sum(maps_low.astype(jnp.float32) * maps_out, axis=-1)

    def circle(turn_index, carry):
        moving, moving_grad, query_grad = carry
        source = (axis_place - turn_index) % axis_count
        key_places = source * seq_part + jnp.arange(seq_part, dtype=jnp.int32)
        key_segment, unused = document_places(lengths, key_places)
        mask = allowed(segment, places, key_segment, key_places, NDOC - 1)[:, None, None]
        keys = moving[0].astype(jnp.bfloat16).reshape(rows_count, seq_part, H, 2, HD)
        values = moving[1].astype(jnp.bfloat16).reshape(rows_count, seq_part, H, VD)
        scores = (
            jnp.einsum("rqhcd,rkhcd->rhcqk", query, keys, preferred_element_type=jnp.float32)
            * scale
        )
        shares = jnp.where(mask, jnp.exp(scores - log_mass[..., None]), 0.0)
        value_term = jnp.einsum(
            "rhcqk,rhcqe->rkhe",
            shares.astype(jnp.bfloat16),
            maps_low,
            preferred_element_type=jnp.float32,
        )
        share_grad = jnp.einsum(
            "rhcqe,rkhe->rhcqk", maps_low, values, preferred_element_type=jnp.float32
        )
        score_low = (shares * (share_grad - offset_term[..., None])).astype(jnp.bfloat16)
        query_grad = query_grad + jnp.einsum(
            "rhcqk,rkhcd->rqhcd", score_low, keys, preferred_element_type=jnp.float32
        )
        key_term = jnp.einsum(
            "rhcqk,rqhcd->rkhcd", score_low, query, preferred_element_type=jnp.float32
        )
        update = jnp.stack(
            [key_term.reshape(rows_count, seq_part, D), value_term.reshape(rows_count, seq_part, D)]
        )
        moving_grad = moving_grad + update
        moving, moving_grad = (
            from_behind(moving.astype(jnp.bfloat16), "blk", 1).astype(moving.dtype),
            from_behind(moving_grad.astype(jnp.bfloat16), "blk", 1).astype(moving_grad.dtype),
        )
        return (moving, moving_grad, query_grad)

    circle_start = (
        jnp.stack([key_own, value_own]).astype(jnp.float32),
        jnp.zeros((2, rows_count, seq_part, D), jnp.float32),
        jnp.zeros((rows_count, seq_part, H, 2, HD), jnp.float32),
    )
    moving, moving_grad, query_grad = lax.fori_loop(0, axis_count, circle, circle_start)
    key_grad = moving_grad[0].reshape(rows_count, seq_part, H, 2, HD) * scale
    query_pre = rotate(query_grad * scale, cosine, -sine).reshape(token_count, D)
    key_pre = rotate(key_grad, cosine, -sine).reshape(token_count, D)
    projected_grad = jnp.concatenate(
        [query_pre, key_pre, moving_grad[1].reshape(token_count, D)], axis=1
    ).astype(jnp.bfloat16)
    normed_one_grad = contract_rows(projected_grad, attention_whole[:, : 3 * D])
    residual_part, gain_one_grad = norm_one_back(normed_one_grad.reshape(rows_count, seq_part, D))
    input_grad = (middle_grad.reshape(rows_count, seq_part, D) + residual_part).astype(jnp.bfloat16)
    (mixers_grad,) = mixer_back(mixer_grad)
    small_local = jnp.concatenate(
        [gain_one_grad, gain_two_grad, head_gain_grad, mixers_grad.reshape(-1)]
    )
    small_grads = lax.psum(small_local, ("batch", "blk"))
    right_side = jnp.concatenate([projected_grad, mixed, gate_up_grad, hidden], axis=1)
    left_sides = (normed_one, middle_low, normed_two, output_grad)
    bounds = (0, 3 * D, 4 * D, 4 * D + 2 * FF, 4 * D + 3 * FF)
    slot_order = jnp.argsort(unit_owner)
    parts = []
    for group in range(4):
        left_rows = left_sides[group]
        parts.append(
            lax.dot_general(
                left_rows,
                right_side[:, bounds[group] : bounds[group + 1]],
                (((0,), (0,)), ((), ())),
                preferred_element_type=jnp.float32,
            )
        )
    row_sums = lax.psum_scatter(
        jnp.concatenate(parts, axis=1).astype(jnp.bfloat16), "blk", scatter_dimension=0, tiled=True
    ).astype(jnp.float32)
    placed = jnp.take(row_sums.reshape(rows_part, UNITS, UW), slot_order, axis=1)
    grad_slots = lax.psum_scatter(
        placed.astype(jnp.bfloat16), "batch", scatter_dimension=1, tiled=True
    ).astype(jnp.float32)
    columns = bases
    turned = lax.psum_scatter(
        jnp.einsum("ksa,ksn->asn", columns, grad_slots, precision=highest).astype(jnp.bfloat16),
        "blk",
        scatter_dimension=0,
        tiled=True,
    ).astype(jnp.float32)
    steps_done = step_count[0].astype(jnp.float32)
    new_first = beta_one * first + (1.0 - beta_one) * turned
    new_second = beta_two * second + (1.0 - beta_two) * turned * turned
    normalized = adam_step(new_first, new_second, steps_done)
    columns = bases
    update = jnp.zeros_like(master) + jnp.einsum(
        "ksa,asn->ksn",
        columns,
        lax.all_gather(normalized.astype(jnp.bfloat16), "blk", axis=0, tiled=True).astype(
            jnp.float32
        ),
        precision=highest,
    )
    new_master = master - learn_rate * (update + weight_decay * master)
    new_small_first = beta_one * small_first + (1.0 - beta_one) * small_grads
    new_small_second = beta_two * small_second + (1.0 - beta_two) * small_grads * small_grads
    new_small = small - small_rate * adam_step(new_small_first, new_small_second, steps_done)
    return (
        block_out,
        input_grad,
        new_master,
        new_first,
        new_second,
        small_grads,
        new_small,
        new_small_first,
        new_small_second,
    )


def solution(mesh):
    in_specs = (
        P("batch", "blk", None),
        P("batch", "blk", None),
        P("batch", None),
        P(),
        P(),
        P("blk", "batch", None),
        P("blk", "batch", None),
        P("blk", "batch", None),
        P("blk", "batch", None),
        P(),
        P(),
        P(),
    )
    out_specs = (
        P("batch", "blk", None),
        P("batch", "blk", None),
        P("blk", "batch", None),
        P("blk", "batch", None),
        P("blk", "batch", None),
        P(),
        P(),
        P(),
        P(),
    )
    return jax.shard_map(local, mesh=mesh, in_specs=in_specs, out_specs=out_specs, check_vma=False)
```

profile of v0, /device:TPU:12, one launch (start us, length us, event | category | flops | bytes accessed | tf_op | source)
XLA Modules:
  0.0 4445.7 jit_solution(609689330076449834)
XLA Ops:
  10.9 51.0 %all-gather.8.cloned.1.call-done = bf16[192,36,512]{2,0,1:T(8,128)(2,1)} async-done(((bf16[192,9,512]{2,0,1:T(8,128)(2,1)}), bf16[192,36,512]{2,0,1:T(8,128)(2,1)}) %all-gather.8.cloned.1.call-update) | async-done | bytes 7077904 | tf_op jit(solution)/shard_map/all_gather | solution.py:127
  61.9 8.6 gather_fusion
  88.4 361.1 %all-gather.10.cloned.1.call-done = bf16[1536,6144]{1,0:T(8,128)(2,1)} async-done(((bf16[192,6144]{1,0:T(8,128)(2,1)}), bf16[1536,6144]{1,0:T(8,128)(2,1)}) %all-gather.10.cloned.1.call-update) | async-done | bytes 18874384 | tf_op jit(solution)/shard_map/all_gather | solution.py:129
  449.5 10.2 fusion.22
  476.9 14.1 fusion.80
  491.0 7.9 copy.155
  498.9 7.9 copy.156
  521.8 7.6 reshape.436
  529.4 14.5 fusion.79
  543.9 9.3 copy.153
  553.1 9.4 copy.154
  570.1 69.3 %all-gather.14.cloned.1.call-done = bf16[2,2048,1536]{2,1,0:T(8,128)(2,1)} async-done(((bf16[2,256,1536]{2,1,0:T(8,128)(2,1)}), bf16[2,2048,1536]{2,1,0:T(8,128)(2,1)}) %all-gather.14.cloned.1.call-update) | async-done | bytes 12582928 | tf_op jit(solution)/shard_map/all_gather | solution.py:156
  639.4 16.1 copy.114
  655.5 161.1 %all-gather.12.cloned.1.call-done = bf16[2,2048,1536]{1,2,0:T(8,128)(2,1)} async-done(((bf16[2,256,1536]{1,2,0:T(8,128)(2,1)}), bf16[2,2048,1536]{1,2,0:T(8,128)(2,1)}) %all-gather.12.cloned.1.call-update) | async-done | bytes 12582928 | tf_op jit(solution)/shard_map/all_gather | solution.py:155
  816.6 40.2 fusion.13
  856.9 32.1 fusion.14
  889.0 42.1 broadcast_divide_fusion
  937.2 7.4 multiply_reduce_fusion.6
  944.7 354.4 %all-gather.16.cloned.1.call-done = bf16[1536,8192]{1,0:T(8,128)(2,1)} async-done(((bf16[192,8192]{1,0:T(8,128)(2,1)}), bf16[1536,8192]{1,0:T(8,128)(2,1)}) %all-gather.16.cloned.1.call-update) | async-done | bytes 25165840 | tf_op jit(solution)/shard_map/all_gather | solution.py:130
  1299.0 22.4 fusion.70
  1321.4 154.3 %all-gather.18.cloned.1.call-done = bf16[1536,4096]{1,0:T(8,128)(2,1)} async-done(((bf16[192,4096]{1,0:T(8,128)(2,1)}), bf16[1536,4096]{1,0:T(8,128)(2,1)}) %all-gather.18.cloned.1.call-update) | async-done | bytes 12582928 | tf_op jit(solution)/shard_map/all_gather | solution.py:131
  1475.7 19.2 fusion.26
  1494.9 22.0 multiply_reduce_fusion.2
  1546.0 1307.1 %while.20 = (s32[]{:T(128)}, bf16[2,2,256,1536]{2,3,1,0:T(8,128)(2,1)}, f32[2,2,256,1536]{2,3,1,0:T(8,128)}, f32[2,256,12,2,64]{1,4,3,2,0:T(8,128)}, s32[2,256]{...) while((s32[]{:T(128)}, ...), condition=%wide.region_17.18_spmd.clone, body=%wide.region_15.17_spmd.clone.sunk | while | flops 2860131840 | bytes 203717232 | solution.py:245
  1583.9 61.9 %collective-permute-done.1 = bf16[2,2,256,1536]{2,3,1,0:T(8,128)(2,1)} collective-permute-done((bf16[2,2,256,1536]{2,3,1,0:T(8,128)(2,1)}, bf16[2,2,256,1536]{2,3,1,0:T(8,128)(2,1)}, u32[]{:S(2)}, u32[]{:S(2)}) %collective-permute-start.1) | collective-permute-done | bytes 3145760 | tf_op jit(solution)/shard_map/while/body/eval_jaxpr/ppermute | solution.py:29
  1650.9 60.7 %collective-permute-done = bf16[2,2,256,1536]{2,3,1,0:T(8,128)(2,1)} collective-permute-done((bf16[2,2,256,1536]{2,3,1,0:T(8,128)(2,1)}, bf16[2,2,256,1536]{2,3,1,0:T(8,128)(2,1)}, u32[]{:S(2)}, u32[]{:S(2)}) %collective-permute-start) | collective-permute-done | bytes 3145760 | tf_op jit(solution)/shard_map/while/body/eval_jaxpr/ppermute | solution.py:29
  1742.8 7.4 bitcast_add_fusion.3
  1750.2 61.0 %collective-permute-done.1 = bf16[2,2,256,1536]{2,3,1,0:T(8,128)(2,1)} collective-permute-done((bf16[2,2,256,1536]{2,3,1,0:T(8,128)(2,1)}, bf16[2,2,256,1536]{2,3,1,0:T(8,128)(2,1)}, u32[]{:S(2)}, u32[]{:S(2)}) %collective-permute-start.1) | collective-permute-done | bytes 3145760 | tf_op jit(solution)/shard_map/while/body/eval_jaxpr/ppermute | solution.py:29
  1816.3 59.8 %collective-permute-done = bf16[2,2,256,1536]{2,3,1,0:T(8,128)(2,1)} collective-permute-done((bf16[2,2,256,1536]{2,3,1,0:T(8,128)(2,1)}, bf16[2,2,256,1536]{2,3,1,0:T(8,128)(2,1)}, u32[]{:S(2)}, u32[]{:S(2)}) %collective-permute-start) | collective-permute-done | bytes 3145760 | tf_op jit(solution)/shard_map/while/body/eval_jaxpr/ppermute | solution.py:29
  1907.3 7.4 bitcast_add_fusion.3
  1914.7 61.0 %collective-permute-done.1 = bf16[2,2,256,1536]{2,3,1,0:T(8,128)(2,1)} collective-permute-done((bf16[2,2,256,1536]{2,3,1,0:T(8,128)(2,1)}, bf16[2,2,256,1536]{2,3,1,0:T(8,128)(2,1)}, u32[]{:S(2)}, u32[]{:S(2)}) %collective-permute-start.1) | collective-permute-done | bytes 3145760 | tf_op jit(solution)/shard_map/while/body/eval_jaxpr/ppermute | solution.py:29
  1980.8 59.4 %collective-permute-done = bf16[2,2,256,1536]{2,3,1,0:T(8,128)(2,1)} collective-permute-done((bf16[2,2,256,1536]{2,3,1,0:T(8,128)(2,1)}, bf16[2,2,256,1536]{2,3,1,0:T(8,128)(2,1)}, u32[]{:S(2)}, u32[]{:S(2)}) %collective-permute-start) | collective-permute-done | bytes 3145760 | tf_op jit(solution)/shard_map/while/body/eval_jaxpr/ppermute | solution.py:29
  2070.8 7.4 bitcast_add_fusion.3
  2078.2 62.8 %collective-permute-done.1 = bf16[2,2,256,1536]{2,3,1,0:T(8,128)(2,1)} collective-permute-done((bf16[2,2,256,1536]{2,3,1,0:T(8,128)(2,1)}, bf16[2,2,256,1536]{2,3,1,0:T(8,128)(2,1)}, u32[]{:S(2)}, u32[]{:S(2)}) %collective-permute-start.1) | collective-permute-done | bytes 3145760 | tf_op jit(solution)/shard_map/while/body/eval_jaxpr/ppermute | solution.py:29
  2146.1 58.5 %collective-permute-done = bf16[2,2,256,1536]{2,3,1,0:T(8,128)(2,1)} collective-permute-done((bf16[2,2,256,1536]{2,3,1,0:T(8,128)(2,1)}, bf16[2,2,256,1536]{2,3,1,0:T(8,128)(2,1)}, u32[]{:S(2)}, u32[]{:S(2)}) %collective-permute-start) | collective-permute-done | bytes 3145760 | tf_op jit(solution)/shard_map/while/body/eval_jaxpr/ppermute | solution.py:29
  2233.5 7.4 bitcast_add_fusion.3
  2240.8 64.6 %collective-permute-done.1 = bf16[2,2,256,1536]{2,3,1,0:T(8,128)(2,1)} collective-permute-done((bf16[2,2,256,1536]{2,3,1,0:T(8,128)(2,1)}, bf16[2,2,256,1536]{2,3,1,0:T(8,128)(2,1)}, u32[]{:S(2)}, u32[]{:S(2)}) %collective-permute-start.1) | collective-permute-done | bytes 3145760 | tf_op jit(solution)/shard_map/while/body/eval_jaxpr/ppermute | solution.py:29
  2310.6 57.5 %collective-permute-done = bf16[2,2,256,1536]{2,3,1,0:T(8,128)(2,1)} collective-permute-done((bf16[2,2,256,1536]{2,3,1,0:T(8,128)(2,1)}, bf16[2,2,256,1536]{2,3,1,0:T(8,128)(2,1)}, u32[]{:S(2)}, u32[]{:S(2)}) %collective-permute-start) | collective-permute-done | bytes 3145760 | tf_op jit(solution)/shard_map/while/body/eval_jaxpr/ppermute | solution.py:29
  2395.4 7.4 bitcast_add_fusion.3
  2402.8 66.1 %collective-permute-done.1 = bf16[2,2,256,1536]{2,3,1,0:T(8,128)(2,1)} collective-permute-done((bf16[2,2,256,1536]{2,3,1,0:T(8,128)(2,1)}, bf16[2,2,256,1536]{2,3,1,0:T(8,128)(2,1)}, u32[]{:S(2)}, u32[]{:S(2)}) %collective-permute-start.1) | collective-permute-done | bytes 3145760 | tf_op jit(solution)/shard_map/while/body/eval_jaxpr/ppermute | solution.py:29
  2474.0 56.6 %collective-permute-done = bf16[2,2,256,1536]{2,3,1,0:T(8,128)(2,1)} collective-permute-done((bf16[2,2,256,1536]{2,3,1,0:T(8,128)(2,1)}, bf16[2,2,256,1536]{2,3,1,0:T(8,128)(2,1)}, u32[]{:S(2)}, u32[]{:S(2)}) %collective-permute-start) | collective-permute-done | bytes 3145760 | tf_op jit(solution)/shard_map/while/body/eval_jaxpr/ppermute | solution.py:29
  2558.0 7.4 bitcast_add_fusion.3
  2565.4 66.1 %collective-permute-done.1 = bf16[2,2,256,1536]{2,3,1,0:T(8,128)(2,1)} collective-permute-done((bf16[2,2,256,1536]{2,3,1,0:T(8,128)(2,1)}, bf16[2,2,256,1536]{2,3,1,0:T(8,128)(2,1)}, u32[]{:S(2)}, u32[]{:S(2)}) %collective-permute-start.1) | collective-permute-done | bytes 3145760 | tf_op jit(solution)/shard_map/while/body/eval_jaxpr/ppermute | solution.py:29
  2636.6 55.7 %collective-permute-done = bf16[2,2,256,1536]{2,3,1,0:T(8,128)(2,1)} collective-permute-done((bf16[2,2,256,1536]{2,3,1,0:T(8,128)(2,1)}, bf16[2,2,256,1536]{2,3,1,0:T(8,128)(2,1)}, u32[]{:S(2)}, u32[]{:S(2)}) %collective-permute-start) | collective-permute-done | bytes 3145760 | tf_op jit(solution)/shard_map/while/body/eval_jaxpr/ppermute | solution.py:29
  2719.6 7.4 bitcast_add_fusion.3
  2727.0 66.1 %collective-permute-done.1 = bf16[2,2,256,1536]{2,3,1,0:T(8,128)(2,1)} collective-permute-done((bf16[2,2,256,1536]{2,3,1,0:T(8,128)(2,1)}, bf16[2,2,256,1536]{2,3,1,0:T(8,128)(2,1)}, u32[]{:S(2)}, u32[]{:S(2)}) %collective-permute-start.1) | collective-permute-done | bytes 3145760 | tf_op jit(solution)/shard_map/while/body/eval_jaxpr/ppermute | solution.py:29
  2798.2 54.8 %collective-permute-done = bf16[2,2,256,1536]{2,3,1,0:T(8,128)(2,1)} collective-permute-done((bf16[2,2,256,1536]{2,3,1,0:T(8,128)(2,1)}, bf16[2,2,256,1536]{2,3,1,0:T(8,128)(2,1)}, u32[]{:S(2)}, u32[]{:S(2)}) %collective-permute-start) | collective-permute-done | bytes 3145760 | tf_op jit(solution)/shard_map/while/body/eval_jaxpr/ppermute | solution.py:29
  2868.1 21.5 convolution_convert_fusion
  2906.6 12.7 fusion.19
  2919.3 13.4 convolution_convert_fusion.1
  2932.8 38.9 pad_maximum_fusion
  2974.4 882.1 %reduce-scatter.6.cloned.1.call-done = bf16[192,18432]{1,0:T(8,128)(2,1)} async-done(((bf16[1536,18432]{1,0:T(8,128)(2,1)}), bf16[192,18432]{1,0:T(8,128)(2,1)}) %reduce-scatter.6.cloned.1.call-update) | async-done | bytes 7077904 | tf_op jit(solution)/shard_map/reduce_scatter | solution.py:275
  3863.3 8.9 gather_fusion.1
  3872.2 8.4 fusion.29
  3880.7 63.8 %reduce-scatter.8.cloned.1.call-done = bf16[192,9,512]{2,0,1:T(8,128)(2,1)} async-done(((bf16[192,36,512]{2,0,1:T(8,128)(2,1)}), bf16[192,9,512]{2,0,1:T(8,128)(2,1)}) %reduce-scatter.8.cloned.1.call-update) | async-done | bytes 1769488 | tf_op jit(solution)/shard_map/reduce_scatter | solution.py:279
  3944.5 18.7 convolution_convert_fusion.3
  3963.2 18.2 copy.151
  3992.6 217.2 %reduce-scatter.10.cloned.1.call-done = bf16[192,4608]{1,0:T(8,128)(2,1)} async-done(((bf16[1536,4608]{1,0:T(8,128)(2,1)}), bf16[192,4608]{1,0:T(8,128)(2,1)}) %reduce-scatter.10.cloned.1.call-update) | async-done | bytes 1769488
  4212.5 8.3 divide_convert_fusion
  4226.5 12.2 fusion.20
  4239.9 46.1 %psum.7 = f32[3456]{0:T(1024)S(1)} all-reduce(f32[3456]{0:T(1024)S(1)} %pad_maximum_fusion.10), channel_id=1, replica_groups=mesh['batch'=4,'blk'=8] {'batch','blk'}, use_global_device_ids=true, to_apply=%region_27.28 | all-reduce | flops 3456 | bytes 27648 | tf_op jit(solution)/shard_map/psum | solution.py:259
  4291.8 10.6 fusion.49
  4314.1 106.6 %all-gather.20.cloned.1.call-done = bf16[1536,9,512]{2,0,1:T(8,128)(2,1)} async-done(((bf16[192,9,512]{2,0,1:T(8,128)(2,1)}), bf16[1536,9,512]{2,0,1:T(8,128)(2,1)}) %all-gather.20.cloned.1.call-update) | async-done | bytes 14155792 | tf_op jit(solution)/shard_map/all_gather | solution.py:297
  4420.7 17.7 fusion.39
  (435 shorter events, 454.2 us)
Async XLA Ops:
  7.2 54.7 %all-gather.8.cloned.1.call-start = ((), (), s32[]{:S(2)}) async-start(), calls=%async_computation.3 | async-start | bytes 8847360 | tf_op jit(solution)/shard_map/all_gather | solution.py:127
  10.7 438.8 %all-gather.10.cloned.1.call-start = ((), (), s32[]{:S(2)}) async-start(), calls=%async_computation.4 | async-start | bytes 21233664 | tf_op jit(solution)/shard_map/all_gather | solution.py:129
  86.0 553.4 %all-gather.14.cloned.1.call-start = ((), (), s32[]{:S(2)}) async-start(), calls=%async_computation.6 | async-start | bytes 14155776 | tf_op jit(solution)/shard_map/all_gather | solution.py:156
  86.8 372.9 %copy-start.35 = (f32[2,256]{1,0:T(2,128)}, f32[2,256]{1,0:T(2,128)S(1)}, u32[]{:S(2)}) copy-start(f32[2,256]{1,0:T(2,128)S(1)} %fusion.62) | copy-start | bytes 6148
  88.4 371.3 %copy-start.23 = (bf16[2,256,1536]{2,1,0:T(8,128)(2,1)}, bf16[2,256,1536]{2,1,0:T(8,128)(2,1)S(1)}, u32[]{:S(2)}) copy-start(bf16[2,256,1536]{2,1,0:T(8,128)(2,1)S(1)} %multiply_convert_fusion.4) | copy-start | bytes 4718596
  464.6 352.0 %all-gather.12.cloned.1.call-start = ((), (), s32[]{:S(2)}) async-start(), calls=%async_computation.5 | async-start | bytes 14155776 | tf_op jit(solution)/shard_map/all_gather | solution.py:155
  465.2 52.1 %copy-start.26 = (s32[2,256]{1,0:T(2,128)}, s32[2,256]{1,0:T(2,128)S(1)}, u32[]{:S(2)}) copy-start(s32[2,256]{1,0:T(2,128)S(1)} %fusion.59) | copy-start | bytes 6148
  466.2 97.9 %copy-start.24 = (f32[2,256,32]{1,2,0:T(8,128)}, f32[2,256,32]{1,2,0:T(8,128)S(1)}, u32[]{:S(2)}) copy-start(f32[2,256,32]{1,2,0:T(8,128)S(1)} %get-tuple-element.458) | copy-start | bytes 196612
  508.6 790.4 %all-gather.16.cloned.1.call-start = ((), (), s32[]{:S(2)}) async-start(), calls=%async_computation.7 | async-start | bytes 28311552 | tf_op jit(solution)/shard_map/all_gather | solution.py:130
  512.6 963.2 %all-gather.18.cloned.1.call-start = ((), (), s32[]{:S(2)}) async-start(), calls=%async_computation.8 | async-start | bytes 14155776 | tf_op jit(solution)/shard_map/all_gather | solution.py:131
  521.8 3334.7 %reduce-scatter.6.cloned.1.call-start = ((), (), s32[]{:S(2)}) async-start(), calls=%async_computation.9 | async-start | bytes 63700992 | tf_op jit(solution)/shard_map/reduce_scatter | solution.py:275
  553.1 9.4 copy-start.8
  570.1 246.5 %copy-start.14 = (bf16[2,256,12,2,32]{1,4,3,2,0:T(8,128)(2,1)S(1)}, bf16[2,256,12,2,32]{1,4,3,2,0:T(8,128)(2,1)}, u32[]{:S(2)}) copy-start(bf16[2,256,12,2,32]{1,4,3,2,0:T(8,128)(2,1)} %copy-done.13) | copy-start | bytes 2359300
  937.2 7.4 copy-start.20
  937.2 361.8 %copy-start.37 = (f32[1536]{0:T(1024)S(1)}, f32[1536]{0:T(1024)}, u32[]{:S(2)}) copy-start(f32[1536]{0:T(1024)} %get-tuple-element.454) | copy-start | bytes 18436
  944.6 572.3 %copy-start.44 = (f32[512]{0:T(512)}, f32[512]{0:T(512)S(1)}, u32[]{:S(2)}) copy-start(f32[512]{0:T(512)S(1)} %fusion.61) | copy-start | bytes 6148
  1534.5 8.8 slice-start.2
  1559.4 9.3 slice-start
  1559.4 9.3 slice-start.1
  1573.5 72.3 %collective-permute-start.1 = (bf16[2,2,256,1536]{2,3,1,0:T(8,128)(2,1)}, bf16[2,2,256,1536]{2,3,1,0:T(8,128)(2,1)}, u32[]{:S(2)}, u32[]{:S(2)}) collective-permute-start(bf16[2,2,256,1536]{2,3,1,0:T(8,128)(2,1)} %fusion.142), channel_id=1, source_target_pairs={{0,1},{1,2},{2,3},{3,4},{4,5},{5,6},{6,7},{7,0},{8,9},{9,10},{10,1... | collective-permute-start | bytes 9437192 | tf_op jit(solution)/shard_map/while/body/eval_jaxpr/ppermute | solution.py:29
  1574.1 137.5 %collective-permute-start = (bf16[2,2,256,1536]{2,3,1,0:T(8,128)(2,1)}, bf16[2,2,256,1536]{2,3,1,0:T(8,128)(2,1)}, u32[]{:S(2)}, u32[]{:S(2)}) collective-permute-start(bf16[2,2,256,1536]{2,3,1,0:T(8,128)(2,1)} %copy.181), channel_id=1, source_target_pairs={{0,1},{1,2},{2,3},{3,4},{4,5},{5,6},{6,7},{7,0},{8,9},{9,10},{10,1... | collective-permute-start | bytes 9437192 | tf_op jit(solution)/shard_map/while/body/eval_jaxpr/ppermute | solution.py:29
  1724.8 9.3 slice-start
  1724.8 9.3 slice-start.1
  1738.9 72.3 %collective-permute-start.1 = (bf16[2,2,256,1536]{2,3,1,0:T(8,128)(2,1)}, bf16[2,2,256,1536]{2,3,1,0:T(8,128)(2,1)}, u32[]{:S(2)}, u32[]{:S(2)}) collective-permute-start(bf16[2,2,256,1536]{2,3,1,0:T(8,128)(2,1)} %fusion.142), channel_id=1, source_target_pairs={{0,1},{1,2},{2,3},{3,4},{4,5},{5,6},{6,7},{7,0},{8,9},{9,10},{10,1... | collective-permute-start | bytes 9437192 | tf_op jit(solution)/shard_map/while/body/eval_jaxpr/ppermute | solution.py:29
  1739.4 136.6 %collective-permute-start = (bf16[2,2,256,1536]{2,3,1,0:T(8,128)(2,1)}, bf16[2,2,256,1536]{2,3,1,0:T(8,128)(2,1)}, u32[]{:S(2)}, u32[]{:S(2)}) collective-permute-start(bf16[2,2,256,1536]{2,3,1,0:T(8,128)(2,1)} %copy.181), channel_id=1, source_target_pairs={{0,1},{1,2},{2,3},{3,4},{4,5},{5,6},{6,7},{7,0},{8,9},{9,10},{10,1... | collective-permute-start | bytes 9437192 | tf_op jit(solution)/shard_map/while/body/eval_jaxpr/ppermute | solution.py:29
  1889.3 9.3 slice-start
  1889.3 9.3 slice-start.1
  1903.4 72.3 %collective-permute-start.1 = (bf16[2,2,256,1536]{2,3,1,0:T(8,128)(2,1)}, bf16[2,2,256,1536]{2,3,1,0:T(8,128)(2,1)}, u32[]{:S(2)}, u32[]{:S(2)}) collective-permute-start(bf16[2,2,256,1536]{2,3,1,0:T(8,128)(2,1)} %fusion.142), channel_id=1, source_target_pairs={{0,1},{1,2},{2,3},{3,4},{4,5},{5,6},{6,7},{7,0},{8,9},{9,10},{10,1... | collective-permute-start | bytes 9437192 | tf_op jit(solution)/shard_map/while/body/eval_jaxpr/ppermute | solution.py:29
  1903.9 136.3 %collective-permute-start = (bf16[2,2,256,1536]{2,3,1,0:T(8,128)(2,1)}, bf16[2,2,256,1536]{2,3,1,0:T(8,128)(2,1)}, u32[]{:S(2)}, u32[]{:S(2)}) collective-permute-start(bf16[2,2,256,1536]{2,3,1,0:T(8,128)(2,1)} %copy.181), channel_id=1, source_target_pairs={{0,1},{1,2},{2,3},{3,4},{4,5},{5,6},{6,7},{7,0},{8,9},{9,10},{10,1... | collective-permute-start | bytes 9437192 | tf_op jit(solution)/shard_map/while/body/eval_jaxpr/ppermute | solution.py:29
  2053.4 9.3 slice-start
  2053.4 9.3 slice-start.1
  2067.5 73.5 %collective-permute-start.1 = (bf16[2,2,256,1536]{2,3,1,0:T(8,128)(2,1)}, bf16[2,2,256,1536]{2,3,1,0:T(8,128)(2,1)}, u32[]{:S(2)}, u32[]{:S(2)}) collective-permute-start(bf16[2,2,256,1536]{2,3,1,0:T(8,128)(2,1)} %fusion.142), channel_id=1, source_target_pairs={{0,1},{1,2},{2,3},{3,4},{4,5},{5,6},{6,7},{7,0},{8,9},{9,10},{10,1... | collective-permute-start | bytes 9437192 | tf_op jit(solution)/shard_map/while/body/eval_jaxpr/ppermute | solution.py:29
  2067.5 137.1 %collective-permute-start = (bf16[2,2,256,1536]{2,3,1,0:T(8,128)(2,1)}, bf16[2,2,256,1536]{2,3,1,0:T(8,128)(2,1)}, u32[]{:S(2)}, u32[]{:S(2)}) collective-permute-start(bf16[2,2,256,1536]{2,3,1,0:T(8,128)(2,1)} %copy.181), channel_id=1, source_target_pairs={{0,1},{1,2},{2,3},{3,4},{4,5},{5,6},{6,7},{7,0},{8,9},{9,10},{10,1... | collective-permute-start | bytes 9437192 | tf_op jit(solution)/shard_map/while/body/eval_jaxpr/ppermute | solution.py:29
  2217.9 9.3 slice-start
  2217.9 9.3 slice-start.1
  2231.9 73.5 %collective-permute-start.1 = (bf16[2,2,256,1536]{2,3,1,0:T(8,128)(2,1)}, bf16[2,2,256,1536]{2,3,1,0:T(8,128)(2,1)}, u32[]{:S(2)}, u32[]{:S(2)}) collective-permute-start(bf16[2,2,256,1536]{2,3,1,0:T(8,128)(2,1)} %fusion.142), channel_id=1, source_target_pairs={{0,1},{1,2},{2,3},{3,4},{4,5},{5,6},{6,7},{7,0},{8,9},{9,10},{10,1... | collective-permute-start | bytes 9437192 | tf_op jit(solution)/shard_map/while/body/eval_jaxpr/ppermute | solution.py:29
  2231.9 136.1 %collective-permute-start = (bf16[2,2,256,1536]{2,3,1,0:T(8,128)(2,1)}, bf16[2,2,256,1536]{2,3,1,0:T(8,128)(2,1)}, u32[]{:S(2)}, u32[]{:S(2)}) collective-permute-start(bf16[2,2,256,1536]{2,3,1,0:T(8,128)(2,1)} %copy.181), channel_id=1, source_target_pairs={{0,1},{1,2},{2,3},{3,4},{4,5},{5,6},{6,7},{7,0},{8,9},{9,10},{10,1... | collective-permute-start | bytes 9437192 | tf_op jit(solution)/shard_map/while/body/eval_jaxpr/ppermute | solution.py:29
  2381.3 9.3 slice-start
  2381.3 9.3 slice-start.1
  2395.4 73.5 %collective-permute-start.1 = (bf16[2,2,256,1536]{2,3,1,0:T(8,128)(2,1)}, bf16[2,2,256,1536]{2,3,1,0:T(8,128)(2,1)}, u32[]{:S(2)}, u32[]{:S(2)}) collective-permute-start(bf16[2,2,256,1536]{2,3,1,0:T(8,128)(2,1)} %fusion.142), channel_id=1, source_target_pairs={{0,1},{1,2},{2,3},{3,4},{4,5},{5,6},{6,7},{7,0},{8,9},{9,10},{10,1... | collective-permute-start | bytes 9437192 | tf_op jit(solution)/shard_map/while/body/eval_jaxpr/ppermute | solution.py:29
  2395.4 135.2 %collective-permute-start = (bf16[2,2,256,1536]{2,3,1,0:T(8,128)(2,1)}, bf16[2,2,256,1536]{2,3,1,0:T(8,128)(2,1)}, u32[]{:S(2)}, u32[]{:S(2)}) collective-permute-start(bf16[2,2,256,1536]{2,3,1,0:T(8,128)(2,1)} %copy.181), channel_id=1, source_target_pairs={{0,1},{1,2},{2,3},{3,4},{4,5},{5,6},{6,7},{7,0},{8,9},{9,10},{10,1... | collective-permute-start | bytes 9437192 | tf_op jit(solution)/shard_map/while/body/eval_jaxpr/ppermute | solution.py:29
  2543.9 9.3 slice-start
  2543.9 9.3 slice-start.1
  2558.0 73.5 %collective-permute-start.1 = (bf16[2,2,256,1536]{2,3,1,0:T(8,128)(2,1)}, bf16[2,2,256,1536]{2,3,1,0:T(8,128)(2,1)}, u32[]{:S(2)}, u32[]{:S(2)}) collective-permute-start(bf16[2,2,256,1536]{2,3,1,0:T(8,128)(2,1)} %fusion.142), channel_id=1, source_target_pairs={{0,1},{1,2},{2,3},{3,4},{4,5},{5,6},{6,7},{7,0},{8,9},{9,10},{10,1... | collective-permute-start | bytes 9437192 | tf_op jit(solution)/shard_map/while/body/eval_jaxpr/ppermute | solution.py:29
  2558.0 134.3 %collective-permute-start = (bf16[2,2,256,1536]{2,3,1,0:T(8,128)(2,1)}, bf16[2,2,256,1536]{2,3,1,0:T(8,128)(2,1)}, u32[]{:S(2)}, u32[]{:S(2)}) collective-permute-start(bf16[2,2,256,1536]{2,3,1,0:T(8,128)(2,1)} %copy.181), channel_id=1, source_target_pairs={{0,1},{1,2},{2,3},{3,4},{4,5},{5,6},{6,7},{7,0},{8,9},{9,10},{10,1... | collective-permute-start | bytes 9437192 | tf_op jit(solution)/shard_map/while/body/eval_jaxpr/ppermute | solution.py:29
  2705.5 9.3 slice-start
  2705.5 9.3 slice-start.1
  2719.6 73.5 %collective-permute-start.1 = (bf16[2,2,256,1536]{2,3,1,0:T(8,128)(2,1)}, bf16[2,2,256,1536]{2,3,1,0:T(8,128)(2,1)}, u32[]{:S(2)}, u32[]{:S(2)}) collective-permute-start(bf16[2,2,256,1536]{2,3,1,0:T(8,128)(2,1)} %fusion.142), channel_id=1, source_target_pairs={{0,1},{1,2},{2,3},{3,4},{4,5},{5,6},{6,7},{7,0},{8,9},{9,10},{10,1... | collective-permute-start | bytes 9437192 | tf_op jit(solution)/shard_map/while/body/eval_jaxpr/ppermute | solution.py:29
  2719.6 133.4 %collective-permute-start = (bf16[2,2,256,1536]{2,3,1,0:T(8,128)(2,1)}, bf16[2,2,256,1536]{2,3,1,0:T(8,128)(2,1)}, u32[]{:S(2)}, u32[]{:S(2)}) collective-permute-start(bf16[2,2,256,1536]{2,3,1,0:T(8,128)(2,1)} %copy.181), channel_id=1, source_target_pairs={{0,1},{1,2},{2,3},{3,4},{4,5},{5,6},{6,7},{7,0},{8,9},{9,10},{10,1... | collective-permute-start | bytes 9437192 | tf_op jit(solution)/shard_map/while/body/eval_jaxpr/ppermute | solution.py:29
  2868.1 21.6 copy-start.2
  2895.1 24.3 copy-start.21
  2906.6 12.7 copy-start.22
  2906.6 26.1 slice-start.4
  2919.3 13.5 slice-start.5
  2971.7 972.8 %reduce-scatter.8.cloned.1.call-start = ((), (), s32[]{:S(2)}) async-start(), calls=%async_computation.10 | async-start | bytes 8847360 | tf_op jit(solution)/shard_map/reduce_scatter | solution.py:279
  3880.6 329.2 %reduce-scatter.10.cloned.1.call-start = ((), (), s32[]{:S(2)}) async-start(), calls=%async_computation.12 | async-start | bytes 15925248
  3981.4 439.4 %all-gather.20.cloned.1.call-start = ((), (), s32[]{:S(2)}) async-start(), calls=%async_computation.11 | async-start | bytes 15925248 | tf_op jit(solution)/shard_map/all_gather | solution.py:297
  4226.5 12.2 copy-start.7
  4226.5 12.3 copy-start.30
  4226.5 12.3 copy-start.36
  4238.8 47.2 %copy-start.40 = (f32[2,256]{1,0:T(2,128)S(1)}, f32[2,256]{1,0:T(2,128)}, u32[]{:S(2)}) copy-start(f32[2,256]{1,0:T(2,128)} %copy-done.39) | copy-start | bytes 6148
  4238.8 47.2 %copy-start.41 = (f32[3456]{0:T(1024)S(1)}, f32[3456]{0:T(1024)}, u32[]{:S(2)}) copy-start(f32[3456]{0:T(1024)} %param.25) | copy-start | bytes 41476
  4238.8 47.2 %copy-start.42 = (f32[3456]{0:T(1024)S(1)}, f32[3456]{0:T(1024)}, u32[]{:S(2)}) copy-start(f32[3456]{0:T(1024)} %param.24) | copy-start | bytes 41476
  4308.4 112.4 %copy-start.4 = (f32[192,9,512]{2,0,1:T(8,128)S(1)}, f32[192,9,512]{2,0,1:T(8,128)}, u32[]{:S(2)}) copy-start(f32[192,9,512]{2,0,1:T(8,128)} %param.19) | copy-start | bytes 10616836
  (50 other events, 135.6 us)
Sparse Core Ops, SparseCore 0:
  10.8 51.0 all-gather.7
  86.1 363.3 all-gather.9
  464.7 174.5 all-gather.13
  641.8 174.7 all-gather.11
  818.6 480.4 all-gather.15
  1301.1 174.5 all-gather.17
  2971.8 884.5 reduce-scatter.5
  3880.8 63.7 reduce-scatter.7
  3981.5 228.2 reduce-scatter.9
  4225.1 195.5 all-gather.19
where the time goes:
time: 4460 us; the launch traced here: 4450 us
  waiting for transfers between devices  3390 us (76%)
  matrix products  459 us (10%)
  local copies, waits for them, and re-layouts  285 us (6%)
  other arithmetic  225 us (5%)
  blocking collectives  46.1 us (1%)
    ppermute x16, waiting for transfers between devices, from_behind(): lax.ppermute(shard, axis, [(i, (i + by) % count) for i in range(count)])  973 us
    reduce_scatter x1, waiting for transfers between devices, local(): lax.psum_scatter(jnp.concatenate(parts, axis=1).astype(jnp.bfloat16), 'bl...  882 us
    all_gather x1, waiting for transfers between devices, local(): lax.all_gather(by_unit[:, :4 * D], 'blk', axis=0, tiled=True)  361 us
    all_gather x1, waiting for transfers between devices, local(): lax.all_gather(by_unit[:, 4 * D:4 * D + 2 * FF], 'blk', axis=0, tiled=True)  354 us
    unnamed x11, waiting for transfers between devices  217 us
    all_gather x1, waiting for transfers between devices, local(): key_piece = lax.all_gather(key_own, 'blk', axis=1, tiled=True)  161 us
    all_gather x1, waiting for transfers between devices, local(): lax.all_gather(by_unit[:, 4 * D + 2 * FF:], 'blk', axis=0, tiled=True)  154 us
    all_gather x1, waiting for transfers between devices, local(): lax.all_gather(normalized.astype(jnp.bfloat16), 'blk', axis=0, tiled=True)  107 us
  transfers between devices with their start and end apart: 26, of which 26 were waited for; matrix products, arithmetic and copies ran while one was open for 9% of the time, Pallas kernels for 0%

commit v1 on v0

--- a/solution.py
+++ b/solution.py
@@ -1,6 +1,10 @@
+import functools
+
 import jax
 import jax.numpy as jnp
 from jax import lax
+from jax.experimental import pallas as pl
+from jax.experimental.pallas import tpu as pltpu
 from jax.sharding import PartitionSpec as P
 
 D = 1536
@@ -59,8 +63,16 @@
     return jax.nn.silu(gate) * up
 
 
+def doc_ends(lengths):
+    count = lengths.shape[1]
+    ends = [lengths[:, 0]]
+    for j in range(1, count):
+        ends.append(ends[-1] + lengths[:, j])
+    return jnp.stack(ends, axis=1)
+
+
 def document_places(lengths, places):
-    ends = jnp.cumsum(lengths, axis=1)
+    ends = doc_ends(lengths)
     starts = ends - lengths
     segment = jnp.sum((places[None, :, None] >= ends[:, None, :]).astype(jnp.int32), axis=2)
     chosen = segment[:, :, None] == jnp.arange(lengths.shape[1], dtype=jnp.int32)[None, None, :]
@@ -96,13 +108,23 @@
     )
 
 
+def take_units(stacked, order):
+    parts = [lax.dynamic_slice_in_dim(stacked, order[i], 1, axis=1) for i in range(UNITS)]
+    return jnp.concatenate(parts, axis=1)
+
+
+def inverse_order(owner):
+    numbers = jnp.arange(UNITS, dtype=jnp.int32)
+    return jnp.sum(jnp.where(owner[None, :] == numbers[:, None], numbers[None, :], 0), axis=1)
+
+
 def contract_rows(left, right):
     return lax.dot_general(
         left, right, (((1,), (1,)), ((), ())), preferred_element_type=jnp.float32
     )
 
 
-def local(
+def any_mesh(
     tokens,
     cotangent,
     lengths,
@@ -125,7 +147,7 @@
     highest = lax.Precision.HIGHEST
     learn_rate = 2.0 / D**0.5
     every_slot = lax.all_gather(master.astype(jnp.bfloat16), "batch", axis=1, tiled=True)
-    by_unit = jnp.take(every_slot, unit_owner, axis=1).reshape(rows_part, UNITS * UW)
+    by_unit = take_units(every_slot, unit_owner).reshape(rows_part, UNITS * UW)
     attention_whole = lax.all_gather(by_unit[:, : 4 * D], "blk", axis=0, tiled=True)
     gate_whole = lax.all_gather(by_unit[:, 4 * D : 4 * D + 2 * FF], "blk", axis=0, tiled=True)
     down_whole = lax.all_gather(by_unit[:, 4 * D + 2 * FF :], "blk", axis=0, tiled=True)
@@ -260,7 +282,7 @@
     right_side = jnp.concatenate([projected_grad, mixed, gate_up_grad, hidden], axis=1)
     left_sides = (normed_one, middle_low, normed_two, output_grad)
     bounds = (0, 3 * D, 4 * D, 4 * D + 2 * FF, 4 * D + 3 * FF)
-    slot_order = jnp.argsort(unit_owner)
+    slot_order = inverse_order(unit_owner)
     parts = []
     for group in range(4):
         left_rows = left_sides[group]
@@ -275,7 +297,7 @@
     row_sums = lax.psum_scatter(
         jnp.concatenate(parts, axis=1).astype(jnp.bfloat16), "blk", scatter_dimension=0, tiled=True
     ).astype(jnp.float32)
-    placed = jnp.take(row_sums.reshape(rows_part, UNITS, UW), slot_order, axis=1)
+    placed = take_units(row_sums.reshape(rows_part, UNITS, UW), slot_order)
     grad_slots = lax.psum_scatter(
         placed.astype(jnp.bfloat16), "batch", scatter_dimension=1, tiled=True
     ).astype(jnp.float32)
@@ -316,6 +338,703 @@
     )
 
 
+BF = jnp.bfloat16
+F32 = jnp.float32
+TILE = 256
+HEADS = 3
+QW = HEADS * VD
+FQ = FF // 4
+VMEM_LIMIT = 56 * 2**20
+
+
+def params(**more):
+    return pltpu.CompilerParams(vmem_limit_bytes=VMEM_LIMIT, **more)
+
+
+def dot_last(left, right):
+    return lax.dot_general(left, right, (((1,), (1,)), ((), ())), preferred_element_type=F32)
+
+
+def dot_first(left, right):
+    return lax.dot_general(left, right, (((0,), (0,)), ((), ())), preferred_element_type=F32)
+
+
+def dot_plain(left, right):
+    return jnp.dot(left, right, preferred_element_type=F32)
+
+
+def swap_core(piece):
+    return lax.ppermute(piece, "batch", [(i, i ^ 1) for i in range(4)])
+
+
+def swap_y(piece):
+    return lax.ppermute(piece, "batch", [(i, i ^ 2) for i in range(4)])
+
+
+LOOP = (0, 2, 4, 6, 7, 5, 3, 1)
+
+
+def ring_up(piece):
+    return lax.ppermute(piece, "blk", [(LOOP[i], LOOP[(i + 1) % 8]) for i in range(8)])
+
+
+def ring_down(piece):
+    return lax.ppermute(piece, "blk", [(LOOP[(i + 1) % 8], LOOP[i]) for i in range(8)])
+
+
+def sum_everywhere(values):
+    values = values + swap_core(values)
+    values = values + swap_y(values)
+    for bit in (1, 2, 4):
+        values = values + lax.ppermute(values, "blk", [(i, i ^ bit) for i in range(8)])
+    return values
+
+
+def after(values, earlier):
+    return lax.optimization_barrier((values, earlier))[0]
+
+
+def ring_place(blk):
+    return jnp.where(blk % 2 == 0, blk // 2, 7 - blk // 2)
+
+
+def ring_owner(place):
+    place = place % 8
+    return jnp.where(place < 4, 2 * place, 2 * (7 - place) + 1)
+
+
+def put(whole, piece, index, axis):
+    return lax.dynamic_update_slice_in_dim(whole, jnp.expand_dims(piece, axis), index, axis)
+
+
+def batch_pieces(piece):
+    far = swap_y(piece)
+    return (piece, swap_core(piece), far, swap_core(far))
+
+
+def batch_gather(piece, me, axis):
+    pieces = batch_pieces(piece)
+    shape = piece.shape[:axis] + (4,) + piece.shape[axis:]
+    whole = jnp.zeros(shape, piece.dtype)
+    for other in range(4):
+        whole = put(whole, pieces[other], me ^ other, axis)
+    return whole
+
+
+def batch_scatter(partial, me, axis):
+    shape = partial.shape
+    split = partial.reshape(shape[:axis] + (2, 2) + shape[axis + 1 :])
+    y, core = me // 2, me % 2
+
+    def pick(array, index, at):
+        return lax.dynamic_index_in_dim(array, index, at, keepdims=False)
+
+    near = pick(split, core, axis + 1).astype(F32) + swap_core(pick(split, 1 - core, axis + 1)).astype(F32)
+    far = swap_y(pick(near, 1 - y, axis).astype(BF))
+    return pick(near, y, axis) + far.astype(F32)
+
+
+def ring_gather(shard, blk, axis):
+    half = shard.shape[axis] // 2
+    place = ring_place(blk)
+    shape = shard.shape[:axis] + (8,) + shard.shape[axis:]
+    whole = put(jnp.zeros(shape, shard.dtype), shard, blk, axis)
+    up = lax.slice_in_dim(shard, 0, half, axis=axis)
+    down = lax.slice_in_dim(shard, half, 2 * half, axis=axis)
+
+    def store(whole, piece, owner, begin):
+        starts = [0] * len(shape)
+        starts[axis] = owner
+        starts[axis + 1] = begin
+        return lax.dynamic_update_slice(whole, jnp.expand_dims(piece, axis), starts)
+
+    for step in range(1, 8):
+        up, down = ring_up(up), ring_down(down)
+        whole = store(whole, up, ring_owner(place - step), 0)
+        whole = store(whole, down, ring_owner(place + step), half)
+    return whole
+
+
+def ring_scatter(part_of, blk):
+    place = ring_place(blk)
+    up, down = part_of(ring_owner(place - 1), 0), part_of(ring_owner(place + 1), 1)
+    for step in range(1, 8):
+        up, down = ring_up(up.astype(BF)), ring_down(down.astype(BF))
+        up = up.astype(F32) + part_of(ring_owner(place - 1 - step), 0).astype(F32)
+        down = down.astype(F32) + part_of(ring_owner(place + 1 + step), 1).astype(F32)
+    return up, down
+
+
+def to_rows(tokens):
+    rows, count, width = tokens.shape
+    pieces = tokens.reshape(rows, 4, count // 4, width)
+    pieces = lax.all_to_all(pieces, "batch", 1, 0, tiled=True)
+    return lax.all_to_all(pieces.reshape(8, count // 4, width), "blk", 0, 0, tiled=True)
+
+
+def from_rows(tokens):
+    count, width = tokens.shape[1:]
+    pieces = lax.all_to_all(tokens, "blk", 0, 0, tiled=True)
+    pieces = lax.all_to_all(pieces.reshape(8, 1, count, width), "batch", 0, 1, tiled=True)
+    return pieces.reshape(2, 4 * count, width)
+
+
+def attention_pieces(me):
+    pieces = []
+    for matrix in range(4):
+        for j in range(HEADS):
+            block = HEADS * me + j
+            pieces.append((3 * matrix + block // 4, block % 4, HEADS * matrix + j))
+    return pieces
+
+
+def pick_kernel(place_ref, me_ref, own, core, far, far_core, attn_ref, ffn_ref, sems):
+    me = me_ref[0]
+    waits = []
+
+    def begin(unit, source, target, sem):
+        at = place_ref[unit]
+        for other, ref in enumerate((own, core, far, far_core)):
+
+            @pl.when(at // 9 == other)
+            def start():
+                pltpu.make_async_copy(source(ref.at[at % 9]), target, sem).start()
+
+        waits.append(pltpu.make_async_copy(source(own.at[0]), target, sem))
+
+    for i, (unit, block, packed) in enumerate(attention_pieces(me)):
+        column = pl.multiple_of(block * 128, 128)
+        begin(unit, lambda r, c=column: r.at[:, pl.ds(c, 128)], attn_ref.at[:, pl.ds(packed * 128, 128)], sems.at[i])
+    for i in range(6):
+        unit = 12 + 8 * (i // 2) + 2 * me + i % 2
+        begin(unit, lambda r: r, ffn_ref.at[:, pl.ds(i * UW, UW)], sems.at[12 + i])
+    for wait in waits:
+        wait.wait()
+
+
+def pick_units(place, me, pieces):
+    rows = pieces[0].shape[1]
+    hbm = pl.BlockSpec(memory_space=pl.ANY)
+    smem = pl.BlockSpec(memory_space=pltpu.SMEM)
+    vmem = pl.BlockSpec(memory_space=pltpu.VMEM)
+    return pl.pallas_call(
+        pick_kernel,
+        in_specs=[smem, smem, hbm, hbm, hbm, hbm],
+        out_specs=[vmem, vmem],
+        out_shape=[
+            jax.ShapeDtypeStruct((rows, 4 * QW), BF),
+            jax.ShapeDtypeStruct((rows, 6 * UW), BF),
+        ],
+        scratch_shapes=[pltpu.SemaphoreType.DMA((18,))],
+        compiler_params=params(),
+        name="pick_units",
+    )(place, me.reshape(1), *pieces)
+
+
+def place_kernel(unit_ref, me_ref, *refs):
+    attn, ffn, out_ref, sems = refs[:4], refs[4:8], refs[8], refs[9]
+    me = me_ref[0]
+    waits = []
+    for i in range(9):
+        unit = unit_ref[i]
+        of_attn = unit < 12
+        f = jnp.maximum(unit - 12, 0)
+        for q in range(4):
+            block = (unit % 3) * 4 + q
+            source = jnp.where(of_attn, block // HEADS, (f % 8) // 2) ^ me
+            column = jnp.where(
+                of_attn, (unit // 3) * QW + (block % HEADS) * 128, (f // 8) * FQ + (f % 2) * UW + q * 128
+            )
+            column = pl.multiple_of(column, 128)
+            target, sem = out_ref.at[i, :, pl.ds(q * 128, 128)], sems.at[i, q]
+            for other in range(4):
+                for mine, pieces in ((of_attn, attn), (jnp.logical_not(of_attn), ffn)):
+
+                    @pl.when(mine & (source == other))
+                    def start(ref=pieces[other], column=column, target=target, sem=sem):
+                        pltpu.make_async_copy(ref.at[:, pl.ds(column, 128)], target, sem).start()
+
+            waits.append(pltpu.make_async_copy(attn[0].at[:, pl.ds(0, 128)], target, sem))
+    for wait in waits:
+        wait.wait()
+
+
+def place_units(units, me, attn_pieces, ffn_pieces):
+    rows = attn_pieces[0].shape[0]
+    hbm = pl.BlockSpec(memory_space=pl.ANY)
+    smem = pl.BlockSpec(memory_space=pltpu.SMEM)
+    return pl.pallas_call(
+        place_kernel,
+        in_specs=[smem, smem] + [hbm] * 8,
+        out_specs=pl.BlockSpec(memory_space=pltpu.VMEM),
+        out_shape=jax.ShapeDtypeStruct((9, rows, UW), BF),
+        scratch_shapes=[pltpu.SemaphoreType.DMA((9, 4))],
+        compiler_params=params(),
+        name="place_units",
+    )(units, me.reshape(1), *attn_pieces, *ffn_pieces)
+
+
+def turn(values, cosine, sine, lane):
+    partner = jnp.where(lane % HD < HD // 2, pltpu.roll(values, 96, 1), pltpu.roll(values, 32, 1))
+    return values * cosine + partner * sine
+
+
+def project_kernel(x_ref, w_ref, gain_ref, cos_ref, sin_ref, n_ref, q_ref, k_ref, v_ref):
+    x = x_ref[...].astype(F32)
+    r = lax.rsqrt(jnp.mean(x * x, axis=-1, keepdims=True) + norm_epsilon)
+    n = (x * r * gain_ref[...]).astype(BF)
+    n_ref[...] = n
+    lane = lax.broadcasted_iota(jnp.int32, (x.shape[0], VD), 1)
+    cosine, sine = cos_ref[...], sin_ref[...]
+    out = dot_plain(n, w_ref[...])
+    for h in range(HEADS):
+        at = slice(h * VD, (h + 1) * VD)
+        q = turn(out[:, h * VD : (h + 1) * VD], cosine, sine, lane)
+        q_ref[:, at] = (q.astype(BF).astype(F32) * HD**-0.5).astype(BF)
+        k = turn(out[:, QW + h * VD : QW + (h + 1) * VD], cosine, sine, lane)
+        k_ref[:, at] = k.astype(BF)
+    v_ref[...] = out[:, 2 * QW :].astype(BF)
+
+
+def project(x, weights, gain, cosine, sine):
+    count = x.shape[0]
+    rows = lambda w: pl.BlockSpec((TILE, w), lambda i: (i, 0))
+    fixed = lambda h, w: pl.BlockSpec((h, w), lambda i: (0, 0), pipeline_mode=pl.Buffered(1))
+    narrow = jax.ShapeDtypeStruct((count, QW), BF)
+    return pl.pallas_call(
+        project_kernel,
+        grid=(count // TILE,),
+        in_specs=[rows(D), fixed(D, 3 * QW), fixed(1, D), rows(VD), rows(VD)],
+        out_specs=[rows(D), rows(QW), rows(QW), rows(QW)],
+        out_shape=[jax.ShapeDtypeStruct((count, D), BF), narrow, narrow, narrow],
+        compiler_params=params(),
+        cost_estimate=pl.CostEstimate(
+            flops=2 * count * D * 3 * QW, bytes_accessed=count * D * 6 + 6 * D * QW, transcendentals=0
+        ),
+        name="project",
+    )(x, weights, gain, cosine, sine)
+
+
+def split_halves(q):
+    lane = lax.broadcasted_iota(jnp.int32, q.shape, 1)
+    zero = jnp.zeros_like(q)
+    return jnp.concatenate([jnp.where(lane < HD, q, zero), jnp.where(lane >= HD, q, zero)], axis=0)
+
+
+def block_mask(j, i, start):
+    key = j * TILE + lax.broadcasted_iota(jnp.int32, (TILE, 2 * TILE), 0)
+    query = i * TILE + lax.broadcasted_iota(jnp.int32, (TILE, TILE), 1)
+    query = jnp.concatenate([query, query], axis=1)
+    return (key >= start) & (key <= query)
+
+
+def attend_kernel(low_ref, lam_ref, q_ref, k_ref, v_ref, start_ref, gain_ref, a_ref, maps_ref, log_ref, vt_ref):
+    i = pl.program_id(1)
+
+    @pl.when(i == 0)
+    def turn_values():
+        for j in range(vt_ref.shape[0]):
+            vt_ref[j] = v_ref[j * TILE : (j + 1) * TILE, :].astype(F32).T.astype(BF)
+
+    q = split_halves(q_ref[...])
+    start = jnp.concatenate([start_ref[...], start_ref[...]], axis=1)
+
+    def step(j, carry):
+        top, mass, total = carry
+        keys = k_ref[pl.ds(pl.multiple_of(j * TILE, TILE), TILE), :]
+        scores = jnp.where(block_mask(j, i, start), dot_last(keys, q), masked_fill)
+        new = jnp.maximum(top, jnp.max(scores, axis=0, keepdims=True))
+        shares = jnp.exp(scores - new)
+        keep = jnp.exp(top - new)
+        mass = mass * keep + jnp.sum(shares, axis=0, keepdims=True)
+        total = total * keep + dot_plain(vt_ref[j], shares.astype(BF))
+        return new, mass, total
+
+    first = (
+        jnp.full((1, 2 * TILE), masked_fill, F32),
+        jnp.zeros((1, 2 * TILE), F32),
+        jnp.zeros((VD, 2 * TILE), F32),
+    )
+    top, mass, total = lax.fori_loop(low_ref[i], i + 1, step, first)
+    maps = total / mass
+    one, two = maps[:, :TILE], maps[:, TILE:]
+    maps_ref[0, 0] = one
+    maps_ref[0, 1] = two
+    log_ref[0, 0] = top + jnp.log(mass)
+    mixed = one - lam_ref[0] * two
+    r = lax.rsqrt(jnp.mean(mixed * mixed, axis=0, keepdims=True) + norm_epsilon)
+    a_ref[...] = (mixed * r * gain_ref[...] * (1.0 - lambda_start)).T.astype(BF)
+
+
+def attend(low, lam, q, k, v, start, gain):
+    count = q.shape[0]
+    blocks = count // TILE
+    smem = pl.BlockSpec(memory_space=pltpu.SMEM)
+    return pl.pallas_call(
+        attend_kernel,
+        grid=(HEADS, blocks),
+        in_specs=[
+            smem,
+            smem,
+            pl.BlockSpec((TILE, VD), lambda h, i: (i, h)),
+            pl.BlockSpec((count, VD), lambda h, i: (0, h)),
+            pl.BlockSpec((count, VD), lambda h, i: (0, h)),
+            pl.BlockSpec((1, TILE), lambda h, i: (0, i)),
+            pl.BlockSpec((VD, 1), lambda h, i: (0, 0)),
+        ],
+        out_specs=[
+            pl.BlockSpec((TILE, VD), lambda h, i: (i, h)),
+            pl.BlockSpec((1, 2, VD, TILE), lambda h, i: (h, 0, 0, i)),
+            pl.BlockSpec((1, 1, 1, 2 * TILE), lambda h, i: (h, i, 0, 0)),
+        ],
+        out_shape=[
+            jax.ShapeDtypeStruct((count, QW), BF),
+            jax.ShapeDtypeStruct((HEADS, 2, VD, count), F32),
+            jax.ShapeDtypeStruct((HEADS, blocks, 1, 2 * TILE), F32),
+        ],
+        scratch_shapes=[pltpu.VMEM((blocks, VD, TILE), BF)],
+        compiler_params=params(),
+        cost_estimate=pl.CostEstimate(
+            flops=8 * count * count * VD * HEADS, bytes_accessed=count * QW * 16, transcendentals=count * count * HEADS
+        ),
+        name="attend",
+    )(low, lam, q, k, v, start, gain)
+
+
+def attend_back_kernel(
+    low_ref, lam_ref, q_ref, k_ref, v_ref, start_ref, gain_ref, maps_ref, log_ref, da_ref, cosq_ref, sinq_ref,
+    cosk_ref, sink_ref, dq_ref, dk_ref, dv_ref, dgain_ref, dlam_ref, kt_ref, dk_sum, dv_sum, dq_sum,
+):
+    i = pl.program_id(1)
+    blocks = kt_ref.shape[0]
+
+    @pl.when(i == 0)
+    def begin():
+        for j in range(blocks):
+            kt_ref[j] = k_ref[j * TILE : (j + 1) * TILE, :].astype(F32).T.astype(BF)
+        dk_sum[...] = jnp.zeros_like(dk_sum)
+        dv_sum[...] = jnp.zeros_like(dv_sum)
+        dgain_ref[...] = jnp.zeros_like(dgain_ref)
+        dlam_ref[...] = jnp.zeros_like(dlam_ref)
+
+    lam = lam_ref[0]
+    q = split_halves(q_ref[...])
+    start = jnp.concatenate([start_ref[...], start_ref[...]], axis=1)
+    log_mass = log_ref[0, 0]
+    one, two = maps_ref[0, 0], maps_ref[0, 1]
+    mixed = one - lam * two
+    r = lax.rsqrt(jnp.mean(mixed * mixed, axis=0, keepdims=True) + norm_epsilon)
+    t = mixed * r
+    da = da_ref[...].T * (1.0 - lambda_start)
+    dgain_ref[0] += da * t
+    e = da * gain_ref[...]
+    dmixed = r * (e - t * jnp.mean(e * t, axis=0, keepdims=True))
+    dlam_ref[0] -= jnp.sum(dmixed * two, axis=0, keepdims=True)
+    dmaps = jnp.concatenate([dmixed, -lam * dmixed], axis=1).astype(BF)
+    maps = jnp.concatenate([one, two], axis=1)
+    offset = jnp.sum(dmaps.astype(F32) * maps, axis=0, keepdims=True)
+    dq_sum[...] = jnp.zeros_like(dq_sum)
+
+    def step(j, carry):
+        at = pl.ds(pl.multiple_of(j * TILE, TILE), TILE)
+        keys, values = k_ref[at, :], v_ref[at, :]
+        scores = dot_last(keys, q)
+        shares = jnp.where(block_mask(j, i, start), jnp.exp(scores - log_mass), 0.0)
+        dshares = dot_plain(values, dmaps)
+        dscores = (shares * (dshares - offset)).astype(BF)
+        dv_sum[at, :] += dot_last(shares.astype(BF), dmaps)
+        dk_sum[at, :] += dot_plain(dscores, q)
+        dq_sum[...] += dot_plain(kt_ref[j], dscores)
+        return carry
+
+    lax.fori_loop(low_ref[i], i + 1, step, 0)
+    lane = lax.broadcasted_iota(jnp.int32, (TILE, VD), 1)
+    dq = jnp.concatenate([dq_sum[:HD, :TILE], dq_sum[HD:, TILE:]], axis=0).T * HD**-0.5
+    dq_ref[...] = turn(dq, cosq_ref[...], -sinq_ref[...], lane).astype(BF)
+
+    @pl.when(i == blocks - 1)
+    def finish():
+        for j in range(blocks):
+            at = slice(j * TILE, (j + 1) * TILE)
+            dk_ref[at, :] = turn(dk_sum[at, :], cosk_ref[at, :], -sink_ref[at, :], lane).astype(BF)
+        dv_ref[...] = dv_sum[...].astype(BF)
+
+
+def attend_back(low, lam, q, k, v, start, gain, maps, log_mass, da, cosine, sine):
+    count = q.shape[0]
+    blocks = count // TILE
+    smem = pl.BlockSpec(memory_space=pltpu.SMEM)
+    tile = pl.BlockSpec((TILE, VD), lambda h, i: (i, h))
+    whole = pl.BlockSpec((count, VD), lambda h, i: (0, h))
+    table = pl.BlockSpec((TILE, VD), lambda h, i: (i, 0))
+    full_table = pl.BlockSpec((count, VD), lambda h, i: (0, 0), pipeline_mode=pl.Buffered(1))
+    narrow = jax.ShapeDtypeStruct((count, QW), BF)
+    return pl.pallas_call(
+        attend_back_kernel,
+        grid=(HEADS, blocks),
+        in_specs=[
+            smem,
+            smem,
+            tile,
+            whole,
+            whole,
+            pl.BlockSpec((1, TILE), lambda h, i: (0, i)),
+            pl.BlockSpec((VD, 1), lambda h, i: (0, 0)),
+            pl.BlockSpec((1, 2, VD, TILE), lambda h, i: (h, 0, 0, i)),
+            pl.BlockSpec((1, 1, 1, 2 * TILE), lambda h, i: (h, i, 0, 0)),
+            tile,
+            table,
+            table,
+            full_table,
+            full_table,
+        ],
+        out_specs=[
+            tile,
+            whole,
+            whole,
+            pl.BlockSpec((1, VD, TILE), lambda h, i: (h, 0, 0)),
+            pl.BlockSpec((1, 1, TILE), lambda h, i: (h, 0, 0)),
+        ],
+        out_shape=[
+            narrow,
+            narrow,
+            narrow,
+            jax.ShapeDtypeStruct((HEADS, VD, TILE), F32),
+            jax.ShapeDtypeStruct((HEADS, 1, TILE), F32),
+        ],
+        scratch_shapes=[
+            pltpu.VMEM((blocks, VD, TILE), BF),
+            pltpu.VMEM((count, VD), F32),
+            pltpu.VMEM((count, VD), F32),
+            pltpu.VMEM((VD, 2 * TILE), F32),
+        ],
+        compiler_params=params(),
+        cost_estimate=pl.CostEstimate(
+            flops=20 * count * count * VD * HEADS, bytes_accessed=count * QW * 24, transcendentals=count * count * HEADS
+        ),
+        name="attend_back",
+    )(low, lam, q, k, v, start, gain, maps, log_mass, da, cosine, sine, cosine, sine)
+
+
+def middle_kernel(me_ref, x_ref, gain_ref, *refs):
+    a_refs, w_refs, (n_ref, own_ref, sum_ref) = refs[:4], refs[4:8], refs[8:]
+    x1 = x_ref[...].astype(F32)
+    for a_ref, w_ref in zip(a_refs, w_refs):
+        x1 += dot_last(a_ref[...], w_ref[...])
+    sum_ref[...] = x1
+    r = lax.rsqrt(jnp.mean(x1 * x1, axis=-1, keepdims=True) + norm_epsilon)
+    n_ref[...] = (x1 * r * gain_ref[...]).astype(BF)
+    part = TILE // 4
+    own_ref[0] = sum_ref[pl.ds(pl.multiple_of(me_ref[0] * part, part), part), :]
+
+
+def middle(me, a, x, weights, gain):
+    count = x.shape[0]
+    rows = pl.BlockSpec((TILE, D), lambda i: (i, 0))
+    return pl.pallas_call(
+        middle_kernel,
+        grid=(count // TILE,),
+        in_specs=[
+            pl.BlockSpec(memory_space=pltpu.SMEM),
+            rows,
+            pl.BlockSpec((1, D), lambda i: (0, 0)),
+        ]
+        + [pl.BlockSpec((TILE, QW), lambda i: (i, 0))] * 4
+        + [pl.BlockSpec((D, QW), lambda i: (0, 0), pipeline_mode=pl.Buffered(1))] * 4,
+        out_specs=[rows, pl.BlockSpec((1, TILE // 4, D), lambda i: (i, 0, 0))],
+        out_shape=[
+            jax.ShapeDtypeStruct((count, D), BF),
+            jax.ShapeDtypeStruct((count // TILE, TILE // 4, D), F32),
+        ],
+        scratch_shapes=[pltpu.VMEM((TILE, D), F32)],
+        compiler_params=params(),
+        cost_estimate=pl.CostEstimate(
+            flops=2 * count * D * D, bytes_accessed=count * D * 7 + 2 * D * D, transcendentals=0
+        ),
+        name="middle",
+    )(me.reshape(1), x, gain, *a, *weights)
+
+
+def feed_kernel(n_ref, dy_ref, w_ref, act_ref, out_ref, dn_ref):
+    n, dy = n_ref[...], dy_ref[...]
+    wg, wu, wd = w_ref[:, :FQ], w_ref[:, FQ : 2 * FQ], w_ref[:, 2 * FQ :]
+    gate = dot_plain(n, wg)
+    up = dot_plain(n, wu)
+    dhidden = dot_plain(dy, wd)
+    share = 1.0 / (1.0 + jnp.exp(-gate))
+    silu = gate * share
+    hidden = (silu * up).astype(BF)
+    dup = (dhidden * silu).astype(BF)
+    dgate = (dhidden * up * (share * (1.0 + gate * (1.0 - share)))).astype(BF)
+    act_ref[:, :FQ] = dgate
+    act_ref[:, FQ : 2 * FQ] = dup
+    act_ref[:, 2 * FQ :] = hidden
+    out_ref[...] = dot_last(hidden, wd).astype(BF)
+    dn_ref[...] = (dot_last(dgate, wg) + dot_last(dup, wu)).astype(BF)
+
+
+def feed(n, dy, weights):
+    count = n.shape[0]
+    rows = lambda w: pl.BlockSpec((TILE, w), lambda i: (i, 0))
+    shape = lambda w: jax.ShapeDtypeStruct((count, w), BF)
+    return pl.pallas_call(
+        feed_kernel,
+        grid=(count // TILE,),
+        in_specs=[rows(D), rows(D), pl.BlockSpec((D, 3 * FQ), lambda i: (0, 0), pipeline_mode=pl.Buffered(1))],
+        out_specs=[rows(3 * FQ), rows(D), rows(D)],
+        out_shape=[shape(3 * FQ), shape(D), shape(D)],
+        compiler_params=params(),
+        cost_estimate=pl.CostEstimate(
+            flops=12 * count * D * FQ, bytes_accessed=count * (8 * D + 6 * FQ) + 6 * D * FQ, transcendentals=count * FQ
+        ),
+        name="feed",
+    )(n, dy, weights)
+
+
+def row_tables(lengths, row, count):
+    everyone = jnp.stack(batch_pieces(lengths))
+    holder = (row // 2) ^ lax.axis_index("batch")
+    mine = jnp.sum(jnp.where(jnp.arange(4)[:, None, None] == holder, everyone, 0), axis=0)
+    mine = jnp.where(row % 2 == 0, mine[:1], mine[1:])
+    ends = doc_ends(mine)[0]
+    places = jnp.arange(count, dtype=jnp.int32)
+    begin = jnp.sum(jnp.where(places[:, None] >= ends[None, :], mine, 0), axis=1)
+    start = jnp.where(places >= ends[NDOC - 2], places, begin)
+    low = start.reshape(-1, TILE)[:, 0] // TILE
+    cosine, sine = turn_tables(places - begin)
+    cosine = jnp.tile(cosine, (1, 4))
+    sine = jnp.tile(jnp.concatenate([-sine, sine], axis=1), (1, 2))
+    return start, low, cosine, sine
+
+
+def row_groups(
+    tokens,
+    cotangent,
+    lengths,
+    unit_owner,
+    step_count,
+    master,
+    first,
+    second,
+    bases,
+    small,
+    small_first,
+    small_second,
+):
+    me, blk = lax.axis_index("batch"), lax.axis_index("blk")
+    count = tokens.shape[1] * 8
+    learn_rate = 2.0 / D**0.5
+    slots = lambda array: jnp.transpose(array, (1, 0, 2))
+    master_slots = slots(master)
+
+    place = ((unit_owner // 9) ^ me) * 9 + unit_owner % 9
+    attn_shard, ffn_shard = pick_units(place, me, batch_pieces(master_slots.astype(BF)))
+    attn = ring_gather(attn_shard, blk, 0).reshape(D, 4 * QW)
+    attn_out = batch_pieces(attn[:, 3 * QW :])
+    ffn_shard = after(ffn_shard, attn)
+    ffn = ring_gather(ffn_shard, blk, 0).reshape(D, 6 * UW)
+
+    x_own = to_rows(tokens)
+    dy_own = to_rows(cotangent)
+    x = batch_gather(x_own, me, 1).reshape(count, D)
+    dy = batch_gather(dy_own, me, 1).reshape(count, D)
+    start, low, cosine, sine = row_tables(lengths, blk, count)
+    start = start.reshape(1, count)
+
+    gain_one = small[:D].reshape(1, D)
+    gain_two = small[D : 2 * D].reshape(1, D)
+    head_gain = small[2 * D : 2 * D + VD].reshape(VD, 1)
+    mixer, mixer_back = jax.vjp(mix_value, small[2 * D + VD :].reshape(4, HD))
+    lam = mixer.reshape(1)
+
+    n1, q, k, v = project(x, attn, gain_one, cosine, sine)
+    a_own, maps, log_mass = attend(low, lam, q, k, v, start, head_gain)
+    a = batch_pieces(a_own)
+    n2, x1 = middle(me, a, x, attn_out, gain_two)
+    acts, out_part, dn2_part = feed(n2, dy, ffn)
+
+    groups = (8, 4, count // 32, D)
+    dn2 = batch_scatter(dn2_part.reshape(groups), me, 1)
+    r2 = lax.rsqrt(jnp.mean(x1 * x1, axis=-1, keepdims=True) + norm_epsilon)
+    t2 = x1 * r2
+    e2 = dn2 * gain_two
+    dx1 = dy_own.astype(F32) + r2 * (e2 - t2 * jnp.mean(e2 * t2, axis=-1, keepdims=True))
+    gain_two_grad = jnp.sum(dn2 * t2, axis=(0, 1))
+    dx1_low = batch_gather(dx1.astype(BF), me, 1).reshape(count, D)
+    da = dot_plain(dx1_low, attn[:, 3 * QW :])
+    dq, dk, dv, head_gain_sums, mixer_sums = attend_back(
+        low, lam, q, k, v, start, head_gain, maps, log_mass, da, cosine, sine
+    )
+    dqkv = jnp.concatenate([dq, dk, dv], axis=1)
+    dn1_part = dot_last(dqkv, attn[:, : 3 * QW]).astype(BF)
+    dn1 = batch_scatter(dn1_part.reshape(groups), me, 1)
+    x_f = x_own.astype(F32)
+    r1 = lax.rsqrt(jnp.mean(x_f * x_f, axis=-1, keepdims=True) + norm_epsilon)
+    t1 = x_f * r1
+    e1 = dn1 * gain_one
+    dx = dx1 + r1 * (e1 - t1 * jnp.mean(e1 * t1, axis=-1, keepdims=True))
+    gain_one_grad = jnp.sum(dn1 * t1, axis=(0, 1))
+    input_grad = from_rows(dx.astype(BF))
+    out = batch_scatter(out_part.reshape(groups), me, 1)
+    block_out = from_rows((x1 + out).astype(BF))
+
+    (mixers_grad,) = mixer_back(jnp.sum(mixer_sums))
+    small_local = jnp.concatenate(
+        [gain_one_grad, gain_two_grad, jnp.sum(head_gain_sums, axis=(0, 2)), mixers_grad.reshape(-1)]
+    )
+    small_grads = sum_everywhere(small_local)
+
+    part = D // 8
+
+    def scatter_rows(grad):
+        def part_of(owner, half):
+            return lax.dynamic_slice_in_dim(grad, owner * part + half * part // 2, part // 2, axis=0)
+
+        return jnp.concatenate(ring_scatter(part_of, blk), axis=0).astype(BF)
+
+    ffn_grad = jnp.concatenate(
+        [dot_first(n2, acts[:, : 2 * FQ]).astype(BF), dot_first(dy, acts[:, 2 * FQ :]).astype(BF)], axis=1
+    )
+    attn_grad = jnp.concatenate(
+        [dot_first(n1, dqkv).astype(BF), dot_first(dx1_low, a_own).astype(BF)], axis=1
+    )
+    ffn_sums = scatter_rows(ffn_grad)
+    attn_sums = scatter_rows(attn_grad)
+
+    unit_of = inverse_order(unit_owner)
+    units = lax.dynamic_slice_in_dim(unit_of, me * 9, 9)
+    grads = place_units(units, me, batch_pieces(attn_sums), batch_pieces(ffn_sums))
+
+    base = slots(bases).astype(BF)
+    turned_part = jnp.einsum("sja,sjn->san", base, grads, preferred_element_type=F32).astype(BF)
+
+    def turned_of(owner, half):
+        return lax.dynamic_slice_in_dim(turned_part, owner * part + half * part // 2, part // 2, axis=1)
+
+    turned = jnp.concatenate(ring_scatter(turned_of, blk), axis=1)
+    steps_done = step_count[0].astype(F32)
+    new_first = beta_one * slots(first) + (1.0 - beta_one) * turned
+    new_second = beta_two * slots(second) + (1.0 - beta_two) * turned * turned
+    normalized = adam_step(new_first, new_second, steps_done).astype(BF)
+    every_step = ring_gather(normalized, blk, 1).reshape(9, D, UW)
+    update = jnp.einsum("sja,san->sjn", base, every_step, preferred_element_type=F32)
+    new_master = master_slots - learn_rate * (update + weight_decay * master_slots)
+    new_small_first = beta_one * small_first + (1.0 - beta_one) * small_grads
+    new_small_second = beta_two * small_second + (1.0 - beta_two) * small_grads * small_grads
+    new_small = small - small_rate * adam_step(new_small_first, new_small_second, steps_done)
+    return (
+        block_out,
+        input_grad,
+        slots(new_master),
+        slots(new_first),
+        slots(new_second),
+        small_grads,
+        new_small,
+        new_small_first,
+        new_small_second,
+    )
+
+
 def solution(mesh):
     in_specs = (
         P("batch", "blk", None),
@@ -342,4 +1061,6 @@
         P(),
         P(),
     )
-    return jax.shard_map(local, mesh=mesh, in_specs=in_specs, out_specs=out_specs, check_vma=False)
+    by_rows = mesh.shape["blk"] == 8 and mesh.shape["batch"] == 4
+    body = row_groups if by_rows else any_mesh
+    return jax.shard_map(body, mesh=mesh, in_specs=in_specs, out_specs=out_specs, check_vma=False)

time: 4460 us -> 1430 us (0.32)
  waiting for transfers between devices: 3390 us -> 713 us
  matrix products: 459 us -> 85 us
  Pallas kernels: 0 us -> 185 us
  local copies, waits for them, and re-layouts: 285 us -> 127 us
  starting transfers between devices: 17.4 us -> 152 us
  other arithmetic: 225 us -> 123 us
    all_gather x7 -> x0, waiting for transfers between devices: 1260 us -> none  [the longest x1 361 us: local(): lax.all_gather(by_unit[:, :4 * D], 'blk', axis=0, tiled=True)]
    reduce_scatter x2 -> x0, waiting for transfers between devices: 946 us -> none  [the longest x1 882 us: local(): lax.psum_scatter(jnp.concatenate(parts, axis=1).astype(jnp.bfloat16), 'bl...]
    dot_general x56 -> x8, matrix products: 459 us -> 85 us  [the longest x4 44.1 us: dot_first(): lax.dot_general(left, right, (((0,), (0,)), ((), ())), preferred_element_...]
    ppermute x16 -> x122, waiting for transfers between devices: 973 us -> 695 us  [the longest x42 312 us: ring_up(): lax.ppermute(piece, 'blk', [(LOOP[i], LOOP[(i + 1) % 8]) for i in range(8)])]
    unnamed x11 -> x0, waiting for transfers between devices: 217 us -> none
    pallas_call x0 -> x7, Pallas kernels: none -> 185 us  [the longest x1 52.8 us: attend_back(): pl.pallas_call(attend_back_kernel, grid=(HEADS, blocks), in_specs=[smem,...]
    ppermute x16 -> x122, starting transfers between devices: 16.5 us -> 115 us  [the longest x42 48 us: ring_down(): lax.ppermute(piece, 'blk', [(LOOP[(i + 1) % 8], LOOP[i]) for i in range(8)])]
    unnamed x123 -> x136, local copies, waits for them, and re-layouts: 91.7 us -> 15.4 us
  transfers between devices with their start and end apart: 26 -> 129, of which waited for: 26 -> 74; matrix products, arithmetic and copies ran while one was open for 9% -> 20% of each run, Pallas kernels for 0% -> 8%
where the time goes in v1:
time: 1430 us; the launch traced here: 1420 us
  waiting for transfers between devices  713 us (50%)
  Pallas kernels  185 us (13%)
  starting transfers between devices  152 us (11%)
  local copies, waits for them, and re-layouts  127 us (9%)
  other arithmetic  123 us (9%)
  matrix products  85 us (6%)
  blocking collectives  23.2 us (2%)
    ppermute x42, waiting for transfers between devices, ring_up(): lax.ppermute(piece, 'blk', [(LOOP[i], LOOP[(i + 1) % 8]) for i in range(8)])  312 us
    ppermute x42, waiting for transfers between devices, ring_down(): lax.ppermute(piece, 'blk', [(LOOP[(i + 1) % 8], LOOP[i]) for i in range(8)])  243 us
    ppermute x13, waiting for transfers between devices, swap_y(): return lax.ppermute(piece, 'batch', [(i, i ^ 2) for i in range(4)])  133 us
    pallas_call x1, Pallas kernels, attend_back(): pl.pallas_call(attend_back_kernel, grid=(HEADS, blocks), in_specs=[smem,...  52.8 us
    convert_element_type x28, other arithmetic, ring_scatter(): up, down = (ring_up(up.astype(BF)), ring_down(down.astype(BF)))  50.8 us
    ppermute x42, starting transfers between devices, ring_down(): lax.ppermute(piece, 'blk', [(LOOP[(i + 1) % 8], LOOP[i]) for i in range(8)])  48 us
    pallas_call x1, Pallas kernels, feed(): pl.pallas_call(feed_kernel, grid=(count // TILE,), in_specs=[rows(D), row...  47.7 us
    dot_general x4, matrix products, dot_first(): lax.dot_general(left, right, (((0,), (0,)), ((), ())), preferred_element_...  44.1 us
  transfers between devices with their start and end apart: 129, of which 74 were waited for; matrix products, arithmetic and copies ran while one was open for 20% of the time, Pallas kernels for 8%

profile of v1, /device:TPU:12, one launch (start us, length us, event | category | flops | bytes accessed | tf_op | source)
XLA Modules:
  0.0 1416.7 jit_solution(698898097536070678)
XLA Ops:
  8.4 18.4 %all-to-all-done = bf16[2,4,64,1536]{3,2,0,1:T(8,128)(2,1)} async-done(((bf16[2,4,64,1536]{3,2,0,1:T(8,128)(2,1)}), bf16[2,4,64,1536]{3,2,0,1:T(8,128)(2,1)}, u32[]{:S(2)}, u32[]{:S(2)}) %all-to-all-start) | async-done | bytes 1572896 | tf_op jit(solution)/shard_map/all_to_all | solution.py:471
  26.8 23.2 %all_to_all.80 = bf16[2,4,64,1536]{3,2,0,1:T(8,128)(2,1)} all-to-all(bf16[2,4,64,1536]{3,2,0,1:T(8,128)(2,1)S(1)} %copy.306), channel_id=1, replica_groups=mesh['batch'=4,'blk'=8] {'batch'}, dimensions={1} | all-to-all | bytes 3145728 | tf_op jit(solution)/shard_map/all_to_all | solution.py:471
  50.0 6.4 all-to-all-start.1
  66.7 33.4 %collective-permute-done.4 = s32[2,6]{1,0:T(2,128)S(1)} collective-permute-done((s32[2,6]{1,0:T(2,128)S(1)}, s32[2,6]{1,0:T(2,128)S(1)}, u32[]{:S(2)}, u32[]{:S(2)}) %collective-permute-start.4) | collective-permute-done | bytes 80 | tf_op jit(solution)/shard_map/ppermute | solution.py:371
  108.8 6.0 all-to-all-start.3
  133.6 22.5 %collective-permute-done.9 = bf16[96,1536]{1,0:T(8,128)(2,1)} collective-permute-done((bf16[96,1536]{1,0:T(8,128)(2,1)S(1)}, bf16[96,1536]{1,0:T(8,128)(2,1)}, u32[]{:S(2)}, u32[]{:S(2)}) %collective-permute-start.9) | collective-permute-done | bytes 294944 | tf_op jit(solution)/shard_map/ppermute | solution.py:378
  173.7 6.6 collective-permute-done.13
  180.7 8.8 collective-permute-done.14
  191.2 6.4 collective-permute-done.15
  198.2 6.8 collective-permute-done.16
  226.1 7.9 collective-permute-done.20
  253.9 9.2 collective-permute-done.32
  265.1 13.0 collective-permute-done.33
  279.7 12.6 collective-permute-done.34
  294.3 11.3 collective-permute-done.35
  311.4 14.9 %project.1 = (bf16[2048,1536]{1,0:T(8,128)(2,1)}, bf16[2048,384]{1,0:T(8,128)(2,1)}, bf16[2048,384]{1,0:T(8,128)(2,1)}, bf16[2048,384]{1,0:T(8,128)(2,1)}) custom-call(bf16[2048,1536]{1,0:T(8,128)(2,1)} %bitcast.13.x_ref, bf16[1536,1536]{1,0:T(8,128)(2,1)} %bitcast.387, f32[1,1536]{1,0:T(1,128)} %reshape.230.gain_ref, ...), custom_call_target="tpu_custom_call" | custom-call | flops 7247757312 | bytes 22413312 | tf_op jit(solution)/shard_map/project/pallas_call | solution.py:604
  326.3 41.5 %attend.1 = (bf16[2048,384]{1,0:T(8,128)(2,1)}, f32[3,2,128,2048]{3,2,1,0:T(8,128)}, f32[3,8,1,512]{3,2,1,0:T(1,128)}) custom-call(s32[8]{0:T(128)} %and_select_fusion.2.low_ref, f32[1]{0:T(128)} %bitcast.21.lam_ref, bf16[2048,384]{1,0:T(8,128)(2,1)} %get-tuple-element.30.q_ref, bf16[2048,384]{1,0:T(8,128)(2,1)} %get-tuple-element.31.k_ref, ...), custom_call_target="tpu_custom_call" | custom-call | flops 12884901888 | bytes 12582912 | tf_op jit(solution)/shard_map/attend/pallas_call | solution.py:673
  373.8 14.8 %collective-permute-done.38 = bf16[96,3072]{1,0:T(8,128)(2,1)S(1)} collective-permute-done((bf16[96,3072]{1,0:T(8,128)(2,1)}, bf16[96,3072]{1,0:T(8,128)(2,1)S(1)}, u32[]{:S(2)}, u32[]{:S(2)}) %collective-permute-start.38) | collective-permute-done | bytes 589856 | tf_op jit(solution)/shard_map/ppermute | solution.py:378
  390.7 12.6 collective-permute-done.39
  404.8 12.5 collective-permute-done.40
  419.9 10.5 collective-permute-done.41
  433.3 9.5 collective-permute-done.42
  445.4 14.0 collective-permute-done.44
  462.0 11.8 collective-permute-done.45
  476.9 20.2 %middle.1 = (bf16[2048,1536]{1,0:T(8,128)(2,1)}, f32[8,64,1536]{2,1,0:T(8,128)}) custom-call(s32[1]{0:T(128)} %bitcast.me_ref, bf16[2048,1536]{1,0:T(8,128)(2,1)} %bitcast.13.x_ref, f32[1,1536]{1,0:T(1,128)} %reshape.227.gain_ref, bf16[2048,384]{1,0:T(8,128)(2,1)} %get-tuple-element.33.refs_0_, bf16[2048,384]{1,0:T(8,128)(2,1)} %copy-done.51, ...), custom_call_target="tpu_custom_call" | custom-call | flops 9663676416 | bytes 26738688 | tf_op jit(solution)/shard_map/middle/pallas_call | solution.py:834
  497.1 47.7 %feed.1 = (bf16[2048,3072]{1,0:T(8,128)(2,1)}, bf16[2048,1536]{1,0:T(8,128)(2,1)}, bf16[2048,1536]{1,0:T(8,128)(2,1)}) custom-call(bf16[2048,1536]{1,0:T(8,128)(2,1)} %get-tuple-element.35.n_ref, bf16[2048,1536]{1,0:T(8,128)(2,1)} %bitcast.397, bf16[1536,3072]{1,0:T(8,128)(2,1)} %bitcast.71.w_ref), custom_call_target="tpu_custom_call" | custom-call | flops 38654705664 | bytes 47185920 | tf_op jit(solution)/shard_map/feed/pallas_call | solution.py:880
  552.7 17.8 %fusion.2 = bf16[1536,2048]{1,0:T(8,128)(2,1)S(1)} fusion(bf16[2048,1536]{1,0:T(8,128)(2,1)} %get-tuple-element.35.n_ref, bf16[2048,3072]{1,0:T(8,128)(2,1)} %get-tuple-element.46), kind=kOutput, calls=%fused_computation.51 | convolution fusion | flops 12888047616 | bytes 20971520 | tf_op jit(solution)/shard_map/dot_general | solution.py:359
  570.5 10.3 fusion.13
  598.3 12.3 collective-permute-done.72
  613.5 10.5 collective-permute-done.47
  624.0 32.8 %collective-permute-done.49 = bf16[8,64,1536]{2,1,0:T(8,128)(2,1)} collective-permute-done((bf16[8,64,1536]{2,1,0:T(8,128)(2,1)}, bf16[8,64,1536]{2,1,0:T(8,128)(2,1)}, u32[]{:S(2)}, u32[]{:S(2)}) %collective-permute-start.49) | collective-permute-done | bytes 1572896 | tf_op jit(solution)/shard_map/ppermute | solution.py:371
  656.8 6.2 multiply_reduce_fusion
  676.1 31.6 %collective-permute-done.51 = bf16[8,64,1536]{2,1,0:T(8,128)(2,1)} collective-permute-done((bf16[8,64,1536]{2,1,0:T(8,128)(2,1)}, bf16[8,64,1536]{2,1,0:T(8,128)(2,1)}, u32[]{:S(2)}, u32[]{:S(2)}) %collective-permute-start.51) | collective-permute-done | bytes 1572896 | tf_op jit(solution)/shard_map/ppermute | solution.py:371
  713.3 7.3 fusion.87.da_ref
  720.6 52.8 %attend_back.1 = (bf16[2048,384]{1,0:T(8,128)(2,1)}, bf16[2048,384]{1,0:T(8,128)(2,1)}, bf16[2048,384]{1,0:T(8,128)(2,1)}, f32[3,128,256]{2,1,0:T(8,128)}, f32[3,1,256]{2,1,0:T(1,128)}) custom-call(s32[8]{0:T(128)} %and_select_fusion.2.low_ref, f32[1]{0:T(128)} %bitcast.21.lam_ref, bf16[2048,384]{1,0:T(8,128)(2,1)} %get-tuple-element.30.q_ref, ...), custom_call_target="tpu_custom_call" | custom-call | flops 32212254720 | bytes 18874368 | tf_op jit(solution)/shard_map/attend_back/pallas_call | solution.py:772
  776.2 12.5 convolution_convert_fusion.1
  795.8 7.6 collective-permute-done.55
  805.1 10.9 collective-permute-done.76
  824.1 10.9 collective-permute-done.77
  843.0 10.9 collective-permute-done.78
  861.9 9.1 collective-permute-done.80
  877.1 9.4 collective-permute-done.81
  894.2 11.0 collective-permute-done.82
  915.4 8.8 collective-permute-done.83
  934.1 9.1 collective-permute-done.84
  952.4 8.9 collective-permute-done.85
  976.1 7.0 collective-permute-done.67
  985.7 6.0 collective-permute-done.87.refs_6_
  992.5 15.2 %collective-permute-done.70.refs_2_ = bf16[192,1536]{1,0:T(8,128)(2,1)S(1)} collective-permute-done((bf16[192,1536]{1,0:T(8,128)(2,1)S(1)}, bf16[192,1536]{1,0:T(8,128)(2,1)S(1)}, u32[]{:S(2)}, u32[]{:S(2)}) %collective-permute-start.70) | collective-permute-done | bytes 589856 | tf_op jit(solution)/shard_map/ppermute | solution.py:371
  1014.1 10.2 convolution_convert_fusion
  1028.0 10.2 convolution_convert_fusion.2
  1040.9 6.8 collective-permute-done.89
  1052.0 18.6 %collective-permute-done.90 = bf16[9,96,512]{2,1,0:T(8,128)(2,1)S(1)} collective-permute-done((bf16[9,96,512]{2,1,0:T(8,128)(2,1)S(1)}, bf16[9,96,512]{2,1,0:T(8,128)(2,1)S(1)}, u32[]{:S(2)}, u32[]{:S(2)}) %collective-permute-start.90) | collective-permute-done | bytes 884768 | tf_op jit(solution)/shard_map/ppermute | solution.py:378
  1076.1 17.3 %collective-permute-done.91 = bf16[9,96,512]{2,1,0:T(8,128)(2,1)S(1)} collective-permute-done((bf16[9,96,512]{2,1,0:T(8,128)(2,1)S(1)}, bf16[9,96,512]{2,1,0:T(8,128)(2,1)S(1)}, u32[]{:S(2)}, u32[]{:S(2)}) %collective-permute-start.91) | collective-permute-done | bytes 884768 | tf_op jit(solution)/shard_map/ppermute | solution.py:378
  1107.4 17.4 %collective-permute-done.92 = bf16[9,96,512]{2,1,0:T(8,128)(2,1)} collective-permute-done((bf16[9,96,512]{2,1,0:T(8,128)(2,1)}, bf16[9,96,512]{2,1,0:T(8,128)(2,1)}, u32[]{:S(2)}, u32[]{:S(2)}) %collective-permute-start.92) | collective-permute-done | bytes 884768 | tf_op jit(solution)/shard_map/ppermute | solution.py:378
  1132.1 37.3 %collective-permute-done.100 = bf16[9,96,512]{2,1,0:T(8,128)(2,1)S(1)} collective-permute-done((bf16[9,96,512]{2,1,0:T(8,128)(2,1)S(1)}, bf16[9,96,512]{2,1,0:T(8,128)(2,1)S(1)}, u32[]{:S(2)}, u32[]{:S(2)}) %collective-permute-start.100) | collective-permute-done | bytes 884768 | tf_op jit(solution)/shard_map/ppermute | solution.py:382
  1184.1 6.4 collective-permute-done.101
  1199.2 10.5 collective-permute-done.102
  1217.3 6.7 broadcast_in_dim.296
  1231.5 33.2 %collective-permute-done.103 = bf16[9,96,512]{2,1,0:T(8,128)(2,1)S(1)} collective-permute-done((bf16[9,96,512]{2,1,0:T(8,128)(2,1)S(1)}, bf16[9,96,512]{2,1,0:T(8,128)(2,1)S(1)}, u32[]{:S(2)}, u32[]{:S(2)}) %collective-permute-start.103) | collective-permute-done | bytes 884768 | tf_op jit(solution)/shard_map/ppermute | solution.py:378
  1267.2 17.1 %collective-permute-done.105 = bf16[9,96,512]{2,1,0:T(8,128)(2,1)} collective-permute-done((bf16[9,96,512]{2,1,0:T(8,128)(2,1)S(1)}, bf16[9,96,512]{2,1,0:T(8,128)(2,1)}, u32[]{:S(2)}, u32[]{:S(2)}) %collective-permute-start.105) | collective-permute-done | bytes 884768 | tf_op jit(solution)/shard_map/ppermute | solution.py:378
  1314.9 7.0 collective-permute-start.120
  1332.6 7.5 fusion.65
  1403.4 13.1 fusion.19
  (523 shorter events, 466.6 us)
Async XLA Ops:
  3.4 23.4 %all-to-all-start = ((bf16[2,4,64,1536]{3,2,0,1:T(8,128)(2,1)}), bf16[2,4,64,1536]{3,2,0,1:T(8,128)(2,1)}, u32[]{:S(2)}, u32[]{:S(2)}) async-start(bf16[2,4,64,1536]{3,2,0,1:T(8,128)(2,1)} %copy.298), calls=%async_computation | async-start | bytes 3145728 | tf_op jit(solution)/shard_map/all_to_all | solution.py:471
  50.0 58.8 %all-to-all-start.1 = ((bf16[8,64,1536]{2,1,0:T(8,128)(2,1)}), bf16[8,64,1536]{2,1,0:T(8,128)(2,1)S(1)}, u32[]{:S(2)}, u32[]{:S(2)}) async-start(bf16[8,64,1536]{2,1,0:T(8,128)(2,1)} %bitcast.4), calls=%async_computation.1 | async-start | bytes 3145728 | tf_op jit(solution)/shard_map/all_to_all | solution.py:472
  59.9 46.7 %collective-permute-start.7 = (bf16[9,192,512]{2,1,0:T(8,128)(2,1)}, bf16[9,192,512]{2,1,0:T(8,128)(2,1)}, u32[]{:S(2)}, u32[]{:S(2)}) collective-permute-start(bf16[9,192,512]{2,1,0:T(8,128)(2,1)} %convert_bitcast_fusion.own), channel_id=1, source_target_pairs={{0,16},{8,24},{16,0},{24,8},{1,17},{9,25},{17,1},{25,9},{2,18},{10... | collective-permute-start | bytes 5308424 | tf_op jit(solution)/shard_map/ppermute | solution.py:371
  61.6 64.7 %collective-permute-start.6 = (bf16[9,192,512]{2,1,0:T(8,128)(2,1)}, bf16[9,192,512]{2,1,0:T(8,128)(2,1)}, u32[]{:S(2)}, u32[]{:S(2)}) collective-permute-start(bf16[9,192,512]{2,1,0:T(8,128)(2,1)} %convert_bitcast_fusion.own), channel_id=1, source_target_pairs={{0,8},{8,0},{16,24},{24,16},{1,9},{9,1},{17,25},{25,17},{2,10},{10... | collective-permute-start | bytes 5308424 | tf_op jit(solution)/shard_map/ppermute | solution.py:367
  61.6 38.5 %collective-permute-start.4 = (s32[2,6]{1,0:T(2,128)S(1)}, s32[2,6]{1,0:T(2,128)S(1)}, u32[]{:S(2)}, u32[]{:S(2)}) collective-permute-start(s32[2,6]{1,0:T(2,128)S(1)} %copy-done.48), channel_id=1, source_target_pairs={{0,16},{8,24},{16,0},{24,8},{1,17},{9,25},{17,1},{25,9},{2,18},{10... | collective-permute-start | bytes 152 | tf_op jit(solution)/shard_map/ppermute | solution.py:371
  61.9 38.1 %collective-permute-start.3 = (s32[2,6]{1,0:T(2,128)S(1)}, s32[2,6]{1,0:T(2,128)S(1)}, u32[]{:S(2)}, u32[]{:S(2)}) collective-permute-start(s32[2,6]{1,0:T(2,128)S(1)} %copy-done.48), channel_id=1, source_target_pairs={{0,8},{8,0},{16,24},{24,16},{1,9},{9,1},{17,25},{25,17},{2,10},{10... | collective-permute-start | bytes 152 | tf_op jit(solution)/shard_map/ppermute | solution.py:367
  106.6 19.6 %collective-permute-start.8 = (bf16[9,192,512]{2,1,0:T(8,128)(2,1)}, bf16[9,192,512]{2,1,0:T(8,128)(2,1)}, u32[]{:S(2)}, u32[]{:S(2)}) collective-permute-start(bf16[9,192,512]{2,1,0:T(8,128)(2,1)} %collective-permute-done.7.far), channel_id=1, source_target_pairs={{0,8},{8,0},{16,24},{24,16},{1,9},{9,1},{17,25},{25,17},{2,10},{10... | collective-permute-start | bytes 5308424 | tf_op jit(solution)/shard_map/ppermute | solution.py:367
  108.8 54.4 %all-to-all-start.3 = ((bf16[8,64,1536]{2,1,0:T(8,128)(2,1)}), bf16[8,64,1536]{2,1,0:T(8,128)(2,1)S(1)}, u32[]{:S(2)}, u32[]{:S(2)}) async-start(bf16[8,64,1536]{2,1,0:T(8,128)(2,1)} %bitcast.401), calls=%async_computation.3 | async-start | bytes 3145728 | tf_op jit(solution)/shard_map/all_to_all | solution.py:472
  131.0 25.0 %collective-permute-start.9 = (bf16[96,1536]{1,0:T(8,128)(2,1)S(1)}, bf16[96,1536]{1,0:T(8,128)(2,1)}, u32[]{:S(2)}, u32[]{:S(2)}) collective-permute-start(bf16[96,1536]{1,0:T(8,128)(2,1)S(1)} %get-tuple-element.147), channel_id=1, source_target_pairs={{0,2},{2,4},{4,6},{6,7},{7,5},{5,3},{3,1},{1,0},{8,10},{10,12},{12... | collective-permute-start | bytes 884744 | tf_op jit(solution)/shard_map/ppermute | solution.py:378
  132.5 26.1 %collective-permute-start.10 = (bf16[96,1536]{1,0:T(8,128)(2,1)S(1)}, bf16[96,1536]{1,0:T(8,128)(2,1)S(1)}, u32[]{:S(2)}, u32[]{:S(2)}) collective-permute-start(bf16[96,1536]{1,0:T(8,128)(2,1)S(1)} %get-tuple-element.146), channel_id=1, source_target_pairs={{2,0},{4,2},{6,4},{7,6},{5,7},{3,5},{1,3},{0,1},{10,8},{12,10},{14... | collective-permute-start | bytes 884744 | tf_op jit(solution)/shard_map/ppermute | solution.py:382
  159.7 75.5 %collective-permute-start = (bf16[8,64,1536]{2,1,0:T(8,128)(2,1)S(1)}, bf16[8,64,1536]{2,1,0:T(8,128)(2,1)}, u32[]{:S(2)}, u32[]{:S(2)}) collective-permute-start(bf16[8,64,1536]{2,1,0:T(8,128)(2,1)S(1)} %all-to-all-done.1), channel_id=1, source_target_pairs={{0,8},{8,0},{16,24},{24,16},{1,9},{9,1},{17,25},{25,17},{2,10},{10... | collective-permute-start | bytes 4718600 | tf_op jit(solution)/shard_map/ppermute | solution.py:367
  161.9 74.2 %collective-permute-start.1 = (bf16[8,64,1536]{2,1,0:T(8,128)(2,1)S(1)}, bf16[8,64,1536]{2,1,0:T(8,128)(2,1)}, u32[]{:S(2)}, u32[]{:S(2)}) collective-permute-start(bf16[8,64,1536]{2,1,0:T(8,128)(2,1)S(1)} %all-to-all-done.1), channel_id=1, source_target_pairs={{0,16},{8,24},{16,0},{24,8},{1,17},{9,25},{17,1},{25,9},{2,18},{10... | collective-permute-start | bytes 4718600 | tf_op jit(solution)/shard_map/ppermute | solution.py:371
  163.2 78.8 %collective-permute-start.29 = (bf16[8,64,1536]{2,1,0:T(8,128)(2,1)S(1)}, bf16[8,64,1536]{2,1,0:T(8,128)(2,1)S(1)}, u32[]{:S(2)}, u32[]{:S(2)}) collective-permute-start(bf16[8,64,1536]{2,1,0:T(8,128)(2,1)S(1)} %all-to-all-done.3), channel_id=1, source_target_pairs={{0,8},{8,0},{16,24},{24,16},{1,9},{9,1},{17,25},{25,17},{2,10},{10... | collective-permute-start | bytes 4718600 | tf_op jit(solution)/shard_map/ppermute | solution.py:367
  168.8 67.3 %collective-permute-start.30 = (bf16[8,64,1536]{2,1,0:T(8,128)(2,1)S(1)}, bf16[8,64,1536]{2,1,0:T(8,128)(2,1)}, u32[]{:S(2)}, u32[]{:S(2)}) collective-permute-start(bf16[8,64,1536]{2,1,0:T(8,128)(2,1)S(1)} %all-to-all-done.3), channel_id=1, source_target_pairs={{0,16},{8,24},{16,0},{24,8},{1,17},{9,25},{17,1},{25,9},{2,18},{10... | collective-permute-start | bytes 4718600 | tf_op jit(solution)/shard_map/ppermute | solution.py:371
  236.1 74.0 %collective-permute-start.2 = (bf16[8,64,1536]{2,1,0:T(8,128)(2,1)}, bf16[8,64,1536]{2,1,0:T(8,128)(2,1)S(1)}, u32[]{:S(2)}, u32[]{:S(2)}) collective-permute-start(bf16[8,64,1536]{2,1,0:T(8,128)(2,1)} %collective-permute-done.1), channel_id=1, source_target_pairs={{0,8},{8,0},{16,24},{24,16},{1,9},{9,1},{17,25},{25,17},{2,10},{10... | collective-permute-start | bytes 4718600 | tf_op jit(solution)/shard_map/ppermute | solution.py:367
  236.1 131.7 %collective-permute-start.31 = (bf16[8,64,1536]{2,1,0:T(8,128)(2,1)}, bf16[8,64,1536]{2,1,0:T(8,128)(2,1)S(1)}, u32[]{:S(2)}, u32[]{:S(2)}) collective-permute-start(bf16[8,64,1536]{2,1,0:T(8,128)(2,1)} %collective-permute-done.30), channel_id=1, source_target_pairs={{0,8},{8,0},{16,24},{24,16},{1,9},{9,1},{17,25},{25,17},{2,10},{10... | collective-permute-start | bytes 4718600 | tf_op jit(solution)/shard_map/ppermute | solution.py:367
  246.6 61.7 %collective-permute-start.27 = (bf16[1536,384]{1,0:T(8,128)(2,1)S(1)}, bf16[1536,384]{1,0:T(8,128)(2,1)}, u32[]{:S(2)}, u32[]{:S(2)}) collective-permute-start(bf16[1536,384]{1,0:T(8,128)(2,1)S(1)} %slice.117.refs_4_), channel_id=1, source_target_pairs={{0,16},{8,24},{16,0},{24,8},{1,17},{9,25},{17,1},{25,9},{2,18},{10... | collective-permute-start | bytes 3538952 | tf_op jit(solution)/shard_map/ppermute | solution.py:371
  247.2 227.4 %collective-permute-start.26 = (bf16[1536,384]{1,0:T(8,128)(2,1)S(1)}, bf16[1536,384]{1,0:T(8,128)(2,1)}, u32[]{:S(2)}, u32[]{:S(2)}) collective-permute-start(bf16[1536,384]{1,0:T(8,128)(2,1)S(1)} %slice.117.refs_4_), channel_id=1, source_target_pairs={{0,8},{8,0},{16,24},{24,16},{1,9},{9,1},{17,25},{25,17},{2,10},{10... | collective-permute-start | bytes 3538952 | tf_op jit(solution)/shard_map/ppermute | solution.py:367
  305.7 65.0 %collective-permute-start.36 = (bf16[96,3072]{1,0:T(8,128)(2,1)S(1)}, bf16[96,3072]{1,0:T(8,128)(2,1)}, u32[]{:S(2)}, u32[]{:S(2)}) collective-permute-start(bf16[96,3072]{1,0:T(8,128)(2,1)S(1)} %collective-permute-done.34), channel_id=1, source_target_pairs={{0,2},{2,4},{4,6},{6,7},{7,5},{5,3},{3,1},{1,0},{8,10},{10,12},{12... | collective-permute-start | bytes 1769480 | tf_op jit(solution)/shard_map/ppermute | solution.py:378
  308.3 64.5 %collective-permute-start.37 = (bf16[96,3072]{1,0:T(8,128)(2,1)}, bf16[96,3072]{1,0:T(8,128)(2,1)S(1)}, u32[]{:S(2)}, u32[]{:S(2)}) collective-permute-start(bf16[96,3072]{1,0:T(8,128)(2,1)} %collective-permute-done.35), channel_id=1, source_target_pairs={{2,0},{4,2},{6,4},{7,6},{5,7},{3,5},{1,3},{0,1},{10,8},{12,10},{14... | collective-permute-start | bytes 1769480 | tf_op jit(solution)/shard_map/ppermute | solution.py:382
  310.1 164.5 %collective-permute-start.28 = (bf16[1536,384]{1,0:T(8,128)(2,1)}, bf16[1536,384]{1,0:T(8,128)(2,1)}, u32[]{:S(2)}, u32[]{:S(2)}) collective-permute-start(bf16[1536,384]{1,0:T(8,128)(2,1)} %collective-permute-done.27.refs_6_), channel_id=1, source_target_pairs={{0,8},{8,0},{16,24},{24,16},{1,9},{9,1},{17,25},{25,17},{2,10},{10... | collective-permute-start | bytes 3538952 | tf_op jit(solution)/shard_map/ppermute | solution.py:367
  367.9 64.3 %collective-permute-start.24 = (bf16[2048,384]{1,0:T(8,128)(2,1)}, bf16[2048,384]{1,0:T(8,128)(2,1)S(1)}, u32[]{:S(2)}, u32[]{:S(2)}) collective-permute-start(bf16[2048,384]{1,0:T(8,128)(2,1)} %get-tuple-element.33.refs_0_), channel_id=1, source_target_pairs={{0,16},{8,24},{16,0},{24,8},{1,17},{9,25},{17,1},{25,9},{2,18},{10... | collective-permute-start | bytes 4718600 | tf_op jit(solution)/shard_map/ppermute | solution.py:371
  370.7 103.9 %collective-permute-start.23 = (bf16[2048,384]{1,0:T(8,128)(2,1)}, bf16[2048,384]{1,0:T(8,128)(2,1)S(1)}, u32[]{:S(2)}, u32[]{:S(2)}) collective-permute-start(bf16[2048,384]{1,0:T(8,128)(2,1)} %get-tuple-element.33.refs_0_), channel_id=1, source_target_pairs={{0,8},{8,0},{16,24},{24,16},{1,9},{9,1},{17,25},{25,17},{2,10},{10... | collective-permute-start | bytes 4718600 | tf_op jit(solution)/shard_map/ppermute | solution.py:367
  442.8 31.8 %collective-permute-start.25 = (bf16[2048,384]{1,0:T(8,128)(2,1)S(1)}, bf16[2048,384]{1,0:T(8,128)(2,1)S(1)}, u32[]{:S(2)}, u32[]{:S(2)}) collective-permute-start(bf16[2048,384]{1,0:T(8,128)(2,1)S(1)} %collective-permute-done.24.refs_2_), channel_id=1, source_target_pairs={{0,8},{8,0},{16,24},{24,16},{1,9},{9,1},{17,25},{25,17},{2,10},{10... | collective-permute-start | bytes 4718600 | tf_op jit(solution)/shard_map/ppermute | solution.py:367
  551.9 29.0 %collective-permute-start.46 = (bf16[8,2,64,1536]{3,2,0,1:T(8,128)(2,1)}, bf16[8,2,64,1536]{3,2,0,1:T(8,128)(2,1)}, u32[]{:S(2)}, u32[]{:S(2)}) collective-permute-start(bf16[8,2,64,1536]{3,2,0,1:T(8,128)(2,1)} %bitcast.379), channel_id=1, source_target_pairs={{0,8},{8,0},{16,24},{24,16},{1,9},{9,1},{17,25},{25,17},{2,10},{10... | collective-permute-start | bytes 9437192 | tf_op jit(solution)/shard_map/ppermute | solution.py:367
  552.1 36.3 %collective-permute-start.48 = (bf16[8,2,64,1536]{3,2,0,1:T(8,128)(2,1)S(1)}, bf16[8,2,64,1536]{3,2,0,1:T(8,128)(2,1)}, u32[]{:S(2)}, u32[]{:S(2)}) collective-permute-start(bf16[8,2,64,1536]{3,2,0,1:T(8,128)(2,1)S(1)} %bitcast.406), channel_id=1, source_target_pairs={{0,8},{8,0},{16,24},{24,16},{1,9},{9,1},{17,25},{25,17},{2,10},{10... | collective-permute-start | bytes 9437192 | tf_op jit(solution)/shard_map/ppermute | solution.py:367
  586.4 37.6 %collective-permute-start.47 = (bf16[8,64,1536]{2,1,0:T(8,128)(2,1)}, bf16[8,64,1536]{2,1,0:T(8,128)(2,1)}, u32[]{:S(2)}, u32[]{:S(2)}) collective-permute-start(bf16[8,64,1536]{2,1,0:T(8,128)(2,1)} %fusion.43), channel_id=1, source_target_pairs={{0,16},{8,24},{16,0},{24,8},{1,17},{9,25},{17,1},{25,9},{2,18},{10... | collective-permute-start | bytes 4718600 | tf_op jit(solution)/shard_map/ppermute | solution.py:371
  592.8 64.0 %collective-permute-start.49 = (bf16[8,64,1536]{2,1,0:T(8,128)(2,1)}, bf16[8,64,1536]{2,1,0:T(8,128)(2,1)}, u32[]{:S(2)}, u32[]{:S(2)}) collective-permute-start(bf16[8,64,1536]{2,1,0:T(8,128)(2,1)} %fusion.44), channel_id=1, source_target_pairs={{0,16},{8,24},{16,0},{24,8},{1,17},{9,25},{17,1},{25,9},{2,18},{10... | collective-permute-start | bytes 4718600 | tf_op jit(solution)/shard_map/ppermute | solution.py:371
  612.8 60.8 %collective-permute-start.73 = (bf16[96,3072]{1,0:T(8,128)(2,1)}, bf16[96,3072]{1,0:T(8,128)(2,1)}, u32[]{:S(2)}, u32[]{:S(2)}) collective-permute-start(bf16[96,3072]{1,0:T(8,128)(2,1)} %add_convert_fusion.13), channel_id=1, source_target_pairs={{0,2},{2,4},{4,6},{6,7},{7,5},{5,3},{3,1},{1,0},{8,10},{10,12},{12... | collective-permute-start | bytes 1769480 | tf_op jit(solution)/shard_map/ppermute | solution.py:378
  671.8 35.8 %collective-permute-start.51 = (bf16[8,64,1536]{2,1,0:T(8,128)(2,1)}, bf16[8,64,1536]{2,1,0:T(8,128)(2,1)}, u32[]{:S(2)}, u32[]{:S(2)}) collective-permute-start(bf16[8,64,1536]{2,1,0:T(8,128)(2,1)} %get-tuple-element.107), channel_id=1, source_target_pairs={{0,16},{8,24},{16,0},{24,8},{1,17},{9,25},{17,1},{25,9},{2,18},{10... | collective-permute-start | bytes 4718600 | tf_op jit(solution)/shard_map/ppermute | solution.py:371
  673.6 36.4 %collective-permute-start.50 = (bf16[8,64,1536]{2,1,0:T(8,128)(2,1)}, bf16[8,64,1536]{2,1,0:T(8,128)(2,1)}, u32[]{:S(2)}, u32[]{:S(2)}) collective-permute-start(bf16[8,64,1536]{2,1,0:T(8,128)(2,1)} %get-tuple-element.107), channel_id=1, source_target_pairs={{0,8},{8,0},{16,24},{24,16},{1,9},{9,1},{17,25},{25,17},{2,10},{10... | collective-permute-start | bytes 4718600 | tf_op jit(solution)/shard_map/ppermute | solution.py:367
  675.7 31.9 %collective-permute-start.74 = (bf16[96,3072]{1,0:T(8,128)(2,1)}, bf16[96,3072]{1,0:T(8,128)(2,1)}, u32[]{:S(2)}, u32[]{:S(2)}) collective-permute-start(bf16[96,3072]{1,0:T(8,128)(2,1)} %add_convert_fusion.12), channel_id=1, source_target_pairs={{0,2},{2,4},{4,6},{6,7},{7,5},{5,3},{3,1},{1,0},{8,10},{10,12},{12... | collective-permute-start | bytes 1769480 | tf_op jit(solution)/shard_map/ppermute | solution.py:378
  709.0 84.2 %collective-permute-start.75 = (bf16[96,3072]{1,0:T(8,128)(2,1)S(1)}, bf16[96,3072]{1,0:T(8,128)(2,1)S(1)}, u32[]{:S(2)}, u32[]{:S(2)}) collective-permute-start(bf16[96,3072]{1,0:T(8,128)(2,1)S(1)} %add_convert_fusion.11), channel_id=1, source_target_pairs={{0,2},{2,4},{4,6},{6,7},{7,5},{5,3},{3,1},{1,0},{8,10},{10,12},{12... | collective-permute-start | bytes 1769480 | tf_op jit(solution)/shard_map/ppermute | solution.py:378
  795.8 20.2 %collective-permute-start.76 = (bf16[96,3072]{1,0:T(8,128)(2,1)}, bf16[96,3072]{1,0:T(8,128)(2,1)}, u32[]{:S(2)}, u32[]{:S(2)}) collective-permute-start(bf16[96,3072]{1,0:T(8,128)(2,1)} %add_convert_fusion.10), channel_id=1, source_target_pairs={{0,2},{2,4},{4,6},{6,7},{7,5},{5,3},{3,1},{1,0},{8,10},{10,12},{12... | collective-permute-start | bytes 1769480 | tf_op jit(solution)/shard_map/ppermute | solution.py:378
  818.1 24.9 %collective-permute-start.79 = (bf16[96,3072]{1,0:T(8,128)(2,1)}, bf16[96,3072]{1,0:T(8,128)(2,1)}, u32[]{:S(2)}, u32[]{:S(2)}) collective-permute-start(bf16[96,3072]{1,0:T(8,128)(2,1)} %get-tuple-element.128), channel_id=1, source_target_pairs={{2,0},{4,2},{6,4},{7,6},{5,7},{3,5},{1,3},{0,1},{10,8},{12,10},{14... | collective-permute-start | bytes 1769480 | tf_op jit(solution)/shard_map/ppermute | solution.py:382
  890.4 21.1 %collective-permute-start.62 = (bf16[96,1536]{1,0:T(8,128)(2,1)}, bf16[96,1536]{1,0:T(8,128)(2,1)}, u32[]{:S(2)}, u32[]{:S(2)}) collective-permute-start(bf16[96,1536]{1,0:T(8,128)(2,1)} %get-tuple-element.138), channel_id=1, source_target_pairs={{2,0},{4,2},{6,4},{7,6},{5,7},{3,5},{1,3},{0,1},{10,8},{12,10},{14... | collective-permute-start | bytes 884744 | tf_op jit(solution)/shard_map/ppermute | solution.py:382
  968.3 23.4 %collective-permute-start.87 = (bf16[192,3072]{1,0:T(8,128)(2,1)}, bf16[192,3072]{1,0:T(8,128)(2,1)}, u32[]{:S(2)}, u32[]{:S(2)}) collective-permute-start(bf16[192,3072]{1,0:T(8,128)(2,1)} %pad_maximum_fusion.1.refs_4_), channel_id=1, source_target_pairs={{0,16},{8,24},{16,0},{24,8},{1,17},{9,25},{17,1},{25,9},{2,18},{10... | collective-permute-start | bytes 3538952 | tf_op jit(solution)/shard_map/ppermute | solution.py:371
  985.7 22.7 %collective-permute-start.86 = (bf16[192,3072]{1,0:T(8,128)(2,1)}, bf16[192,3072]{1,0:T(8,128)(2,1)}, u32[]{:S(2)}, u32[]{:S(2)}) collective-permute-start(bf16[192,3072]{1,0:T(8,128)(2,1)} %pad_maximum_fusion.1.refs_4_), channel_id=1, source_target_pairs={{0,8},{8,0},{16,24},{24,16},{1,9},{9,1},{17,25},{25,17},{2,10},{10... | collective-permute-start | bytes 3538952 | tf_op jit(solution)/shard_map/ppermute | solution.py:367
  1026.0 21.7 %collective-permute-start.89 = (bf16[9,96,512]{2,1,0:T(8,128)(2,1)S(1)}, bf16[9,96,512]{2,1,0:T(8,128)(2,1)S(1)}, u32[]{:S(2)}, u32[]{:S(2)}) collective-permute-start(bf16[9,96,512]{2,1,0:T(8,128)(2,1)S(1)} %get-tuple-element.123), channel_id=1, source_target_pairs={{0,2},{2,4},{4,6},{6,7},{7,5},{5,3},{3,1},{1,0},{8,10},{10,12},{12... | collective-permute-start | bytes 2654216 | tf_op jit(solution)/shard_map/ppermute | solution.py:378
  1026.4 21.4 %collective-permute-start.96 = (bf16[9,96,512]{2,1,0:T(8,128)(2,1)S(1)}, bf16[9,96,512]{2,1,0:T(8,128)(2,1)S(1)}, u32[]{:S(2)}, u32[]{:S(2)}) collective-permute-start(bf16[9,96,512]{2,1,0:T(8,128)(2,1)S(1)} %get-tuple-element.124), channel_id=1, source_target_pairs={{2,0},{4,2},{6,4},{7,6},{5,7},{3,5},{1,3},{0,1},{10,8},{12,10},{14... | collective-permute-start | bytes 2654216 | tf_op jit(solution)/shard_map/ppermute | solution.py:382
  1040.9 63.6 %collective-permute-start.53 = (bf16[8,2,64,1536]{3,2,0,1:T(8,128)(2,1)}, bf16[8,2,64,1536]{3,2,0,1:T(8,128)(2,1)}, u32[]{:S(2)}, u32[]{:S(2)}) collective-permute-start(bf16[8,2,64,1536]{3,2,0,1:T(8,128)(2,1)} %bitcast.377), channel_id=1, source_target_pairs={{0,8},{8,0},{16,24},{24,16},{1,9},{9,1},{17,25},{25,17},{2,10},{10... | collective-permute-start | bytes 9437192 | tf_op jit(solution)/shard_map/ppermute | solution.py:367
  1049.8 20.8 %collective-permute-start.90 = (bf16[9,96,512]{2,1,0:T(8,128)(2,1)S(1)}, bf16[9,96,512]{2,1,0:T(8,128)(2,1)S(1)}, u32[]{:S(2)}, u32[]{:S(2)}) collective-permute-start(bf16[9,96,512]{2,1,0:T(8,128)(2,1)S(1)} %get-tuple-element.121), channel_id=1, source_target_pairs={{0,2},{2,4},{4,6},{6,7},{7,5},{5,3},{3,1},{1,0},{8,10},{10,12},{12... | collective-permute-start | bytes 2654216 | tf_op jit(solution)/shard_map/ppermute | solution.py:378
  1051.6 20.4 %collective-permute-start.97 = (bf16[9,96,512]{2,1,0:T(8,128)(2,1)S(1)}, bf16[9,96,512]{2,1,0:T(8,128)(2,1)S(1)}, u32[]{:S(2)}, u32[]{:S(2)}) collective-permute-start(bf16[9,96,512]{2,1,0:T(8,128)(2,1)S(1)} %get-tuple-element.122), channel_id=1, source_target_pairs={{2,0},{4,2},{6,4},{7,6},{5,7},{3,5},{1,3},{0,1},{10,8},{12,10},{14... | collective-permute-start | bytes 2654216 | tf_op jit(solution)/shard_map/ppermute | solution.py:382
  1097.3 27.5 %collective-permute-start.92 = (bf16[9,96,512]{2,1,0:T(8,128)(2,1)}, bf16[9,96,512]{2,1,0:T(8,128)(2,1)}, u32[]{:S(2)}, u32[]{:S(2)}) collective-permute-start(bf16[9,96,512]{2,1,0:T(8,128)(2,1)} %get-tuple-element.117), channel_id=1, source_target_pairs={{0,2},{2,4},{4,6},{6,7},{7,5},{5,3},{3,1},{1,0},{8,10},{10,12},{12... | collective-permute-start | bytes 2654216 | tf_op jit(solution)/shard_map/ppermute | solution.py:378
  1098.1 26.7 %collective-permute-start.99 = (bf16[9,96,512]{2,1,0:T(8,128)(2,1)}, bf16[9,96,512]{2,1,0:T(8,128)(2,1)}, u32[]{:S(2)}, u32[]{:S(2)}) collective-permute-start(bf16[9,96,512]{2,1,0:T(8,128)(2,1)} %get-tuple-element.118), channel_id=1, source_target_pairs={{2,0},{4,2},{6,4},{7,6},{5,7},{3,5},{1,3},{0,1},{10,8},{12,10},{14... | collective-permute-start | bytes 2654216 | tf_op jit(solution)/shard_map/ppermute | solution.py:382
  1099.3 76.5 %all-to-all-start.4 = ((bf16[8,64,1536]{2,1,0:T(8,128)(2,1)}), bf16[8,64,1536]{2,1,0:T(8,128)(2,1)}, u32[]{:S(2)}, u32[]{:S(2)}) async-start(bf16[8,64,1536]{2,1,0:T(8,128)(2,1)} %get-tuple-element.141), calls=%async_computation.4 | async-start | bytes 3145728 | tf_op jit(solution)/shard_map/all_to_all | solution.py:477
  1127.4 42.0 %collective-permute-start.100 = (bf16[9,96,512]{2,1,0:T(8,128)(2,1)S(1)}, bf16[9,96,512]{2,1,0:T(8,128)(2,1)S(1)}, u32[]{:S(2)}, u32[]{:S(2)}) collective-permute-start(bf16[9,96,512]{2,1,0:T(8,128)(2,1)S(1)} %get-tuple-element.116), channel_id=1, source_target_pairs={{2,0},{4,2},{6,4},{7,6},{5,7},{3,5},{1,3},{0,1},{10,8},{12,10},{14... | collective-permute-start | bytes 2654216 | tf_op jit(solution)/shard_map/ppermute | solution.py:382
  1130.1 39.3 %collective-permute-start.93 = (bf16[9,96,512]{2,1,0:T(8,128)(2,1)S(1)}, bf16[9,96,512]{2,1,0:T(8,128)(2,1)S(1)}, u32[]{:S(2)}, u32[]{:S(2)}) collective-permute-start(bf16[9,96,512]{2,1,0:T(8,128)(2,1)S(1)} %get-tuple-element.115), channel_id=1, source_target_pairs={{0,2},{2,4},{4,6},{6,7},{7,5},{5,3},{3,1},{1,0},{8,10},{10,12},{12... | collective-permute-start | bytes 2654216 | tf_op jit(solution)/shard_map/ppermute | solution.py:378
  1131.4 49.1 %collective-permute-start.54 = (bf16[8,64,1536]{2,1,0:T(8,128)(2,1)}, bf16[8,64,1536]{2,1,0:T(8,128)(2,1)S(1)}, u32[]{:S(2)}, u32[]{:S(2)}) collective-permute-start(bf16[8,64,1536]{2,1,0:T(8,128)(2,1)} %fusion.45), channel_id=1, source_target_pairs={{0,16},{8,24},{16,0},{24,8},{1,17},{9,25},{17,1},{25,9},{2,18},{10... | collective-permute-start | bytes 4718600 | tf_op jit(solution)/shard_map/ppermute | solution.py:371
  1175.8 36.2 %all-to-all-start.5 = ((bf16[8,1,64,1536]{3,2,1,0:T(8,128)(2,1)}), bf16[8,1,64,1536]{3,2,1,0:T(8,128)(2,1)}, u32[]{:S(2)}, u32[]{:S(2)}) async-start(bf16[8,1,64,1536]{3,2,1,0:T(8,128)(2,1)} %bitcast.78), calls=%async_computation.5 | async-start | bytes 3145728 | tf_op jit(solution)/shard_map/all_to_all | solution.py:478
  1212.0 74.8 %all-to-all-start.6 = ((bf16[8,64,1536]{2,1,0:T(8,128)(2,1)}), bf16[8,64,1536]{2,1,0:T(8,128)(2,1)}, u32[]{:S(2)}, u32[]{:S(2)}) async-start(bf16[8,64,1536]{2,1,0:T(8,128)(2,1)} %fusion.24), calls=%async_computation.6 | async-start | bytes 3145728 | tf_op jit(solution)/shard_map/all_to_all | solution.py:477
  1229.4 35.3 %collective-permute-start.103 = (bf16[9,96,512]{2,1,0:T(8,128)(2,1)S(1)}, bf16[9,96,512]{2,1,0:T(8,128)(2,1)S(1)}, u32[]{:S(2)}, u32[]{:S(2)}) collective-permute-start(bf16[9,96,512]{2,1,0:T(8,128)(2,1)S(1)} %get-tuple-element.143), channel_id=1, source_target_pairs={{0,2},{2,4},{4,6},{6,7},{7,5},{5,3},{3,1},{1,0},{8,10},{10,12},{12... | collective-permute-start | bytes 2654216 | tf_op jit(solution)/shard_map/ppermute | solution.py:378
  1230.9 36.2 %collective-permute-start.104 = (bf16[9,96,512]{2,1,0:T(8,128)(2,1)S(1)}, bf16[9,96,512]{2,1,0:T(8,128)(2,1)}, u32[]{:S(2)}, u32[]{:S(2)}) collective-permute-start(bf16[9,96,512]{2,1,0:T(8,128)(2,1)S(1)} %get-tuple-element.142), channel_id=1, source_target_pairs={{2,0},{4,2},{6,4},{7,6},{5,7},{3,5},{1,3},{0,1},{10,8},{12,10},{14... | collective-permute-start | bytes 2654216 | tf_op jit(solution)/shard_map/ppermute | solution.py:382
  1264.7 19.6 %collective-permute-start.105 = (bf16[9,96,512]{2,1,0:T(8,128)(2,1)S(1)}, bf16[9,96,512]{2,1,0:T(8,128)(2,1)}, u32[]{:S(2)}, u32[]{:S(2)}) collective-permute-start(bf16[9,96,512]{2,1,0:T(8,128)(2,1)S(1)} %collective-permute-done.103), channel_id=1, source_target_pairs={{0,2},{2,4},{4,6},{6,7},{7,5},{5,3},{3,1},{1,0},{8,10},{10,12},{12... | collective-permute-start | bytes 2654216 | tf_op jit(solution)/shard_map/ppermute | solution.py:378
  1267.2 23.9 %collective-permute-start.106 = (bf16[9,96,512]{2,1,0:T(8,128)(2,1)}, bf16[9,96,512]{2,1,0:T(8,128)(2,1)}, u32[]{:S(2)}, u32[]{:S(2)}) collective-permute-start(bf16[9,96,512]{2,1,0:T(8,128)(2,1)} %collective-permute-done.104), channel_id=1, source_target_pairs={{2,0},{4,2},{6,4},{7,6},{5,7},{3,5},{1,3},{0,1},{10,8},{12,10},{14... | collective-permute-start | bytes 2654216 | tf_op jit(solution)/shard_map/ppermute | solution.py:382
  1284.3 19.6 %collective-permute-start.107 = (bf16[9,96,512]{2,1,0:T(8,128)(2,1)}, bf16[9,96,512]{2,1,0:T(8,128)(2,1)}, u32[]{:S(2)}, u32[]{:S(2)}) collective-permute-start(bf16[9,96,512]{2,1,0:T(8,128)(2,1)} %collective-permute-done.105), channel_id=1, source_target_pairs={{0,2},{2,4},{4,6},{6,7},{7,5},{5,3},{3,1},{1,0},{8,10},{10,12},{12... | collective-permute-start | bytes 2654216 | tf_op jit(solution)/shard_map/ppermute | solution.py:378
  1286.8 43.2 %all-to-all-start.7 = ((bf16[8,1,64,1536]{3,2,1,0:T(8,128)(2,1)}), bf16[8,1,64,1536]{3,2,1,0:T(8,128)(2,1)}, u32[]{:S(2)}, u32[]{:S(2)}) async-start(bf16[8,1,64,1536]{3,2,1,0:T(8,128)(2,1)} %bitcast.102), calls=%async_computation.7 | async-start | bytes 3145728 | tf_op jit(solution)/shard_map/all_to_all | solution.py:478
  1291.1 37.5 %collective-permute-start.108 = (bf16[9,96,512]{2,1,0:T(8,128)(2,1)}, bf16[9,96,512]{2,1,0:T(8,128)(2,1)}, u32[]{:S(2)}, u32[]{:S(2)}) collective-permute-start(bf16[9,96,512]{2,1,0:T(8,128)(2,1)} %collective-permute-done.106), channel_id=1, source_target_pairs={{2,0},{4,2},{6,4},{7,6},{5,7},{3,5},{1,3},{0,1},{10,8},{12,10},{14... | collective-permute-start | bytes 2654216 | tf_op jit(solution)/shard_map/ppermute | solution.py:382
  1303.9 36.3 %collective-permute-start.109 = (bf16[9,96,512]{2,1,0:T(8,128)(2,1)}, bf16[9,96,512]{2,1,0:T(8,128)(2,1)}, u32[]{:S(2)}, u32[]{:S(2)}) collective-permute-start(bf16[9,96,512]{2,1,0:T(8,128)(2,1)} %collective-permute-done.107), channel_id=1, source_target_pairs={{0,2},{2,4},{4,6},{6,7},{7,5},{5,3},{3,1},{1,0},{8,10},{10,12},{12... | collective-permute-start | bytes 2654216 | tf_op jit(solution)/shard_map/ppermute | solution.py:378
  1328.6 19.8 %collective-permute-start.110 = (bf16[9,96,512]{2,1,0:T(8,128)(2,1)}, bf16[9,96,512]{2,1,0:T(8,128)(2,1)}, u32[]{:S(2)}, u32[]{:S(2)}) collective-permute-start(bf16[9,96,512]{2,1,0:T(8,128)(2,1)} %collective-permute-done.108), channel_id=1, source_target_pairs={{2,0},{4,2},{6,4},{7,6},{5,7},{3,5},{1,3},{0,1},{10,8},{12,10},{14... | collective-permute-start | bytes 2654216 | tf_op jit(solution)/shard_map/ppermute | solution.py:382
  1340.2 20.5 %collective-permute-start.111 = (bf16[9,96,512]{2,1,0:T(8,128)(2,1)}, bf16[9,96,512]{2,1,0:T(8,128)(2,1)S(1)}, u32[]{:S(2)}, u32[]{:S(2)}) collective-permute-start(bf16[9,96,512]{2,1,0:T(8,128)(2,1)} %collective-permute-done.109), channel_id=1, source_target_pairs={{0,2},{2,4},{4,6},{6,7},{7,5},{5,3},{3,1},{1,0},{8,10},{10,12},{12... | collective-permute-start | bytes 2654216 | tf_op jit(solution)/shard_map/ppermute | solution.py:378
  1348.4 20.0 %collective-permute-start.112 = (bf16[9,96,512]{2,1,0:T(8,128)(2,1)}, bf16[9,96,512]{2,1,0:T(8,128)(2,1)S(1)}, u32[]{:S(2)}, u32[]{:S(2)}) collective-permute-start(bf16[9,96,512]{2,1,0:T(8,128)(2,1)} %collective-permute-done.110), channel_id=1, source_target_pairs={{2,0},{4,2},{6,4},{7,6},{5,7},{3,5},{1,3},{0,1},{10,8},{12,10},{14... | collective-permute-start | bytes 2654216 | tf_op jit(solution)/shard_map/ppermute | solution.py:382
  1360.7 19.8 %collective-permute-start.113 = (bf16[9,96,512]{2,1,0:T(8,128)(2,1)S(1)}, bf16[9,96,512]{2,1,0:T(8,128)(2,1)S(1)}, u32[]{:S(2)}, u32[]{:S(2)}) collective-permute-start(bf16[9,96,512]{2,1,0:T(8,128)(2,1)S(1)} %collective-permute-done.111), channel_id=1, source_target_pairs={{0,2},{2,4},{4,6},{6,7},{7,5},{5,3},{3,1},{1,0},{8,10},{10,12},{12... | collective-permute-start | bytes 2654216 | tf_op jit(solution)/shard_map/ppermute | solution.py:378
  1368.4 19.8 %collective-permute-start.114 = (bf16[9,96,512]{2,1,0:T(8,128)(2,1)S(1)}, bf16[9,96,512]{2,1,0:T(8,128)(2,1)S(1)}, u32[]{:S(2)}, u32[]{:S(2)}) collective-permute-start(bf16[9,96,512]{2,1,0:T(8,128)(2,1)S(1)} %collective-permute-done.112), channel_id=1, source_target_pairs={{2,0},{4,2},{6,4},{7,6},{5,7},{3,5},{1,3},{0,1},{10,8},{12,10},{14... | collective-permute-start | bytes 2654216 | tf_op jit(solution)/shard_map/ppermute | solution.py:382
  (132 other events, 2035.1 us)

commit v2 on v1

--- a/solution.py
+++ b/solution.py
@@ -434,7 +434,7 @@
     return pick(near, y, axis) + far.astype(F32)
 
 
-def ring_gather(shard, blk, axis):
+def ring_gather(shard, blk, axis, waits=()):
     half = shard.shape[axis] // 2
     place = ring_place(blk)
     shape = shard.shape[:axis] + (8,) + shard.shape[axis:]
@@ -449,6 +449,9 @@
         return lax.dynamic_update_slice(whole, jnp.expand_dims(piece, axis), starts)
 
     for step in range(1, 8):
+        for at, arrays in waits:
+            if at == step:
+                up, down = after((up, down), arrays)
         up, down = ring_up(up), ring_down(down)
         whole = store(whole, up, ring_owner(place - step), 0)
         whole = store(whole, down, ring_owner(place + step), half)
@@ -458,25 +461,49 @@
 def ring_scatter(part_of, blk):
     place = ring_place(blk)
     up, down = part_of(ring_owner(place - 1), 0), part_of(ring_owner(place + 1), 1)
+    states = []
     for step in range(1, 8):
         up, down = ring_up(up.astype(BF)), ring_down(down.astype(BF))
-        up = up.astype(F32) + part_of(ring_owner(place - 1 - step), 0).astype(F32)
-        down = down.astype(F32) + part_of(ring_owner(place + 1 + step), 1).astype(F32)
-    return up, down
-
-
-def to_rows(tokens):
+        up = (up.astype(F32) + part_of(ring_owner(place - 1 - step), 0).astype(F32)).astype(BF)
+        down = (down.astype(F32) + part_of(ring_owner(place + 1 + step), 1).astype(F32)).astype(BF)
+        states.append((up, down))
+    return states
+
+
+def swap_blk(piece, bit):
+    return lax.ppermute(piece, "blk", [(i, i ^ bit) for i in range(8)])
+
+
+def choose(flag, zero, one):
+    return jnp.where(flag == 0, zero, one)
+
+
+def to_batch(tokens, me):
     rows, count, width = tokens.shape
     pieces = tokens.reshape(rows, 4, count // 4, width)
-    pieces = lax.all_to_all(pieces, "batch", 1, 0, tiled=True)
-    return lax.all_to_all(pieces.reshape(8, count // 4, width), "blk", 0, 0, tiled=True)
-
-
-def from_rows(tokens):
+    whole = jnp.zeros((4, rows, count // 4, width), tokens.dtype)
+    for other in range(4):
+        piece = lax.dynamic_index_in_dim(pieces, me ^ other, 1, keepdims=False)
+        if other:
+            piece = lax.ppermute(piece, "batch", [(i, i ^ other) for i in range(4)])
+        whole = put(whole, piece, me ^ other, 0)
+    return whole.reshape(8, count // 4, width)
+
+
+def to_rows(pieces):
+    return lax.all_to_all(pieces, "blk", 0, 0, tiled=True)
+
+
+def from_rows(tokens, me):
     count, width = tokens.shape[1:]
-    pieces = lax.all_to_all(tokens, "blk", 0, 0, tiled=True)
-    pieces = lax.all_to_all(pieces.reshape(8, 1, count, width), "batch", 0, 1, tiled=True)
-    return pieces.reshape(2, 4 * count, width)
+    pieces = lax.all_to_all(tokens, "blk", 0, 0, tiled=True).reshape(4, 2, count, width)
+    whole = jnp.zeros((2, 4, count, width), tokens.dtype)
+    for other in range(4):
+        piece = lax.dynamic_index_in_dim(pieces, me ^ other, 0, keepdims=False)
+        if other:
+            piece = lax.ppermute(piece, "batch", [(i, i ^ other) for i in range(4)])
+        whole = put(whole, piece, me ^ other, 1)
+    return whole.reshape(2, 4 * count, width)
 
 
 def attention_pieces(me):
@@ -855,40 +882,410 @@
     )(me.reshape(1), x, gain, *a, *weights)
 
 
-def feed_kernel(n_ref, dy_ref, w_ref, act_ref, out_ref, dn_ref):
-    n, dy = n_ref[...], dy_ref[...]
-    wg, wu, wd = w_ref[:, :FQ], w_ref[:, FQ : 2 * FQ], w_ref[:, 2 * FQ :]
-    gate = dot_plain(n, wg)
-    up = dot_plain(n, wu)
-    dhidden = dot_plain(dy, wd)
-    share = 1.0 / (1.0 + jnp.exp(-gate))
-    silu = gate * share
-    hidden = (silu * up).astype(BF)
-    dup = (dhidden * silu).astype(BF)
-    dgate = (dhidden * up * (share * (1.0 + gate * (1.0 - share)))).astype(BF)
-    act_ref[:, :FQ] = dgate
-    act_ref[:, FQ : 2 * FQ] = dup
-    act_ref[:, 2 * FQ :] = hidden
-    out_ref[...] = dot_last(hidden, wd).astype(BF)
-    dn_ref[...] = (dot_last(dgate, wg) + dot_last(dup, wu)).astype(BF)
-
-
-def feed(n, dy, weights):
+MESH = pl.DeviceIdType.MESH
+
+
+def greet(devices):
+    barrier = pltpu.get_barrier_semaphore()
+    for device in devices:
+        pl.semaphore_signal(barrier, inc=1, device_id=device, device_id_type=MESH)
+    pl.semaphore_wait(barrier, len(devices))
+
+
+def remote(source, target, sems, at, device):
+    return pltpu.make_async_remote_copy(
+        src_ref=source,
+        dst_ref=target,
+        send_sem=sems.at[0, at],
+        recv_sem=sems.at[1, at],
+        device_id=device,
+        device_id_type=MESH,
+    )
+
+
+def feed_kernel(
+    n_ref, dy_ref, w_ref, x1_ref, dyo_ref, wo_ref, gain_ref, act_ref, out_ref, dx_ref, low_ref, da_ref, dgain_ref,
+    part, near_in, near, far_in, gathered, s_near, s_far, s_y, s_core, s_relay,
+):
+    i = pl.program_id(0)
+    me = lax.axis_index("batch")
+    y, core = me // 2, me % 2
+    to_core = {"batch": y * 2 + 1 - core}
+    to_y = {"batch": (1 - y) * 2 + core}
+    blocks = part.shape[0]
+
+    def near_copy(b):
+        return remote(part.at[b, :, 1 - core], near_in.at[b], s_near, b, to_core)
+
+    def far_copy(b):
+        return remote(near.at[b], far_in.at[b], s_far, b, to_y)
+
+    def own_copy(b, sems, device):
+        return remote(gathered.at[b, me], gathered.at[b, me], sems, b, device)
+
+    def relay_copy(b):
+        slab = (1 - y) * 2 + core
+        return remote(gathered.at[b, slab], gathered.at[b, slab], s_relay, b, to_core)
+
+    @pl.when(i == 0)
+    def begin():
+        greet((to_core, to_y))
+        dgain_ref[...] = jnp.zeros_like(dgain_ref)
+
+    @pl.when((i >= 1) & (i < blocks + 1))
+    def send_far():
+        b = i - 1
+        near_copy(b).wait_recv()
+        both = part[b, 1 - y, core].astype(F32) + near_in[b, 1 - y].astype(F32)
+        near[b] = both.astype(BF)
+        far_copy(b).start()
+
+    @pl.when((i >= 2) & (i < blocks + 2))
+    def send_own():
+        b = i - 2
+        far_copy(b).wait_recv()
+        dn = part[b, y, core].astype(F32) + near_in[b, y].astype(F32) + far_in[b].astype(F32)
+        x1 = x1_ref[0]
+        r = lax.rsqrt(jnp.mean(x1 * x1, axis=-1, keepdims=True) + norm_epsilon)
+        t = x1 * r
+        e = dn * gain_ref[...]
+        dx = dyo_ref[0].astype(F32) + r * (e - t * jnp.mean(e * t, axis=-1, keepdims=True))
+        dgain_ref[...] += jnp.sum(dn * t, axis=0, keepdims=True)
+        dx_ref[0] = dx
+        gathered[b, me] = dx.astype(BF)
+        own_copy(b, s_y, to_y).start()
+        own_copy(b, s_core, to_core).start()
+
+    @pl.when((i >= 3) & (i < blocks + 3))
+    def send_relay():
+        b = i - 3
+        own_copy(b, s_y, to_y).wait_recv()
+        relay_copy(b).start()
+
+    @pl.when(i >= 4)
+    def use():
+        b = i - 4
+        own_copy(b, s_core, to_core).wait_recv()
+        relay_copy(b).wait_recv()
+        whole = jnp.concatenate([gathered[b, other] for other in range(4)], axis=0)
+        low_ref[...] = whole
+        da_ref[...] = dot_plain(whole, wo_ref[...])
+
+    @pl.when(i < blocks)
+    def compute():
+        n, dy = n_ref[...], dy_ref[...]
+        wg, wu, wd = w_ref[:, :FQ], w_ref[:, FQ : 2 * FQ], w_ref[:, 2 * FQ :]
+        gate = dot_plain(n, wg)
+        up = dot_plain(n, wu)
+        dhidden = dot_plain(dy, wd)
+        share = 1.0 / (1.0 + jnp.exp(-gate))
+        silu = gate * share
+        hidden = (silu * up).astype(BF)
+        dup = (dhidden * silu).astype(BF)
+        dgate = (dhidden * up * (share * (1.0 + gate * (1.0 - share)))).astype(BF)
+        act_ref[:, :FQ] = dgate
+        act_ref[:, FQ : 2 * FQ] = dup
+        act_ref[:, 2 * FQ :] = hidden
+        dn = (dot_last(dgate, wg) + dot_last(dup, wu)).astype(BF)
+        size = dn.shape[0] // 4
+        for other in range(4):
+            part[i, other // 2, other % 2] = dn[other * size : (other + 1) * size]
+        near_copy(i).start()
+        out_ref[...] = dot_last(hidden, wd).astype(BF)
+
+    @pl.when(i == blocks + 3)
+    def finish():
+        for b in range(blocks):
+            near_copy(b).wait_send()
+            far_copy(b).wait_send()
+            own_copy(b, s_y, to_y).wait_send()
+            own_copy(b, s_core, to_core).wait_send()
+            relay_copy(b).wait_send()
+
+
+def feed(n, dy, weights, x1, dy_own, attn, gain):
     count = n.shape[0]
-    rows = lambda w: pl.BlockSpec((TILE, w), lambda i: (i, 0))
-    shape = lambda w: jax.ShapeDtypeStruct((count, w), BF)
+    blocks = count // TILE
+    size = TILE // 4
+    late = lambda lag: lambda i: (jnp.clip(i - lag, 0, blocks - 1), 0)
+    late3 = lambda lag: lambda i: (jnp.clip(i - lag, 0, blocks - 1), 0, 0)
+    rows = lambda w, lag: pl.BlockSpec((TILE, w), late(lag))
+    own = pl.BlockSpec((1, size, D), late3(2))
+    shape = lambda w, kind=BF: jax.ShapeDtypeStruct((count, w), kind)
+    sems = pltpu.SemaphoreType.DMA((2, blocks))
     return pl.pallas_call(
         feed_kernel,
-        grid=(count // TILE,),
-        in_specs=[rows(D), rows(D), pl.BlockSpec((D, 3 * FQ), lambda i: (0, 0), pipeline_mode=pl.Buffered(1))],
-        out_specs=[rows(3 * FQ), rows(D), rows(D)],
-        out_shape=[shape(3 * FQ), shape(D), shape(D)],
-        compiler_params=params(),
+        grid=(blocks + 4,),
+        in_specs=[
+            rows(D, 0),
+            rows(D, 0),
+            pl.BlockSpec((D, 3 * FQ), lambda i: (0, 0), pipeline_mode=pl.Buffered(1)),
+            own,
+            own,
+            pl.BlockSpec((D, QW), lambda i: (0, 3), pipeline_mode=pl.Buffered(1)),
+            pl.BlockSpec((1, D), lambda i: (0, 0)),
+        ],
+        out_specs=[
+            rows(3 * FQ, 0),
+            rows(D, 0),
+            own,
+            rows(D, 4),
+            rows(QW, 4),
+            pl.BlockSpec((1, D), lambda i: (0, 0)),
+        ],
+        out_shape=[
+            shape(3 * FQ),
+            shape(D),
+            jax.ShapeDtypeStruct((blocks, size, D), F32),
+            shape(D),
+            shape(QW, F32),
+            jax.ShapeDtypeStruct((1, D), F32),
+        ],
+        scratch_shapes=[
+            pltpu.VMEM((blocks, 2, 2, size, D), BF),
+            pltpu.VMEM((blocks, 2, size, D), BF),
+            pltpu.VMEM((blocks, size, D), BF),
+            pltpu.VMEM((blocks, size, D), BF),
+            pltpu.VMEM((blocks, 4, size, D), BF),
+            sems,
+            sems,
+            sems,
+            sems,
+            sems,
+        ],
+        compiler_params=params(collective_id=1, has_side_effects=True),
         cost_estimate=pl.CostEstimate(
             flops=12 * count * D * FQ, bytes_accessed=count * (8 * D + 6 * FQ) + 6 * D * FQ, transcendentals=count * FQ
         ),
         name="feed",
-    )(n, dy, weights)
+    )(n, dy, weights, x1, dy_own, attn, gain)
+
+
+def rotate_kernel(
+    g_ref, base_ref, other_ref, first_ref, second_ref, master_ref, scale_ref, new_first_ref, new_second_ref,
+    new_master_ref, g, base, other, firsts, seconds, masters, g_in, part, x_in, near, z_in, far, p_in, step, steps,
+    back, back_in, steps_own, load, store, s_g, s_x, s_z, s_p, s_step, s_back, s_up, s_side,
+):
+    blk = lax.axis_index("blk")
+    zh, zl, xx = blk // 4, (blk // 2) % 2, blk % 2
+    to_x = {"blk": blk + 1 - 2 * xx}
+    to_z = {"blk": blk + 4 - 8 * zh}
+    to_pair = {"blk": blk + 2 - 4 * zl}
+    count = g.shape[0]
+    half = UW // 2
+    own = pl.ds(pl.multiple_of(zl * half, half), half)
+    away = pl.ds(pl.multiple_of((1 - zl) * half, half), half)
+    block = 4 * zh + xx
+    loads = [
+        (g_ref, g), (base_ref, base), (other_ref, other), (first_ref, firsts), (second_ref, seconds), (master_ref, masters),
+    ]
+    stores = [(firsts, new_first_ref), (seconds, new_second_ref), (masters, new_master_ref)]
+
+    def loading(i, s):
+        return pltpu.make_async_copy(loads[i][0].at[s], loads[i][1].at[s], load.at[i, s])
+
+    def storing(i, s):
+        return pltpu.make_async_copy(stores[i][0].at[s], stores[i][1].at[s], store.at[i, s])
+
+    def send_g(s):
+        return remote(g.at[s, :, away], g_in.at[s], s_g, s, to_pair)
+
+    def send_x(s):
+        return remote(part.at[s % 3, :, 1 - xx], x_in.at[s], s_x, s, to_x)
+
+    def send_z(s):
+        return remote(near.at[s % 3, 1 - zh], z_in.at[s], s_z, s, to_z)
+
+    def send_p(s):
+        return remote(far.at[s % 3], p_in.at[s], s_p, s, to_pair)
+
+    def step_pair(s):
+        return remote(step.at[s, :, away], steps.at[s, block + 2 * zl], s_step, s, to_pair)
+
+    def step_z(s, a):
+        return remote(steps.at[s, block + 2 * a], steps.at[s, block + 2 * a], s_up, 2 * s + a, to_z)
+
+    def step_x(s, a):
+        at = 2 * a + xx
+        return remote(steps.at[s, at], steps.at[s, at], s_side, 4 * s + a, to_x)
+
+    def send_back(s):
+        return remote(back.at[s % 3], back_in.at[s], s_back, s, to_pair)
+
+    for i in range(len(loads)):
+        for s in range(count):
+            loading(i, s).start()
+    greet((to_x, to_z, to_pair))
+    for s in range(count):
+        loading(0, s).wait()
+        send_g(s).start()
+
+    rows = base.shape[1]
+
+    def tick(t, carry):
+        def stage(lag, act):
+            @pl.when((t >= lag) & (t < count + lag))
+            def run():
+                act(t - lag)
+
+        def finish(s):
+            send_back(s).wait_recv()
+            loading(5, s).wait()
+            for at, update in ((own, steps_own[s % 2]), (away, back_in[s].astype(F32))):
+                value = masters[s, :, at]
+                masters[s, :, at] = value - scale_ref[0] * (update + weight_decay * value)
+            storing(2, s).start()
+
+        def update(s):
+            for a in range(4):
+                step_x(s, a).wait_recv()
+            whole = jnp.concatenate([steps[s, b] for b in range(8)], axis=0)
+            steps_own[s % 2] = dot_plain(base[s], whole)
+
+            @pl.when(s >= 3)
+            def reuse():
+                send_back(s - 3).wait_send()
+
+            back[s % 3] = dot_plain(other[s], whole).astype(BF)
+            send_back(s).start()
+
+        def relay_x(s):
+            for a in range(2):
+                step_z(s, a).wait_recv()
+            for a in range(4):
+                step_x(s, a).start()
+
+        def relay_z(s):
+            step_pair(s).wait_recv()
+            for a in range(2):
+                step_z(s, a).start()
+
+        def adam(s):
+            send_p(s).wait_recv()
+            loading(3, s).wait()
+            loading(4, s).wait()
+            mine = near[s % 3, zh, zl].astype(F32) + z_in[s, zl].astype(F32)
+            for at, turned in ((own, mine), (away, p_in[s].astype(F32))):
+                new_first = beta_one * firsts[s, :, at] + (1.0 - beta_one) * turned
+                new_second = beta_two * seconds[s, :, at] + (1.0 - beta_two) * turned * turned
+                firsts[s, :, at] = new_first
+                seconds[s, :, at] = new_second
+                moved = new_first / scale_ref[1] / (jnp.sqrt(new_second / scale_ref[2]) + adam_epsilon)
+                step[s, :, at] = moved.astype(BF)
+            storing(0, s).start()
+            storing(1, s).start()
+            steps[s, block + 2 * zl] = step[s, :, own]
+            step_pair(s).start()
+
+        def send_far(s):
+            send_z(s).wait_recv()
+
+            @pl.when(s >= 3)
+            def reuse():
+                send_p(s - 3).wait_send()
+
+            far[s % 3] = (near[s % 3, zh, 1 - zl].astype(F32) + z_in[s, 1 - zl].astype(F32)).astype(BF)
+            send_p(s).start()
+
+        def send_near(s):
+            send_x(s).wait_recv()
+
+            @pl.when(s >= 3)
+            def reuse():
+                send_z(s - 3).wait_send()
+
+            for a in range(2):
+                for b in range(2):
+                    at = 2 * a + b
+                    total = part[s % 3, at, xx].astype(F32) + x_in[s, at].astype(F32)
+                    near[s % 3, a, b] = total.astype(BF)
+            send_z(s).start()
+
+        def turn_slot(s):
+            loading(1, s).wait()
+            loading(2, s).wait()
+            send_g(s).wait_recv()
+
+            @pl.when(s >= 3)
+            def reuse():
+                send_x(s - 3).wait_send()
+
+            turned = dot_first(base[s], g[s, :, own]) + dot_first(other[s], g_in[s])
+            for b in range(8):
+                part[s % 3, b // 2, b % 2] = turned[b * rows : (b + 1) * rows].astype(BF)
+            send_x(s).start()
+
+        stage(7, finish)
+        stage(6, update)
+        stage(5, relay_x)
+        stage(4, relay_z)
+        stage(3, adam)
+        stage(2, send_far)
+        stage(1, send_near)
+        stage(0, turn_slot)
+        return carry
+
+    lax.fori_loop(0, count + 7, tick, 0)
+    for s in range(count):
+        send_g(s).wait_send()
+        step_pair(s).wait_send()
+        for a in range(2):
+            step_z(s, a).wait_send()
+        for a in range(4):
+            step_x(s, a).wait_send()
+        for i in range(3):
+            storing(i, s).wait()
+    for s in range(count - 3, count):
+        send_x(s).wait_send()
+        send_z(s).wait_send()
+        send_p(s).wait_send()
+        send_back(s).wait_send()
+
+
+def rotate_slots(grads, base, other, first, second, master, scales):
+    count, rows, width = grads.shape
+    half = width // 2
+    hbm = pl.BlockSpec(memory_space=pl.ANY)
+    shape = jax.ShapeDtypeStruct(master.shape, F32)
+    sems = lambda n: pltpu.SemaphoreType.DMA((2, n))
+    return pl.pallas_call(
+        rotate_kernel,
+        in_specs=[hbm] * 6 + [pl.BlockSpec(memory_space=pltpu.SMEM)],
+        out_specs=[hbm] * 3,
+        out_shape=[shape] * 3,
+        scratch_shapes=[
+            pltpu.VMEM((count, rows, width), BF),
+            pltpu.VMEM((count, rows, D), BF),
+            pltpu.VMEM((count, rows, D), BF),
+            pltpu.VMEM((count, rows, width), F32),
+            pltpu.VMEM((count, rows, width), F32),
+            pltpu.VMEM((count, rows, width), F32),
+            pltpu.VMEM((count, rows, half), BF),
+            pltpu.VMEM((3, 4, 2, rows, half), BF),
+            pltpu.VMEM((count, 4, rows, half), BF),
+            pltpu.VMEM((3, 2, 2, rows, half), BF),
+            pltpu.VMEM((count, 2, rows, half), BF),
+            pltpu.VMEM((3, rows, half), BF),
+            pltpu.VMEM((count, rows, half), BF),
+            pltpu.VMEM((count, rows, width), BF),
+            pltpu.VMEM((count, 8, rows, half), BF),
+            pltpu.VMEM((3, rows, half), BF),
+            pltpu.VMEM((count, rows, half), BF),
+            pltpu.VMEM((2, rows, half), F32),
+            pltpu.SemaphoreType.DMA((6, count)),
+            pltpu.SemaphoreType.DMA((3, count)),
+            sems(count),
+            sems(count),
+            sems(count),
+            sems(count),
+            sems(count),
+            sems(count),
+            sems(2 * count),
+            sems(4 * count),
+        ],
+        compiler_params=params(collective_id=2, has_side_effects=True),
+        name="rotate_slots",
+    )(grads, base, other, first, second, master, scales)
 
 
 def row_tables(lengths, row, count):
@@ -927,19 +1324,21 @@
     slots = lambda array: jnp.transpose(array, (1, 0, 2))
     master_slots = slots(master)
 
+    groups = (8, 4, count // 32, D)
+    zh, zl, xx = blk // 4, (blk // 2) % 2, blk % 2
+
+    x_parts = to_batch(tokens, me)
     place = ((unit_owner // 9) ^ me) * 9 + unit_owner % 9
     attn_shard, ffn_shard = pick_units(place, me, batch_pieces(master_slots.astype(BF)))
-    attn = ring_gather(attn_shard, blk, 0).reshape(D, 4 * QW)
-    attn_out = batch_pieces(attn[:, 3 * QW :])
-    ffn_shard = after(ffn_shard, attn)
-    ffn = ring_gather(ffn_shard, blk, 0).reshape(D, 6 * UW)
-
-    x_own = to_rows(tokens)
-    dy_own = to_rows(cotangent)
-    x = batch_gather(x_own, me, 1).reshape(count, D)
-    dy = batch_gather(dy_own, me, 1).reshape(count, D)
+    x_own = to_rows(x_parts)
     start, low, cosine, sine = row_tables(lengths, blk, count)
     start = start.reshape(1, count)
+    base = slots(bases).astype(BF)
+    attn = ring_gather(attn_shard, blk, 0).reshape(D, 4 * QW)
+    x = batch_gather(x_own, me, 1).reshape(count, D)
+    dy_own = to_rows(after(to_batch(after(cotangent, attn_shard), me), attn))
+    dy = batch_gather(dy_own, me, 1).reshape(count, D)
+    attn_out = batch_pieces(attn[:, 3 * QW :])
 
     gain_one = small[:D].reshape(1, D)
     gain_two = small[D : 2 * D].reshape(1, D)
@@ -950,23 +1349,35 @@
     n1, q, k, v = project(x, attn, gain_one, cosine, sine)
     a_own, maps, log_mass = attend(low, lam, q, k, v, start, head_gain)
     a = batch_pieces(a_own)
+    ffn = lax.all_gather(ffn_shard, "blk", axis=0, tiled=True)
+    base_other = swap_blk(after(base, attn), 2)
     n2, x1 = middle(me, a, x, attn_out, gain_two)
-    acts, out_part, dn2_part = feed(n2, dy, ffn)
-
-    groups = (8, 4, count // 32, D)
-    dn2 = batch_scatter(dn2_part.reshape(groups), me, 1)
-    r2 = lax.rsqrt(jnp.mean(x1 * x1, axis=-1, keepdims=True) + norm_epsilon)
-    t2 = x1 * r2
-    e2 = dn2 * gain_two
-    dx1 = dy_own.astype(F32) + r2 * (e2 - t2 * jnp.mean(e2 * t2, axis=-1, keepdims=True))
-    gain_two_grad = jnp.sum(dn2 * t2, axis=(0, 1))
-    dx1_low = batch_gather(dx1.astype(BF), me, 1).reshape(count, D)
-    da = dot_plain(dx1_low, attn[:, 3 * QW :])
+    acts, out_part, dx1, dx1_low, da, gain_two_grad = feed(n2, dy, ffn, x1, dy_own, attn, gain_two)
+    gain_two_grad = gain_two_grad.reshape(D)
+
+    part = D // 8
+
+    def scatter_rows(grad):
+        def part_of(owner, half):
+            return lax.dynamic_slice_in_dim(grad, owner * part + half * part // 2, part // 2, axis=0)
+
+        return ring_scatter(part_of, blk)
+
+    ffn_grad = jnp.concatenate(
+        [dot_first(n2, acts[:, : 2 * FQ]).astype(BF), dot_first(dy, acts[:, 2 * FQ :]).astype(BF)], axis=1
+    )
+    ffn_sums = lax.psum_scatter(ffn_grad, "blk", scatter_dimension=0, tiled=True)
+
+    out_grad = dot_first(dx1_low, a_own).astype(BF)
+    da, out_grad = after((da, out_grad), base_other)
     dq, dk, dv, head_gain_sums, mixer_sums = attend_back(
         low, lam, q, k, v, start, head_gain, maps, log_mass, da, cosine, sine
     )
     dqkv = jnp.concatenate([dq, dk, dv], axis=1)
-    dn1_part = dot_last(dqkv, attn[:, : 3 * QW]).astype(BF)
+    attn_states = scatter_rows(jnp.concatenate([dot_first(n1, dqkv).astype(BF), out_grad], axis=1))
+    ffn_pieces = batch_pieces(ffn_sums)
+
+    dn1_part = dot_last(after(dqkv, attn_states[0]), attn[:, : 3 * QW]).astype(BF)
     dn1 = batch_scatter(dn1_part.reshape(groups), me, 1)
     x_f = x_own.astype(F32)
     r1 = lax.rsqrt(jnp.mean(x_f * x_f, axis=-1, keepdims=True) + norm_epsilon)
@@ -974,9 +1385,9 @@
     e1 = dn1 * gain_one
     dx = dx1 + r1 * (e1 - t1 * jnp.mean(e1 * t1, axis=-1, keepdims=True))
     gain_one_grad = jnp.sum(dn1 * t1, axis=(0, 1))
-    input_grad = from_rows(dx.astype(BF))
+    input_grad = from_rows(dx.astype(BF), me)
     out = batch_scatter(out_part.reshape(groups), me, 1)
-    block_out = from_rows((x1 + out).astype(BF))
+    block_out = from_rows((x1 + out).astype(BF), me)
 
     (mixers_grad,) = mixer_back(jnp.sum(mixer_sums))
     small_local = jnp.concatenate(
@@ -984,41 +1395,16 @@
     )
     small_grads = sum_everywhere(small_local)
 
-    part = D // 8
-
-    def scatter_rows(grad):
-        def part_of(owner, half):
-            return lax.dynamic_slice_in_dim(grad, owner * part + half * part // 2, part // 2, axis=0)
-
-        return jnp.concatenate(ring_scatter(part_of, blk), axis=0).astype(BF)
-
-    ffn_grad = jnp.concatenate(
-        [dot_first(n2, acts[:, : 2 * FQ]).astype(BF), dot_first(dy, acts[:, 2 * FQ :]).astype(BF)], axis=1
-    )
-    attn_grad = jnp.concatenate(
-        [dot_first(n1, dqkv).astype(BF), dot_first(dx1_low, a_own).astype(BF)], axis=1
-    )
-    ffn_sums = scatter_rows(ffn_grad)
-    attn_sums = scatter_rows(attn_grad)
-
     unit_of = inverse_order(unit_owner)
     units = lax.dynamic_slice_in_dim(unit_of, me * 9, 9)
-    grads = place_units(units, me, batch_pieces(attn_sums), batch_pieces(ffn_sums))
-
-    base = slots(bases).astype(BF)
-    turned_part = jnp.einsum("sja,sjn->san", base, grads, preferred_element_type=F32).astype(BF)
-
-    def turned_of(owner, half):
-        return lax.dynamic_slice_in_dim(turned_part, owner * part + half * part // 2, part // 2, axis=1)
-
-    turned = jnp.concatenate(ring_scatter(turned_of, blk), axis=1)
+    attn_pieces = batch_pieces(jnp.concatenate(attn_states[6], axis=0))
+    grads = place_units(units, me, attn_pieces, ffn_pieces)
+
     steps_done = step_count[0].astype(F32)
-    new_first = beta_one * slots(first) + (1.0 - beta_one) * turned
-    new_second = beta_two * slots(second) + (1.0 - beta_two) * turned * turned
-    normalized = adam_step(new_first, new_second, steps_done).astype(BF)
-    every_step = ring_gather(normalized, blk, 1).reshape(9, D, UW)
-    update = jnp.einsum("sja,san->sjn", base, every_step, preferred_element_type=F32)
-    new_master = master_slots - learn_rate * (update + weight_decay * master_slots)
+    scales = jnp.stack([jnp.float32(learn_rate), 1.0 - beta_one**steps_done, 1.0 - beta_two**steps_done])
+    new_first, new_second, new_master = rotate_slots(
+        grads, base, base_other, slots(first), slots(second), master_slots, scales
+    )
     new_small_first = beta_one * small_first + (1.0 - beta_one) * small_grads
     new_small_second = beta_two * small_second + (1.0 - beta_two) * small_grads * small_grads
     new_small = small - small_rate * adam_step(new_small_first, new_small_second, steps_done)

time: 1430 us -> 1280 us (0.90)
  Pallas kernels: 185 us -> 428 us
  waiting for transfers between devices: 713 us -> 496 us
  starting transfers between devices: 152 us -> 87.8 us
  other arithmetic: 123 us -> 63.2 us
  matrix products: 85 us -> 58 us
  blocking collectives: 23.2 us -> 0 us
  local copies, waits for them, and re-layouts: 127 us -> 111 us
    pallas_call x1 -> x2, Pallas kernels: 47.7 us -> 287 us  [the longest x1 198 us: rotate_slots(): pl.pallas_call(rotate_kernel, in_specs=[hbm] * 6 + [pl.BlockSpec(memory_s...]
    ppermute x42 -> x14, waiting for transfers between devices: 312 us -> 107 us  [ring_up(): lax.ppermute(piece, 'blk', [(LOOP[i], LOOP[(i + 1) % 8]) for i in range(8)])]
    ppermute x42 -> x14, waiting for transfers between devices: 243 us -> 143 us  [ring_down(): lax.ppermute(piece, 'blk', [(LOOP[(i + 1) % 8], LOOP[i]) for i in range(8)])]
    ppermute x0 -> x13, waiting for transfers between devices: none -> 99.5 us  [the longest x6 72.3 us: to_batch(): piece = lax.ppermute(piece, 'batch', [(i, i ^ other) for i in range(4)])]
    ppermute x42 -> x14, starting transfers between devices: 48 us -> 10.6 us  [ring_down(): lax.ppermute(piece, 'blk', [(LOOP[(i + 1) % 8], LOOP[i]) for i in range(8)])]
    dot_general x3 -> x0, matrix products: 30.6 us -> none  [the longest x1 13.1 us: row_groups(): jnp.einsum('sja,san->sjn', base, every_step, preferred_element_type=F32)]
    dynamic_update_slice x42 -> x14, local copies, waits for them, and re-layouts: 39.6 us -> 12.4 us  [store(): return lax.dynamic_update_slice(whole, jnp.expand_dims(piece, axis), starts)]
    dynamic_update_slice x13 -> x27, local copies, waits for them, and re-layouts: 15.7 us -> 41 us  [put(): lax.dynamic_update_slice_in_dim(whole, jnp.expand_dims(piece, axis), inde...]
  transfers between devices with their start and end apart: 129 -> 80, of which waited for: 74 -> 39; matrix products, arithmetic and copies ran while one was open for 20% -> 16% of each run, Pallas kernels for 8% -> 13%
where the time goes in v2:
time: 1280 us; the launch traced here: 1270 us
  waiting for transfers between devices  496 us (39%)
  Pallas kernels  428 us (33%)
  local copies, waits for them, and re-layouts  111 us (9%)
  starting transfers between devices  87.8 us (7%)
  other arithmetic  63.2 us (5%)
  matrix products  58 us (5%)
  between operations  23 us (2%)
    pallas_call x1, Pallas kernels, rotate_slots(): pl.pallas_call(rotate_kernel, in_specs=[hbm] * 6 + [pl.BlockSpec(memory_s...  198 us
    ppermute x14, waiting for transfers between devices, ring_down(): lax.ppermute(piece, 'blk', [(LOOP[(i + 1) % 8], LOOP[i]) for i in range(8)])  143 us
    ppermute x11, waiting for transfers between devices, swap_y(): return lax.ppermute(piece, 'batch', [(i, i ^ 2) for i in range(4)])  125 us
    ppermute x14, waiting for transfers between devices, ring_up(): lax.ppermute(piece, 'blk', [(LOOP[i], LOOP[(i + 1) % 8]) for i in range(8)])  107 us
    pallas_call x1, Pallas kernels, feed(): pl.pallas_call(feed_kernel, grid=(blocks + 4,), in_specs=[rows(D, 0), row...  88.9 us
    ppermute x6, waiting for transfers between devices, to_batch(): piece = lax.ppermute(piece, 'batch', [(i, i ^ other) for i in range(4)])  72.3 us
    pallas_call x1, Pallas kernels, attend_back(): pl.pallas_call(attend_back_kernel, grid=(HEADS, blocks), in_specs=[smem,...  54.4 us
    dot_general x4, matrix products, dot_first(): lax.dot_general(left, right, (((0,), (0,)), ((), ())), preferred_element_...  46.1 us
  transfers between devices with their start and end apart: 80, of which 39 were waited for; matrix products, arithmetic and copies ran while one was open for 16% of the time, Pallas kernels for 13%

profile of v2, /device:TPU:12, one launch (start us, length us, event | category | flops | bytes accessed | tf_op | source)
XLA Modules:
  0.0 1267.0 jit_solution(14633946828890808361)
XLA Ops:
  17.3 41.1 %collective-permute-done.1 = bf16[2,64,1536]{2,1,0:T(8,128)(2,1)S(1)} collective-permute-done((bf16[2,64,1536]{2,1,0:T(8,128)(2,1)}, bf16[2,64,1536]{2,1,0:T(8,128)(2,1)S(1)}, u32[]{:S(2)}, u32[]{:S(2)}) %collective-permute-start.1) | collective-permute-done | bytes 393248 | tf_op jit(solution)/shard_map/ppermute | solution.py:488
  58.5 10.7 collective-permute-done.2
  70.4 6.3 all-to-all-start
  99.4 10.2 all-to-all-done
  109.6 3.2 collective-permute-start.4
  112.8 3.4 broadcast.137.clone
  117.5 3.8 pick_units.1
  140.8 15.6 %collective-permute-done.33 = bf16[2,64,1536]{2,1,0:T(8,128)(2,1)S(1)} collective-permute-done((bf16[2,64,1536]{2,1,0:T(8,128)(2,1)S(1)}, bf16[2,64,1536]{2,1,0:T(8,128)(2,1)S(1)}, u32[]{:S(2)}, u32[]{:S(2)}) %collective-permute-start.33) | collective-permute-done | bytes 393248 | tf_op jit(solution)/shard_map/ppermute | solution.py:488
  159.7 4.8 collective-permute-done.34
  165.9 12.6 collective-permute-done.15
  184.1 4.0 collective-permute-start.18
  191.4 2.7 bitcast_dynamic-update-slice_fusion.6
  194.1 2.8 bitcast_dynamic-update-slice_fusion.5
  200.4 17.1 %collective-permute-done.20 = bf16[96,1536]{1,0:T(8,128)(2,1)S(1)} collective-permute-done((bf16[96,1536]{1,0:T(8,128)(2,1)S(1)}, bf16[96,1536]{1,0:T(8,128)(2,1)S(1)}, u32[]{:S(2)}, u32[]{:S(2)}) %collective-permute-start.20) | collective-permute-done | bytes 294944 | tf_op jit(solution)/shard_map/ppermute | solution.py:378
  217.5 2.7 collective-permute-start.22
  222.3 16.7 %collective-permute-done.22 = bf16[96,1536]{1,0:T(8,128)(2,1)S(1)} collective-permute-done((bf16[96,1536]{1,0:T(8,128)(2,1)S(1)}, bf16[96,1536]{1,0:T(8,128)(2,1)S(1)}, u32[]{:S(2)}, u32[]{:S(2)}) %collective-permute-start.22) | collective-permute-done | bytes 294944 | tf_op jit(solution)/shard_map/ppermute | solution.py:378
  239.0 3.7 collective-permute-start.24
  244.4 17.5 %collective-permute-done.24 = bf16[96,1536]{1,0:T(8,128)(2,1)S(1)} collective-permute-done((bf16[96,1536]{1,0:T(8,128)(2,1)S(1)}, bf16[96,1536]{1,0:T(8,128)(2,1)S(1)}, u32[]{:S(2)}, u32[]{:S(2)}) %collective-permute-start.24) | collective-permute-done | bytes 294944 | tf_op jit(solution)/shard_map/ppermute | solution.py:378
  265.0 8.5 all-to-all-start.1
  273.7 2.7 bitcast_dynamic-update-slice_fusion.4
  276.4 6.0 copy.64
  282.4 14.9 %project.1 = (bf16[2048,1536]{1,0:T(8,128)(2,1)}, bf16[2048,384]{1,0:T(8,128)(2,1)}, bf16[2048,384]{1,0:T(8,128)(2,1)}, bf16[2048,384]{1,0:T(8,128)(2,1)}) custom-call(bf16[2048,1536]{1,0:T(8,128)(2,1)} %bitcast.193, bf16[1536,1536]{1,0:T(8,128)(2,1)} %bitcast.39.w_ref.wo_ref, f32[1,1536]{1,0:T(1,128)} %reshape.210.gain_ref, ...), custom_call_target="tpu_custom_call" | custom-call | flops 7247757312 | bytes 22413312 | tf_op jit(solution)/shard_map/project/pallas_call | solution.py:631
  297.3 43.0 %attend.1 = (bf16[2048,384]{1,0:T(8,128)(2,1)}, f32[3,2,128,2048]{3,2,1,0:T(8,128)}, f32[3,8,1,512]{3,2,1,0:T(1,128)}) custom-call(s32[8]{0:T(128)} %and_select_fusion.2.low_ref, f32[1]{0:T(128)} %bitcast.22.lam_ref, bf16[2048,384]{1,0:T(8,128)(2,1)} %get-tuple-element.41.q_ref, bf16[2048,384]{1,0:T(8,128)(2,1)} %get-tuple-element.42.k_ref, ...), custom_call_target="tpu_custom_call" | custom-call | flops 12884901888 | bytes 12582912 | tf_op jit(solution)/shard_map/attend/pallas_call | solution.py:700
  344.5 33.6 %collective-permute-done.27.refs_2_ = bf16[2048,384]{1,0:T(8,128)(2,1)} collective-permute-done((bf16[2048,384]{1,0:T(8,128)(2,1)}, bf16[2048,384]{1,0:T(8,128)(2,1)}, u32[]{:S(2)}, u32[]{:S(2)}) %collective-permute-start.27) | collective-permute-done | bytes 1572896 | tf_op jit(solution)/shard_map/ppermute | solution.py:371
  378.1 25.3 %collective-permute-done.30.refs_6_ = bf16[1536,384]{1,0:T(8,128)(2,1)} collective-permute-done((bf16[1536,384]{1,0:T(8,128)(2,1)S(1)}, bf16[1536,384]{1,0:T(8,128)(2,1)}, u32[]{:S(2)}, u32[]{:S(2)}) %collective-permute-start.30) | collective-permute-done | bytes 1179680 | tf_op jit(solution)/shard_map/ppermute | solution.py:371
  403.9 7.0 convert_bitcast_fusion.base_ref
  412.5 19.4 %collective-permute-done.36 = bf16[8,64,1536]{2,1,0:T(8,128)(2,1)} collective-permute-done((bf16[8,64,1536]{2,1,0:T(8,128)(2,1)S(1)}, bf16[8,64,1536]{2,1,0:T(8,128)(2,1)}, u32[]{:S(2)}, u32[]{:S(2)}) %collective-permute-start.36) | collective-permute-done | bytes 1572896 | tf_op jit(solution)/shard_map/ppermute | solution.py:371
  431.9 20.2 %middle.1 = (bf16[2048,1536]{1,0:T(8,128)(2,1)}, f32[8,64,1536]{2,1,0:T(8,128)}) custom-call(s32[1]{0:T(128)} %bitcast.me_ref, bf16[2048,1536]{1,0:T(8,128)(2,1)} %bitcast.194, f32[1,1536]{1,0:T(1,128)} %reshape.207.gain_ref, bf16[2048,384]{1,0:T(8,128)(2,1)} %get-tuple-element.44.refs_0_, bf16[2048,384]{1,0:T(8,128)(2,1)} %collective-permute-done.26.refs_1_, ...), custom_call_target="tpu_custom_call" | custom-call | flops 9663676416 | bytes 26738688 | tf_op jit(solution)/shard_map/middle/pallas_call | solution.py:861
  455.3 3.3 copy.68
  461.3 88.9 %feed.1 = (bf16[2048,3072]{1,0:T(8,128)(2,1)}, bf16[2048,1536]{1,0:T(8,128)(2,1)}, f32[8,64,1536]{2,1,0:T(8,128)}, bf16[2048,1536]{1,0:T(8,128)(2,1)}, f32[2048,384]{1,0:T(8,128)}, /*index=5*/f32[1,1536]{1,0:T(1,128)}) custom-call(bf16[2048,1536]{1,0:T(8,128)(2,1)} %get-tuple-element.46.n_ref, bf16[2048,1536]{1,0:T(8,128)(2,1)} %bitcast.58.dy_ref, ...), custom_call_target="tpu_custom_call" | custom-call | flops 38654705664 | bytes 47185920 | tf_op jit(solution)/shard_map/feed/pallas_call | solution.py:1016
  550.2 6.2 convolution_convert_fusion.2
  556.5 54.4 %attend_back.1 = (bf16[2048,384]{1,0:T(8,128)(2,1)}, bf16[2048,384]{1,0:T(8,128)(2,1)}, bf16[2048,384]{1,0:T(8,128)(2,1)}, f32[3,128,256]{2,1,0:T(8,128)}, f32[3,1,256]{2,1,0:T(1,128)}) custom-call(s32[8]{0:T(128)} %and_select_fusion.2.low_ref, f32[1]{0:T(128)} %bitcast.22.lam_ref, bf16[2048,384]{1,0:T(8,128)(2,1)} %get-tuple-element.41.q_ref, ...), custom_call_target="tpu_custom_call" | custom-call | flops 32212254720 | bytes 18874368 | tf_op jit(solution)/shard_map/attend_back/pallas_call | solution.py:799
  613.6 12.3 convolution_convert_fusion.1
  628.3 8.4 collective-permute-done.44
  639.9 7.6 collective-permute-done.51
  650.0 17.5 %fusion.2 = bf16[1536,2048]{1,0:T(8,128)(2,1)S(1)} fusion(bf16[2048,1536]{1,0:T(8,128)(2,1)} %get-tuple-element.46.n_ref, bf16[2048,3072]{1,0:T(8,128)(2,1)} %get-tuple-element.64), kind=kOutput, calls=%fused_computation.19 | convolution fusion | flops 12888047616 | bytes 20971520 | tf_op jit(solution)/shard_map/dot_general | solution.py:359
  669.2 10.1 fusion.10
  680.6 4.6 pad_maximum_fusion
  691.6 16.4 %collective-permute-done.55 = bf16[96,1536]{1,0:T(8,128)(2,1)} collective-permute-done((bf16[96,1536]{1,0:T(8,128)(2,1)}, bf16[96,1536]{1,0:T(8,128)(2,1)}, u32[]{:S(2)}, u32[]{:S(2)}) %collective-permute-start.55) | collective-permute-done | bytes 294944 | tf_op jit(solution)/shard_map/ppermute | solution.py:378
  709.7 3.0 collective-permute-start.56
  712.7 17.7 %collective-permute-done.56 = bf16[96,1536]{1,0:T(8,128)(2,1)} collective-permute-done((bf16[96,1536]{1,0:T(8,128)(2,1)}, bf16[96,1536]{1,0:T(8,128)(2,1)}, u32[]{:S(2)}, u32[]{:S(2)}) %collective-permute-start.56) | collective-permute-done | bytes 294944 | tf_op jit(solution)/shard_map/ppermute | solution.py:378
  732.4 11.9 convolution_convert_fusion
  744.3 3.2 constant_dynamic-slice_fusion.1
  751.9 3.5 collective-permute-done.46
  755.4 3.9 convert_add_fusion
  761.7 15.0 %collective-permute-done.57 = bf16[96,1536]{1,0:T(8,128)(2,1)S(1)} collective-permute-done((bf16[96,1536]{1,0:T(8,128)(2,1)}, bf16[96,1536]{1,0:T(8,128)(2,1)S(1)}, u32[]{:S(2)}, u32[]{:S(2)}) %collective-permute-start.57) | collective-permute-done | bytes 294944 | tf_op jit(solution)/shard_map/ppermute | solution.py:382
  777.5 5.5 convert_add_fusion.1
  783.0 13.1 %collective-permute-done.47 = bf16[8,64,1536]{2,1,0:T(8,128)(2,1)S(1)} collective-permute-done((bf16[8,64,1536]{2,1,0:T(8,128)(2,1)S(1)}, bf16[8,64,1536]{2,1,0:T(8,128)(2,1)S(1)}, u32[]{:S(2)}, u32[]{:S(2)}) %collective-permute-start.47) | collective-permute-done | bytes 1572896 | tf_op jit(solution)/shard_map/ppermute | solution.py:371
  799.9 7.1 all-to-all-start.3
  807.0 3.3 fusion.23
  812.5 72.8 %collective-permute-done.59 = bf16[96,1536]{1,0:T(8,128)(2,1)} collective-permute-done((bf16[96,1536]{1,0:T(8,128)(2,1)}, bf16[96,1536]{1,0:T(8,128)(2,1)}, u32[]{:S(2)}, u32[]{:S(2)}) %collective-permute-start.59) | collective-permute-done | bytes 294944 | tf_op jit(solution)/shard_map/ppermute | solution.py:382
  889.0 5.1 collective-permute-done.60
  896.8 4.4 fusion.22
  901.3 7.4 all-to-all-start.2
  915.7 34.2 %collective-permute-done.62 = bf16[96,1536]{1,0:T(8,128)(2,1)} collective-permute-done((bf16[96,1536]{1,0:T(8,128)(2,1)}, bf16[96,1536]{1,0:T(8,128)(2,1)}, u32[]{:S(2)}, u32[]{:S(2)}) %collective-permute-start.62) | collective-permute-done | bytes 294944 | tf_op jit(solution)/shard_map/ppermute | solution.py:382
  954.4 10.1 collective-permute-done.70
  969.1 2.9 collective-permute-done.72
  994.3 5.9 collective-permute-done.50
  1002.6 23.5 %collective-permute-done.67.refs_6_ = bf16[192,3072]{1,0:T(8,128)(2,1)S(1)} collective-permute-done((bf16[192,3072]{1,0:T(8,128)(2,1)}, bf16[192,3072]{1,0:T(8,128)(2,1)S(1)}, u32[]{:S(2)}, u32[]{:S(2)}) %collective-permute-start.67) | collective-permute-done | bytes 1179680 | tf_op jit(solution)/shard_map/ppermute | solution.py:371
  1026.1 8.0 collective-permute-done.41
  1034.2 11.5 collective-permute-done.42
  1048.0 3.9 place_units.1.g_ref
  1052.0 198.3 %rotate_slots.1 = (f32[9,192,512]{2,1,0:T(8,128)}, f32[9,192,512]{2,1,0:T(8,128)}, f32[9,192,512]{2,1,0:T(8,128)}) custom-call(bf16[9,192,512]{2,1,0:T(8,128)(2,1)} %place_units.1.g_ref, bf16[9,192,1536]{2,1,0:T(8,128)(2,1)} %convert_bitcast_fusion.base_ref, bf16[9,192,1536]{2,1,0:T(8,128)(2,1)} %collective-permute-done.43.other_ref, ...), custom_call_target="tpu_custom_call" | custom-call | tf_op jit(solution)/shard_map/rotate_slots/pallas_call | solution.py:1251
  1250.3 4.3 copy.140
  (332 shorter events, 175.5 us)
Async XLA Ops:
  9.6 77.2 %collective-permute-start.10 = (bf16[9,192,512]{2,1,0:T(8,128)(2,1)S(1)}, bf16[9,192,512]{2,1,0:T(8,128)(2,1)}, u32[]{:S(2)}, u32[]{:S(2)}) collective-permute-start(bf16[9,192,512]{2,1,0:T(8,128)(2,1)S(1)} %bitcast_convert_fusion.own), channel_id=1, source_target_pairs={{0,16},{8,24},{16,0},{24,8},{1,17},{9,25},{17,1},{25,9},{2,18},{10... | collective-permute-start | bytes 5308424 | tf_op jit(solution)/shard_map/ppermute | solution.py:371
  10.2 107.4 %collective-permute-start.9 = (bf16[9,192,512]{2,1,0:T(8,128)(2,1)S(1)}, bf16[9,192,512]{2,1,0:T(8,128)(2,1)}, u32[]{:S(2)}, u32[]{:S(2)}) collective-permute-start(bf16[9,192,512]{2,1,0:T(8,128)(2,1)S(1)} %bitcast_convert_fusion.own), channel_id=1, source_target_pairs={{0,8},{8,0},{16,24},{24,16},{1,9},{9,1},{17,25},{25,17},{2,10},{10... | collective-permute-start | bytes 5308424 | tf_op jit(solution)/shard_map/ppermute | solution.py:367
  10.2 70.2 %collective-permute-start.7 = (s32[2,6]{1,0:T(2,128)S(1)}, s32[2,6]{1,0:T(2,128)S(1)}, u32[]{:S(2)}, u32[]{:S(2)}) collective-permute-start(s32[2,6]{1,0:T(2,128)S(1)} %copy-done.38), channel_id=1, source_target_pairs={{0,16},{8,24},{16,0},{24,8},{1,17},{9,25},{17,1},{25,9},{2,18},{10... | collective-permute-start | bytes 152 | tf_op jit(solution)/shard_map/ppermute | solution.py:371
  11.7 68.7 %collective-permute-start.6 = (s32[2,6]{1,0:T(2,128)S(1)}, s32[2,6]{1,0:T(2,128)S(1)}, u32[]{:S(2)}, u32[]{:S(2)}) collective-permute-start(s32[2,6]{1,0:T(2,128)S(1)} %copy-done.38), channel_id=1, source_target_pairs={{0,8},{8,0},{16,24},{24,16},{1,9},{9,1},{17,25},{25,17},{2,10},{10... | collective-permute-start | bytes 152 | tf_op jit(solution)/shard_map/ppermute | solution.py:367
  15.1 43.3 %collective-permute-start.1 = (bf16[2,64,1536]{2,1,0:T(8,128)(2,1)}, bf16[2,64,1536]{2,1,0:T(8,128)(2,1)S(1)}, u32[]{:S(2)}, u32[]{:S(2)}) collective-permute-start(bf16[2,64,1536]{2,1,0:T(8,128)(2,1)} %get-tuple-element.97), channel_id=1, source_target_pairs={{0,16},{8,24},{16,0},{24,8},{1,17},{9,25},{17,1},{25,9},{2,18},{10... | collective-permute-start | bytes 1179656 | tf_op jit(solution)/shard_map/ppermute | solution.py:488
  70.4 39.2 %all-to-all-start = ((bf16[8,64,1536]{2,1,0:T(8,128)(2,1)}), bf16[8,64,1536]{2,1,0:T(8,128)(2,1)S(1)}, u32[]{:S(2)}, u32[]{:S(2)}) async-start(bf16[8,64,1536]{2,1,0:T(8,128)(2,1)} %bitcast.195), calls=%async_computation | async-start | bytes 3145728 | tf_op jit(solution)/shard_map/all_to_all | solution.py:494
  76.7 384.6 %all-gather.2.cloned.1.call-start = ((), (), s32[]{:S(2)}) async-start(), calls=%async_computation.5 | async-start | bytes 10616832 | tf_op jit(solution)/shard_map/all_gather | solution.py:1352
  86.8 30.7 %collective-permute-start.11 = (bf16[9,192,512]{2,1,0:T(8,128)(2,1)}, bf16[9,192,512]{2,1,0:T(8,128)(2,1)}, u32[]{:S(2)}, u32[]{:S(2)}) collective-permute-start(bf16[9,192,512]{2,1,0:T(8,128)(2,1)} %collective-permute-done.10.far), channel_id=1, source_target_pairs={{0,8},{8,0},{16,24},{24,16},{1,9},{9,1},{17,25},{25,17},{2,10},{10... | collective-permute-start | bytes 5308424 | tf_op jit(solution)/shard_map/ppermute | solution.py:367
  109.6 81.8 %collective-permute-start.3 = (bf16[8,64,1536]{2,1,0:T(8,128)(2,1)S(1)}, bf16[8,64,1536]{2,1,0:T(8,128)(2,1)}, u32[]{:S(2)}, u32[]{:S(2)}) collective-permute-start(bf16[8,64,1536]{2,1,0:T(8,128)(2,1)S(1)} %all-to-all-done), channel_id=1, source_target_pairs={{0,8},{8,0},{16,24},{24,16},{1,9},{9,1},{17,25},{25,17},{2,10},{10... | collective-permute-start | bytes 4718600 | tf_op jit(solution)/shard_map/ppermute | solution.py:367
  109.6 81.8 %collective-permute-start.4 = (bf16[8,64,1536]{2,1,0:T(8,128)(2,1)S(1)}, bf16[8,64,1536]{2,1,0:T(8,128)(2,1)}, u32[]{:S(2)}, u32[]{:S(2)}) collective-permute-start(bf16[8,64,1536]{2,1,0:T(8,128)(2,1)S(1)} %all-to-all-done), channel_id=1, source_target_pairs={{0,16},{8,24},{16,0},{24,8},{1,17},{9,25},{17,1},{25,9},{2,18},{10... | collective-permute-start | bytes 4718600 | tf_op jit(solution)/shard_map/ppermute | solution.py:371
  123.9 11.5 collective-permute-start.13
  125.8 12.2 collective-permute-start.32
  133.4 23.1 %collective-permute-start.33 = (bf16[2,64,1536]{2,1,0:T(8,128)(2,1)S(1)}, bf16[2,64,1536]{2,1,0:T(8,128)(2,1)S(1)}, u32[]{:S(2)}, u32[]{:S(2)}) collective-permute-start(bf16[2,64,1536]{2,1,0:T(8,128)(2,1)S(1)} %get-tuple-element.94), channel_id=1, source_target_pairs={{0,16},{8,24},{16,0},{24,8},{1,17},{9,25},{17,1},{25,9},{2,18},{10... | collective-permute-start | bytes 1179656 | tf_op jit(solution)/shard_map/ppermute | solution.py:488
  135.4 29.1 %collective-permute-start.34 = (bf16[2,64,1536]{2,1,0:T(8,128)(2,1)S(1)}, bf16[2,64,1536]{2,1,0:T(8,128)(2,1)S(1)}, u32[]{:S(2)}, u32[]{:S(2)}) collective-permute-start(bf16[2,64,1536]{2,1,0:T(8,128)(2,1)S(1)} %get-tuple-element.93), channel_id=1, source_target_pairs={{0,24},{8,16},{16,8},{24,0},{1,25},{9,17},{17,9},{25,1},{2,26},{10... | collective-permute-start | bytes 1179656 | tf_op jit(solution)/shard_map/ppermute | solution.py:488
  137.9 27.3 %collective-permute-start.14 = (bf16[96,1536]{1,0:T(8,128)(2,1)}, bf16[96,1536]{1,0:T(8,128)(2,1)S(1)}, u32[]{:S(2)}, u32[]{:S(2)}) collective-permute-start(bf16[96,1536]{1,0:T(8,128)(2,1)} %collective-permute-done.12), channel_id=1, source_target_pairs={{0,2},{2,4},{4,6},{6,7},{7,5},{5,3},{3,1},{1,0},{8,10},{10,12},{12... | collective-permute-start | bytes 884744 | tf_op jit(solution)/shard_map/ppermute | solution.py:378
  156.5 22.0 %collective-permute-start.15 = (bf16[96,1536]{1,0:T(8,128)(2,1)}, bf16[96,1536]{1,0:T(8,128)(2,1)S(1)}, u32[]{:S(2)}, u32[]{:S(2)}) collective-permute-start(bf16[96,1536]{1,0:T(8,128)(2,1)} %collective-permute-done.13), channel_id=1, source_target_pairs={{2,0},{4,2},{6,4},{7,6},{5,7},{3,5},{1,3},{0,1},{10,8},{12,10},{14... | collective-permute-start | bytes 884744 | tf_op jit(solution)/shard_map/ppermute | solution.py:382
  165.3 18.9 %collective-permute-start.16 = (bf16[96,1536]{1,0:T(8,128)(2,1)S(1)}, bf16[96,1536]{1,0:T(8,128)(2,1)S(1)}, u32[]{:S(2)}, u32[]{:S(2)}) collective-permute-start(bf16[96,1536]{1,0:T(8,128)(2,1)S(1)} %collective-permute-done.14), channel_id=1, source_target_pairs={{0,2},{2,4},{4,6},{6,7},{7,5},{5,3},{3,1},{1,0},{8,10},{10,12},{12... | collective-permute-start | bytes 884744 | tf_op jit(solution)/shard_map/ppermute | solution.py:378
  178.5 11.2 collective-permute-start.17
  184.1 12.8 %collective-permute-start.18 = (bf16[96,1536]{1,0:T(8,128)(2,1)S(1)}, bf16[96,1536]{1,0:T(8,128)(2,1)S(1)}, u32[]{:S(2)}, u32[]{:S(2)}) collective-permute-start(bf16[96,1536]{1,0:T(8,128)(2,1)S(1)} %collective-permute-done.16), channel_id=1, source_target_pairs={{0,2},{2,4},{4,6},{6,7},{7,5},{5,3},{3,1},{1,0},{8,10},{10,12},{12... | collective-permute-start | bytes 884744 | tf_op jit(solution)/shard_map/ppermute | solution.py:378
  191.4 82.3 %collective-permute-start.5 = (bf16[8,64,1536]{2,1,0:T(8,128)(2,1)}, bf16[8,64,1536]{2,1,0:T(8,128)(2,1)}, u32[]{:S(2)}, u32[]{:S(2)}) collective-permute-start(bf16[8,64,1536]{2,1,0:T(8,128)(2,1)} %collective-permute-done.4), channel_id=1, source_target_pairs={{0,8},{8,0},{16,24},{24,16},{1,9},{9,1},{17,25},{25,17},{2,10},{10... | collective-permute-start | bytes 4718600 | tf_op jit(solution)/shard_map/ppermute | solution.py:367
  196.9 20.6 %collective-permute-start.20 = (bf16[96,1536]{1,0:T(8,128)(2,1)S(1)}, bf16[96,1536]{1,0:T(8,128)(2,1)S(1)}, u32[]{:S(2)}, u32[]{:S(2)}) collective-permute-start(bf16[96,1536]{1,0:T(8,128)(2,1)S(1)} %collective-permute-done.18), channel_id=1, source_target_pairs={{0,2},{2,4},{4,6},{6,7},{7,5},{5,3},{3,1},{1,0},{8,10},{10,12},{12... | collective-permute-start | bytes 884744 | tf_op jit(solution)/shard_map/ppermute | solution.py:378
  198.7 21.6 %collective-permute-start.21 = (bf16[96,1536]{1,0:T(8,128)(2,1)S(1)}, bf16[96,1536]{1,0:T(8,128)(2,1)S(1)}, u32[]{:S(2)}, u32[]{:S(2)}) collective-permute-start(bf16[96,1536]{1,0:T(8,128)(2,1)S(1)} %collective-permute-done.19), channel_id=1, source_target_pairs={{2,0},{4,2},{6,4},{7,6},{5,7},{3,5},{1,3},{0,1},{10,8},{12,10},{14... | collective-permute-start | bytes 884744 | tf_op jit(solution)/shard_map/ppermute | solution.py:382
  217.5 21.5 %collective-permute-start.22 = (bf16[96,1536]{1,0:T(8,128)(2,1)S(1)}, bf16[96,1536]{1,0:T(8,128)(2,1)S(1)}, u32[]{:S(2)}, u32[]{:S(2)}) collective-permute-start(bf16[96,1536]{1,0:T(8,128)(2,1)S(1)} %collective-permute-done.20), channel_id=1, source_target_pairs={{0,2},{2,4},{4,6},{6,7},{7,5},{5,3},{3,1},{1,0},{8,10},{10,12},{12... | collective-permute-start | bytes 884744 | tf_op jit(solution)/shard_map/ppermute | solution.py:378
  220.3 22.4 %collective-permute-start.23 = (bf16[96,1536]{1,0:T(8,128)(2,1)S(1)}, bf16[96,1536]{1,0:T(8,128)(2,1)S(1)}, u32[]{:S(2)}, u32[]{:S(2)}) collective-permute-start(bf16[96,1536]{1,0:T(8,128)(2,1)S(1)} %collective-permute-done.21), channel_id=1, source_target_pairs={{2,0},{4,2},{6,4},{7,6},{5,7},{3,5},{1,3},{0,1},{10,8},{12,10},{14... | collective-permute-start | bytes 884744 | tf_op jit(solution)/shard_map/ppermute | solution.py:382
  239.0 22.9 %collective-permute-start.24 = (bf16[96,1536]{1,0:T(8,128)(2,1)S(1)}, bf16[96,1536]{1,0:T(8,128)(2,1)S(1)}, u32[]{:S(2)}, u32[]{:S(2)}) collective-permute-start(bf16[96,1536]{1,0:T(8,128)(2,1)S(1)} %collective-permute-done.22), channel_id=1, source_target_pairs={{0,2},{2,4},{4,6},{6,7},{7,5},{5,3},{3,1},{1,0},{8,10},{10,12},{12... | collective-permute-start | bytes 884744 | tf_op jit(solution)/shard_map/ppermute | solution.py:378
  242.7 21.6 %collective-permute-start.25 = (bf16[96,1536]{1,0:T(8,128)(2,1)S(1)}, bf16[96,1536]{1,0:T(8,128)(2,1)S(1)}, u32[]{:S(2)}, u32[]{:S(2)}) collective-permute-start(bf16[96,1536]{1,0:T(8,128)(2,1)S(1)} %collective-permute-done.23), channel_id=1, source_target_pairs={{2,0},{4,2},{6,4},{7,6},{5,7},{3,5},{1,3},{0,1},{10,8},{12,10},{14... | collective-permute-start | bytes 884744 | tf_op jit(solution)/shard_map/ppermute | solution.py:382
  265.0 79.4 %all-to-all-start.1 = ((bf16[8,64,1536]{2,1,0:T(8,128)(2,1)}), bf16[8,64,1536]{2,1,0:T(8,128)(2,1)S(1)}, u32[]{:S(2)}, u32[]{:S(2)}) async-start(bf16[8,64,1536]{2,1,0:T(8,128)(2,1)} %bitcast.52), calls=%async_computation.1 | async-start | bytes 3145728 | tf_op jit(solution)/shard_map/all_to_all | solution.py:494
  273.5 715.1 %reduce-scatter.2.cloned.1.call-start = ((), (), s32[]{:S(2)}) async-start(), calls=%async_computation.6 | async-start | bytes 10616832 | tf_op jit(solution)/shard_map/reduce_scatter | solution.py:1369
  340.3 37.7 %collective-permute-start.27 = (bf16[2048,384]{1,0:T(8,128)(2,1)}, bf16[2048,384]{1,0:T(8,128)(2,1)}, u32[]{:S(2)}, u32[]{:S(2)}) collective-permute-start(bf16[2048,384]{1,0:T(8,128)(2,1)} %get-tuple-element.44.refs_0_), channel_id=1, source_target_pairs={{0,16},{8,24},{16,0},{24,8},{1,17},{9,25},{17,1},{25,9},{2,18},{10... | collective-permute-start | bytes 4718600 | tf_op jit(solution)/shard_map/ppermute | solution.py:371
  341.8 61.5 %collective-permute-start.30 = (bf16[1536,384]{1,0:T(8,128)(2,1)S(1)}, bf16[1536,384]{1,0:T(8,128)(2,1)}, u32[]{:S(2)}, u32[]{:S(2)}) collective-permute-start(bf16[1536,384]{1,0:T(8,128)(2,1)S(1)} %slice.100.refs_4_), channel_id=1, source_target_pairs={{0,16},{8,24},{16,0},{24,8},{1,17},{9,25},{17,1},{25,9},{2,18},{10... | collective-permute-start | bytes 3538952 | tf_op jit(solution)/shard_map/ppermute | solution.py:371
  343.9 59.4 %collective-permute-start.29 = (bf16[1536,384]{1,0:T(8,128)(2,1)S(1)}, bf16[1536,384]{1,0:T(8,128)(2,1)}, u32[]{:S(2)}, u32[]{:S(2)}) collective-permute-start(bf16[1536,384]{1,0:T(8,128)(2,1)S(1)} %slice.100.refs_4_), channel_id=1, source_target_pairs={{0,8},{8,0},{16,24},{24,16},{1,9},{9,1},{17,25},{25,17},{2,10},{10... | collective-permute-start | bytes 3538952 | tf_op jit(solution)/shard_map/ppermute | solution.py:367
  343.9 68.5 %collective-permute-start.26 = (bf16[2048,384]{1,0:T(8,128)(2,1)}, bf16[2048,384]{1,0:T(8,128)(2,1)}, u32[]{:S(2)}, u32[]{:S(2)}) collective-permute-start(bf16[2048,384]{1,0:T(8,128)(2,1)} %get-tuple-element.44.refs_0_), channel_id=1, source_target_pairs={{0,8},{8,0},{16,24},{24,16},{1,9},{9,1},{17,25},{25,17},{2,10},{10... | collective-permute-start | bytes 4718600 | tf_op jit(solution)/shard_map/ppermute | solution.py:367
  344.4 87.5 %collective-permute-start.36 = (bf16[8,64,1536]{2,1,0:T(8,128)(2,1)S(1)}, bf16[8,64,1536]{2,1,0:T(8,128)(2,1)}, u32[]{:S(2)}, u32[]{:S(2)}) collective-permute-start(bf16[8,64,1536]{2,1,0:T(8,128)(2,1)S(1)} %all-to-all-done.1.dyo_ref), channel_id=1, source_target_pairs={{0,16},{8,24},{16,0},{24,8},{1,17},{9,25},{17,1},{25,9},{2,18},{10... | collective-permute-start | bytes 4718600 | tf_op jit(solution)/shard_map/ppermute | solution.py:371
  378.1 53.9 %collective-permute-start.28 = (bf16[2048,384]{1,0:T(8,128)(2,1)}, bf16[2048,384]{1,0:T(8,128)(2,1)}, u32[]{:S(2)}, u32[]{:S(2)}) collective-permute-start(bf16[2048,384]{1,0:T(8,128)(2,1)} %collective-permute-done.27.refs_2_), channel_id=1, source_target_pairs={{0,8},{8,0},{16,24},{24,16},{1,9},{9,1},{17,25},{25,17},{2,10},{10... | collective-permute-start | bytes 4718600 | tf_op jit(solution)/shard_map/ppermute | solution.py:367
  403.3 28.6 %collective-permute-start.31 = (bf16[1536,384]{1,0:T(8,128)(2,1)}, bf16[1536,384]{1,0:T(8,128)(2,1)}, u32[]{:S(2)}, u32[]{:S(2)}) collective-permute-start(bf16[1536,384]{1,0:T(8,128)(2,1)} %collective-permute-done.30.refs_6_), channel_id=1, source_target_pairs={{0,8},{8,0},{16,24},{24,16},{1,9},{9,1},{17,25},{25,17},{2,10},{10... | collective-permute-start | bytes 3538952 | tf_op jit(solution)/shard_map/ppermute | solution.py:367
  403.3 48.8 %collective-permute-start.35 = (bf16[8,64,1536]{2,1,0:T(8,128)(2,1)S(1)}, bf16[8,64,1536]{2,1,0:T(8,128)(2,1)}, u32[]{:S(2)}, u32[]{:S(2)}) collective-permute-start(bf16[8,64,1536]{2,1,0:T(8,128)(2,1)S(1)} %all-to-all-done.1.dyo_ref), channel_id=1, source_target_pairs={{0,8},{8,0},{16,24},{24,16},{1,9},{9,1},{17,25},{25,17},{2,10},{10... | collective-permute-start | bytes 4718600 | tf_op jit(solution)/shard_map/ppermute | solution.py:367
  412.4 144.1 %collective-permute-start.43 = (bf16[9,192,1536]{2,1,0:T(8,128)(2,1)}, bf16[9,192,1536]{2,1,0:T(8,128)(2,1)}, u32[]{:S(2)}, u32[]{:S(2)}) collective-permute-start(bf16[9,192,1536]{2,1,0:T(8,128)(2,1)} %convert_bitcast_fusion.base_ref), channel_id=1, source_target_pairs={{0,2},{1,3},{2,0},{3,1},{4,6},{5,7},{6,4},{7,5},{8,10},{9,11},{10,... | collective-permute-start | bytes 15925256 | tf_op jit(solution)/shard_map/ppermute | solution.py:474
  431.9 26.7 %collective-permute-start.37 = (bf16[8,64,1536]{2,1,0:T(8,128)(2,1)}, bf16[8,64,1536]{2,1,0:T(8,128)(2,1)}, u32[]{:S(2)}, u32[]{:S(2)}) collective-permute-start(bf16[8,64,1536]{2,1,0:T(8,128)(2,1)} %collective-permute-done.36), channel_id=1, source_target_pairs={{0,8},{8,0},{16,24},{24,16},{1,9},{9,1},{17,25},{25,17},{2,10},{10... | collective-permute-start | bytes 4718600 | tf_op jit(solution)/shard_map/ppermute | solution.py:367
  648.6 18.9 %collective-permute-start.52 = (bf16[96,1536]{1,0:T(8,128)(2,1)S(1)}, bf16[96,1536]{1,0:T(8,128)(2,1)S(1)}, u32[]{:S(2)}, u32[]{:S(2)}) collective-permute-start(bf16[96,1536]{1,0:T(8,128)(2,1)S(1)} %add_convert_fusion.11), channel_id=1, source_target_pairs={{0,2},{2,4},{4,6},{6,7},{7,5},{5,3},{3,1},{1,0},{8,10},{10,12},{12... | collective-permute-start | bytes 884744 | tf_op jit(solution)/shard_map/ppermute | solution.py:378
  667.6 11.7 collective-permute-start.53
  689.6 18.4 %collective-permute-start.55 = (bf16[96,1536]{1,0:T(8,128)(2,1)}, bf16[96,1536]{1,0:T(8,128)(2,1)}, u32[]{:S(2)}, u32[]{:S(2)}) collective-permute-start(bf16[96,1536]{1,0:T(8,128)(2,1)} %add_convert_fusion.8), channel_id=1, source_target_pairs={{0,2},{2,4},{4,6},{6,7},{7,5},{5,3},{3,1},{1,0},{8,10},{10,12},{12... | collective-permute-start | bytes 884744 | tf_op jit(solution)/shard_map/ppermute | solution.py:378
  690.2 22.5 %collective-permute-start.45 = (bf16[96,1536]{1,0:T(8,128)(2,1)}, bf16[96,1536]{1,0:T(8,128)(2,1)}, u32[]{:S(2)}, u32[]{:S(2)}) collective-permute-start(bf16[96,1536]{1,0:T(8,128)(2,1)} %get-tuple-element.85), channel_id=1, source_target_pairs={{2,0},{4,2},{6,4},{7,6},{5,7},{3,5},{1,3},{0,1},{10,8},{12,10},{14... | collective-permute-start | bytes 884744 | tf_op jit(solution)/shard_map/ppermute | solution.py:382
  709.7 20.7 %collective-permute-start.56 = (bf16[96,1536]{1,0:T(8,128)(2,1)}, bf16[96,1536]{1,0:T(8,128)(2,1)}, u32[]{:S(2)}, u32[]{:S(2)}) collective-permute-start(bf16[96,1536]{1,0:T(8,128)(2,1)} %add_convert_fusion.7), channel_id=1, source_target_pairs={{0,2},{2,4},{4,6},{6,7},{7,5},{5,3},{3,1},{1,0},{8,10},{10,12},{12... | collective-permute-start | bytes 884744 | tf_op jit(solution)/shard_map/ppermute | solution.py:378
  751.3 26.1 %collective-permute-start.38 = (bf16[8,2,64,1536]{3,2,0,1:T(8,128)(2,1)}, bf16[8,2,64,1536]{3,2,0,1:T(8,128)(2,1)}, u32[]{:S(2)}, u32[]{:S(2)}) collective-permute-start(bf16[8,2,64,1536]{3,2,0,1:T(8,128)(2,1)} %bitcast.191), channel_id=1, source_target_pairs={{0,8},{8,0},{16,24},{24,16},{1,9},{9,1},{17,25},{25,17},{2,10},{10... | collective-permute-start | bytes 9437192 | tf_op jit(solution)/shard_map/ppermute | solution.py:367
  751.9 24.8 %collective-permute-start.57 = (bf16[96,1536]{1,0:T(8,128)(2,1)}, bf16[96,1536]{1,0:T(8,128)(2,1)S(1)}, u32[]{:S(2)}, u32[]{:S(2)}) collective-permute-start(bf16[96,1536]{1,0:T(8,128)(2,1)} %get-tuple-element.84), channel_id=1, source_target_pairs={{2,0},{4,2},{6,4},{7,6},{5,7},{3,5},{1,3},{0,1},{10,8},{12,10},{14... | collective-permute-start | bytes 884744 | tf_op jit(solution)/shard_map/ppermute | solution.py:382
  759.5 36.5 %collective-permute-start.47 = (bf16[8,64,1536]{2,1,0:T(8,128)(2,1)S(1)}, bf16[8,64,1536]{2,1,0:T(8,128)(2,1)S(1)}, u32[]{:S(2)}, u32[]{:S(2)}) collective-permute-start(bf16[8,64,1536]{2,1,0:T(8,128)(2,1)S(1)} %fusion.24), channel_id=1, source_target_pairs={{0,16},{8,24},{16,0},{24,8},{1,17},{9,25},{17,1},{25,9},{2,18},{10... | collective-permute-start | bytes 4718600 | tf_op jit(solution)/shard_map/ppermute | solution.py:371
  777.5 33.2 %collective-permute-start.58 = (bf16[96,1536]{1,0:T(8,128)(2,1)}, bf16[96,1536]{1,0:T(8,128)(2,1)}, u32[]{:S(2)}, u32[]{:S(2)}) collective-permute-start(bf16[96,1536]{1,0:T(8,128)(2,1)} %add_convert_fusion.5), channel_id=1, source_target_pairs={{2,0},{4,2},{6,4},{7,6},{5,7},{3,5},{1,3},{0,1},{10,8},{12,10},{14... | collective-permute-start | bytes 884744 | tf_op jit(solution)/shard_map/ppermute | solution.py:382
  799.9 101.3 %all-to-all-start.3 = ((bf16[8,64,1536]{2,1,0:T(8,128)(2,1)}), bf16[8,64,1536]{2,1,0:T(8,128)(2,1)}, u32[]{:S(2)}, u32[]{:S(2)}) async-start(bf16[8,64,1536]{2,1,0:T(8,128)(2,1)} %fusion.18), calls=%async_computation.3 | async-start | bytes 3145728 | tf_op jit(solution)/shard_map/all_to_all | solution.py:499
  810.3 86.5 %collective-permute-start.39 = (bf16[8,64,1536]{2,1,0:T(8,128)(2,1)}, bf16[8,64,1536]{2,1,0:T(8,128)(2,1)}, u32[]{:S(2)}, u32[]{:S(2)}) collective-permute-start(bf16[8,64,1536]{2,1,0:T(8,128)(2,1)} %fusion.23), channel_id=1, source_target_pairs={{0,16},{8,24},{16,0},{24,8},{1,17},{9,25},{17,1},{25,9},{2,18},{10... | collective-permute-start | bytes 4718600 | tf_op jit(solution)/shard_map/ppermute | solution.py:371
  812.5 72.8 %collective-permute-start.59 = (bf16[96,1536]{1,0:T(8,128)(2,1)}, bf16[96,1536]{1,0:T(8,128)(2,1)}, u32[]{:S(2)}, u32[]{:S(2)}) collective-permute-start(bf16[96,1536]{1,0:T(8,128)(2,1)} %add_convert_fusion.4), channel_id=1, source_target_pairs={{2,0},{4,2},{6,4},{7,6},{5,7},{3,5},{1,3},{0,1},{10,8},{12,10},{14... | collective-permute-start | bytes 884744 | tf_op jit(solution)/shard_map/ppermute | solution.py:382
  895.9 12.8 %collective-permute-start.61 = (bf16[96,1536]{1,0:T(8,128)(2,1)}, bf16[96,1536]{1,0:T(8,128)(2,1)}, u32[]{:S(2)}, u32[]{:S(2)}) collective-permute-start(bf16[96,1536]{1,0:T(8,128)(2,1)} %add_convert_fusion.2), channel_id=1, source_target_pairs={{2,0},{4,2},{6,4},{7,6},{5,7},{3,5},{1,3},{0,1},{10,8},{12,10},{14... | collective-permute-start | bytes 884744 | tf_op jit(solution)/shard_map/ppermute | solution.py:382
  901.3 83.9 %all-to-all-start.2 = ((bf16[8,64,1536]{2,1,0:T(8,128)(2,1)}), bf16[8,64,1536]{2,1,0:T(8,128)(2,1)}, u32[]{:S(2)}, u32[]{:S(2)}) async-start(bf16[8,64,1536]{2,1,0:T(8,128)(2,1)} %fusion.22), calls=%async_computation.2 | async-start | bytes 3145728 | tf_op jit(solution)/shard_map/all_to_all | solution.py:499
  910.4 39.4 %collective-permute-start.62 = (bf16[96,1536]{1,0:T(8,128)(2,1)}, bf16[96,1536]{1,0:T(8,128)(2,1)}, u32[]{:S(2)}, u32[]{:S(2)}) collective-permute-start(bf16[96,1536]{1,0:T(8,128)(2,1)} %add_convert_fusion.1), channel_id=1, source_target_pairs={{2,0},{4,2},{6,4},{7,6},{5,7},{3,5},{1,3},{0,1},{10,8},{12,10},{14... | collective-permute-start | bytes 884744 | tf_op jit(solution)/shard_map/ppermute | solution.py:382
  951.0 23.8 %collective-permute-start.64 = (bf16[192,1536]{1,0:T(8,128)(2,1)S(1)}, bf16[192,1536]{1,0:T(8,128)(2,1)S(1)}, u32[]{:S(2)}, u32[]{:S(2)}) collective-permute-start(bf16[192,1536]{1,0:T(8,128)(2,1)S(1)} %pad_maximum_fusion.1.refs_0_), channel_id=1, source_target_pairs={{0,16},{8,24},{16,0},{24,8},{1,17},{9,25},{17,1},{25,9},{2,18},{10... | collective-permute-start | bytes 1769480 | tf_op jit(solution)/shard_map/ppermute | solution.py:371
  952.7 11.8 collective-permute-start.70
  974.7 71.0 %collective-permute-start.63 = (bf16[192,1536]{1,0:T(8,128)(2,1)S(1)}, bf16[192,1536]{1,0:T(8,128)(2,1)S(1)}, u32[]{:S(2)}, u32[]{:S(2)}) collective-permute-start(bf16[192,1536]{1,0:T(8,128)(2,1)S(1)} %pad_maximum_fusion.1.refs_0_), channel_id=1, source_target_pairs={{0,8},{8,0},{16,24},{24,16},{1,9},{9,1},{17,25},{25,17},{2,10},{10... | collective-permute-start | bytes 1769480 | tf_op jit(solution)/shard_map/ppermute | solution.py:367
  974.7 71.0 %collective-permute-start.65 = (bf16[192,1536]{1,0:T(8,128)(2,1)S(1)}, bf16[192,1536]{1,0:T(8,128)(2,1)}, u32[]{:S(2)}, u32[]{:S(2)}) collective-permute-start(bf16[192,1536]{1,0:T(8,128)(2,1)S(1)} %collective-permute-done.64.refs_2_), channel_id=1, source_target_pairs={{0,8},{8,0},{16,24},{24,16},{1,9},{9,1},{17,25},{25,17},{2,10},{10... | collective-permute-start | bytes 1769480 | tf_op jit(solution)/shard_map/ppermute | solution.py:367
  980.3 12.2 collective-permute-start.49
  980.6 19.5 %collective-permute-start.50 = (bf16[2,64,1536]{2,1,0:T(8,128)(2,1)}, bf16[2,64,1536]{2,1,0:T(8,128)(2,1)}, u32[]{:S(2)}, u32[]{:S(2)}) collective-permute-start(bf16[2,64,1536]{2,1,0:T(8,128)(2,1)} %get-tuple-element.87), channel_id=1, source_target_pairs={{0,24},{8,16},{16,8},{24,0},{1,25},{9,17},{17,9},{25,1},{2,26},{10... | collective-permute-start | bytes 1179656 | tf_op jit(solution)/shard_map/ppermute | solution.py:504
  988.6 37.5 %collective-permute-start.67 = (bf16[192,3072]{1,0:T(8,128)(2,1)}, bf16[192,3072]{1,0:T(8,128)(2,1)S(1)}, u32[]{:S(2)}, u32[]{:S(2)}) collective-permute-start(bf16[192,3072]{1,0:T(8,128)(2,1)} %reduce-scatter.2.cloned.1.call-done.refs_4_), channel_id=1, source_target_pairs={{0,16},{8,24},{16,0},{24,8},{1,17},{9,25},{17,1},{25,9},{2,18},{10... | collective-permute-start | bytes 3538952 | tf_op jit(solution)/shard_map/ppermute | solution.py:371
  1000.1 34.0 %collective-permute-start.41 = (bf16[2,64,1536]{2,1,0:T(8,128)(2,1)}, bf16[2,64,1536]{2,1,0:T(8,128)(2,1)S(1)}, u32[]{:S(2)}, u32[]{:S(2)}) collective-permute-start(bf16[2,64,1536]{2,1,0:T(8,128)(2,1)} %get-tuple-element.91), channel_id=1, source_target_pairs={{0,16},{8,24},{16,0},{24,8},{1,17},{9,25},{17,1},{25,9},{2,18},{10... | collective-permute-start | bytes 1179656 | tf_op jit(solution)/shard_map/ppermute | solution.py:504
  1002.2 43.5 %collective-permute-start.66 = (bf16[192,3072]{1,0:T(8,128)(2,1)}, bf16[192,3072]{1,0:T(8,128)(2,1)S(1)}, u32[]{:S(2)}, u32[]{:S(2)}) collective-permute-start(bf16[192,3072]{1,0:T(8,128)(2,1)} %reduce-scatter.2.cloned.1.call-done.refs_4_), channel_id=1, source_target_pairs={{0,8},{8,0},{16,24},{24,16},{1,9},{9,1},{17,25},{25,17},{2,10},{10... | collective-permute-start | bytes 3538952 | tf_op jit(solution)/shard_map/ppermute | solution.py:367
  1026.1 19.7 %collective-permute-start.68 = (bf16[192,3072]{1,0:T(8,128)(2,1)S(1)}, bf16[192,3072]{1,0:T(8,128)(2,1)S(1)}, u32[]{:S(2)}, u32[]{:S(2)}) collective-permute-start(bf16[192,3072]{1,0:T(8,128)(2,1)S(1)} %collective-permute-done.67.refs_6_), channel_id=1, source_target_pairs={{0,8},{8,0},{16,24},{24,16},{1,9},{9,1},{17,25},{25,17},{2,10},{10... | collective-permute-start | bytes 3538952 | tf_op jit(solution)/shard_map/ppermute | solution.py:367
  1034.1 11.5 collective-permute-start.42
  (60 other events, 1160.9 us)
Sparse Core Ops, SparseCore 0:
  126.0 195.1 all-gather.1
  685.3 199.7 reduce-scatter.1

commit v3 on v2

--- a/solution.py
+++ b/solution.py
@@ -371,17 +371,6 @@
     return lax.ppermute(piece, "batch", [(i, i ^ 2) for i in range(4)])
 
 
-LOOP = (0, 2, 4, 6, 7, 5, 3, 1)
-
-
-def ring_up(piece):
-    return lax.ppermute(piece, "blk", [(LOOP[i], LOOP[(i + 1) % 8]) for i in range(8)])
-
-
-def ring_down(piece):
-    return lax.ppermute(piece, "blk", [(LOOP[(i + 1) % 8], LOOP[i]) for i in range(8)])
-
-
 def sum_everywhere(values):
     values = values + swap_core(values)
     values = values + swap_y(values)
@@ -395,16 +384,14 @@
 
 
 def ring_place(blk):
-    return jnp.where(blk % 2 == 0, blk // 2, 7 - blk // 2)
+    side = blk % 2
+    return (1 - side) * (blk // 2) + side * (7 - blk // 2)
 
 
 def ring_owner(place):
-    place = place % 8
-    return jnp.where(place < 4, 2 * place, 2 * (7 - place) + 1)
-
-
-def put(whole, piece, index, axis):
-    return lax.dynamic_update_slice_in_dim(whole, jnp.expand_dims(piece, axis), index, axis)
+    place = (place + 16) % 8
+    side = place // 4
+    return 2 * ((1 - side) * place + side * (7 - place)) + side
 
 
 def batch_pieces(piece):
@@ -412,98 +399,275 @@
     return (piece, swap_core(piece), far, swap_core(far))
 
 
-def batch_gather(piece, me, axis):
-    pieces = batch_pieces(piece)
-    shape = piece.shape[:axis] + (4,) + piece.shape[axis:]
-    whole = jnp.zeros(shape, piece.dtype)
-    for other in range(4):
-        whole = put(whole, pieces[other], me ^ other, axis)
-    return whole
-
-
-def batch_scatter(partial, me, axis):
-    shape = partial.shape
-    split = partial.reshape(shape[:axis] + (2, 2) + shape[axis + 1 :])
-    y, core = me // 2, me % 2
-
-    def pick(array, index, at):
-        return lax.dynamic_index_in_dim(array, index, at, keepdims=False)
-
-    near = pick(split, core, axis + 1).astype(F32) + swap_core(pick(split, 1 - core, axis + 1)).astype(F32)
-    far = swap_y(pick(near, 1 - y, axis).astype(BF))
-    return pick(near, y, axis) + far.astype(F32)
-
-
-def ring_gather(shard, blk, axis, waits=()):
-    half = shard.shape[axis] // 2
-    place = ring_place(blk)
-    shape = shard.shape[:axis] + (8,) + shard.shape[axis:]
-    whole = put(jnp.zeros(shape, shard.dtype), shard, blk, axis)
-    up = lax.slice_in_dim(shard, 0, half, axis=axis)
-    down = lax.slice_in_dim(shard, half, 2 * half, axis=axis)
-
-    def store(whole, piece, owner, begin):
-        starts = [0] * len(shape)
-        starts[axis] = owner
-        starts[axis + 1] = begin
-        return lax.dynamic_update_slice(whole, jnp.expand_dims(piece, axis), starts)
-
-    for step in range(1, 8):
-        for at, arrays in waits:
-            if at == step:
-                up, down = after((up, down), arrays)
-        up, down = ring_up(up), ring_down(down)
-        whole = store(whole, up, ring_owner(place - step), 0)
-        whole = store(whole, down, ring_owner(place + step), half)
-    return whole
-
-
-def ring_scatter(part_of, blk):
-    place = ring_place(blk)
-    up, down = part_of(ring_owner(place - 1), 0), part_of(ring_owner(place + 1), 1)
-    states = []
-    for step in range(1, 8):
-        up, down = ring_up(up.astype(BF)), ring_down(down.astype(BF))
-        up = (up.astype(F32) + part_of(ring_owner(place - 1 - step), 0).astype(F32)).astype(BF)
-        down = (down.astype(F32) + part_of(ring_owner(place + 1 + step), 1).astype(F32)).astype(BF)
-        states.append((up, down))
-    return states
+def pick(array, index, axis):
+    return lax.dynamic_index_in_dim(array, index, axis, keepdims=False)
+
+
+def near_sum(partial, me):
+    split = partial.reshape(partial.shape[:1] + (2, 2) + partial.shape[2:])
+    core = me % 2
+    return (pick(split, core, 2).astype(F32) + swap_core(pick(split, 1 - core, 2)).astype(F32)).astype(BF)
+
+
+def far_sum(near, me):
+    y = me // 2
+    return pick(near, y, 1).astype(F32) + swap_y(pick(near, 1 - y, 1)).astype(F32)
 
 
 def swap_blk(piece, bit):
     return lax.ppermute(piece, "blk", [(i, i ^ bit) for i in range(8)])
 
 
-def choose(flag, zero, one):
-    return jnp.where(flag == 0, zero, one)
-
-
-def to_batch(tokens, me):
-    rows, count, width = tokens.shape
-    pieces = tokens.reshape(rows, 4, count // 4, width)
-    whole = jnp.zeros((4, rows, count // 4, width), tokens.dtype)
-    for other in range(4):
-        piece = lax.dynamic_index_in_dim(pieces, me ^ other, 1, keepdims=False)
-        if other:
-            piece = lax.ppermute(piece, "batch", [(i, i ^ other) for i in range(4)])
-        whole = put(whole, piece, me ^ other, 0)
-    return whole.reshape(8, count // 4, width)
-
-
-def to_rows(pieces):
-    return lax.all_to_all(pieces, "blk", 0, 0, tiled=True)
-
-
-def from_rows(tokens, me):
-    count, width = tokens.shape[1:]
-    pieces = lax.all_to_all(tokens, "blk", 0, 0, tiled=True).reshape(4, 2, count, width)
-    whole = jnp.zeros((2, 4, count, width), tokens.dtype)
-    for other in range(4):
-        piece = lax.dynamic_index_in_dim(pieces, me ^ other, 0, keepdims=False)
-        if other:
-            piece = lax.ppermute(piece, "batch", [(i, i ^ other) for i in range(4)])
-        whole = put(whole, piece, me ^ other, 1)
-    return whole.reshape(2, 4 * count, width)
+MESH = pl.DeviceIdType.MESH
+
+
+def greet(devices):
+    barrier = pltpu.get_barrier_semaphore()
+    for device in devices:
+        pl.semaphore_signal(barrier, inc=1, device_id=device, device_id_type=MESH)
+    pl.semaphore_wait(barrier, len(devices))
+
+
+def greet_all():
+    barrier = pltpu.get_barrier_semaphore()
+    me, blk = lax.axis_index("batch"), lax.axis_index("blk")
+
+    def signal(n, carry):
+        at = (me * 8 + blk + n) % 32
+        pl.semaphore_signal(barrier, inc=1, device_id=(at // 8, at % 8), device_id_type=MESH)
+        return carry
+
+    lax.fori_loop(1, 32, signal, 0)
+    pl.semaphore_wait(barrier, 31)
+
+
+def remote(source, target, sems, at, device):
+    return pltpu.make_async_remote_copy(
+        src_ref=source,
+        dst_ref=target,
+        send_sem=sems.at[0, at],
+        recv_sem=sems.at[1, at],
+        device_id=device,
+        device_id_type=MESH,
+    )
+
+
+def scatter_rows_copies(source, target, sems, me, blk):
+    size = target.shape[1]
+
+    def each(act):
+        for i in range(2):
+            for j in range(4):
+                piece = source.at[i, pl.ds(j * size, size)]
+                here = (me == j) & (blk == 2 * me + i)
+
+                @pl.when(here)
+                def stay():
+                    act(pltpu.make_async_copy(piece, target.at[blk], sems.at[0, 4 * i + j]), True)
+
+                @pl.when(jnp.logical_not(here))
+                def go():
+                    act(
+                        pltpu.make_async_remote_copy(
+                            src_ref=piece,
+                            dst_ref=target.at[blk],
+                            send_sem=sems.at[0, 4 * i + j],
+                            recv_sem=sems.at[1, blk],
+                            device_id=(j, 2 * me + i),
+                            device_id_type=MESH,
+                        ),
+                        False,
+                    )
+
+    def start():
+        each(lambda copy, local: copy.start())
+
+    def wait_sent():
+        each(lambda copy, local: copy.wait() if local else copy.wait_send())
+
+    def wait_arrived():
+        for k in range(8):
+
+            @pl.when((blk != k) | (me != blk // 2))
+            def arrived():
+                pltpu.make_async_remote_copy(
+                    src_ref=source.at[0, pl.ds(0, size)],
+                    dst_ref=target.at[k],
+                    send_sem=sems.at[0, 0],
+                    recv_sem=sems.at[1, k],
+                    device_id=(me, blk),
+                    device_id_type=MESH,
+                ).wait_recv()
+
+    return start, wait_sent, wait_arrived
+
+
+def begin_kernel(master_ref, tokens_ref, pieces_ref, x_ref, s_core, s_y, s_relay, s_x):
+    me, blk = lax.axis_index("batch"), lax.axis_index("blk")
+    y, core = me // 2, me % 2
+    to_core = {"batch": y * 2 + 1 - core}
+    to_y = {"batch": (1 - y) * 2 + core}
+    x_start, x_sent, x_arrived = scatter_rows_copies(tokens_ref, x_ref, s_x, me, blk)
+
+    def copies(c):
+        at = pl.ds(3 * c, 3)
+        return (
+            lambda: remote(master_ref.at[at], pieces_ref.at[0, at], s_core, c, to_core),
+            lambda: remote(master_ref.at[at], pieces_ref.at[1, at], s_y, c, to_y),
+            lambda: remote(pieces_ref.at[1, at], pieces_ref.at[2, at], s_relay, c, to_core),
+        )
+
+    greet_all()
+    for c in range(3):
+        copies(c)[1]().start()
+    for c in range(3):
+        copies(c)[0]().start()
+    x_start()
+    for c in range(3):
+        copies(c)[1]().wait_recv()
+        copies(c)[2]().start()
+    for c in range(3):
+        near, far, relay = copies(c)
+        near().wait()
+        far().wait_send()
+        relay().wait()
+    x_sent()
+    x_arrived()
+
+
+def begin(master, tokens):
+    hbm = pl.BlockSpec(memory_space=pl.ANY)
+    size = tokens.shape[1] // 4
+    sems = lambda n: pltpu.SemaphoreType.DMA((2, n))
+    return pl.pallas_call(
+        begin_kernel,
+        in_specs=[hbm, hbm],
+        out_specs=[hbm, hbm],
+        out_shape=[
+            jax.ShapeDtypeStruct((3,) + master.shape, BF),
+            jax.ShapeDtypeStruct((8, size, D), BF),
+        ],
+        scratch_shapes=[sems(3), sems(3), sems(3), sems(8)],
+        compiler_params=params(collective_id=3, has_side_effects=True),
+        name="begin",
+    )(master, tokens)
+
+
+def gather_kernel(
+    shard_ref, down_ref, x_ref, grad_ref, attn_ref, downs_ref, xs_ref, dy_ref, dys_ref, s_local, s_up, s_down, s_up2,
+    s_down2, s_x, s_dy, s_dys,
+):
+    me, blk = lax.axis_index("batch"), lax.axis_index("blk")
+    y, core = me // 2, me % 2
+    to_core = {"batch": y * 2 + 1 - core}
+    to_y = {"batch": (1 - y) * 2 + core}
+    place = ring_place(blk)
+    after_me, before_me = {"blk": ring_owner(place + 1)}, {"blk": ring_owner(place - 1)}
+    half = shard_ref.shape[0] // 2
+    sub = half // 2
+    far_slab = (1 - y) * 2 + core
+
+    def ring(t, up, part, second=False):
+        owner = ring_owner(place - t) if up else ring_owner(place + t)
+        at = pl.ds((0 if up else half) + part * sub, sub)
+        target = (downs_ref if second else attn_ref).at[owner, at]
+        source = (down_ref if second else shard_ref).at[at] if t == 0 else target
+        sems = (s_up2 if up else s_down2) if second else (s_up if up else s_down)
+        return remote(source, target, sems, 2 * t + part, after_me if up else before_me)
+
+    def spread(source, whole, sems, c):
+        at = pl.ds(4 * c, 4)
+        return (
+            lambda: remote(source.at[at], whole.at[at, me], sems, c, to_core),
+            lambda: remote(source.at[at], whole.at[at, me], sems, 2 + c, to_y),
+            lambda: remote(whole.at[at, far_slab], whole.at[at, far_slab], sems, 4 + c, to_core),
+        )
+
+    dy_start, dy_sent, dy_arrived = scatter_rows_copies(grad_ref, dy_ref, s_dy, me, blk)
+    locals_ = [
+        pltpu.make_async_copy(shard_ref, attn_ref.at[blk], s_local.at[0]),
+        pltpu.make_async_copy(x_ref, xs_ref.at[:, me], s_local.at[1]),
+        pltpu.make_async_copy(dy_ref, dys_ref.at[:, me], s_local.at[2]),
+        pltpu.make_async_copy(down_ref, downs_ref.at[blk], s_local.at[3]),
+    ]
+    greet_all()
+    for part in range(2):
+        ring(0, True, part).start()
+        ring(0, False, part).start()
+    for c in range(2):
+        spread(x_ref, xs_ref, s_x, c)[1]().start()
+        spread(x_ref, xs_ref, s_x, c)[0]().start()
+    locals_[0].start()
+    locals_[1].start()
+    locals_[3].start()
+    dy_start()
+    for t in range(1, 7):
+        for part in range(2):
+            for up in (True, False):
+                ring(t - 1, up, part).wait_recv()
+                ring(t, up, part).start()
+        if t in (4, 5):
+            copies = spread(x_ref, xs_ref, s_x, t - 4)
+            copies[1]().wait_recv()
+            copies[2]().start()
+        if t == 5:
+            dy_arrived()
+            dy_sent()
+            for c in range(2):
+                spread(dy_ref, dys_ref, s_dys, c)[1]().start()
+                spread(dy_ref, dys_ref, s_dys, c)[0]().start()
+            locals_[2].start()
+    for part in range(2):
+        for up in (True, False):
+            ring(0, up, part, True).start()
+            ring(6, up, part).wait_recv()
+    for t in range(1, 7):
+        for part in range(2):
+            for up in (True, False):
+                ring(t - 1, up, part, True).wait_recv()
+                ring(t, up, part, True).start()
+        if t in (3, 5):
+            copies = spread(dy_ref, dys_ref, s_dys, (t - 3) // 2)
+            copies[1]().wait_recv()
+            copies[2]().start()
+    for part in range(2):
+        for up in (True, False):
+            ring(6, up, part, True).wait_recv()
+    for t in range(7):
+        for part in range(2):
+            for up in (True, False):
+                ring(t, up, part).wait_send()
+                ring(t, up, part, True).wait_send()
+    for source, whole, sems in ((x_ref, xs_ref, s_x), (dy_ref, dys_ref, s_dys)):
+        for c in range(2):
+            near, far, relay = spread(source, whole, sems, c)
+            near().wait()
+            far().wait_send()
+            relay().wait()
+    for copy in locals_:
+        copy.wait()
+
+
+def gather(shard, down, x, cotangent):
+    hbm = pl.BlockSpec(memory_space=pl.ANY)
+    size = x.shape[1]
+    sems = lambda n: pltpu.SemaphoreType.DMA((2, n))
+    whole = jax.ShapeDtypeStruct((8, 4, size, D), BF)
+    return pl.pallas_call(
+        gather_kernel,
+        in_specs=[hbm] * 4,
+        out_specs=[hbm] * 5,
+        out_shape=[
+            jax.ShapeDtypeStruct((8,) + shard.shape, BF),
+            jax.ShapeDtypeStruct((8,) + down.shape, BF),
+            whole,
+            jax.ShapeDtypeStruct((8, size, D), BF),
+            whole,
+        ],
+        scratch_shapes=[pltpu.SemaphoreType.DMA((4,))] + [sems(14)] * 4 + [sems(6), sems(8), sems(6)],
+        compiler_params=params(collective_id=4, has_side_effects=True),
+        name="gather",
+    )(shard, down, x, cotangent)
 
 
 def attention_pieces(me):
@@ -515,13 +679,13 @@
     return pieces
 
 
-def pick_kernel(place_ref, me_ref, own, core, far, far_core, attn_ref, ffn_ref, sems):
+def pick_kernel(place_ref, me_ref, own, pieces, attn_ref, ffn_ref, down_ref, sems):
     me = me_ref[0]
     waits = []
 
     def begin(unit, source, target, sem):
         at = place_ref[unit]
-        for other, ref in enumerate((own, core, far, far_core)):
+        for other, ref in enumerate((own, pieces.at[0], pieces.at[1], pieces.at[2])):
 
             @pl.when(at // 9 == other)
             def start():
@@ -534,71 +698,72 @@
         begin(unit, lambda r, c=column: r.at[:, pl.ds(c, 128)], attn_ref.at[:, pl.ds(packed * 128, 128)], sems.at[i])
     for i in range(6):
         unit = 12 + 8 * (i // 2) + 2 * me + i % 2
-        begin(unit, lambda r: r, ffn_ref.at[:, pl.ds(i * UW, UW)], sems.at[12 + i])
+        target = ffn_ref.at[:, pl.ds(i * UW, UW)] if i < 4 else down_ref.at[:, pl.ds((i - 4) * UW, UW)]
+        begin(unit, lambda r: r, target, sems.at[12 + i])
     for wait in waits:
         wait.wait()
 
 
-def pick_units(place, me, pieces):
-    rows = pieces[0].shape[1]
+def pick_units(place, me, own, pieces):
+    rows = own.shape[1]
     hbm = pl.BlockSpec(memory_space=pl.ANY)
     smem = pl.BlockSpec(memory_space=pltpu.SMEM)
     vmem = pl.BlockSpec(memory_space=pltpu.VMEM)
     return pl.pallas_call(
         pick_kernel,
-        in_specs=[smem, smem, hbm, hbm, hbm, hbm],
-        out_specs=[vmem, vmem],
+        in_specs=[smem, smem, hbm, hbm],
+        out_specs=[vmem, vmem, vmem],
         out_shape=[
             jax.ShapeDtypeStruct((rows, 4 * QW), BF),
-            jax.ShapeDtypeStruct((rows, 6 * UW), BF),
+            jax.ShapeDtypeStruct((rows, 4 * UW), BF),
+            jax.ShapeDtypeStruct((rows, 2 * UW), BF),
         ],
         scratch_shapes=[pltpu.SemaphoreType.DMA((18,))],
         compiler_params=params(),
         name="pick_units",
-    )(place, me.reshape(1), *pieces)
-
-
-def place_kernel(unit_ref, me_ref, *refs):
-    attn, ffn, out_ref, sems = refs[:4], refs[4:8], refs[8], refs[9]
+    )(place, me.reshape(1), own, pieces)
+
+
+def place_kernel(unit_ref, me_ref, attn, gate_up, down, out_ref, sems):
     me = me_ref[0]
     waits = []
     for i in range(9):
         unit = unit_ref[i]
-        of_attn = unit < 12
         f = jnp.maximum(unit - 12, 0)
         for q in range(4):
             block = (unit % 3) * 4 + q
-            source = jnp.where(of_attn, block // HEADS, (f % 8) // 2) ^ me
-            column = jnp.where(
-                of_attn, (unit // 3) * QW + (block % HEADS) * 128, (f // 8) * FQ + (f % 2) * UW + q * 128
+            low = f % 16
+            choices = (
+                (unit < 12, attn, block // HEADS, (unit // 3) * QW + (block % HEADS) * 128),
+                ((unit >= 12) & (unit < 28), gate_up, (low % 8) // 2, (low // 8) * FQ + (low % 2) * UW + q * 128),
+                (unit >= 28, down, (f % 8) // 2, (f % 2) * UW + q * 128),
             )
-            column = pl.multiple_of(column, 128)
             target, sem = out_ref.at[i, :, pl.ds(q * 128, 128)], sems.at[i, q]
-            for other in range(4):
-                for mine, pieces in ((of_attn, attn), (jnp.logical_not(of_attn), ffn)):
-
-                    @pl.when(mine & (source == other))
-                    def start(ref=pieces[other], column=column, target=target, sem=sem):
-                        pltpu.make_async_copy(ref.at[:, pl.ds(column, 128)], target, sem).start()
-
-            waits.append(pltpu.make_async_copy(attn[0].at[:, pl.ds(0, 128)], target, sem))
+            for chosen, pieces, holder, column in choices:
+
+                @pl.when(chosen)
+                def start(pieces=pieces, holder=holder, column=column, target=target, sem=sem):
+                    source = pieces.at[holder ^ me, :, pl.ds(pl.multiple_of(column, 128), 128)]
+                    pltpu.make_async_copy(source, target, sem).start()
+
+            waits.append(pltpu.make_async_copy(attn.at[0, :, pl.ds(0, 128)], target, sem))
     for wait in waits:
         wait.wait()
 
 
-def place_units(units, me, attn_pieces, ffn_pieces):
-    rows = attn_pieces[0].shape[0]
+def place_units(units, me, attn_pieces, gate_up_pieces, down_pieces):
+    rows = attn_pieces.shape[1]
     hbm = pl.BlockSpec(memory_space=pl.ANY)
     smem = pl.BlockSpec(memory_space=pltpu.SMEM)
     return pl.pallas_call(
         place_kernel,
-        in_specs=[smem, smem] + [hbm] * 8,
+        in_specs=[smem, smem] + [hbm] * 3,
         out_specs=pl.BlockSpec(memory_space=pltpu.VMEM),
         out_shape=jax.ShapeDtypeStruct((9, rows, UW), BF),
         scratch_shapes=[pltpu.SemaphoreType.DMA((9, 4))],
         compiler_params=params(),
         name="place_units",
-    )(units, me.reshape(1), *attn_pieces, *ffn_pieces)
+    )(units, me.reshape(1), attn_pieces, gate_up_pieces, down_pieces)
 
 
 def turn(values, cosine, sine, lane):
@@ -843,68 +1008,120 @@
     )(low, lam, q, k, v, start, gain, maps, log_mass, da, cosine, sine, cosine, sine)
 
 
-def middle_kernel(me_ref, x_ref, gain_ref, *refs):
-    a_refs, w_refs, (n_ref, own_ref, sum_ref) = refs[:4], refs[4:8], refs[8:]
-    x1 = x_ref[...].astype(F32)
-    for a_ref, w_ref in zip(a_refs, w_refs):
-        x1 += dot_last(a_ref[...], w_ref[...])
-    sum_ref[...] = x1
-    r = lax.rsqrt(jnp.mean(x1 * x1, axis=-1, keepdims=True) + norm_epsilon)
-    n_ref[...] = (x1 * r * gain_ref[...]).astype(BF)
-    part = TILE // 4
-    own_ref[0] = sum_ref[pl.ds(pl.multiple_of(me_ref[0] * part, part), part), :]
-
-
-def middle(me, a, x, weights, gain):
+def middle_kernel(
+    x_ref, gain_ref, a_ref, w_ref, a_hbm, attn_hbm, n_ref, own_ref, a_in, w_in, total, s_a, s_ay, s_ar, s_w
+):
+    i = pl.program_id(0)
+    me = lax.axis_index("batch")
+    y, core = me // 2, me % 2
+    to_core = {"batch": y * 2 + 1 - core}
+    to_y = {"batch": (1 - y) * 2 + core}
+    blocks = a_in.shape[1]
+    mine = attn_hbm.at[:, pl.ds(3 * QW, QW)]
+
+    def a_copies(b):
+        source = a_hbm.at[pl.ds(b * TILE, TILE)]
+        return (
+            lambda: remote(source, a_in.at[0, b], s_a, b, to_core),
+            lambda: remote(source, a_in.at[1, b], s_ay, b, to_y),
+            lambda: remote(a_in.at[1, b], a_in.at[2, b], s_ar, b, to_core),
+        )
+
+    w_copies = (
+        lambda: remote(mine, w_in.at[0], s_w, 0, to_core),
+        lambda: remote(mine, w_in.at[1], s_w, 1, to_y),
+        lambda: remote(w_in.at[1], w_in.at[2], s_w, 2, to_core),
+    )
+
+    @pl.when(i == 0)
+    def begin():
+        greet((to_core, to_y))
+        w_copies[1]().start()
+        for b in range(blocks):
+            a_copies(b)[1]().start()
+        w_copies[0]().start()
+        for b in range(blocks):
+            a_copies(b)[0]().start()
+        w_copies[1]().wait_recv()
+        w_copies[2]().start()
+
+    @pl.when(i < blocks)
+    def relay():
+        a_copies(i)[1]().wait_recv()
+        a_copies(i)[2]().start()
+
+    @pl.when(i == 1)
+    def weights():
+        w_copies[0]().wait_recv()
+        w_copies[2]().wait_recv()
+
+    @pl.when(i >= 1)
+    def compute():
+        b = i - 1
+        a_copies(b)[0]().wait_recv()
+        a_copies(b)[2]().wait_recv()
+        x1 = x_ref[...].astype(F32) + dot_last(a_ref[...], w_ref[...])
+        for other in range(3):
+            x1 += dot_last(a_in[other, b], w_in[other])
+        total[...] = x1
+        r = lax.rsqrt(jnp.mean(x1 * x1, axis=-1, keepdims=True) + norm_epsilon)
+        n_ref[...] = (x1 * r * gain_ref[...]).astype(BF)
+        part = TILE // 4
+        own_ref[0] = total[pl.ds(pl.multiple_of(me * part, part), part), :]
+
+    @pl.when(i == blocks)
+    def finish():
+        for copy in w_copies:
+            copy().wait_send()
+        for b in range(blocks):
+            for copy in a_copies(b):
+                copy().wait_send()
+
+
+def middle(a, x, attn, gain):
     count = x.shape[0]
-    rows = pl.BlockSpec((TILE, D), lambda i: (i, 0))
+    blocks = count // TILE
+    late = lambda i: (jnp.maximum(i - 1, 0), 0)
+    hbm = pl.BlockSpec(memory_space=pl.ANY)
+    sems = lambda n: pltpu.SemaphoreType.DMA((2, n))
     return pl.pallas_call(
         middle_kernel,
-        grid=(count // TILE,),
+        grid=(blocks + 1,),
         in_specs=[
-            pl.BlockSpec(memory_space=pltpu.SMEM),
-            rows,
+            pl.BlockSpec((TILE, D), late),
             pl.BlockSpec((1, D), lambda i: (0, 0)),
-        ]
-        + [pl.BlockSpec((TILE, QW), lambda i: (i, 0))] * 4
-        + [pl.BlockSpec((D, QW), lambda i: (0, 0), pipeline_mode=pl.Buffered(1))] * 4,
-        out_specs=[rows, pl.BlockSpec((1, TILE // 4, D), lambda i: (i, 0, 0))],
+            pl.BlockSpec((TILE, QW), late),
+            pl.BlockSpec((D, QW), lambda i: (0, 3), pipeline_mode=pl.Buffered(1)),
+            hbm,
+            hbm,
+        ],
+        out_specs=[
+            pl.BlockSpec((TILE, D), late),
+            pl.BlockSpec((1, TILE // 4, D), lambda i: (jnp.maximum(i - 1, 0), 0, 0)),
+        ],
         out_shape=[
             jax.ShapeDtypeStruct((count, D), BF),
-            jax.ShapeDtypeStruct((count // TILE, TILE // 4, D), F32),
-        ],
-        scratch_shapes=[pltpu.VMEM((TILE, D), F32)],
-        compiler_params=params(),
+            jax.ShapeDtypeStruct((blocks, TILE // 4, D), F32),
+        ],
+        scratch_shapes=[
+            pltpu.VMEM((3, blocks, TILE, QW), BF),
+            pltpu.VMEM((3, D, QW), BF),
+            pltpu.VMEM((TILE, D), F32),
+            sems(blocks),
+            sems(blocks),
+            sems(blocks),
+            sems(3),
+        ],
+        compiler_params=params(collective_id=5, has_side_effects=True),
         cost_estimate=pl.CostEstimate(
             flops=2 * count * D * D, bytes_accessed=count * D * 7 + 2 * D * D, transcendentals=0
         ),
         name="middle",
-    )(me.reshape(1), x, gain, *a, *weights)
-
-
-MESH = pl.DeviceIdType.MESH
-
-
-def greet(devices):
-    barrier = pltpu.get_barrier_semaphore()
-    for device in devices:
-        pl.semaphore_signal(barrier, inc=1, device_id=device, device_id_type=MESH)
-    pl.semaphore_wait(barrier, len(devices))
-
-
-def remote(source, target, sems, at, device):
-    return pltpu.make_async_remote_copy(
-        src_ref=source,
-        dst_ref=target,
-        send_sem=sems.at[0, at],
-        recv_sem=sems.at[1, at],
-        device_id=device,
-        device_id_type=MESH,
-    )
+    )(x, gain, a, attn, a, attn)
 
 
 def feed_kernel(
-    n_ref, dy_ref, w_ref, x1_ref, dyo_ref, wo_ref, gain_ref, act_ref, out_ref, dx_ref, low_ref, da_ref, dgain_ref,
+    n_ref, dy_ref, w_ref, wd_ref, x1_ref, dyo_ref, wo_ref, gain_ref, act_ref, out_ref, dx_ref, low_ref, da_ref, dgain_ref,
     part, near_in, near, far_in, gathered, s_near, s_far, s_y, s_core, s_relay,
 ):
     i = pl.program_id(0)
@@ -974,7 +1191,7 @@
     @pl.when(i < blocks)
     def compute():
         n, dy = n_ref[...], dy_ref[...]
-        wg, wu, wd = w_ref[:, :FQ], w_ref[:, FQ : 2 * FQ], w_ref[:, 2 * FQ :]
+        wg, wu, wd = w_ref[:, :FQ], w_ref[:, FQ:], wd_ref[...]
         gate = dot_plain(n, wg)
         up = dot_plain(n, wu)
         dhidden = dot_plain(dy, wd)
@@ -1003,7 +1220,7 @@
             relay_copy(b).wait_send()
 
 
-def feed(n, dy, weights, x1, dy_own, attn, gain):
+def feed(n, dy, weights, down, x1, dy_own, attn, gain):
     count = n.shape[0]
     blocks = count // TILE
     size = TILE // 4
@@ -1019,7 +1236,8 @@
         in_specs=[
             rows(D, 0),
             rows(D, 0),
-            pl.BlockSpec((D, 3 * FQ), lambda i: (0, 0), pipeline_mode=pl.Buffered(1)),
+            pl.BlockSpec((D, 2 * FQ), lambda i: (0, 0), pipeline_mode=pl.Buffered(1)),
+            pl.BlockSpec((D, FQ), lambda i: (0, 0), pipeline_mode=pl.Buffered(1)),
             own,
             own,
             pl.BlockSpec((D, QW), lambda i: (0, 3), pipeline_mode=pl.Buffered(1)),
@@ -1058,13 +1276,191 @@
             flops=12 * count * D * FQ, bytes_accessed=count * (8 * D + 6 * FQ) + 6 * D * FQ, transcendentals=count * FQ
         ),
         name="feed",
-    )(n, dy, weights, x1, dy_own, attn, gain)
+    )(n, dy, weights, down, x1, dy_own, attn, gain)
+
+
+def return_rows_copies(source, target, sems, me, blk):
+    size = source.shape[1]
+
+    def copies(act_local, act_remote):
+        for k in range(8):
+            here = (me == blk // 2) & (blk == k)
+            piece = target.at[blk % 2, pl.ds(pl.multiple_of(me * size, size), size)]
+
+            @pl.when(here)
+            def stay():
+                act_local(pltpu.make_async_copy(source.at[k], piece, sems.at[0, k]))
+
+            @pl.when(jnp.logical_not(here))
+            def go():
+                act_remote(
+                    pltpu.make_async_remote_copy(
+                        src_ref=source.at[k],
+                        dst_ref=piece,
+                        send_sem=sems.at[0, k],
+                        recv_sem=sems.at[1, (blk % 2) * 4 + me],
+                        device_id=(blk // 2, k),
+                        device_id_type=MESH,
+                    )
+                )
+
+    def start():
+        copies(lambda copy: copy.start(), lambda copy: copy.start())
+
+    def finish():
+        copies(lambda copy: copy.wait(), lambda copy: copy.wait_send())
+        for i in range(2):
+            for other in range(4):
+
+                @pl.when((me != other) | (blk != 2 * me + i))
+                def arrived():
+                    pltpu.make_async_remote_copy(
+                        src_ref=source.at[0],
+                        dst_ref=target.at[i, pl.ds(other * size, size)],
+                        send_sem=sems.at[0, 0],
+                        recv_sem=sems.at[1, 4 * i + other],
+                        device_id=(me, blk),
+                        device_id_type=MESH,
+                    ).wait_recv()
+
+    return start, finish
+
+
+def ring_kernel(exchanged, sent_back, *refs):
+    refs = list(refs)
+    grad = refs.pop(0)
+    extras = [refs.pop(0) for _ in range(exchanged)]
+    rows_ref = refs.pop(0) if sent_back else None
+    sums_ref = refs.pop(0)
+    extra_outs = [refs.pop(0) for _ in range(exchanged)]
+    back_ref = refs.pop(0) if sent_back else None
+    up_in, down_in, total, s_up, s_down, s_out, s_extra, s_back, s_local = refs
+    me, blk = lax.axis_index("batch"), lax.axis_index("blk")
+    y, core = me // 2, me % 2
+    to_core = {"batch": y * 2 + 1 - core}
+    to_y = {"batch": (1 - y) * 2 + core}
+    place = ring_place(blk)
+    after_me, before_me = {"blk": ring_owner(place + 1)}, {"blk": ring_owner(place - 1)}
+    part = grad.shape[0] // 8
+    half = part // 2
+    parts = up_in.shape[1]
+    width = grad.shape[1] // parts
+
+    def own(t, up, p):
+        owner = ring_owner(place - 1 - t) if up else ring_owner(place + 1 + t)
+        begin = pl.multiple_of(owner * part + (0 if up else half), half)
+        return grad.at[pl.ds(begin, half), pl.ds(p * width, width)]
+
+    def ring(t, up, p):
+        here = up_in if up else down_in
+        source = own(0, up, p) if t == 0 else here.at[t - 1, p]
+        return remote(source, here.at[t, p], s_up if up else s_down, parts * t + p, after_me if up else before_me)
+
+    def exchange(source, out, sems, n):
+        return (
+            lambda: remote(source, out.at[1], sems, 3 * n, to_core),
+            lambda: remote(source, out.at[2], sems, 3 * n + 1, to_y),
+            lambda: remote(out.at[2], out.at[3], sems, 3 * n + 2, to_core),
+        )
+
+    extra_sets = [exchange(extras[n], extra_outs[n], s_extra, n) for n in range(exchanged)]
+    extra_locals = [pltpu.make_async_copy(extras[n], extra_outs[n].at[0], s_local.at[1 + n]) for n in range(exchanged)]
+    greet_all()
+    for p in range(parts):
+        ring(0, True, p).start()
+        ring(0, False, p).start()
+    for n in range(exchanged):
+        extra_sets[n][1]().start()
+        extra_sets[n][0]().start()
+        extra_locals[n].start()
+    if sent_back:
+        back_start, back_finish = return_rows_copies(rows_ref, back_ref, s_back, me, blk)
+        back_start()
+    for t in range(1, 8):
+        for p in range(parts):
+            for up in (True, False):
+                here = up_in if up else down_in
+                ring(t - 1, up, p).wait_recv()
+                value = (here[t - 1, p].astype(F32) + own(t, up, p)[...].astype(F32)).astype(BF)
+                if t < 7:
+                    here[t - 1, p] = value
+                    ring(t, up, p).start()
+                else:
+                    total[0 if up else half : half if up else part, p * width : (p + 1) * width] = value
+        if t == 5:
+            for n in range(exchanged):
+                extra_sets[n][1]().wait_recv()
+                extra_sets[n][2]().start()
+    if exchanged:
+        near, far, relay = exchange(total, sums_ref, s_out, 0)
+        local = pltpu.make_async_copy(total, sums_ref.at[0], s_local.at[0])
+        far().start()
+        near().start()
+        local.start()
+        far().wait_recv()
+        relay().start()
+        near().wait()
+        far().wait_send()
+        relay().wait()
+        local.wait()
+    else:
+        local = pltpu.make_async_copy(total, sums_ref, s_local.at[0])
+        local.start()
+        local.wait()
+    for n in range(exchanged):
+        near, far, relay = extra_sets[n]
+        near().wait()
+        far().wait_send()
+        relay().wait()
+        extra_locals[n].wait()
+    if sent_back:
+        back_finish()
+    for t in range(7):
+        for p in range(parts):
+            ring(t, True, p).wait_send()
+            ring(t, False, p).wait_send()
+
+
+def ring_sums(grad, extras, rows, collective_id):
+    height, width = grad.shape
+    part = height // 8
+    parts = 2
+    hbm = pl.BlockSpec(memory_space=pl.ANY)
+    sems = lambda n: pltpu.SemaphoreType.DMA((2, n))
+    four = lambda array: jax.ShapeDtypeStruct((4,) + array, BF)
+    out_shape = [four((part, width)) if extras else jax.ShapeDtypeStruct((part, width), BF)]
+    out_shape += [four(extra.shape) for extra in extras]
+    operands = [grad, *extras]
+    if rows is not None:
+        out_shape.append(jax.ShapeDtypeStruct((2, 4 * rows.shape[1], rows.shape[2]), BF))
+        operands.append(rows)
+    buffers = pltpu.VMEM((7, parts, part // 2, width // parts), BF)
+    return pl.pallas_call(
+        functools.partial(ring_kernel, len(extras), rows is not None),
+        in_specs=[pl.BlockSpec(memory_space=pltpu.VMEM)] + [hbm] * (len(operands) - 1),
+        out_specs=[hbm] * len(out_shape),
+        out_shape=out_shape,
+        scratch_shapes=[
+            buffers,
+            buffers,
+            pltpu.VMEM((part, width), BF),
+            sems(7 * parts),
+            sems(7 * parts),
+            sems(3),
+            sems(3 * max(1, len(extras))),
+            sems(8),
+            pltpu.SemaphoreType.DMA((1 + len(extras),)),
+        ],
+        compiler_params=params(collective_id=collective_id, has_side_effects=True),
+        cost_estimate=pl.CostEstimate(flops=6 * 10**10, bytes_accessed=3 * height * width, transcendentals=0),
+        name=f"ring_sums_{collective_id}",
+    )(*operands)
 
 
 def rotate_kernel(
-    g_ref, base_ref, other_ref, first_ref, second_ref, master_ref, scale_ref, new_first_ref, new_second_ref,
-    new_master_ref, g, base, other, firsts, seconds, masters, g_in, part, x_in, near, z_in, far, p_in, step, steps,
-    back, back_in, steps_own, load, store, s_g, s_x, s_z, s_p, s_step, s_back, s_up, s_side,
+    g_ref, base_ref, other_ref, first_ref, second_ref, master_ref, rows_ref, scale_ref, new_first_ref, new_second_ref,
+    new_master_ref, rows_out_ref, g, base, other, firsts, seconds, masters, g_in, part, x_in, near, z_in, far, p_in, step, steps,
+    back, back_in, steps_own, load, store, s_g, s_x, s_z, s_p, s_step, s_back, s_up, s_side, s_rows,
 ):
     blk = lax.axis_index("blk")
     zh, zl, xx = blk // 4, (blk // 2) % 2, blk % 2
@@ -1115,10 +1511,12 @@
     for i in range(len(loads)):
         for s in range(count):
             loading(i, s).start()
-    greet((to_x, to_z, to_pair))
+    rows_start, rows_finish = return_rows_copies(rows_ref, rows_out_ref, s_rows, lax.axis_index("batch"), blk)
+    greet_all()
     for s in range(count):
         loading(0, s).wait()
         send_g(s).start()
+    rows_start()
 
     rows = base.shape[1]
 
@@ -1226,6 +1624,7 @@
         return carry
 
     lax.fori_loop(0, count + 7, tick, 0)
+    rows_finish()
     for s in range(count):
         send_g(s).wait_send()
         step_pair(s).wait_send()
@@ -1242,7 +1641,7 @@
         send_back(s).wait_send()
 
 
-def rotate_slots(grads, base, other, first, second, master, scales):
+def rotate_slots(grads, base, other, first, second, master, tokens, scales):
     count, rows, width = grads.shape
     half = width // 2
     hbm = pl.BlockSpec(memory_space=pl.ANY)
@@ -1250,9 +1649,9 @@
     sems = lambda n: pltpu.SemaphoreType.DMA((2, n))
     return pl.pallas_call(
         rotate_kernel,
-        in_specs=[hbm] * 6 + [pl.BlockSpec(memory_space=pltpu.SMEM)],
-        out_specs=[hbm] * 3,
-        out_shape=[shape] * 3,
+        in_specs=[hbm] * 7 + [pl.BlockSpec(memory_space=pltpu.SMEM)],
+        out_specs=[hbm] * 4,
+        out_shape=[shape] * 3 + [jax.ShapeDtypeStruct((2, 4 * tokens.shape[1], D), BF)],
         scratch_shapes=[
             pltpu.VMEM((count, rows, width), BF),
             pltpu.VMEM((count, rows, D), BF),
@@ -1282,10 +1681,11 @@
             sems(count),
             sems(2 * count),
             sems(4 * count),
+            sems(8),
         ],
         compiler_params=params(collective_id=2, has_side_effects=True),
         name="rotate_slots",
-    )(grads, base, other, first, second, master, scales)
+    )(grads, base, other, first, second, master, tokens, scales)
 
 
 def row_tables(lengths, row, count):
@@ -1325,20 +1725,18 @@
     master_slots = slots(master)
 
     groups = (8, 4, count // 32, D)
-    zh, zl, xx = blk // 4, (blk // 2) % 2, blk % 2
-
-    x_parts = to_batch(tokens, me)
+
     place = ((unit_owner // 9) ^ me) * 9 + unit_owner % 9
-    attn_shard, ffn_shard = pick_units(place, me, batch_pieces(master_slots.astype(BF)))
-    x_own = to_rows(x_parts)
+    master_low = master_slots.astype(BF)
+    pieces, x_own = begin(master_low, tokens)
     start, low, cosine, sine = row_tables(lengths, blk, count)
     start = start.reshape(1, count)
+    attn_shard, gate_up_shard, down_shard = pick_units(place, me, master_low, pieces)
+    attn, down, x, dy_own, dy = gather(attn_shard, down_shard, x_own, cotangent)
+    down = down.reshape(D, FQ)
+    gate_up = lax.all_gather(after(gate_up_shard, attn), "blk", axis=0, tiled=True)
+    attn, x, dy = attn.reshape(D, 4 * QW), x.reshape(count, D), dy.reshape(count, D)
     base = slots(bases).astype(BF)
-    attn = ring_gather(attn_shard, blk, 0).reshape(D, 4 * QW)
-    x = batch_gather(x_own, me, 1).reshape(count, D)
-    dy_own = to_rows(after(to_batch(after(cotangent, attn_shard), me), attn))
-    dy = batch_gather(dy_own, me, 1).reshape(count, D)
-    attn_out = batch_pieces(attn[:, 3 * QW :])
 
     gain_one = small[:D].reshape(1, D)
     gain_two = small[D : 2 * D].reshape(1, D)
@@ -1348,46 +1746,38 @@
 
     n1, q, k, v = project(x, attn, gain_one, cosine, sine)
     a_own, maps, log_mass = attend(low, lam, q, k, v, start, head_gain)
-    a = batch_pieces(a_own)
-    ffn = lax.all_gather(ffn_shard, "blk", axis=0, tiled=True)
-    base_other = swap_blk(after(base, attn), 2)
-    n2, x1 = middle(me, a, x, attn_out, gain_two)
-    acts, out_part, dx1, dx1_low, da, gain_two_grad = feed(n2, dy, ffn, x1, dy_own, attn, gain_two)
+    n2, x1 = middle(a_own, x, attn, gain_two)
+    base_other = swap_blk(after(base, gate_up), 2)
+    acts, out_part, dx1, dx1_low, da, gain_two_grad = feed(
+        n2, dy, gate_up, down, x1, dy_own, attn, gain_two
+    )
     gain_two_grad = gain_two_grad.reshape(D)
 
-    part = D // 8
-
-    def scatter_rows(grad):
-        def part_of(owner, half):
-            return lax.dynamic_slice_in_dim(grad, owner * part + half * part // 2, part // 2, axis=0)
-
-        return ring_scatter(part_of, blk)
-
-    ffn_grad = jnp.concatenate(
-        [dot_first(n2, acts[:, : 2 * FQ]).astype(BF), dot_first(dy, acts[:, 2 * FQ :]).astype(BF)], axis=1
-    )
-    ffn_sums = lax.psum_scatter(ffn_grad, "blk", scatter_dimension=0, tiled=True)
-
+    near_out = near_sum(out_part.reshape(groups), me)
+    down_sums = lax.psum_scatter(
+        dot_first(dy, acts[:, 2 * FQ :]).astype(BF), "blk", scatter_dimension=0, tiled=True
+    )
+    gate_up_grad = dot_first(n2, acts[:, : 2 * FQ]).astype(BF)
     out_grad = dot_first(dx1_low, a_own).astype(BF)
-    da, out_grad = after((da, out_grad), base_other)
+    da = after(da, (near_out, gate_up_grad, out_grad, base_other))
     dq, dk, dv, head_gain_sums, mixer_sums = attend_back(
         low, lam, q, k, v, start, head_gain, maps, log_mass, da, cosine, sine
     )
     dqkv = jnp.concatenate([dq, dk, dv], axis=1)
-    attn_states = scatter_rows(jnp.concatenate([dot_first(n1, dqkv).astype(BF), out_grad], axis=1))
-    ffn_pieces = batch_pieces(ffn_sums)
-
-    dn1_part = dot_last(after(dqkv, attn_states[0]), attn[:, : 3 * QW]).astype(BF)
-    dn1 = batch_scatter(dn1_part.reshape(groups), me, 1)
+    attn_grad = jnp.concatenate([dot_first(n1, dqkv).astype(BF), out_grad], axis=1)
+    near_dn1 = near_sum(dot_last(dqkv, attn[:, : 3 * QW]).astype(BF).reshape(groups), me)
+    out_rows = (x1 + far_sum(near_out, me)).astype(BF)
+    gate_up_grad = after(gate_up_grad, (near_dn1, attn_grad))
+    gate_up_sums, block_out = ring_sums(gate_up_grad, [], out_rows, 6)
+    attn_pieces, gate_up_pieces, down_pieces = ring_sums(attn_grad, [gate_up_sums, down_sums], None, 7)
+
+    dn1 = far_sum(near_dn1, me)
     x_f = x_own.astype(F32)
     r1 = lax.rsqrt(jnp.mean(x_f * x_f, axis=-1, keepdims=True) + norm_epsilon)
     t1 = x_f * r1
     e1 = dn1 * gain_one
     dx = dx1 + r1 * (e1 - t1 * jnp.mean(e1 * t1, axis=-1, keepdims=True))
     gain_one_grad = jnp.sum(dn1 * t1, axis=(0, 1))
-    input_grad = from_rows(dx.astype(BF), me)
-    out = batch_scatter(out_part.reshape(groups), me, 1)
-    block_out = from_rows((x1 + out).astype(BF), me)
 
     (mixers_grad,) = mixer_back(jnp.sum(mixer_sums))
     small_local = jnp.concatenate(
@@ -1397,13 +1787,12 @@
 
     unit_of = inverse_order(unit_owner)
     units = lax.dynamic_slice_in_dim(unit_of, me * 9, 9)
-    attn_pieces = batch_pieces(jnp.concatenate(attn_states[6], axis=0))
-    grads = place_units(units, me, attn_pieces, ffn_pieces)
+    grads = place_units(units, me, attn_pieces, gate_up_pieces, down_pieces)
 
     steps_done = step_count[0].astype(F32)
     scales = jnp.stack([jnp.float32(learn_rate), 1.0 - beta_one**steps_done, 1.0 - beta_two**steps_done])
-    new_first, new_second, new_master = rotate_slots(
-        grads, base, base_other, slots(first), slots(second), master_slots, scales
+    new_first, new_second, new_master, input_grad = rotate_slots(
+        grads, base, base_other, slots(first), slots(second), master_slots, dx.astype(BF), scales
     )
     new_small_first = beta_one * small_first + (1.0 - beta_one) * small_grads
     new_small_second = beta_two * small_second + (1.0 - beta_two) * small_grads * small_grads

time: 1280 us -> 1140 us (0.89)
  Pallas kernels: 428 us -> 922 us
  waiting for transfers between devices: 496 us -> 51.6 us
  local copies, waits for them, and re-layouts: 111 us -> 30.9 us
  starting transfers between devices: 87.8 us -> 9.12 us
  other arithmetic: 63.2 us -> 35.1 us
    pallas_call x4 -> x8, Pallas kernels: 226 us -> 722 us  [the longest x1 229 us: rotate_slots(): pl.pallas_call(rotate_kernel, in_specs=[hbm] * 7 + [pl.BlockSpec(memory_s...]
    ppermute x40 -> x0, waiting for transfers between devices: 349 us -> none  [the longest x14 143 us: ring_down(): lax.ppermute(piece, 'blk', [(LOOP[(i + 1) % 8], LOOP[i]) for i in range(8)])]
    ppermute x11 -> x4, waiting for transfers between devices: 125 us -> 48 us  [swap_y(): return lax.ppermute(piece, 'batch', [(i, i ^ 2) for i in range(4)])]
    dynamic_update_slice x41 -> x0, local copies, waits for them, and re-layouts: 53.3 us -> none  [the longest x27 41 us: put(): lax.dynamic_update_slice_in_dim(whole, jnp.expand_dims(piece, axis), inde...]
    ppermute x40 -> x0, starting transfers between devices: 40.1 us -> none  [the longest x14 24.7 us: ring_up(): lax.ppermute(piece, 'blk', [(LOOP[i], LOOP[(i + 1) % 8]) for i in range(8)])]
    all_to_all x4 -> x0, starting transfers between devices: 29.2 us -> none  [the longest x2 14.7 us: to_rows(): return lax.all_to_all(pieces, 'blk', 0, 0, tiled=True)]
    convert_element_type x16 -> x5, other arithmetic: 27.1 us -> 16.1 us  [the longest x1 4.64 us: row_groups(): out_rows = (x1 + far_sum(near_out, me)).astype(BF)]
  transfers between devices with their start and end apart: 80 -> 15, of which waited for: 39 -> 4; matrix products, arithmetic and copies ran while one was open for 16% -> 8% of each run, Pallas kernels for 13% -> 56%
where the time goes in v3:
time: 1140 us; the launch traced here: 1130 us
  Pallas kernels  922 us (81%)
  matrix products  55.5 us (5%)
  waiting for transfers between devices  51.6 us (5%)
  other arithmetic  35.1 us (3%)
  local copies, waits for them, and re-layouts  30.9 us (3%)
  between operations  22.2 us (2%)
    pallas_call x1, Pallas kernels, rotate_slots(): pl.pallas_call(rotate_kernel, in_specs=[hbm] * 7 + [pl.BlockSpec(memory_s...  229 us
    pallas_call x2, Pallas kernels, ring_sums(): pl.pallas_call(functools.partial(ring_kernel, len(extras), rows is not No...  179 us
    pallas_call x1, Pallas kernels, gather(): pl.pallas_call(gather_kernel, in_specs=[hbm] * 4, out_specs=[hbm] * 5, ou...  158 us
    pallas_call x1, Pallas kernels, feed(): pl.pallas_call(feed_kernel, grid=(blocks + 4,), in_specs=[rows(D, 0), row...  88.7 us
    pallas_call x1, Pallas kernels, begin(): pl.pallas_call(begin_kernel, in_specs=[hbm, hbm], out_specs=[hbm, hbm], o...  77.5 us
    pallas_call x1, Pallas kernels, middle(): pl.pallas_call(middle_kernel, grid=(blocks + 1,), in_specs=[pl.BlockSpec(...  70.1 us
    pallas_call x1, Pallas kernels, attend_back(): pl.pallas_call(attend_back_kernel, grid=(HEADS, blocks), in_specs=[smem,...  54 us
    ppermute x4, waiting for transfers between devices, swap_y(): return lax.ppermute(piece, 'batch', [(i, i ^ 2) for i in range(4)])  48 us
  transfers between devices with their start and end apart: 15, of which 4 were waited for; matrix products, arithmetic and copies ran while one was open for 8% of the time, Pallas kernels for 56%

profile of v3, /device:TPU:12, one launch (start us, length us, event | category | flops | bytes accessed | tf_op | source)
XLA Modules:
  0.0 1126.4 jit_solution(6225046713328331224)
XLA Ops:
  7.2 3.4 bitcast_convert_fusion.master_ref.own
  11.2 77.5 %begin.1 = (bf16[3,9,192,512]{3,2,1,0:T(8,128)(2,1)}, bf16[8,64,1536]{2,1,0:T(8,128)(2,1)}) custom-call(bf16[9,192,512]{2,1,0:T(8,128)(2,1)} %bitcast_convert_fusion.master_ref.own, bf16[2,256,1536]{2,1,0:T(8,128)(2,1)} %tokens_ref.1), custom_call_target="tpu_custom_call" | custom-call | tf_op jit(solution)/shard_map/begin/pallas_call | solution.py:542
  88.7 3.6 pick_units.1
  92.4 158.2 %gather.1 = (bf16[8,192,1536]{2,1,0:T(8,128)(2,1)}, bf16[8,192,1024]{2,1,0:T(8,128)(2,1)}, bf16[8,4,64,1536]{3,2,1,0:T(8,128)(2,1)}, bf16[8,64,1536]{2,1,0:T(8,128)(2,1)}, bf16[8,4,64,1536]{3,2,1,0:T(8,128)(2,1)}) custom-call(bf16[192,1536]{1,0:T(8,128)(2,1)} %get-tuple-element.53.shard_ref, bf16[192,1024]{1,0:T(8,128)(2,1)} %get-tuple-element.54.down_ref, ...), custom_call_target="tpu_custom_call" | custom-call | tf_op jit(solution)/shard_map/gather/pallas_call | solution.py:656
  252.0 0.7 multiply_reduce_fusion
  254.1 0.7 copy.55.gain_ref
  256.3 0.6 dynamic_slice.35.unit_ref
  256.9 0.6 pad_maximum_fusion.3.scale_ref
  257.9 0.6 add_rsqrt_fusion
  258.5 7.6 convert_bitcast_fusion.base_ref
  266.5 0.8 collective-permute-done.2
  267.5 0.6 fusion.33
  271.9 0.7 stack.36
  272.7 1.0 fusion.26
  273.8 1.3 copy.54.sin_ref.sinq_ref.sink_ref
  275.3 1.3 copy.53.cos_ref.cosq_ref.cosk_ref
  277.2 0.6 compare_select_fusion.start_ref
  277.8 15.1 %project.1 = (bf16[2048,1536]{1,0:T(8,128)(2,1)}, bf16[2048,384]{1,0:T(8,128)(2,1)}, bf16[2048,384]{1,0:T(8,128)(2,1)}, bf16[2048,384]{1,0:T(8,128)(2,1)}) custom-call(bf16[2048,1536]{1,0:T(8,128)(2,1)} %bitcast.96, bf16[1536,1536]{1,0:T(8,128)(2,1)} %bitcast.98, f32[1,1536]{1,0:T(1,128)} %reshape.184.gain_ref, f32[2048,128]{1,0:T(8,128)} %copy.53.cos_ref.cosq_ref.cosk_ref, ...), custom_call_target="tpu_custom_call" | custom-call | flops 7247757312 | bytes 22413312 | tf_op jit(solution)/shard_map/project/pallas_call | solution.py:796
  293.0 42.3 %attend.1 = (bf16[2048,384]{1,0:T(8,128)(2,1)}, f32[3,2,128,2048]{3,2,1,0:T(8,128)}, f32[3,8,1,512]{3,2,1,0:T(1,128)}) custom-call(s32[8]{0:T(128)} %and_select_fusion.low_ref, f32[1]{0:T(128)} %bitcast.10.lam_ref, bf16[2048,384]{1,0:T(8,128)(2,1)} %get-tuple-element.58.q_ref, bf16[2048,384]{1,0:T(8,128)(2,1)} %get-tuple-element.59.k_ref, ...), custom_call_target="tpu_custom_call" | custom-call | flops 12884901888 | bytes 12582912 | tf_op jit(solution)/shard_map/attend/pallas_call | solution.py:865
  335.3 70.1 %middle.1 = (bf16[2048,1536]{1,0:T(8,128)(2,1)}, f32[8,64,1536]{2,1,0:T(8,128)}) custom-call(bf16[2048,1536]{1,0:T(8,128)(2,1)} %bitcast.97, f32[1,1536]{1,0:T(1,128)} %reshape.181.gain_ref, bf16[2048,384]{1,0:T(8,128)(2,1)} %get-tuple-element.61.a_ref.a_hbm, bf16[1536,1536]{1,0:T(8,128)(2,1)} %bitcast.99, bf16[2048,384]{1,0:T(8,128)(2,1)} %get-tuple-element.61.a_ref.a_hbm, ...), custom_call_target="tpu_custom_call" | custom-call | flops 9663676416 | bytes 26738688 | tf_op jit(solution)/shard_map/middle/pallas_call | solution.py:1087
  405.4 1.0 collective-permute-start.4
  406.4 88.7 %feed.1 = (bf16[2048,3072]{1,0:T(8,128)(2,1)}, bf16[2048,1536]{1,0:T(8,128)(2,1)}, f32[8,64,1536]{2,1,0:T(8,128)}, bf16[2048,1536]{1,0:T(8,128)(2,1)}, f32[2048,384]{1,0:T(8,128)}, /*index=5*/f32[1,1536]{1,0:T(1,128)}) custom-call(bf16[2048,1536]{1,0:T(8,128)(2,1)} %get-tuple-element.62.n_ref, bf16[2048,1536]{1,0:T(8,128)(2,1)} %bitcast.92, ...), custom_call_target="tpu_custom_call" | custom-call | flops 38654705664 | bytes 47185920 | tf_op jit(solution)/shard_map/feed/pallas_call | solution.py:1233
  495.1 3.4 constant_dynamic-slice_fusion.3
  499.0 0.9 copy-done.26
  499.9 7.6 convolution_convert_fusion.2
  507.4 16.6 %fusion.2.refs_0_ = bf16[1536,2048]{1,0:T(8,128)(2,1)} fusion(bf16[2048,1536]{1,0:T(8,128)(2,1)} %get-tuple-element.62.n_ref, bf16[2048,3072]{1,0:T(8,128)(2,1)S(1)} %bitcast.107), kind=kOutput, calls=%fused_computation.2 | convolution fusion | flops 12888047616 | bytes 20971520 | tf_op jit(solution)/shard_map/dot_general | solution.py:359
  524.1 1.0 fusion.6
  525.1 54.0 %attend_back.1 = (bf16[2048,384]{1,0:T(8,128)(2,1)}, bf16[2048,384]{1,0:T(8,128)(2,1)}, bf16[2048,384]{1,0:T(8,128)(2,1)}, f32[3,128,256]{2,1,0:T(8,128)}, f32[3,1,256]{2,1,0:T(1,128)}) custom-call(s32[8]{0:T(128)} %and_select_fusion.low_ref, f32[1]{0:T(128)} %bitcast.10.lam_ref, bf16[2048,384]{1,0:T(8,128)(2,1)} %get-tuple-element.58.q_ref, ...), custom_call_target="tpu_custom_call" | custom-call | flops 32212254720 | bytes 18874368 | tf_op jit(solution)/shard_map/attend_back/pallas_call | solution.py:964
  579.1 1.7 constant_dynamic-update-slice_fusion.2
  581.8 9.4 convolution_convert_fusion.1
  591.3 0.7 constant_dynamic-slice_fusion.1
  591.9 2.0 copy.79
  594.0 1.2 dynamic-slice_bitcast_fusion.1
  595.3 1.1 collective-permute-start.6
  596.4 9.7 fusion.12
  606.1 0.7 copy-done.22
  606.8 25.4 %collective-permute-done.6 = bf16[8,64,1536]{2,1,0:T(8,128)(2,1)} collective-permute-done((bf16[8,64,1536]{2,1,0:T(8,128)(2,1)}, bf16[8,64,1536]{2,1,0:T(8,128)(2,1)}, u32[]{:S(2)}, u32[]{:S(2)}) %collective-permute-start.6) | collective-permute-done | bytes 1572896 | tf_op jit(solution)/shard_map/ppermute | solution.py:371
  632.3 4.6 fusion.24.refs_1_
  636.9 0.6 reduce_sum.105
  638.8 0.9 multiply_bitcast_fusion.3
  640.0 2.8 fusion.5
  642.9 1.2 collective-permute-start.7
  644.2 12.2 %convolution_convert_fusion = bf16[1536,1152]{1,0:T(8,128)(2,1)S(1)} fusion(bf16[2048,1536]{1,0:T(8,128)(2,1)} %get-tuple-element.80, bf16[2048,1152]{1,0:T(8,128)(2,1)} %copy-done.13), kind=kOutput, calls=%fused_computation.3 | convolution fusion | flops 7249526784 | bytes 14548992 | tf_op jit(solution)/shard_map/dot_general | solution.py:359
  656.4 22.6 %collective-permute-done.7 = bf16[8,64,1536]{2,1,0:T(8,128)(2,1)S(1)} collective-permute-done((bf16[8,64,1536]{2,1,0:T(8,128)(2,1)S(1)}, bf16[8,64,1536]{2,1,0:T(8,128)(2,1)S(1)}, u32[]{:S(2)}, u32[]{:S(2)}) %collective-permute-start.7) | collective-permute-done | bytes 1572896 | tf_op jit(solution)/shard_map/ppermute | solution.py:371
  678.9 1.2 fusion.21
  680.2 2.5 pad_maximum_fusion.refs_0_
  682.8 1.2 collective-permute-start.9
  684.0 107.6 %ring_sums_6.1 = (bf16[192,2048]{1,0:T(8,128)(2,1)}, bf16[2,256,1536]{2,1,0:T(8,128)(2,1)}) custom-call(bf16[1536,2048]{1,0:T(8,128)(2,1)} %fusion.2.refs_0_, bf16[8,64,1536]{2,1,0:T(8,128)(2,1)} %fusion.24.refs_1_), custom_call_target="tpu_custom_call" | custom-call | flops 60000002048 | bytes 9437184 | tf_op jit(solution)/shard_map/ring_sums_6/pallas_call | solution.py:1438
  791.8 71.6 %ring_sums_7.1 = (bf16[4,192,1536]{2,1,0:T(8,128)(2,1)}, bf16[4,192,2048]{2,1,0:T(8,128)(2,1)}, bf16[4,192,1024]{2,1,0:T(8,128)(2,1)}) custom-call(bf16[1536,1536]{1,0:T(8,128)(2,1)} %pad_maximum_fusion.refs_0_, bf16[192,2048]{1,0:T(8,128)(2,1)} %get-tuple-element.83.refs_1_, bf16[192,1024]{1,0:T(8,128)(2,1)} %reduce-scatter.2.cloned.1.call-done.refs_2_), custom_call_target="tpu_custom_call" | custom-call | flops 60000002048 | bytes 7077888 | tf_op jit(solution)/shard_map/ring_sums_7/pallas_call | solution.py:1438
  863.4 4.0 place_units.1.g_ref
  867.5 1.1 collective-permute-start.11
  868.6 2.7 collective-permute-done.11
  871.3 2.4 collective-permute-start.12
  873.7 4.1 fusion.20.rows_ref
  877.8 229.2 %rotate_slots.1 = (f32[9,192,512]{2,1,0:T(8,128)}, f32[9,192,512]{2,1,0:T(8,128)}, f32[9,192,512]{2,1,0:T(8,128)}, bf16[2,256,1536]{2,1,0:T(8,128)(2,1)}) custom-call(bf16[9,192,512]{2,1,0:T(8,128)(2,1)} %place_units.1.g_ref, bf16[9,192,1536]{2,1,0:T(8,128)(2,1)} %convert_bitcast_fusion.base_ref, bf16[9,192,1536]{2,1,0:T(8,128)(2,1)} %collective-permute-done.4.other_ref, ...), custom_call_target="tpu_custom_call" | custom-call | tf_op jit(solution)/shard_map/rotate_slots/pallas_call | solution.py:1650
  1107.1 0.6 divide_subtract_fusion
  1107.7 1.1 copy.89
  1108.9 1.1 copy.90
  1110.0 1.0 copy-done.7
  1111.0 1.8 copy.91
  1112.8 1.5 copy-done.6
  1114.3 1.8 copy.92
  1116.1 1.5 copy-done.5
  1117.6 1.8 copy.93
  (122 shorter events, 6.8 us)
Async XLA Ops:
  7.2 3.5 copy-start.25
  7.2 398.2 %all-gather.2.cloned.1.call-start = ((), (), s32[]{:S(2)}) async-start(), calls=%async_computation.1 | async-start | bytes 7077888 | tf_op jit(solution)/shard_map/all_gather | solution.py:1737
  92.3 158.3 %copy-start.24 = (s32[2,6]{1,0:T(2,128)S(1)}, s32[2,6]{1,0:T(2,128)}, u32[]{:S(2)}) copy-start(s32[2,6]{1,0:T(2,128)} %param.14) | copy-start | bytes 148
  92.3 158.5 %copy-start.17 = (f32[3456]{0:T(1024)S(1)}, f32[3456]{0:T(1024)}, u32[]{:S(2)}) copy-start(f32[3456]{0:T(1024)} %param.21) | copy-start | bytes 41476
  92.3 165.2 %copy-start = (bf16[8,64,1536]{2,1,0:T(8,128)(2,1)S(1)}, bf16[8,64,1536]{2,1,0:T(8,128)(2,1)}, u32[]{:S(2)}) copy-start(bf16[8,64,1536]{2,1,0:T(8,128)(2,1)} %get-tuple-element.55.x_ref) | copy-start | bytes 4718596
  250.6 541.2 %reduce-scatter.2.cloned.1.call-start = ((), (), s32[]{:S(2)}) async-start(), calls=%async_computation.2 | async-start | bytes 3538944 | tf_op jit(solution)/shard_map/reduce_scatter | solution.py:1757
  250.6 15.5 %collective-permute-start.1 = (s32[2,6]{1,0:T(2,128)S(1)}, s32[2,6]{1,0:T(2,128)S(1)}, u32[]{:S(2)}, u32[]{:S(2)}) collective-permute-start(s32[2,6]{1,0:T(2,128)S(1)} %copy-done.24), channel_id=1, source_target_pairs={{0,16},{8,24},{16,0},{24,8},{1,17},{9,25},{17,1},{25,9},{2,18},{10... | collective-permute-start | bytes 152 | tf_op jit(solution)/shard_map/ppermute | solution.py:371
  250.7 15.8 %collective-permute-start = (s32[2,6]{1,0:T(2,128)S(1)}, s32[2,6]{1,0:T(2,128)S(1)}, u32[]{:S(2)}, u32[]{:S(2)}) collective-permute-start(s32[2,6]{1,0:T(2,128)S(1)} %copy-done.24), channel_id=1, source_target_pairs={{0,8},{8,0},{16,24},{24,16},{1,9},{9,1},{17,25},{25,17},{2,10},{10... | collective-permute-start | bytes 152 | tf_op jit(solution)/shard_map/ppermute | solution.py:367
  250.8 0.6 copy-start.15
  266.1 1.3 collective-permute-start.2
  405.4 119.8 %collective-permute-start.4 = (bf16[9,192,1536]{2,1,0:T(8,128)(2,1)}, bf16[9,192,1536]{2,1,0:T(8,128)(2,1)}, u32[]{:S(2)}, u32[]{:S(2)}) collective-permute-start(bf16[9,192,1536]{2,1,0:T(8,128)(2,1)} %convert_bitcast_fusion.base_ref), channel_id=1, source_target_pairs={{0,2},{1,3},{2,0},{3,1},{4,6},{5,7},{6,4},{7,5},{8,10},{9,11},{10,... | collective-permute-start | bytes 15925256 | tf_op jit(solution)/shard_map/ppermute | solution.py:418
  498.5 1.4 copy-start.26
  498.5 9.0 slice-start.4
  498.8 25.3 %collective-permute-start.3 = (bf16[8,2,64,1536]{3,2,0,1:T(8,128)(2,1)S(1)}, bf16[8,2,64,1536]{3,2,0,1:T(8,128)(2,1)S(1)}, u32[]{:S(2)}, u32[]{:S(2)}) collective-permute-start(bf16[8,2,64,1536]{3,2,0,1:T(8,128)(2,1)S(1)} %bitcast.85), channel_id=1, source_target_pairs={{0,8},{8,0},{16,24},{24,16},{1,9},{9,1},{17,25},{25,17},{2,10},{10... | collective-permute-start | bytes 9437192 | tf_op jit(solution)/shard_map/ppermute | solution.py:367
  499.9 7.6 slice-start.5
  499.9 7.6 slice-start.6
  524.1 57.7 %slice-start.2 = ((s8[4718592]{0:T(1024)(128)(4,1)}), s8[4194304]{0:T(1024)(128)(4,1)S(1)}, s32[]{:S(2)}) async-start(s8[4718592]{0:T(1024)(128)(4,1)} %bitcast.102), calls=%async_computation.5 | async-start | bytes 8388608
  525.1 68.9 %copy-start.4 = (bf16[8,2,64,1536]{3,2,0,1:T(8,128)(2,1)}, bf16[8,2,64,1536]{3,2,0,1:T(8,128)(2,1)S(1)}, u32[]{:S(2)}) copy-start(bf16[8,2,64,1536]{3,2,0,1:T(8,128)(2,1)S(1)} %fusion.6) | copy-start | bytes 9437188
  525.1 56.7 %slice-start.3 = ((s8[4718592]{0:T(1024)(128)(4,1)}), s8[524288]{0:T(1024)(128)(4,1)S(1)}, s32[]{:S(2)}) async-start(s8[4718592]{0:T(1024)(128)(4,1)} %bitcast.102), calls=%async_computation.6 | async-start | bytes 1048576
  579.1 1.9 copy-start.11
  579.1 2.3 copy-start.10
  581.0 15.4 %slice-start = ((s8[6291456]{0:T(1024)(128)(4,1)}), s8[4194304]{0:T(1024)(128)(4,1)S(1)}, s32[]{:S(2)}) async-start(s8[6291456]{0:T(1024)(128)(4,1)} %bitcast.93), calls=%async_computation.3 | async-start | bytes 8388608
  581.8 9.4 copy-start.13
  581.8 14.6 %slice-start.1 = ((s8[6291456]{0:T(1024)(128)(4,1)}), s8[2097152]{0:T(1024)(128)(4,1)S(1)}, s32[]{:S(2)}) async-start(s8[6291456]{0:T(1024)(128)(4,1)} %bitcast.93), calls=%async_computation.4 | async-start | bytes 4194304
  593.9 46.1 %collective-permute-start.5 = (bf16[8,2,64,1536]{3,2,0,1:T(8,128)(2,1)}, bf16[8,2,64,1536]{3,2,0,1:T(8,128)(2,1)}, u32[]{:S(2)}, u32[]{:S(2)}) collective-permute-start(bf16[8,2,64,1536]{3,2,0,1:T(8,128)(2,1)} %bitcast.73), channel_id=1, source_target_pairs={{0,8},{8,0},{16,24},{24,16},{1,9},{9,1},{17,25},{25,17},{2,10},{10... | collective-permute-start | bytes 9437192 | tf_op jit(solution)/shard_map/ppermute | solution.py:367
  595.3 37.0 %collective-permute-start.6 = (bf16[8,64,1536]{2,1,0:T(8,128)(2,1)}, bf16[8,64,1536]{2,1,0:T(8,128)(2,1)}, u32[]{:S(2)}, u32[]{:S(2)}) collective-permute-start(bf16[8,64,1536]{2,1,0:T(8,128)(2,1)} %dynamic-slice_bitcast_fusion.1), channel_id=1, source_target_pairs={{0,16},{8,24},{16,0},{24,8},{1,17},{9,25},{17,1},{25,9},{2,18},{10... | collective-permute-start | bytes 4718600 | tf_op jit(solution)/shard_map/ppermute | solution.py:371
  606.1 0.7 copy-start.22
  606.8 30.1 %copy-start.23 = (f32[3,1,256]{2,1,0:T(1,128)S(1)}, f32[3,1,256]{2,1,0:T(1,128)}, u32[]{:S(2)}) copy-start(f32[3,1,256]{2,1,0:T(1,128)} %get-tuple-element.94) | copy-start | bytes 9220
  606.8 33.0 %copy-start.14 = (f32[3,128,256]{2,1,0:T(8,128)S(1)}, f32[3,128,256]{2,1,0:T(8,128)}, u32[]{:S(2)}) copy-start(f32[3,128,256]{2,1,0:T(8,128)} %get-tuple-element.93) | copy-start | bytes 1179652
  642.8 36.1 %copy-start.2 = (bf16[8,2,64,1536]{3,2,0,1:T(8,128)(2,1)}, bf16[8,2,64,1536]{3,2,0,1:T(8,128)(2,1)S(1)}, u32[]{:S(2)}) copy-start(bf16[8,2,64,1536]{3,2,0,1:T(8,128)(2,1)S(1)} %fusion.5) | copy-start | bytes 9437188
  642.9 36.0 %collective-permute-start.7 = (bf16[8,64,1536]{2,1,0:T(8,128)(2,1)S(1)}, bf16[8,64,1536]{2,1,0:T(8,128)(2,1)S(1)}, u32[]{:S(2)}, u32[]{:S(2)}) collective-permute-start(bf16[8,64,1536]{2,1,0:T(8,128)(2,1)S(1)} %dynamic-slice_bitcast_fusion), channel_id=1, source_target_pairs={{0,16},{8,24},{16,0},{24,8},{1,17},{9,25},{17,1},{25,9},{2,18},{10... | collective-permute-start | bytes 4718600 | tf_op jit(solution)/shard_map/ppermute | solution.py:371
  644.1 34.8 %copy-start.1 = (bf16[8,64,1536]{2,1,0:T(8,128)(2,1)S(1)}, bf16[8,64,1536]{2,1,0:T(8,128)(2,1)}, u32[]{:S(2)}) copy-start(bf16[8,64,1536]{2,1,0:T(8,128)(2,1)} %get-tuple-element.55.x_ref) | copy-start | bytes 4718596
  644.1 34.8 %copy-start.16 = (f32[1536]{0:T(1024)S(1)}, f32[1536]{0:T(1024)}, u32[]{:S(2)}) copy-start(f32[1536]{0:T(1024)} %copy-done.15) | copy-start | bytes 18436
  644.2 34.8 %copy-start.19 = (f32[8,64]{1,0:T(8,128)S(1)}, f32[8,64]{1,0:T(8,128)}, u32[]{:S(2)}) copy-start(f32[8,64]{1,0:T(8,128)} %add_rsqrt_fusion) | copy-start | bytes 6148
  656.3 23.9 %copy-start.12 = (bf16[1536,384]{1,0:T(8,128)(2,1)S(1)}, bf16[1536,384]{1,0:T(8,128)(2,1)}, u32[]{:S(2)}) copy-start(bf16[1536,384]{1,0:T(8,128)(2,1)} %convolution_convert_fusion.2) | copy-start | bytes 3538948
  680.2 2.6 collective-permute-start.8
  682.8 108.8 %collective-permute-start.9 = (f32[3456]{0:T(1024)S(1)}, f32[3456]{0:T(1024)S(1)}, u32[]{:S(2)}, u32[]{:S(2)}) collective-permute-start(f32[3456]{0:T(1024)S(1)} %fusion.41), channel_id=1, source_target_pairs={{0,16},{8,24},{16,0},{24,8},{1,17},{9,25},{17,1},{25,9},{2,18},{10... | collective-permute-start | bytes 41480 | tf_op jit(solution)/shard_map/ppermute | solution.py:371
  791.6 75.8 %collective-permute-start.10 = (f32[3456]{0:T(1024)S(1)}, f32[3456]{0:T(1024)S(1)}, u32[]{:S(2)}, u32[]{:S(2)}) collective-permute-start(f32[3456]{0:T(1024)S(1)} %add.161), channel_id=1, source_target_pairs={{0,1},{1,0},{2,3},{3,2},{4,5},{5,4},{6,7},{7,6},{8,9},{9,8},{10,11... | collective-permute-start | bytes 41480 | tf_op jit(solution)/shard_map/ppermute | solution.py:378
  863.4 10.3 copy-start.3
  867.5 3.8 collective-permute-start.11
  871.3 235.8 %collective-permute-start.12 = (f32[3456]{0:T(1024)S(1)}, f32[3456]{0:T(1024)S(1)}, u32[]{:S(2)}, u32[]{:S(2)}) collective-permute-start(f32[3456]{0:T(1024)S(1)} %add.163), channel_id=1, source_target_pairs={{0,4},{1,5},{2,6},{3,7},{4,0},{5,1},{6,2},{7,3},{8,12},{9,13},{10,... | collective-permute-start | bytes 41480 | tf_op jit(solution)/shard_map/ppermute | solution.py:378
  877.8 229.3 %copy-start.18 = (f32[3456]{0:T(1024)S(1)}, f32[3456]{0:T(1024)}, u32[]{:S(2)}) copy-start(f32[3456]{0:T(1024)} %param.21) | copy-start | bytes 41476
  877.8 229.3 %copy-start.20 = (f32[3456]{0:T(1024)S(1)}, f32[3456]{0:T(1024)}, u32[]{:S(2)}) copy-start(f32[3456]{0:T(1024)} %param.23) | copy-start | bytes 41476
  877.8 229.3 %copy-start.21 = (f32[3456]{0:T(1024)S(1)}, f32[3456]{0:T(1024)}, u32[]{:S(2)}) copy-start(f32[3456]{0:T(1024)} %param.22) | copy-start | bytes 41476
  877.8 229.9 %copy-start.8 = (bf16[2,256,1536]{2,1,0:T(8,128)(2,1)S(1)}, bf16[2,256,1536]{2,1,0:T(8,128)(2,1)}, u32[]{:S(2)}) copy-start(bf16[2,256,1536]{2,1,0:T(8,128)(2,1)} %get-tuple-element.131) | copy-start | bytes 4718596
  1107.0 1.8 copy-start.9
  1107.7 3.3 copy-start.7
  1111.0 3.3 copy-start.6
  1114.3 3.3 copy-start.5
Sparse Core Ops, SparseCore 0:
  250.7 100.2 all-gather.1
  606.2 75.7 reduce-scatter.1

commit v4 on v3

--- a/solution.py
+++ b/solution.py
@@ -347,8 +347,8 @@
 VMEM_LIMIT = 56 * 2**20
 
 
-def params(**more):
-    return pltpu.CompilerParams(vmem_limit_bytes=VMEM_LIMIT, **more)
+def params(limit=VMEM_LIMIT, **more):
+    return pltpu.CompilerParams(vmem_limit_bytes=limit, **more)
 
 
 def dot_last(left, right):
@@ -397,21 +397,6 @@
 def batch_pieces(piece):
     far = swap_y(piece)
     return (piece, swap_core(piece), far, swap_core(far))
-
-
-def pick(array, index, axis):
-    return lax.dynamic_index_in_dim(array, index, axis, keepdims=False)
-
-
-def near_sum(partial, me):
-    split = partial.reshape(partial.shape[:1] + (2, 2) + partial.shape[2:])
-    core = me % 2
-    return (pick(split, core, 2).astype(F32) + swap_core(pick(split, 1 - core, 2)).astype(F32)).astype(BF)
-
-
-def far_sum(near, me):
-    y = me // 2
-    return pick(near, y, 1).astype(F32) + swap_y(pick(near, 1 - y, 1)).astype(F32)
 
 
 def swap_blk(piece, bit):
@@ -452,62 +437,114 @@
     )
 
 
-def scatter_rows_copies(source, target, sems, me, blk):
+def to_group_copies(source, between, target, s_batch, s_blk, me, blk):
     size = target.shape[1]
 
-    def each(act):
+    def over_group(n):
+        other = (me + n) % 4
+        return pltpu.make_async_remote_copy(
+            src_ref=source.at[:, pl.ds(pl.multiple_of(other * size, size), size)],
+            dst_ref=between.at[pl.ds(2 * me, 2)],
+            send_sem=s_batch.at[0, n],
+            recv_sem=s_batch.at[1, 4 - n],
+            device_id={"batch": other},
+            device_id_type=MESH,
+        )
+
+    def group_arrival(n):
+        other = (me + n) % 4
+        return pltpu.make_async_remote_copy(
+            src_ref=source.at[:, pl.ds(0, size)],
+            dst_ref=between.at[pl.ds(2 * other, 2)],
+            send_sem=s_batch.at[0, n],
+            recv_sem=s_batch.at[1, n],
+            device_id={"batch": other},
+            device_id_type=MESH,
+        )
+
+    def over_blk(n, i, local, remote_act):
+        other = (me + n) % 4
+        row = 2 * other + i
+        if n == 0:
+            piece = source.at[i, pl.ds(pl.multiple_of(me * size, size), size)]
+        else:
+            piece = between.at[row]
+
+        @pl.when(row == blk)
+        def stay():
+            local(pltpu.make_async_copy(piece, target.at[blk], s_blk.at[0, 2 * n + i]))
+
+        @pl.when(row != blk)
+        def go():
+            remote_act(
+                pltpu.make_async_remote_copy(
+                    src_ref=piece,
+                    dst_ref=target.at[blk],
+                    send_sem=s_blk.at[0, 2 * n + i],
+                    recv_sem=s_blk.at[1, blk],
+                    device_id={"blk": row},
+                    device_id_type=MESH,
+                )
+            )
+
+    def start_group():
+        for n in (2, 3, 1):
+            over_group(n).start()
+
+    def start_blk(n):
+        if n:
+            group_arrival(n).wait_recv()
         for i in range(2):
-            for j in range(4):
-                piece = source.at[i, pl.ds(j * size, size)]
-                here = (me == j) & (blk == 2 * me + i)
-
-                @pl.when(here)
-                def stay():
-                    act(pltpu.make_async_copy(piece, target.at[blk], sems.at[0, 4 * i + j]), True)
-
-                @pl.when(jnp.logical_not(here))
-                def go():
-                    act(
-                        pltpu.make_async_remote_copy(
-                            src_ref=piece,
-                            dst_ref=target.at[blk],
-                            send_sem=sems.at[0, 4 * i + j],
-                            recv_sem=sems.at[1, blk],
-                            device_id=(j, 2 * me + i),
-                            device_id_type=MESH,
-                        ),
-                        False,
-                    )
-
-    def start():
-        each(lambda copy, local: copy.start())
-
-    def wait_sent():
-        each(lambda copy, local: copy.wait() if local else copy.wait_send())
-
-    def wait_arrived():
+            over_blk(n, i, lambda copy: copy.start(), lambda copy: copy.start())
+
+    def finish():
+        for n in (1, 2, 3):
+            over_group(n).wait_send()
+        for n in range(4):
+            for i in range(2):
+                over_blk(n, i, lambda copy: copy.wait(), lambda copy: copy.wait_send())
         for k in range(8):
 
-            @pl.when((blk != k) | (me != blk // 2))
+            @pl.when(blk != k)
             def arrived():
                 pltpu.make_async_remote_copy(
-                    src_ref=source.at[0, pl.ds(0, size)],
+                    src_ref=between.at[0],
                     dst_ref=target.at[k],
-                    send_sem=sems.at[0, 0],
-                    recv_sem=sems.at[1, k],
-                    device_id=(me, blk),
+                    send_sem=s_blk.at[0, 0],
+                    recv_sem=s_blk.at[1, k],
+                    device_id={"blk": k},
                     device_id_type=MESH,
                 ).wait_recv()
 
-    return start, wait_sent, wait_arrived
-
-
-def begin_kernel(master_ref, tokens_ref, pieces_ref, x_ref, s_core, s_y, s_relay, s_x):
+    return start_group, start_blk, finish
+
+
+def begin_kernel(
+    master_ref, tokens_ref, grad_ref, bases_ref, pieces_ref, x_ref, dy_ref, base_ref, wide, narrow, x_between,
+    dy_between, s_core, s_y, s_relay, s_x, s_x2, s_dy, s_dy2, s_load, s_store,
+):
     me, blk = lax.axis_index("batch"), lax.axis_index("blk")
     y, core = me // 2, me % 2
     to_core = {"batch": y * 2 + 1 - core}
     to_y = {"batch": (1 - y) * 2 + core}
-    x_start, x_sent, x_arrived = scatter_rows_copies(tokens_ref, x_ref, s_x, me, blk)
+    x_group, x_blk, x_finish = to_group_copies(tokens_ref, x_between, x_ref, s_x, s_x2, me, blk)
+    dy_group, dy_blk, dy_finish = to_group_copies(grad_ref, dy_between, dy_ref, s_dy, s_dy2, me, blk)
+    slots = bases_ref.shape[0]
+
+    def load(n):
+        return pltpu.make_async_copy(bases_ref.at[n], wide.at[n % 2], s_load.at[n])
+
+    def store(n):
+        return pltpu.make_async_copy(narrow.at[n % 2], base_ref.at[n], s_store.at[n])
+
+    def cast(n):
+        load(n).wait()
+        if n >= 2:
+            store(n - 2).wait()
+        narrow[n % 2] = wide[n % 2].astype(BF)
+        store(n).start()
+        if n + 2 < slots:
+            load(n + 2).start()
 
     def copies(c):
         at = pl.ds(3 * c, 3)
@@ -517,12 +554,26 @@
             lambda: remote(pieces_ref.at[1, at], pieces_ref.at[2, at], s_relay, c, to_core),
         )
 
-    greet_all()
+    greet([{"batch": (me + n) % 4} for n in (1, 2, 3)] + [{"blk": (blk + n) % 8} for n in range(1, 8)])
+    x_group()
+    load(0).start()
+    load(1).start()
+    x_blk(0)
+    cast(0)
+    cast(1)
     for c in range(3):
         copies(c)[1]().start()
+    dy_group()
     for c in range(3):
         copies(c)[0]().start()
-    x_start()
+    for n in (1, 2, 3):
+        x_blk(n)
+    for n in range(2, slots):
+        cast(n)
+    store(slots - 2).wait()
+    store(slots - 1).wait()
+    for n in range(4):
+        dy_blk(n)
     for c in range(3):
         copies(c)[1]().wait_recv()
         copies(c)[2]().start()
@@ -531,31 +582,47 @@
         near().wait()
         far().wait_send()
         relay().wait()
-    x_sent()
-    x_arrived()
-
-
-def begin(master, tokens):
+    x_finish()
+    dy_finish()
+
+
+def begin(master, tokens, cotangent, bases):
     hbm = pl.BlockSpec(memory_space=pl.ANY)
     size = tokens.shape[1] // 4
     sems = lambda n: pltpu.SemaphoreType.DMA((2, n))
     return pl.pallas_call(
         begin_kernel,
-        in_specs=[hbm, hbm],
-        out_specs=[hbm, hbm],
+        in_specs=[hbm] * 4,
+        out_specs=[hbm] * 4,
         out_shape=[
             jax.ShapeDtypeStruct((3,) + master.shape, BF),
             jax.ShapeDtypeStruct((8, size, D), BF),
-        ],
-        scratch_shapes=[sems(3), sems(3), sems(3), sems(8)],
+            jax.ShapeDtypeStruct((8, size, D), BF),
+            jax.ShapeDtypeStruct(bases.shape, BF),
+        ],
+        scratch_shapes=[
+            pltpu.VMEM((2,) + bases.shape[1:], F32),
+            pltpu.VMEM((2,) + bases.shape[1:], BF),
+            pltpu.VMEM((8, size, D), BF),
+            pltpu.VMEM((8, size, D), BF),
+            sems(3),
+            sems(3),
+            sems(3),
+            sems(4),
+            sems(8),
+            sems(4),
+            sems(8),
+            pltpu.SemaphoreType.DMA((bases.shape[0],)),
+            pltpu.SemaphoreType.DMA((bases.shape[0],)),
+        ],
         compiler_params=params(collective_id=3, has_side_effects=True),
         name="begin",
-    )(master, tokens)
+    )(master, tokens, cotangent, bases)
 
 
 def gather_kernel(
-    shard_ref, down_ref, x_ref, grad_ref, attn_ref, downs_ref, xs_ref, dy_ref, dys_ref, s_local, s_up, s_down, s_up2,
-    s_down2, s_x, s_dy, s_dys,
+    shard_ref, down_ref, x_ref, dy_ref, attn_ref, downs_ref, xs_ref, dys_ref, outs_ref, s_local, s_up, s_down, s_up2,
+    s_down2, s_x, s_dys, s_out,
 ):
     me, blk = lax.axis_index("batch"), lax.axis_index("blk")
     y, core = me // 2, me % 2
@@ -583,91 +650,102 @@
             lambda: remote(whole.at[at, far_slab], whole.at[at, far_slab], sems, 4 + c, to_core),
         )
 
-    dy_start, dy_sent, dy_arrived = scatter_rows_copies(grad_ref, dy_ref, s_dy, me, blk)
+    mine = attn_ref.at[:, :, pl.ds(3 * QW, QW)]
+    out = (
+        lambda: remote(mine, outs_ref.at[0], s_out, 0, to_core),
+        lambda: remote(mine, outs_ref.at[1], s_out, 1, to_y),
+        lambda: remote(outs_ref.at[1], outs_ref.at[2], s_out, 2, to_core),
+    )
     locals_ = [
         pltpu.make_async_copy(shard_ref, attn_ref.at[blk], s_local.at[0]),
         pltpu.make_async_copy(x_ref, xs_ref.at[:, me], s_local.at[1]),
         pltpu.make_async_copy(dy_ref, dys_ref.at[:, me], s_local.at[2]),
         pltpu.make_async_copy(down_ref, downs_ref.at[blk], s_local.at[3]),
     ]
-    greet_all()
+    both = ((x_ref, xs_ref, s_x), (dy_ref, dys_ref, s_dys))
+    greet((to_core, to_y, after_me, before_me))
     for part in range(2):
         ring(0, True, part).start()
         ring(0, False, part).start()
-    for c in range(2):
-        spread(x_ref, xs_ref, s_x, c)[1]().start()
-        spread(x_ref, xs_ref, s_x, c)[0]().start()
-    locals_[0].start()
-    locals_[1].start()
-    locals_[3].start()
-    dy_start()
+    for source, whole, sems in both:
+        for c in range(2):
+            spread(source, whole, sems, c)[1]().start()
+    for source, whole, sems in both:
+        for c in range(2):
+            spread(source, whole, sems, c)[0]().start()
+    for copy in locals_:
+        copy.start()
+
+    def relay(n):
+        source, whole, sems = both[n // 2]
+        copies = spread(source, whole, sems, n % 2)
+        copies[1]().wait_recv()
+        copies[2]().start()
+
     for t in range(1, 7):
         for part in range(2):
             for up in (True, False):
                 ring(t - 1, up, part).wait_recv()
                 ring(t, up, part).start()
-        if t in (4, 5):
-            copies = spread(x_ref, xs_ref, s_x, t - 4)
-            copies[1]().wait_recv()
-            copies[2]().start()
-        if t == 5:
-            dy_arrived()
-            dy_sent()
-            for c in range(2):
-                spread(dy_ref, dys_ref, s_dys, c)[1]().start()
-                spread(dy_ref, dys_ref, s_dys, c)[0]().start()
-            locals_[2].start()
     for part in range(2):
         for up in (True, False):
             ring(0, up, part, True).start()
             ring(6, up, part).wait_recv()
+    locals_[0].wait()
+    out[1]().start()
+    out[0]().start()
     for t in range(1, 7):
         for part in range(2):
             for up in (True, False):
                 ring(t - 1, up, part, True).wait_recv()
                 ring(t, up, part, True).start()
-        if t in (3, 5):
-            copies = spread(dy_ref, dys_ref, s_dys, (t - 3) // 2)
-            copies[1]().wait_recv()
-            copies[2]().start()
+        if t in (3, 4):
+            relay(t - 3)
     for part in range(2):
         for up in (True, False):
             ring(6, up, part, True).wait_recv()
+    relay(2)
+    relay(3)
+    out[1]().wait_recv()
+    out[2]().start()
     for t in range(7):
         for part in range(2):
             for up in (True, False):
                 ring(t, up, part).wait_send()
                 ring(t, up, part, True).wait_send()
-    for source, whole, sems in ((x_ref, xs_ref, s_x), (dy_ref, dys_ref, s_dys)):
+    for source, whole, sems in both:
         for c in range(2):
-            near, far, relay = spread(source, whole, sems, c)
+            near, far, again = spread(source, whole, sems, c)
             near().wait()
             far().wait_send()
-            relay().wait()
-    for copy in locals_:
+            again().wait()
+    out[0]().wait()
+    out[1]().wait_send()
+    out[2]().wait()
+    for copy in locals_[1:]:
         copy.wait()
 
 
-def gather(shard, down, x, cotangent):
+def gather(shard, down, x, dy):
     hbm = pl.BlockSpec(memory_space=pl.ANY)
     size = x.shape[1]
     sems = lambda n: pltpu.SemaphoreType.DMA((2, n))
     whole = jax.ShapeDtypeStruct((8, 4, size, D), BF)
     return pl.pallas_call(
         gather_kernel,
-        in_specs=[hbm] * 4,
+        in_specs=[pl.BlockSpec(memory_space=pltpu.VMEM)] * 4,
         out_specs=[hbm] * 5,
         out_shape=[
             jax.ShapeDtypeStruct((8,) + shard.shape, BF),
             jax.ShapeDtypeStruct((8,) + down.shape, BF),
             whole,
-            jax.ShapeDtypeStruct((8, size, D), BF),
             whole,
-        ],
-        scratch_shapes=[pltpu.SemaphoreType.DMA((4,))] + [sems(14)] * 4 + [sems(6), sems(8), sems(6)],
+            jax.ShapeDtypeStruct((3, 8, shard.shape[0], QW), BF),
+        ],
+        scratch_shapes=[pltpu.SemaphoreType.DMA((4,))] + [sems(14)] * 4 + [sems(6), sems(6), sems(3)],
         compiler_params=params(collective_id=4, has_side_effects=True),
         name="gather",
-    )(shard, down, x, cotangent)
+    )(shard, down, x, dy)
 
 
 def attention_pieces(me):
@@ -1009,7 +1087,7 @@
 
 
 def middle_kernel(
-    x_ref, gain_ref, a_ref, w_ref, a_hbm, attn_hbm, n_ref, own_ref, a_in, w_in, total, s_a, s_ay, s_ar, s_w
+    x_ref, gain_ref, a_ref, w_ref, w_in, a_hbm, n_ref, own_ref, a_in, total, s_a, s_ay, s_ar
 ):
     i = pl.program_id(0)
     me = lax.axis_index("batch")
@@ -1017,7 +1095,6 @@
     to_core = {"batch": y * 2 + 1 - core}
     to_y = {"batch": (1 - y) * 2 + core}
     blocks = a_in.shape[1]
-    mine = attn_hbm.at[:, pl.ds(3 * QW, QW)]
 
     def a_copies(b):
         source = a_hbm.at[pl.ds(b * TILE, TILE)]
@@ -1027,33 +1104,18 @@
             lambda: remote(a_in.at[1, b], a_in.at[2, b], s_ar, b, to_core),
         )
 
-    w_copies = (
-        lambda: remote(mine, w_in.at[0], s_w, 0, to_core),
-        lambda: remote(mine, w_in.at[1], s_w, 1, to_y),
-        lambda: remote(w_in.at[1], w_in.at[2], s_w, 2, to_core),
-    )
-
     @pl.when(i == 0)
     def begin():
         greet((to_core, to_y))
-        w_copies[1]().start()
         for b in range(blocks):
             a_copies(b)[1]().start()
-        w_copies[0]().start()
         for b in range(blocks):
             a_copies(b)[0]().start()
-        w_copies[1]().wait_recv()
-        w_copies[2]().start()
 
     @pl.when(i < blocks)
     def relay():
         a_copies(i)[1]().wait_recv()
         a_copies(i)[2]().start()
-
-    @pl.when(i == 1)
-    def weights():
-        w_copies[0]().wait_recv()
-        w_copies[2]().wait_recv()
 
     @pl.when(i >= 1)
     def compute():
@@ -1071,14 +1133,12 @@
 
     @pl.when(i == blocks)
     def finish():
-        for copy in w_copies:
-            copy().wait_send()
         for b in range(blocks):
             for copy in a_copies(b):
                 copy().wait_send()
 
 
-def middle(a, x, attn, gain):
+def middle(a, x, attn, others, gain):
     count = x.shape[0]
     blocks = count // TILE
     late = lambda i: (jnp.maximum(i - 1, 0), 0)
@@ -1092,7 +1152,7 @@
             pl.BlockSpec((1, D), lambda i: (0, 0)),
             pl.BlockSpec((TILE, QW), late),
             pl.BlockSpec((D, QW), lambda i: (0, 3), pipeline_mode=pl.Buffered(1)),
-            hbm,
+            pl.BlockSpec((3, D, QW), lambda i: (0, 0, 0), pipeline_mode=pl.Buffered(1)),
             hbm,
         ],
         out_specs=[
@@ -1105,34 +1165,43 @@
         ],
         scratch_shapes=[
             pltpu.VMEM((3, blocks, TILE, QW), BF),
-            pltpu.VMEM((3, D, QW), BF),
             pltpu.VMEM((TILE, D), F32),
             sems(blocks),
             sems(blocks),
             sems(blocks),
-            sems(3),
         ],
         compiler_params=params(collective_id=5, has_side_effects=True),
         cost_estimate=pl.CostEstimate(
             flops=2 * count * D * D, bytes_accessed=count * D * 7 + 2 * D * D, transcendentals=0
         ),
         name="middle",
-    )(x, gain, a, attn, a, attn)
+    )(x, gain, a, attn, others, a)
 
 
 def feed_kernel(
-    n_ref, dy_ref, w_ref, wd_ref, x1_ref, dyo_ref, wo_ref, gain_ref, act_ref, out_ref, dx_ref, low_ref, da_ref, dgain_ref,
-    part, near_in, near, far_in, gathered, s_near, s_far, s_y, s_core, s_relay,
+    n_ref, dy_ref, w_ref, wd_ref, x1_ref, dyo_ref, wo_ref, gain_ref, dup_ref, out_ref, dx_ref, low_ref, da_ref, dgain_ref,
+    gate_grad_ref, down_grad_ref, part, near_in, near, far_in, gathered, gate_sum, down_sum, staged, s_near, s_far, s_y,
+    s_core, s_relay, s_grad, s_low,
 ):
     i = pl.program_id(0)
     me = lax.axis_index("batch")
     y, core = me // 2, me % 2
     to_core = {"batch": y * 2 + 1 - core}
     to_y = {"batch": (1 - y) * 2 + core}
-    blocks = part.shape[0]
+    blocks = near_in.shape[0]
 
     def near_copy(b):
-        return remote(part.at[b, :, 1 - core], near_in.at[b], s_near, b, to_core)
+        return remote(part.at[b % 3, :, 1 - core], near_in.at[b], s_near, b, to_core)
+
+    def low_copy(b):
+        return pltpu.make_async_copy(gathered.at[b], low_ref.at[b], s_low.at[b])
+
+    grads = ((gate_sum, gate_grad_ref), (down_sum, down_grad_ref))
+    strip = gate_sum.shape[0] // 4
+
+    def grad_copy(n, which):
+        at = pl.ds(pl.multiple_of(n * strip, strip), strip)
+        return pltpu.make_async_copy(staged.at[which], grads[which][1].at[at], s_grad.at[which, n])
 
     def far_copy(b):
         return remote(near.at[b], far_in.at[b], s_far, b, to_y)
@@ -1148,12 +1217,14 @@
     def begin():
         greet((to_core, to_y))
         dgain_ref[...] = jnp.zeros_like(dgain_ref)
+        gate_sum[...] = jnp.zeros_like(gate_sum)
+        down_sum[...] = jnp.zeros_like(down_sum)
 
     @pl.when((i >= 1) & (i < blocks + 1))
     def send_far():
         b = i - 1
         near_copy(b).wait_recv()
-        both = part[b, 1 - y, core].astype(F32) + near_in[b, 1 - y].astype(F32)
+        both = part[b % 3, 1 - y, core].astype(F32) + near_in[b, 1 - y].astype(F32)
         near[b] = both.astype(BF)
         far_copy(b).start()
 
@@ -1161,7 +1232,7 @@
     def send_own():
         b = i - 2
         far_copy(b).wait_recv()
-        dn = part[b, y, core].astype(F32) + near_in[b, y].astype(F32) + far_in[b].astype(F32)
+        dn = part[b % 3, y, core].astype(F32) + near_in[b, y].astype(F32) + far_in[b].astype(F32)
         x1 = x1_ref[0]
         r = lax.rsqrt(jnp.mean(x1 * x1, axis=-1, keepdims=True) + norm_epsilon)
         t = x1 * r
@@ -1185,7 +1256,7 @@
         own_copy(b, s_core, to_core).wait_recv()
         relay_copy(b).wait_recv()
         whole = jnp.concatenate([gathered[b, other] for other in range(4)], axis=0)
-        low_ref[...] = whole
+        low_copy(b).start()
         da_ref[...] = dot_plain(whole, wo_ref[...])
 
     @pl.when(i < blocks)
@@ -1200,24 +1271,47 @@
         hidden = (silu * up).astype(BF)
         dup = (dhidden * silu).astype(BF)
         dgate = (dhidden * up * (share * (1.0 + gate * (1.0 - share)))).astype(BF)
-        act_ref[:, :FQ] = dgate
-        act_ref[:, FQ : 2 * FQ] = dup
-        act_ref[:, 2 * FQ :] = hidden
+        dup_ref[...] = dup
         dn = (dot_last(dgate, wg) + dot_last(dup, wu)).astype(BF)
         size = dn.shape[0] // 4
+
+        @pl.when(i >= 3)
+        def reuse():
+            near_copy(i - 3).wait_send()
+
         for other in range(4):
-            part[i, other // 2, other % 2] = dn[other * size : (other + 1) * size]
+            part[i % 3, other // 2, other % 2] = dn[other * size : (other + 1) * size]
         near_copy(i).start()
         out_ref[...] = dot_last(hidden, wd).astype(BF)
+        for c in range(0, n.shape[1], TILE):
+            gate_sum[c : c + TILE, :] += dot_first(n[:, c : c + TILE], dgate)
+            down_sum[c : c + TILE, :] += dot_first(dy[:, c : c + TILE], hidden)
+
+    @pl.when(i >= blocks)
+    def keep():
+        n = i - blocks
+        for which in range(2):
+
+            @pl.when(n >= 1)
+            def reuse(which=which):
+                grad_copy(n - 1, which).wait()
+
+            at = pl.ds(pl.multiple_of(n * strip, strip), strip)
+            staged[which] = grads[which][0][at, :].astype(BF)
+            grad_copy(n, which).start()
 
     @pl.when(i == blocks + 3)
     def finish():
+        for which in range(2):
+            grad_copy(3, which).wait()
+        for b in range(blocks - 3, blocks):
+            near_copy(b).wait_send()
         for b in range(blocks):
-            near_copy(b).wait_send()
             far_copy(b).wait_send()
             own_copy(b, s_y, to_y).wait_send()
             own_copy(b, s_core, to_core).wait_send()
             relay_copy(b).wait_send()
+            low_copy(b).wait()
 
 
 def feed(n, dy, weights, down, x1, dy_own, attn, gain):
@@ -1244,34 +1338,43 @@
             pl.BlockSpec((1, D), lambda i: (0, 0)),
         ],
         out_specs=[
-            rows(3 * FQ, 0),
+            rows(FQ, 0),
             rows(D, 0),
             own,
-            rows(D, 4),
+            pl.BlockSpec(memory_space=pl.ANY),
             rows(QW, 4),
             pl.BlockSpec((1, D), lambda i: (0, 0)),
+            pl.BlockSpec(memory_space=pl.ANY),
+            pl.BlockSpec(memory_space=pl.ANY),
         ],
         out_shape=[
-            shape(3 * FQ),
+            shape(FQ),
             shape(D),
             jax.ShapeDtypeStruct((blocks, size, D), F32),
-            shape(D),
+            jax.ShapeDtypeStruct((blocks, 4, size, D), BF),
             shape(QW, F32),
             jax.ShapeDtypeStruct((1, D), F32),
+            jax.ShapeDtypeStruct((D, FQ), BF),
+            jax.ShapeDtypeStruct((D, FQ), BF),
         ],
         scratch_shapes=[
-            pltpu.VMEM((blocks, 2, 2, size, D), BF),
+            pltpu.VMEM((3, 2, 2, size, D), BF),
             pltpu.VMEM((blocks, 2, size, D), BF),
             pltpu.VMEM((blocks, size, D), BF),
             pltpu.VMEM((blocks, size, D), BF),
             pltpu.VMEM((blocks, 4, size, D), BF),
+            pltpu.VMEM((D, FQ), F32),
+            pltpu.VMEM((D, FQ), F32),
+            pltpu.VMEM((2, D // 4, FQ), BF),
             sems,
             sems,
             sems,
             sems,
             sems,
-        ],
-        compiler_params=params(collective_id=1, has_side_effects=True),
+            pltpu.SemaphoreType.DMA((2, 4)),
+            pltpu.SemaphoreType.DMA((blocks,)),
+        ],
+        compiler_params=params(63 * 2**20, collective_id=1, has_side_effects=True),
         cost_estimate=pl.CostEstimate(
             flops=12 * count * D * FQ, bytes_accessed=count * (8 * D + 6 * FQ) + 6 * D * FQ, transcendentals=count * FQ
         ),
@@ -1326,135 +1429,199 @@
     return start, finish
 
 
-def ring_kernel(exchanged, sent_back, *refs):
-    refs = list(refs)
-    grad = refs.pop(0)
-    extras = [refs.pop(0) for _ in range(exchanged)]
-    rows_ref = refs.pop(0) if sent_back else None
-    sums_ref = refs.pop(0)
-    extra_outs = [refs.pop(0) for _ in range(exchanged)]
-    back_ref = refs.pop(0) if sent_back else None
-    up_in, down_in, total, s_up, s_down, s_out, s_extra, s_back, s_local = refs
+def collect_kernel(
+    gate, up, qkv, out, down_ref, out_part_ref, dn1_part_ref, x1_ref, dx1_ref, x_ref, gain_ref, attn_ref, gate_up_ref,
+    downs_ref, dx_ref, back_ref, dgain_ref, first_in, second_in, first_sum, second_sum, own, near_in, near, far_in,
+    out_rows, s_up, s_down, s_up2, s_down2, s_near, s_own, s_far, s_pieces, s_local, s_back,
+):
     me, blk = lax.axis_index("batch"), lax.axis_index("blk")
     y, core = me // 2, me % 2
     to_core = {"batch": y * 2 + 1 - core}
     to_y = {"batch": (1 - y) * 2 + core}
     place = ring_place(blk)
     after_me, before_me = {"blk": ring_owner(place + 1)}, {"blk": ring_owner(place - 1)}
-    part = grad.shape[0] // 8
+    part = first_sum.shape[0]
     half = part // 2
-    parts = up_in.shape[1]
-    width = grad.shape[1] // parts
-
-    def own(t, up, p):
-        owner = ring_owner(place - 1 - t) if up else ring_owner(place + 1 + t)
-        begin = pl.multiple_of(owner * part + (0 if up else half), half)
-        return grad.at[pl.ds(begin, half), pl.ds(p * width, width)]
-
-    def ring(t, up, p):
-        here = up_in if up else down_in
-        source = own(0, up, p) if t == 0 else here.at[t - 1, p]
-        return remote(source, here.at[t, p], s_up if up else s_down, parts * t + p, after_me if up else before_me)
-
-    def exchange(source, out, sems, n):
+    blocks = dx1_ref.shape[0]
+
+    wide = QW + 256
+    plans = (
+        ((gate, 0, FQ, 0), (up, 0, FQ, FQ)),
+        ((qkv, 0, wide, 0), (qkv, wide, 3 * QW - wide, wide), (out, 0, QW, 3 * QW)),
+    )
+    buffers, totals = (first_in, second_in), (first_sum, second_sum)
+    ring_sems = ((s_up, s_down), (s_up2, s_down2))
+
+    def mine(r, t, up_way, p):
+        grad, column, width, _ = plans[r][p]
+        owner = ring_owner(place - 1 - t) if up_way else ring_owner(place + 1 + t)
+        begin = pl.multiple_of(owner * part + (0 if up_way else half), half)
+        return grad.at[pl.ds(begin, half), pl.ds(column, width)]
+
+    def landing(r, t, up_way, p):
+        _, _, width, to = plans[r][p]
+        return buffers[r].at[0 if up_way else 1, t, :, pl.ds(to, width)]
+
+    def ring(r, t, up_way, p):
+        source = mine(r, 0, up_way, p) if t == 0 else landing(r, t - 1, up_way, p)
+        sems = ring_sems[r][0 if up_way else 1]
+        at = len(plans[r]) * t + p
+        return remote(source, landing(r, t, up_way, p), sems, at, after_me if up_way else before_me)
+
+    def ring_start(r):
+        for p in range(len(plans[r])):
+            ring(r, 0, True, p).start()
+            ring(r, 0, False, p).start()
+
+    def ring_step(r, t, p):
+        _, _, width, to = plans[r][p]
+        for up_way in (True, False):
+            ring(r, t - 1, up_way, p).wait_recv()
+            here = landing(r, t - 1, up_way, p)
+            value = (here[...].astype(F32) + mine(r, t, up_way, p)[...].astype(F32)).astype(BF)
+            if t < 7:
+                here[...] = value
+                ring(r, t, up_way, p).start()
+            else:
+                totals[r][0 if up_way else half : half if up_way else part, to : to + width] = value
+
+    def exchange(source, target, n):
         return (
-            lambda: remote(source, out.at[1], sems, 3 * n, to_core),
-            lambda: remote(source, out.at[2], sems, 3 * n + 1, to_y),
-            lambda: remote(out.at[2], out.at[3], sems, 3 * n + 2, to_core),
+            lambda: remote(source, target.at[1], s_pieces, 3 * n, to_core),
+            lambda: remote(source, target.at[2], s_pieces, 3 * n + 1, to_y),
+            lambda: remote(target.at[2], target.at[3], s_pieces, 3 * n + 2, to_core),
+            lambda: pltpu.make_async_copy(source, target.at[0], s_local.at[n]),
         )
 
-    extra_sets = [exchange(extras[n], extra_outs[n], s_extra, n) for n in range(exchanged)]
-    extra_locals = [pltpu.make_async_copy(extras[n], extra_outs[n].at[0], s_local.at[1 + n]) for n in range(exchanged)]
+    exchanges = (exchange(down_ref, downs_ref, 0), exchange(first_sum, gate_up_ref, 1), exchange(second_sum, attn_ref, 2))
+
+    def spread(n):
+        for way in (1, 0, 3):
+            exchanges[n][way]().start()
+
+    def relay(n):
+        exchanges[n][1]().wait_recv()
+        exchanges[n][2]().start()
+
+    parts = (out_part_ref, dn1_part_ref)
+
+    def near_copy(j):
+        return remote(parts[j // blocks].at[j % blocks, :, 1 - core], near_in.at[j], s_near, j, to_core)
+
+    def own_copy(j):
+        return pltpu.make_async_copy(parts[j // blocks].at[j % blocks, :, core], own.at[j], s_own.at[j])
+
+    def far_copy(j):
+        return remote(near.at[j], far_in.at[j], s_far, j, to_y)
+
+    def near_step(j):
+        near_copy(j).wait_recv()
+        own_copy(j).wait()
+        near[j] = (own[j, 1 - y].astype(F32) + near_in[j, 1 - y].astype(F32)).astype(BF)
+        far_copy(j).start()
+
+    def far_step(j):
+        far_copy(j).wait_recv()
+        total = own[j, y].astype(F32) + near_in[j, y].astype(F32) + far_in[j].astype(F32)
+        b = j % blocks
+        if j < blocks:
+            out_rows[b] = (x1_ref[b] + total).astype(BF)
+            return
+        x = x_ref[b].astype(F32)
+        r = lax.rsqrt(jnp.mean(x * x, axis=-1, keepdims=True) + norm_epsilon)
+        t = x * r
+        e = total * gain_ref[...]
+        dx = dx1_ref[b] + r * (e - t * jnp.mean(e * t, axis=-1, keepdims=True))
+        dx_ref[b] = dx.astype(BF)
+        dgain_ref[...] += jnp.sum(total * t, axis=0, keepdims=True)
+
+    back_start, back_finish = return_rows_copies(out_rows, back_ref, s_back, me, blk)
+    dgain_ref[...] = jnp.zeros_like(dgain_ref)
     greet_all()
-    for p in range(parts):
-        ring(0, True, p).start()
-        ring(0, False, p).start()
-    for n in range(exchanged):
-        extra_sets[n][1]().start()
-        extra_sets[n][0]().start()
-        extra_locals[n].start()
-    if sent_back:
-        back_start, back_finish = return_rows_copies(rows_ref, back_ref, s_back, me, blk)
-        back_start()
-    for t in range(1, 8):
-        for p in range(parts):
-            for up in (True, False):
-                here = up_in if up else down_in
-                ring(t - 1, up, p).wait_recv()
-                value = (here[t - 1, p].astype(F32) + own(t, up, p)[...].astype(F32)).astype(BF)
-                if t < 7:
-                    here[t - 1, p] = value
-                    ring(t, up, p).start()
-                else:
-                    total[0 if up else half : half if up else part, p * width : (p + 1) * width] = value
-        if t == 5:
-            for n in range(exchanged):
-                extra_sets[n][1]().wait_recv()
-                extra_sets[n][2]().start()
-    if exchanged:
-        near, far, relay = exchange(total, sums_ref, s_out, 0)
-        local = pltpu.make_async_copy(total, sums_ref.at[0], s_local.at[0])
-        far().start()
-        near().start()
-        local.start()
-        far().wait_recv()
-        relay().start()
-        near().wait()
-        far().wait_send()
-        relay().wait()
-        local.wait()
-    else:
-        local = pltpu.make_async_copy(total, sums_ref, s_local.at[0])
-        local.start()
-        local.wait()
-    for n in range(exchanged):
-        near, far, relay = extra_sets[n]
-        near().wait()
-        far().wait_send()
-        relay().wait()
-        extra_locals[n].wait()
-    if sent_back:
-        back_finish()
-    for t in range(7):
-        for p in range(parts):
-            ring(t, True, p).wait_send()
-            ring(t, False, p).wait_send()
-
-
-def ring_sums(grad, extras, rows, collective_id):
-    height, width = grad.shape
-    part = height // 8
-    parts = 2
+    ring_start(0)
+    for j in range(2 * blocks):
+        own_copy(j).start()
+        near_copy(j).start()
+    spread(0)
+    groups = [(r, t, p) for r in range(2) for t in range(1, 8) for p in range(len(plans[r]))]
+    for g, (r, t, p) in enumerate(groups):
+        ring_step(r, t, p)
+        if g < 2 * blocks:
+            near_step(g)
+        if 3 <= g < 2 * blocks + 3:
+            far_step(g - 3)
+        if (r, t, p) == (0, 6, 1):
+            ring_start(1)
+            relay(0)
+        if (r, t, p) == (0, 7, 1):
+            spread(1)
+            back_start()
+        if (r, t, p) == (1, 5, 0):
+            relay(1)
+    spread(2)
+    relay(2)
+    back_finish()
+    for n in range(3):
+        near_piece, far_piece, relay_piece, local = exchanges[n]
+        near_piece().wait()
+        far_piece().wait_send()
+        relay_piece().wait()
+        local().wait()
+    for j in range(2 * blocks):
+        near_copy(j).wait_send()
+        far_copy(j).wait_send()
+    for r in range(2):
+        for t in range(7):
+            for p in range(len(plans[r])):
+                ring(r, t, True, p).wait_send()
+                ring(r, t, False, p).wait_send()
+
+
+def collect(gate, up, qkv, out, down, out_part, dn1_part, x1, dx1, x, gain):
+    part = D // 8
+    size = x.shape[1]
+    items = 2 * x.shape[0]
     hbm = pl.BlockSpec(memory_space=pl.ANY)
+    vmem = pl.BlockSpec(memory_space=pltpu.VMEM)
     sems = lambda n: pltpu.SemaphoreType.DMA((2, n))
-    four = lambda array: jax.ShapeDtypeStruct((4,) + array, BF)
-    out_shape = [four((part, width)) if extras else jax.ShapeDtypeStruct((part, width), BF)]
-    out_shape += [four(extra.shape) for extra in extras]
-    operands = [grad, *extras]
-    if rows is not None:
-        out_shape.append(jax.ShapeDtypeStruct((2, 4 * rows.shape[1], rows.shape[2]), BF))
-        operands.append(rows)
-    buffers = pltpu.VMEM((7, parts, part // 2, width // parts), BF)
+    four = lambda width: jax.ShapeDtypeStruct((4, part, width), BF)
     return pl.pallas_call(
-        functools.partial(ring_kernel, len(extras), rows is not None),
-        in_specs=[pl.BlockSpec(memory_space=pltpu.VMEM)] + [hbm] * (len(operands) - 1),
-        out_specs=[hbm] * len(out_shape),
-        out_shape=out_shape,
+        collect_kernel,
+        in_specs=[vmem] * 4 + [hbm] * 3 + [vmem] * 4,
+        out_specs=[hbm] * 3 + [vmem, hbm, vmem],
+        out_shape=[
+            four(4 * QW),
+            four(2 * FQ),
+            four(FQ),
+            jax.ShapeDtypeStruct(x.shape, BF),
+            jax.ShapeDtypeStruct((2, 4 * size, D), BF),
+            jax.ShapeDtypeStruct((1, D), F32),
+        ],
         scratch_shapes=[
-            buffers,
-            buffers,
-            pltpu.VMEM((part, width), BF),
-            sems(7 * parts),
-            sems(7 * parts),
-            sems(3),
-            sems(3 * max(1, len(extras))),
+            pltpu.VMEM((2, 7, part // 2, 2 * FQ), BF),
+            pltpu.VMEM((2, 7, part // 2, 4 * QW), BF),
+            pltpu.VMEM((part, 2 * FQ), BF),
+            pltpu.VMEM((part, 4 * QW), BF),
+            pltpu.VMEM((items, 2, size, D), BF),
+            pltpu.VMEM((items, 2, size, D), BF),
+            pltpu.VMEM((items, size, D), BF),
+            pltpu.VMEM((items, size, D), BF),
+            pltpu.VMEM(x.shape, BF),
+            sems(14),
+            sems(14),
+            sems(21),
+            sems(21),
+            sems(items),
+            pltpu.SemaphoreType.DMA((items,)),
+            sems(items),
+            sems(9),
+            pltpu.SemaphoreType.DMA((3,)),
             sems(8),
-            pltpu.SemaphoreType.DMA((1 + len(extras),)),
-        ],
-        compiler_params=params(collective_id=collective_id, has_side_effects=True),
-        cost_estimate=pl.CostEstimate(flops=6 * 10**10, bytes_accessed=3 * height * width, transcendentals=0),
-        name=f"ring_sums_{collective_id}",
-    )(*operands)
+        ],
+        compiler_params=params(collective_id=6, has_side_effects=True),
+        cost_estimate=pl.CostEstimate(flops=10**11, bytes_accessed=2**25, transcendentals=0),
+        name="collect",
+    )(gate, up, qkv, out, down, out_part, dn1_part, x1, dx1, x, gain)
 
 
 def rotate_kernel(
@@ -1724,19 +1891,16 @@
     slots = lambda array: jnp.transpose(array, (1, 0, 2))
     master_slots = slots(master)
 
-    groups = (8, 4, count // 32, D)
-
     place = ((unit_owner // 9) ^ me) * 9 + unit_owner % 9
     master_low = master_slots.astype(BF)
-    pieces, x_own = begin(master_low, tokens)
+    pieces, x_own, dy_own, base = begin(master_low, tokens, cotangent, slots(bases))
     start, low, cosine, sine = row_tables(lengths, blk, count)
     start = start.reshape(1, count)
     attn_shard, gate_up_shard, down_shard = pick_units(place, me, master_low, pieces)
-    attn, down, x, dy_own, dy = gather(attn_shard, down_shard, x_own, cotangent)
+    attn, down, x, dy, other_out = gather(attn_shard, down_shard, x_own, dy_own)
     down = down.reshape(D, FQ)
     gate_up = lax.all_gather(after(gate_up_shard, attn), "blk", axis=0, tiled=True)
     attn, x, dy = attn.reshape(D, 4 * QW), x.reshape(count, D), dy.reshape(count, D)
-    base = slots(bases).astype(BF)
 
     gain_one = small[:D].reshape(1, D)
     gain_two = small[D : 2 * D].reshape(1, D)
@@ -1746,42 +1910,32 @@
 
     n1, q, k, v = project(x, attn, gain_one, cosine, sine)
     a_own, maps, log_mass = attend(low, lam, q, k, v, start, head_gain)
-    n2, x1 = middle(a_own, x, attn, gain_two)
+    n2, x1 = middle(a_own, x, attn, other_out.reshape(3, D, QW), gain_two)
     base_other = swap_blk(after(base, gate_up), 2)
-    acts, out_part, dx1, dx1_low, da, gain_two_grad = feed(
+    dup, out_part, dx1, dx1_low, da, gain_two_grad, gate_grad, down_grad = feed(
         n2, dy, gate_up, down, x1, dy_own, attn, gain_two
     )
-    gain_two_grad = gain_two_grad.reshape(D)
-
-    near_out = near_sum(out_part.reshape(groups), me)
-    down_sums = lax.psum_scatter(
-        dot_first(dy, acts[:, 2 * FQ :]).astype(BF), "blk", scatter_dimension=0, tiled=True
-    )
-    gate_up_grad = dot_first(n2, acts[:, : 2 * FQ]).astype(BF)
+
+    down_sums = lax.psum_scatter(down_grad, "blk", scatter_dimension=0, tiled=True)
+    up_grad = dot_first(n2, dup).astype(BF)
+    dx1_low = dx1_low.reshape(count, D)
     out_grad = dot_first(dx1_low, a_own).astype(BF)
-    da = after(da, (near_out, gate_up_grad, out_grad, base_other))
+    da = after(da, (up_grad, out_grad, base_other))
     dq, dk, dv, head_gain_sums, mixer_sums = attend_back(
         low, lam, q, k, v, start, head_gain, maps, log_mass, da, cosine, sine
     )
     dqkv = jnp.concatenate([dq, dk, dv], axis=1)
-    attn_grad = jnp.concatenate([dot_first(n1, dqkv).astype(BF), out_grad], axis=1)
-    near_dn1 = near_sum(dot_last(dqkv, attn[:, : 3 * QW]).astype(BF).reshape(groups), me)
-    out_rows = (x1 + far_sum(near_out, me)).astype(BF)
-    gate_up_grad = after(gate_up_grad, (near_dn1, attn_grad))
-    gate_up_sums, block_out = ring_sums(gate_up_grad, [], out_rows, 6)
-    attn_pieces, gate_up_pieces, down_pieces = ring_sums(attn_grad, [gate_up_sums, down_sums], None, 7)
-
-    dn1 = far_sum(near_dn1, me)
-    x_f = x_own.astype(F32)
-    r1 = lax.rsqrt(jnp.mean(x_f * x_f, axis=-1, keepdims=True) + norm_epsilon)
-    t1 = x_f * r1
-    e1 = dn1 * gain_one
-    dx = dx1 + r1 * (e1 - t1 * jnp.mean(e1 * t1, axis=-1, keepdims=True))
-    gain_one_grad = jnp.sum(dn1 * t1, axis=(0, 1))
+    qkv_grad = dot_first(n1, dqkv).astype(BF)
+    dn1_part = dot_last(dqkv, attn[:, : 3 * QW]).astype(BF)
+    groups = (8, 2, 2, count // 32, D)
+    attn_pieces, gate_up_pieces, down_pieces, dx, block_out, gain_one_grad = collect(
+        gate_grad, up_grad, qkv_grad, out_grad, down_sums, out_part.reshape(groups), dn1_part.reshape(groups),
+        x1, dx1, x_own, gain_one,
+    )
 
     (mixers_grad,) = mixer_back(jnp.sum(mixer_sums))
     small_local = jnp.concatenate(
-        [gain_one_grad, gain_two_grad, jnp.sum(head_gain_sums, axis=(0, 2)), mixers_grad.reshape(-1)]
+        [gain_one_grad.reshape(D), gain_two_grad.reshape(D), jnp.sum(head_gain_sums, axis=(0, 2)), mixers_grad.reshape(-1)]
     )
     small_grads = sum_everywhere(small_local)
 
@@ -1792,7 +1946,7 @@
     steps_done = step_count[0].astype(F32)
     scales = jnp.stack([jnp.float32(learn_rate), 1.0 - beta_one**steps_done, 1.0 - beta_two**steps_done])
     new_first, new_second, new_master, input_grad = rotate_slots(
-        grads, base, base_other, slots(first), slots(second), master_slots, dx.astype(BF), scales
+        grads, base, base_other, slots(first), slots(second), master_slots, dx, scales
     )
     new_small_first = beta_one * small_first + (1.0 - beta_one) * small_grads
     new_small_second = beta_two * small_second + (1.0 - beta_two) * small_grads * small_grads

time: 1140 us -> 1010 us (0.89)
  Pallas kernels: 922 us -> 878 us
  waiting for transfers between devices: 51.6 us -> 23.6 us
  other arithmetic: 35.1 us -> 13.4 us
  matrix products: 55.5 us -> 38.6 us
    ppermute x4 -> x2, waiting for transfers between devices: 48 us -> 3.73 us  [swap_y(): return lax.ppermute(piece, 'batch', [(i, i ^ 2) for i in range(4)])]
    pallas_call x1, Pallas kernels: 70.1 us -> 45.5 us  [middle(): pl.pallas_call(middle_kernel, grid=(blocks + 1,), in_specs=[pl.BlockSpec(...]
    convert_element_type x5 -> x0, other arithmetic: 20.2 us -> none  [the longest x1 7.57 us: row_groups(): base = slots(bases).astype(BF)]
    dot_general x4 -> x3, matrix products: 46.1 us -> 28.3 us  [dot_first(): lax.dot_general(left, right, (((0,), (0,)), ((), ())), preferred_element_...]
    pallas_call x4 -> x3, Pallas kernels: 415 us -> 407 us  [the longest x1 201 us: collect(): pl.pallas_call(collect_kernel, in_specs=[vmem] * 4 + [hbm] * 3 + [vmem] *...]
  transfers between devices with their start and end apart: 15 -> 11, of which waited for: 4 -> 6; matrix products, arithmetic and copies ran while one was open for 8% -> 6% of each run, Pallas kernels for 56% -> 47%
where the time goes in v4:
time: 1010 us; the launch traced here: 998 us
  Pallas kernels  878 us (87%)
  matrix products  38.6 us (4%)
  waiting for transfers between devices  23.6 us (2%)
  between operations  22 us (2%)
  local copies, waits for them, and re-layouts  21.3 us (2%)
  other arithmetic  13.4 us (1%)
    pallas_call x1, Pallas kernels, rotate_slots(): pl.pallas_call(rotate_kernel, in_specs=[hbm] * 7 + [pl.BlockSpec(memory_s...  228 us
    pallas_call x1, Pallas kernels, collect(): pl.pallas_call(collect_kernel, in_specs=[vmem] * 4 + [hbm] * 3 + [vmem] *...  201 us
    pallas_call x1, Pallas kernels, gather(): pl.pallas_call(gather_kernel, in_specs=[pl.BlockSpec(memory_space=pltpu.V...  107 us
    pallas_call x1, Pallas kernels, begin(): pl.pallas_call(begin_kernel, in_specs=[hbm] * 4, out_specs=[hbm] * 4, out...  99.1 us
    pallas_call x1, Pallas kernels, feed(): pl.pallas_call(feed_kernel, grid=(blocks + 4,), in_specs=[rows(D, 0), row...  94.5 us
    pallas_call x1, Pallas kernels, middle(): pl.pallas_call(middle_kernel, grid=(blocks + 1,), in_specs=[pl.BlockSpec(...  45.5 us
    pallas_call x1, Pallas kernels, attend_back(): pl.pallas_call(attend_back_kernel, grid=(HEADS, blocks), in_specs=[smem,...  45 us
    pallas_call x1, Pallas kernels, attend(): pl.pallas_call(attend_kernel, grid=(HEADS, blocks), in_specs=[smem, smem,...  34.8 us
  transfers between devices with their start and end apart: 11, of which 6 were waited for; matrix products, arithmetic and copies ran while one was open for 6% of the time, Pallas kernels for 47%

profile of v4, /device:TPU:12, one launch (start us, length us, event | category | flops | bytes accessed | tf_op | source)
XLA Modules:
  0.0 998.3 jit_solution(138348339284934961)
XLA Ops:
  7.2 3.4 bitcast_convert_fusion.master_ref.own
  10.7 0.5 fusion.5.place_ref
  11.2 99.1 %begin.1 = (bf16[3,9,192,512]{3,2,1,0:T(8,128)(2,1)}, bf16[8,64,1536]{2,1,0:T(8,128)(2,1)}, bf16[8,64,1536]{2,1,0:T(8,128)(2,1)}, bf16[9,192,1536]{2,1,0:T(8,128)(2,1)}) custom-call(bf16[9,192,512]{2,1,0:T(8,128)(2,1)} %bitcast_convert_fusion.master_ref.own, bf16[2,256,1536]{2,1,0:T(8,128)(2,1)} %tokens_ref.1, bf16[2,256,1536]{2,1,0:T(8,128)(2,1)} %grad_ref.1, ...), custom_call_target="tpu_custom_call" | custom-call | tf_op jit(solution)/shard_map/begin/pallas_call | solution.py:593
  110.4 3.6 pick_units.1
  114.0 107.0 %gather.1 = (bf16[8,192,1536]{2,1,0:T(8,128)(2,1)}, bf16[8,192,1024]{2,1,0:T(8,128)(2,1)}, bf16[8,4,64,1536]{3,2,1,0:T(8,128)(2,1)}, bf16[8,4,64,1536]{3,2,1,0:T(8,128)(2,1)}, bf16[3,8,192,384]{3,2,1,0:T(8,128)(2,1)}) custom-call(bf16[192,1536]{1,0:T(8,128)(2,1)} %get-tuple-element.57.shard_ref, bf16[192,1024]{1,0:T(8,128)(2,1)} %get-tuple-element.58.down_ref, ...), custom_call_target="tpu_custom_call" | custom-call | tf_op jit(solution)/shard_map/gather/pallas_call | solution.py:734
  221.1 0.1 collective-permute-start.1
  221.2 0.4 collective-permute-start
  221.7 0.6 reshape.178.gain_ref
  222.3 0.7 multiply_reduce_fusion
  224.3 0.7 copy.41.gain_ref
  225.1 0.6 reshape.175.gain_ref
  225.7 0.2 collective-permute-start.2
  225.9 1.0 collective-permute-done.2
  226.9 0.1 fusion.4
  227.0 0.6 fusion.8
  231.5 0.8 stack.36
  232.3 0.1 select_reduce_fusion
  232.4 1.0 fusion.1
  233.4 0.1 tile.20
  233.5 1.3 copy.40.sin_ref.sinq_ref.sink_ref
  234.8 0.1 tile.8
  234.9 1.3 copy.39.cos_ref.cosq_ref.cosk_ref
  236.3 0.1 fusion.3
  236.4 0.6 and_select_fusion.low_ref
  237.0 0.6 compare_select_fusion.start_ref
  237.6 15.1 %project.1 = (bf16[2048,1536]{1,0:T(8,128)(2,1)}, bf16[2048,384]{1,0:T(8,128)(2,1)}, bf16[2048,384]{1,0:T(8,128)(2,1)}, bf16[2048,384]{1,0:T(8,128)(2,1)}) custom-call(bf16[2048,1536]{1,0:T(8,128)(2,1)} %bitcast.64, bf16[1536,1536]{1,0:T(8,128)(2,1)} %bitcast.66, f32[1,1536]{1,0:T(1,128)} %reshape.178.gain_ref, f32[2048,128]{1,0:T(8,128)} %copy.39.cos_ref.cosq_ref.cosk_ref, ...), custom_call_target="tpu_custom_call" | custom-call | flops 7247757312 | bytes 22413312 | tf_op jit(solution)/shard_map/project/pallas_call | solution.py:874
  252.7 34.8 %attend.1 = (bf16[2048,384]{1,0:T(8,128)(2,1)}, f32[3,2,128,2048]{3,2,1,0:T(8,128)}, f32[3,8,1,512]{3,2,1,0:T(1,128)}) custom-call(s32[8]{0:T(128)} %and_select_fusion.low_ref, f32[1]{0:T(128)} %bitcast.11.lam_ref, bf16[2048,384]{1,0:T(8,128)(2,1)} %get-tuple-element.63.q_ref, bf16[2048,384]{1,0:T(8,128)(2,1)} %get-tuple-element.64.k_ref, ...), custom_call_target="tpu_custom_call" | custom-call | flops 12884901888 | bytes 12582912 | tf_op jit(solution)/shard_map/attend/pallas_call | solution.py:943
  287.5 45.5 %middle.1 = (bf16[2048,1536]{1,0:T(8,128)(2,1)}, f32[8,64,1536]{2,1,0:T(8,128)}) custom-call(bf16[2048,1536]{1,0:T(8,128)(2,1)} %bitcast.65, f32[1,1536]{1,0:T(1,128)} %reshape.175.gain_ref, bf16[2048,384]{1,0:T(8,128)(2,1)} %get-tuple-element.66.a_ref.a_hbm, bf16[1536,1536]{1,0:T(8,128)(2,1)} %bitcast.67, bf16[3,1536,384]{2,1,0:T(8,128)(2,1)} %bitcast.72, ...), custom_call_target="tpu_custom_call" | custom-call | flops 9663676416 | bytes 26738688 | tf_op jit(solution)/shard_map/middle/pallas_call | solution.py:1147
  333.0 0.1 collective-permute-start.3
  333.1 94.5 %feed.1 = (bf16[2048,1024]{1,0:T(8,128)(2,1)}, bf16[2048,1536]{1,0:T(8,128)(2,1)}, f32[8,64,1536]{2,1,0:T(8,128)}, bf16[8,4,64,1536]{3,2,1,0:T(8,128)(2,1)}, f32...) custom-call(bf16[2048,1536]{1,0:T(8,128)(2,1)} %get-tuple-element.68.n_ref, ...), custom_call_target="tpu_custom_call" | custom-call | flops 38654705664 | bytes 47185920 | tf_op jit(solution)/shard_map/feed/pallas_call | solution.py:1327
  427.7 1.5 reduce.2
  429.1 7.9 convolution_convert_fusion.3.out
  437.0 8.2 convolution_convert_fusion.2.up
  445.2 11.4 %collective-permute-done.3.other_ref = bf16[9,192,1536]{2,1,0:T(8,128)(2,1)} collective-permute-done((bf16[9,192,1536]{2,1,0:T(8,128)(2,1)}, bf16[9,192,1536]{2,1,0:T(8,128)(2,1)}, u32[]{:S(2)}, u32[]{:S(2)}) %collective-permute-start.3) | collective-permute-done | bytes 5308448 | tf_op jit(solution)/shard_map/ppermute | solution.py:403
  456.6 45.0 %attend_back.1 = (bf16[2048,384]{1,0:T(8,128)(2,1)}, bf16[2048,384]{1,0:T(8,128)(2,1)}, bf16[2048,384]{1,0:T(8,128)(2,1)}, f32[3,128,256]{2,1,0:T(8,128)}, f32[3,1,256]{2,1,0:T(1,128)}) custom-call(s32[8]{0:T(128)} %and_select_fusion.low_ref, f32[1]{0:T(128)} %bitcast.11.lam_ref, bf16[2048,384]{1,0:T(8,128)(2,1)} %get-tuple-element.63.q_ref, ...), custom_call_target="tpu_custom_call" | custom-call | flops 32212254720 | bytes 18874368 | tf_op jit(solution)/shard_map/attend_back/pallas_call | solution.py:1042
  501.6 1.4 reduce_sum.75
  504.4 0.1 multiply_bitcast_fusion.3
  504.4 0.1 reshape.188
  504.5 1.1 reduce_sum.74
  505.6 1.6 constant_dynamic-update-slice_fusion.2
  507.3 0.3 constant_dynamic-update-slice_fusion.1
  507.6 0.3 constant_dynamic-update-slice_fusion
  507.9 12.2 %convolution_convert_fusion.1.qkv = bf16[1536,1152]{1,0:T(8,128)(2,1)} fusion(bf16[2048,1536]{1,0:T(8,128)(2,1)} %get-tuple-element.76, bf16[2048,1152]{1,0:T(8,128)(2,1)S(1)} %constant_dynamic-update-slice_fusion), kind=kOutput, calls=%fused_computation.1 | convolution fusion | flops 7249526784 | bytes 14548992 | tf_op jit(solution)/shard_map/dot_general | solution.py:359
  520.1 10.4 %convolution_convert_fusion = bf16[2048,1536]{1,0:T(8,128)(2,1)} fusion(bf16[2048,1152]{1,0:T(8,128)(2,1)S(1)} %constant_dynamic-update-slice_fusion, bf16[1536,1536]{1,0:T(8,128)(2,1)S(1)} %bitcast.71), kind=kOutput, calls=%fused_computation | convolution fusion | flops 7250903040 | bytes 14548992 | tf_op jit(solution)/shard_map/dot_general | solution.py:355
  530.5 201.2 %collect.1 = (bf16[4,192,1536]{2,1,0:T(8,128)(2,1)}, bf16[4,192,2048]{2,1,0:T(8,128)(2,1)}, bf16[4,192,1024]{2,1,0:T(8,128)(2,1)}, bf16[8,64,1536]{2,1,0:T(8,128...) custom-call(bf16[1536,1024]{1,0:T(8,128)(2,1)} %get-tuple-element.74.gate, ...), custom_call_target="tpu_custom_call" | custom-call | flops 99999997952 | bytes 33554432 | tf_op jit(solution)/shard_map/collect/pallas_call | solution.py:1588
  731.7 0.7 reduce.1
  732.5 0.4 collective-permute-start.4
  732.9 0.8 collective-permute-done.4
  733.8 3.7 collective-permute-done.5
  737.6 3.7 collective-permute-done.6
  741.3 0.1 select_reduce_fusion.1
  742.2 2.9 collective-permute-done.7
  745.1 0.6 pad_maximum_fusion.2.scale_ref
  745.6 0.6 dynamic_slice.3.unit_ref
  746.2 3.8 place_units.1.g_ref
  750.1 228.3 %rotate_slots.1 = (f32[9,192,512]{2,1,0:T(8,128)}, f32[9,192,512]{2,1,0:T(8,128)}, f32[9,192,512]{2,1,0:T(8,128)}, bf16[2,256,1536]{2,1,0:T(8,128)(2,1)}) custom-call(bf16[9,192,512]{2,1,0:T(8,128)(2,1)} %place_units.1.g_ref, bf16[9,192,1536]{2,1,0:T(8,128)(2,1)} %get-tuple-element.82.base_ref, bf16[9,192,1536]{2,1,0:T(8,128)(2,1)} %collective-permute-done.3.other_ref, ...), custom_call_target="tpu_custom_call" | custom-call | tf_op jit(solution)/shard_map/rotate_slots/pallas_call | solution.py:1817
  978.5 0.6 divide_subtract_fusion
  979.1 1.1 copy.55
  980.3 2.7 copy.56
  982.9 1.8 copy.57
  984.7 1.5 copy-done.1
  986.2 1.8 copy.58
  988.0 1.5 copy-done
  989.5 1.8 copy.59
  (64 shorter events, 0.4 us)
Async XLA Ops:
  7.2 3.5 copy-start.11
  7.2 325.8 %all-gather.2.cloned.1.call-start = ((), (), s32[]{:S(2)}) async-start(), calls=%async_computation.1 | async-start | bytes 7077888 | tf_op jit(solution)/shard_map/all_gather | solution.py:1902
  114.0 107.1 %copy-start.10 = (s32[2,6]{1,0:T(2,128)S(1)}, s32[2,6]{1,0:T(2,128)}, u32[]{:S(2)}) copy-start(s32[2,6]{1,0:T(2,128)} %param.14) | copy-start | bytes 148
  114.0 107.6 %copy-start.6 = (f32[3456]{0:T(1024)S(1)}, f32[3456]{0:T(1024)}, u32[]{:S(2)}) copy-start(f32[3456]{0:T(1024)} %param.21) | copy-start | bytes 41476
  221.1 309.4 %reduce-scatter.2.cloned.1.call-start = ((), (), s32[]{:S(2)}) async-start(), calls=%async_computation.2 | async-start | bytes 3538944 | tf_op jit(solution)/shard_map/reduce_scatter | solution.py:1919
  221.1 4.5 collective-permute-start.1
  221.2 4.7 collective-permute-start
  225.7 1.2 collective-permute-start.2
  333.0 123.6 %collective-permute-start.3 = (bf16[9,192,1536]{2,1,0:T(8,128)(2,1)}, bf16[9,192,1536]{2,1,0:T(8,128)(2,1)}, u32[]{:S(2)}, u32[]{:S(2)}) collective-permute-start(bf16[9,192,1536]{2,1,0:T(8,128)(2,1)} %get-tuple-element.82.base_ref), channel_id=1, source_target_pairs={{0,2},{1,3},{2,0},{3,1},{4,6},{5,7},{6,4},{7,5},{8,10},{9,11},{10,... | collective-permute-start | bytes 15925256 | tf_op jit(solution)/shard_map/ppermute | solution.py:403
  427.6 9.4 slice-start.2
  429.1 7.9 slice-start.3
  429.1 7.9 copy-start.13
  501.6 5.7 copy-start.5
  501.6 6.0 copy-start.4
  507.3 12.9 %slice-start = ((s8[4718592]{0:T(1024)(128)(4,1)}), s8[4194304]{0:T(1024)(128)(4,1)S(1)}, s32[]{:S(2)}) async-start(s8[4718592]{0:T(1024)(128)(4,1)} %bitcast.69), calls=%async_computation.3 | async-start | bytes 8388608
  507.9 12.2 %slice-start.1 = ((s8[4718592]{0:T(1024)(128)(4,1)}), s8[524288]{0:T(1024)(128)(4,1)S(1)}, s32[]{:S(2)}) async-start(s8[4718592]{0:T(1024)(128)(4,1)} %bitcast.69), calls=%async_computation.4 | async-start | bytes 1048576
  530.5 201.9 %copy-start.7 = (f32[1536]{0:T(1024)S(1)}, f32[1536]{0:T(1024)}, u32[]{:S(2)}) copy-start(f32[1536]{0:T(1024)} %reduce.2) | copy-start | bytes 18436
  530.5 210.8 %copy-start.12 = (s32[36]{0:T(128)S(1)}, s32[36]{0:T(128)}, u32[]{:S(2)}) copy-start(s32[36]{0:T(128)} %param.15) | copy-start | bytes 436
  732.5 1.3 collective-permute-start.4
  733.7 3.8 collective-permute-start.5
  737.6 3.7 collective-permute-start.6
  741.3 3.7 collective-permute-start.7
  745.0 233.4 %collective-permute-start.8 = (f32[3456]{0:T(1024)S(1)}, f32[3456]{0:T(1024)S(1)}, u32[]{:S(2)}, u32[]{:S(2)}) collective-permute-start(f32[3456]{0:T(1024)S(1)} %add.96), channel_id=1, source_target_pairs={{0,4},{1,5},{2,6},{3,7},{4,0},{5,1},{6,2},{7,3},{8,12},{9,13},{10,... | collective-permute-start | bytes 41480 | tf_op jit(solution)/shard_map/ppermute | solution.py:378
  750.1 228.4 %copy-start.8 = (f32[3456]{0:T(1024)S(1)}, f32[3456]{0:T(1024)}, u32[]{:S(2)}) copy-start(f32[3456]{0:T(1024)} %param.23) | copy-start | bytes 41476
  750.1 228.4 %copy-start.9 = (f32[3456]{0:T(1024)S(1)}, f32[3456]{0:T(1024)}, u32[]{:S(2)}) copy-start(f32[3456]{0:T(1024)} %param.22) | copy-start | bytes 41476
  750.1 229.0 %copy-start.3 = (bf16[2,256,1536]{2,1,0:T(8,128)(2,1)S(1)}, bf16[2,256,1536]{2,1,0:T(8,128)(2,1)}, u32[]{:S(2)}) copy-start(bf16[2,256,1536]{2,1,0:T(8,128)(2,1)} %get-tuple-element.133) | copy-start | bytes 4718596
  978.4 4.5 copy-start.2
  982.9 3.3 copy-start.1
  986.2 3.3 copy-start
Sparse Core Ops, SparseCore 0:
  221.2 99.8 all-gather.1
  427.8 94.0 reduce-scatter.1

commit v5 on v4

--- a/solution.py
+++ b/solution.py
@@ -344,6 +344,7 @@
 HEADS = 3
 QW = HEADS * VD
 FQ = FF // 4
+EARLY = 2
 VMEM_LIMIT = 56 * 2**20
 
 
@@ -369,14 +370,6 @@
 
 def swap_y(piece):
     return lax.ppermute(piece, "batch", [(i, i ^ 2) for i in range(4)])
-
-
-def sum_everywhere(values):
-    values = values + swap_core(values)
-    values = values + swap_y(values)
-    for bit in (1, 2, 4):
-        values = values + lax.ppermute(values, "blk", [(i, i ^ bit) for i in range(8)])
-    return values
 
 
 def after(values, earlier):
@@ -392,15 +385,6 @@
     place = (place + 16) % 8
     side = place // 4
     return 2 * ((1 - side) * place + side * (7 - place)) + side
-
-
-def batch_pieces(piece):
-    far = swap_y(piece)
-    return (piece, swap_core(piece), far, swap_core(far))
-
-
-def swap_blk(piece, bit):
-    return lax.ppermute(piece, "blk", [(i, i ^ bit) for i in range(8)])
 
 
 MESH = pl.DeviceIdType.MESH
@@ -520,8 +504,8 @@
 
 
 def begin_kernel(
-    master_ref, tokens_ref, grad_ref, bases_ref, pieces_ref, x_ref, dy_ref, base_ref, wide, narrow, x_between,
-    dy_between, s_core, s_y, s_relay, s_x, s_x2, s_dy, s_dy2, s_load, s_store,
+    master_ref, tokens_ref, grad_ref, bases_ref, lengths_ref, pieces_ref, x_ref, dy_ref, base_ref, other_ref, lens_ref, wide, narrow, x_between,
+    dy_between, s_core, s_y, s_relay, s_x, s_x2, s_dy, s_dy2, s_load, s_store, s_len, s_other,
 ):
     me, blk = lax.axis_index("batch"), lax.axis_index("blk")
     y, core = me // 2, me % 2
@@ -537,10 +521,27 @@
     def store(n):
         return pltpu.make_async_copy(narrow.at[n % 2], base_ref.at[n], s_store.at[n])
 
+    def lengths_copy(n, at):
+        return pltpu.make_async_remote_copy(
+            src_ref=lengths_ref,
+            dst_ref=lens_ref.at[at],
+            send_sem=s_len.at[0, n],
+            recv_sem=s_len.at[1, 4 - n if at is me else n],
+            device_id={"batch": (me + n) % 4},
+            device_id_type=MESH,
+        )
+
+    zl = (blk // 2) % 2
+
+    def share(n):
+        return remote(base_ref.at[n], other_ref.at[n], s_other, n, {"blk": blk + 2 - 4 * zl})
+
     def cast(n):
         load(n).wait()
         if n >= 2:
             store(n - 2).wait()
+            if n - 2 < EARLY:
+                share(n - 2).start()
         narrow[n % 2] = wide[n % 2].astype(BF)
         store(n).start()
         if n + 2 < slots:
@@ -556,6 +557,10 @@
 
     greet([{"batch": (me + n) % 4} for n in (1, 2, 3)] + [{"blk": (blk + n) % 8} for n in range(1, 8)])
     x_group()
+    own_lengths = pltpu.make_async_copy(lengths_ref, lens_ref.at[me], s_len.at[0, 0])
+    own_lengths.start()
+    for n in (1, 2, 3):
+        lengths_copy(n, me).start()
     load(0).start()
     load(1).start()
     x_blk(0)
@@ -582,23 +587,31 @@
         near().wait()
         far().wait_send()
         relay().wait()
+    for n in range(EARLY):
+        share(n).wait()
+    own_lengths.wait()
+    for n in (1, 2, 3):
+        lengths_copy(n, me).wait_send()
+        lengths_copy(n, (me + n) % 4).wait_recv()
     x_finish()
     dy_finish()
 
 
-def begin(master, tokens, cotangent, bases):
+def begin(master, tokens, cotangent, bases, lengths):
     hbm = pl.BlockSpec(memory_space=pl.ANY)
     size = tokens.shape[1] // 4
     sems = lambda n: pltpu.SemaphoreType.DMA((2, n))
     return pl.pallas_call(
         begin_kernel,
-        in_specs=[hbm] * 4,
-        out_specs=[hbm] * 4,
+        in_specs=[hbm] * 4 + [pl.BlockSpec(memory_space=pltpu.VMEM)],
+        out_specs=[hbm] * 6,
         out_shape=[
             jax.ShapeDtypeStruct((3,) + master.shape, BF),
             jax.ShapeDtypeStruct((8, size, D), BF),
             jax.ShapeDtypeStruct((8, size, D), BF),
             jax.ShapeDtypeStruct(bases.shape, BF),
+            jax.ShapeDtypeStruct((EARLY,) + bases.shape[1:], BF),
+            jax.ShapeDtypeStruct((4,) + lengths.shape, jnp.int32),
         ],
         scratch_shapes=[
             pltpu.VMEM((2,) + bases.shape[1:], F32),
@@ -614,15 +627,17 @@
             sems(8),
             pltpu.SemaphoreType.DMA((bases.shape[0],)),
             pltpu.SemaphoreType.DMA((bases.shape[0],)),
+            sems(4),
+            sems(EARLY),
         ],
         compiler_params=params(collective_id=3, has_side_effects=True),
         name="begin",
-    )(master, tokens, cotangent, bases)
+    )(master, tokens, cotangent, bases, lengths)
 
 
 def gather_kernel(
-    shard_ref, down_ref, x_ref, dy_ref, attn_ref, downs_ref, xs_ref, dys_ref, outs_ref, s_local, s_up, s_down, s_up2,
-    s_down2, s_x, s_dys, s_out,
+    shard_ref, down_ref, x_ref, rate_ref, lens_ref, attn_ref, downs_ref, xs_ref, outs_ref, cos_ref, sin_ref, start_ref,
+    s_local, s_up, s_down, s_up2, s_down2, s_x, s_out,
 ):
     me, blk = lax.axis_index("batch"), lax.axis_index("blk")
     y, core = me // 2, me % 2
@@ -659,29 +674,48 @@
     locals_ = [
         pltpu.make_async_copy(shard_ref, attn_ref.at[blk], s_local.at[0]),
         pltpu.make_async_copy(x_ref, xs_ref.at[:, me], s_local.at[1]),
-        pltpu.make_async_copy(dy_ref, dys_ref.at[:, me], s_local.at[2]),
-        pltpu.make_async_copy(down_ref, downs_ref.at[blk], s_local.at[3]),
+        pltpu.make_async_copy(down_ref, downs_ref.at[blk], s_local.at[2]),
     ]
-    both = ((x_ref, xs_ref, s_x), (dy_ref, dys_ref, s_dys))
+
+    def tables():
+        lens = [lens_ref[blk // 2, blk % 2, j] for j in range(NDOC)]
+        ends = [lens[0]]
+        for j in range(1, NDOC):
+            ends.append(ends[-1] + lens[j])
+
+        def first_of(places):
+            first = jnp.zeros_like(places)
+            for j in range(NDOC):
+                first += jnp.where(places >= ends[j], lens[j], 0)
+            return first
+
+        places = lax.broadcasted_iota(jnp.int32, start_ref.shape, 1)
+        start_ref[...] = jnp.where(places >= ends[NDOC - 2], places, first_of(places))
+        lane = lax.broadcasted_iota(jnp.int32, (TILE, VD), 1)
+        for b in range(cos_ref.shape[0] // TILE):
+            places = b * TILE + lax.broadcasted_iota(jnp.int32, (TILE, VD), 0)
+            angle = (places - first_of(places)).astype(F32) * rate_ref[...]
+            sine = jnp.sin(angle)
+            at = slice(b * TILE, (b + 1) * TILE)
+            cos_ref[at, :] = jnp.cos(angle)
+            sin_ref[at, :] = jnp.where(lane % HD < HD // 2, -sine, sine)
+
     greet((to_core, to_y, after_me, before_me))
     for part in range(2):
         ring(0, True, part).start()
         ring(0, False, part).start()
-    for source, whole, sems in both:
+    for way in (1, 0):
         for c in range(2):
-            spread(source, whole, sems, c)[1]().start()
-    for source, whole, sems in both:
-        for c in range(2):
-            spread(source, whole, sems, c)[0]().start()
+            spread(x_ref, xs_ref, s_x, c)[way]().start()
     for copy in locals_:
         copy.start()
 
-    def relay(n):
-        source, whole, sems = both[n // 2]
-        copies = spread(source, whole, sems, n % 2)
+    def relay(c):
+        copies = spread(x_ref, xs_ref, s_x, c)
         copies[1]().wait_recv()
         copies[2]().start()
 
+    tables()
     for t in range(1, 7):
         for part in range(2):
             for up in (True, False):
@@ -704,8 +738,6 @@
     for part in range(2):
         for up in (True, False):
             ring(6, up, part, True).wait_recv()
-    relay(2)
-    relay(3)
     out[1]().wait_recv()
     out[2]().start()
     for t in range(7):
@@ -713,12 +745,11 @@
             for up in (True, False):
                 ring(t, up, part).wait_send()
                 ring(t, up, part, True).wait_send()
-    for source, whole, sems in both:
-        for c in range(2):
-            near, far, again = spread(source, whole, sems, c)
-            near().wait()
-            far().wait_send()
-            again().wait()
+    for c in range(2):
+        near, far, again = spread(x_ref, xs_ref, s_x, c)
+        near().wait()
+        far().wait_send()
+        again().wait()
     out[0]().wait()
     out[1]().wait_send()
     out[2]().wait()
@@ -726,26 +757,30 @@
         copy.wait()
 
 
-def gather(shard, down, x, dy):
+def gather(shard, down, x, lens):
     hbm = pl.BlockSpec(memory_space=pl.ANY)
     size = x.shape[1]
     sems = lambda n: pltpu.SemaphoreType.DMA((2, n))
-    whole = jax.ShapeDtypeStruct((8, 4, size, D), BF)
+    count = 32 * size
+    vmem = pl.BlockSpec(memory_space=pltpu.VMEM)
+    rates = jnp.tile(rope_base ** (-2.0 * jnp.arange(HD // 2, dtype=F32) / HD), 4).reshape(1, VD)
     return pl.pallas_call(
         gather_kernel,
-        in_specs=[pl.BlockSpec(memory_space=pltpu.VMEM)] * 4,
-        out_specs=[hbm] * 5,
+        in_specs=[vmem] * 4 + [pl.BlockSpec(memory_space=pltpu.SMEM)],
+        out_specs=[hbm] * 4 + [vmem] * 3,
         out_shape=[
             jax.ShapeDtypeStruct((8,) + shard.shape, BF),
             jax.ShapeDtypeStruct((8,) + down.shape, BF),
-            whole,
-            whole,
+            jax.ShapeDtypeStruct((8, 4, size, D), BF),
             jax.ShapeDtypeStruct((3, 8, shard.shape[0], QW), BF),
+            jax.ShapeDtypeStruct((count, VD), F32),
+            jax.ShapeDtypeStruct((count, VD), F32),
+            jax.ShapeDtypeStruct((1, count), jnp.int32),
         ],
-        scratch_shapes=[pltpu.SemaphoreType.DMA((4,))] + [sems(14)] * 4 + [sems(6), sems(6), sems(3)],
+        scratch_shapes=[pltpu.SemaphoreType.DMA((3,))] + [sems(14)] * 4 + [sems(6), sems(3)],
         compiler_params=params(collective_id=4, has_side_effects=True),
         name="gather",
-    )(shard, down, x, dy)
+    )(shard, down, x, rates, lens)
 
 
 def attention_pieces(me):
@@ -1179,9 +1214,9 @@
 
 
 def feed_kernel(
-    n_ref, dy_ref, w_ref, wd_ref, x1_ref, dyo_ref, wo_ref, gain_ref, dup_ref, out_ref, dx_ref, low_ref, da_ref, dgain_ref,
-    gate_grad_ref, down_grad_ref, part, near_in, near, far_in, gathered, gate_sum, down_sum, staged, s_near, s_far, s_y,
-    s_core, s_relay, s_grad, s_low,
+    n_ref, dy0_ref, dy1_ref, dy2_ref, dy3_ref, w_ref, wd_ref, x1_ref, dyo_ref, wo_ref, gain_ref, base_ref, dup_ref, out_ref, dx_ref, low_ref, da_ref, dgain_ref,
+    gate_grad_ref, down_grad_ref, other_ref, dy_ref, part, near_in, near, far_in, gathered, gate_sum, down_sum, staged, s_near, s_far, s_y,
+    s_core, s_relay, s_grad, s_low, s_other,
 ):
     i = pl.program_id(0)
     me = lax.axis_index("batch")
@@ -1193,6 +1228,12 @@
     def near_copy(b):
         return remote(part.at[b % 3, :, 1 - core], near_in.at[b], s_near, b, to_core)
 
+    blk = lax.axis_index("blk")
+    to_pair = {"blk": blk + 2 - 4 * ((blk // 2) % 2)}
+
+    def share(n):
+        return remote(base_ref.at[EARLY + n], other_ref.at[n], s_other, n, to_pair)
+
     def low_copy(b):
         return pltpu.make_async_copy(gathered.at[b], low_ref.at[b], s_low.at[b])
 
@@ -1215,7 +1256,9 @@
 
     @pl.when(i == 0)
     def begin():
-        greet((to_core, to_y))
+        greet((to_core, to_y, to_pair))
+        for n in range(other_ref.shape[0]):
+            share(n).start()
         dgain_ref[...] = jnp.zeros_like(dgain_ref)
         gate_sum[...] = jnp.zeros_like(gate_sum)
         down_sum[...] = jnp.zeros_like(down_sum)
@@ -1261,6 +1304,10 @@
 
     @pl.when(i < blocks)
     def compute():
+        size = dy0_ref.shape[1]
+        slabs = (me, 2 * y + 1 - core, 2 * (1 - y) + core, 2 * (1 - y) + 1 - core)
+        for slab, piece in zip(slabs, (dy0_ref, dy1_ref, dy2_ref, dy3_ref)):
+            dy_ref[pl.ds(pl.multiple_of(slab * size, size), size), :] = piece[0]
         n, dy = n_ref[...], dy_ref[...]
         wg, wu, wd = w_ref[:, :FQ], w_ref[:, FQ:], wd_ref[...]
         gate = dot_plain(n, wg)
@@ -1273,7 +1320,6 @@
         dgate = (dhidden * up * (share * (1.0 + gate * (1.0 - share)))).astype(BF)
         dup_ref[...] = dup
         dn = (dot_last(dgate, wg) + dot_last(dup, wu)).astype(BF)
-        size = dn.shape[0] // 4
 
         @pl.when(i >= 3)
         def reuse():
@@ -1312,9 +1358,11 @@
             own_copy(b, s_core, to_core).wait_send()
             relay_copy(b).wait_send()
             low_copy(b).wait()
-
-
-def feed(n, dy, weights, down, x1, dy_own, attn, gain):
+        for n in range(other_ref.shape[0]):
+            share(n).wait()
+
+
+def feed(n, dy, weights, down, x1, dy_own, attn, gain, base):
     count = n.shape[0]
     blocks = count // TILE
     size = TILE // 4
@@ -1329,13 +1377,17 @@
         grid=(blocks + 4,),
         in_specs=[
             rows(D, 0),
-            rows(D, 0),
+            pl.BlockSpec((1, size, D), late3(0)),
+            pl.BlockSpec((1, size, D), late3(0)),
+            pl.BlockSpec((1, size, D), late3(0)),
+            pl.BlockSpec((1, size, D), late3(0)),
             pl.BlockSpec((D, 2 * FQ), lambda i: (0, 0), pipeline_mode=pl.Buffered(1)),
             pl.BlockSpec((D, FQ), lambda i: (0, 0), pipeline_mode=pl.Buffered(1)),
             own,
             own,
             pl.BlockSpec((D, QW), lambda i: (0, 3), pipeline_mode=pl.Buffered(1)),
             pl.BlockSpec((1, D), lambda i: (0, 0)),
+            pl.BlockSpec(memory_space=pl.ANY),
         ],
         out_specs=[
             rows(FQ, 0),
@@ -1344,6 +1396,7 @@
             pl.BlockSpec(memory_space=pl.ANY),
             rows(QW, 4),
             pl.BlockSpec((1, D), lambda i: (0, 0)),
+            pl.BlockSpec(memory_space=pl.ANY),
             pl.BlockSpec(memory_space=pl.ANY),
             pl.BlockSpec(memory_space=pl.ANY),
         ],
@@ -1356,8 +1409,10 @@
             jax.ShapeDtypeStruct((1, D), F32),
             jax.ShapeDtypeStruct((D, FQ), BF),
             jax.ShapeDtypeStruct((D, FQ), BF),
+            jax.ShapeDtypeStruct((base.shape[0] - EARLY,) + base.shape[1:], BF),
         ],
         scratch_shapes=[
+            pltpu.VMEM((TILE, D), BF),
             pltpu.VMEM((3, 2, 2, size, D), BF),
             pltpu.VMEM((blocks, 2, size, D), BF),
             pltpu.VMEM((blocks, size, D), BF),
@@ -1373,13 +1428,14 @@
             sems,
             pltpu.SemaphoreType.DMA((2, 4)),
             pltpu.SemaphoreType.DMA((blocks,)),
+            pltpu.SemaphoreType.DMA((2, base.shape[0] - EARLY)),
         ],
         compiler_params=params(63 * 2**20, collective_id=1, has_side_effects=True),
         cost_estimate=pl.CostEstimate(
             flops=12 * count * D * FQ, bytes_accessed=count * (8 * D + 6 * FQ) + 6 * D * FQ, transcendentals=count * FQ
         ),
         name="feed",
-    )(n, dy, weights, down, x1, dy_own, attn, gain)
+    )(n, *dy, weights, down, x1, dy_own, attn, gain, base)
 
 
 def return_rows_copies(source, target, sems, me, blk):
@@ -1430,9 +1486,10 @@
 
 
 def collect_kernel(
-    gate, up, qkv, out, down_ref, out_part_ref, dn1_part_ref, x1_ref, dx1_ref, x_ref, gain_ref, attn_ref, gate_up_ref,
-    downs_ref, dx_ref, back_ref, dgain_ref, first_in, second_in, first_sum, second_sum, own, near_in, near, far_in,
+    gate, up, dqkv, a_own, n1_ref, low_ref, down_ref, out_part_ref, dn1_part_ref, x1_ref, dx1_ref, x_ref, gain_ref, attn_ref, gate_up_ref,
+    downs_ref, dx_ref, back_ref, dgain_ref, qkv, out, strips, first_in, second_in, first_sum, second_sum, own, near_in, near, far_in,
     out_rows, s_up, s_down, s_up2, s_down2, s_near, s_own, s_far, s_pieces, s_local, s_back,
+    s_strip,
 ):
     me, blk = lax.axis_index("batch"), lax.axis_index("blk")
     y, core = me // 2, me % 2
@@ -1493,7 +1550,25 @@
             lambda: pltpu.make_async_copy(source, target.at[0], s_local.at[n]),
         )
 
-    exchanges = (exchange(down_ref, downs_ref, 0), exchange(first_sum, gate_up_ref, 1), exchange(second_sum, attn_ref, 2))
+    exchanges = [exchange(down_ref, downs_ref, 0), exchange(first_sum, gate_up_ref, 1)]
+    for p, (_, _, width, to) in enumerate(plans[1]):
+        at = pl.ds(to, width)
+        exchanges.append(exchange(second_sum.at[:, at], attn_ref.at[:, :, at], 2 + p))
+
+    strip = strips.shape[2]
+    count = D // strip
+    lefts, rights, results = (n1_ref, low_ref), (dqkv, a_own), (qkv, out)
+
+    def strip_copy(n):
+        source = lefts[n // count].at[:, pl.ds((n % count) * strip, strip)]
+        return pltpu.make_async_copy(source, strips.at[n % 2], s_strip.at[n])
+
+    def strip_product(n):
+        strip_copy(n).wait()
+        at = pl.ds((n % count) * strip, strip)
+        results[n // count][at, :] = dot_first(strips[n % 2], rights[n // count][...]).astype(BF)
+        if n + 2 < 2 * count:
+            strip_copy(n + 2).start()
 
     def spread(n):
         for way in (1, 0, 3):
@@ -1543,9 +1618,13 @@
         own_copy(j).start()
         near_copy(j).start()
     spread(0)
+    strip_copy(0).start()
+    strip_copy(1).start()
     groups = [(r, t, p) for r in range(2) for t in range(1, 8) for p in range(len(plans[r]))]
     for g, (r, t, p) in enumerate(groups):
         ring_step(r, t, p)
+        if g < 2 * count:
+            strip_product(g)
         if g < 2 * blocks:
             near_step(g)
         if 3 <= g < 2 * blocks + 3:
@@ -1558,10 +1637,12 @@
             back_start()
         if (r, t, p) == (1, 5, 0):
             relay(1)
-    spread(2)
-    relay(2)
+        if (r, t) == (1, 7):
+            spread(2 + p)
+    for p in range(3):
+        relay(2 + p)
     back_finish()
-    for n in range(3):
+    for n in range(5):
         near_piece, far_piece, relay_piece, local = exchanges[n]
         near_piece().wait()
         far_piece().wait_send()
@@ -1577,7 +1658,7 @@
                 ring(r, t, False, p).wait_send()
 
 
-def collect(gate, up, qkv, out, down, out_part, dn1_part, x1, dx1, x, gain):
+def collect(gate, up, n1, dqkv, low, a_own, down, out_part, dn1_part, x1, dx1, x, gain):
     part = D // 8
     size = x.shape[1]
     items = 2 * x.shape[0]
@@ -1587,7 +1668,7 @@
     four = lambda width: jax.ShapeDtypeStruct((4, part, width), BF)
     return pl.pallas_call(
         collect_kernel,
-        in_specs=[vmem] * 4 + [hbm] * 3 + [vmem] * 4,
+        in_specs=[vmem] * 4 + [hbm] * 5 + [vmem] * 4,
         out_specs=[hbm] * 3 + [vmem, hbm, vmem],
         out_shape=[
             four(4 * QW),
@@ -1598,6 +1679,9 @@
             jax.ShapeDtypeStruct((1, D), F32),
         ],
         scratch_shapes=[
+            pltpu.VMEM((D, 3 * QW), BF),
+            pltpu.VMEM((D, QW), BF),
+            pltpu.VMEM((2, n1.shape[0], TILE), BF),
             pltpu.VMEM((2, 7, part // 2, 2 * FQ), BF),
             pltpu.VMEM((2, 7, part // 2, 4 * QW), BF),
             pltpu.VMEM((part, 2 * FQ), BF),
@@ -1614,20 +1698,22 @@
             sems(items),
             pltpu.SemaphoreType.DMA((items,)),
             sems(items),
-            sems(9),
-            pltpu.SemaphoreType.DMA((3,)),
+            sems(15),
+            pltpu.SemaphoreType.DMA((5,)),
             sems(8),
+            pltpu.SemaphoreType.DMA((2 * D // TILE,)),
         ],
-        compiler_params=params(collective_id=6, has_side_effects=True),
+        compiler_params=params(63 * 2**20, collective_id=6, has_side_effects=True),
         cost_estimate=pl.CostEstimate(flops=10**11, bytes_accessed=2**25, transcendentals=0),
         name="collect",
-    )(gate, up, qkv, out, down, out_part, dn1_part, x1, dx1, x, gain)
+    )(gate, up, dqkv, a_own, n1, low, down, out_part, dn1_part, x1, dx1, x, gain)
 
 
 def rotate_kernel(
-    g_ref, base_ref, other_ref, first_ref, second_ref, master_ref, rows_ref, scale_ref, new_first_ref, new_second_ref,
-    new_master_ref, rows_out_ref, g, base, other, firsts, seconds, masters, g_in, part, x_in, near, z_in, far, p_in, step, steps,
+    g_ref, base_ref, early_ref, other_ref, first_ref, second_ref, master_ref, rows_ref, small_ref, scale_ref, new_first_ref,
+    new_second_ref, new_master_ref, rows_out_ref, small_out_ref, group_small, blk_small, g, base, other, firsts, seconds, masters, g_in, part, x_in, near, z_in, far, p_in, step, steps,
     back, back_in, steps_own, load, store, s_g, s_x, s_z, s_p, s_step, s_back, s_up, s_side, s_rows,
+    s_small, s_small2,
 ):
     blk = lax.axis_index("blk")
     zh, zl, xx = blk // 4, (blk // 2) % 2, blk % 2
@@ -1645,6 +1731,10 @@
     stores = [(firsts, new_first_ref), (seconds, new_second_ref), (masters, new_master_ref)]
 
     def loading(i, s):
+        if i == 2:
+            early = isinstance(s, int) and s < EARLY
+            source = early_ref.at[s] if early else other_ref.at[jnp.maximum(s - EARLY, 0)]
+            return pltpu.make_async_copy(source, other.at[s], load.at[i, s])
         return pltpu.make_async_copy(loads[i][0].at[s], loads[i][1].at[s], load.at[i, s])
 
     def storing(i, s):
@@ -1684,6 +1774,37 @@
         loading(0, s).wait()
         send_g(s).start()
     rows_start()
+    me = lax.axis_index("batch")
+    group_small[me] = small_ref[...]
+
+    def small_over(buffer, at, n, size, axis, sems):
+        return pltpu.make_async_remote_copy(
+            src_ref=buffer.at[at],
+            dst_ref=buffer.at[at],
+            send_sem=sems.at[0, n],
+            recv_sem=sems.at[1, size - n],
+            device_id={axis: (at + n) % size},
+            device_id_type=MESH,
+        )
+
+    def small_from(buffer, at, n, size, axis, sems):
+        other = (at + n) % size
+        return pltpu.make_async_remote_copy(
+            src_ref=buffer.at[other],
+            dst_ref=buffer.at[other],
+            send_sem=sems.at[0, n],
+            recv_sem=sems.at[1, n],
+            device_id={axis: other},
+            device_id_type=MESH,
+        )
+
+    over_group = (group_small, me, 4, "batch", s_small)
+    over_blk = (blk_small, blk, 8, "blk", s_small2)
+
+    def small_each(which, act, begin):
+        buffer, at, size, axis, sems = which
+        for n in range(1, size):
+            act(begin(buffer, at, n, size, axis, sems))
 
     rows = base.shape[1]
 
@@ -1780,6 +1901,19 @@
                 part[s % 3, b // 2, b % 2] = turned[b * rows : (b + 1) * rows].astype(BF)
             send_x(s).start()
 
+        @pl.when(t == 2)
+        def small_start():
+            small_each(over_group, lambda copy: copy.start(), small_over)
+
+        @pl.when(t == 8)
+        def small_middle():
+            small_each(over_group, lambda copy: copy.wait_recv(), small_from)
+            total = group_small[0]
+            for n in range(1, 4):
+                total += group_small[n]
+            blk_small[blk] = total
+            small_each(over_blk, lambda copy: copy.start(), small_over)
+
         stage(7, finish)
         stage(6, update)
         stage(5, relay_x)
@@ -1791,6 +1925,13 @@
         return carry
 
     lax.fori_loop(0, count + 7, tick, 0)
+    small_each(over_blk, lambda copy: copy.wait_recv(), small_from)
+    small = blk_small[0]
+    for n in range(1, 8):
+        small += blk_small[n]
+    small_each(over_group, lambda copy: copy.wait_send(), small_over)
+    small_each(over_blk, lambda copy: copy.wait_send(), small_over)
+    small_out_ref[...] = small
     rows_finish()
     for s in range(count):
         send_g(s).wait_send()
@@ -1808,7 +1949,7 @@
         send_back(s).wait_send()
 
 
-def rotate_slots(grads, base, other, first, second, master, tokens, scales):
+def rotate_slots(grads, base, early, other, first, second, master, tokens, small, scales):
     count, rows, width = grads.shape
     half = width // 2
     hbm = pl.BlockSpec(memory_space=pl.ANY)
@@ -1816,10 +1957,13 @@
     sems = lambda n: pltpu.SemaphoreType.DMA((2, n))
     return pl.pallas_call(
         rotate_kernel,
-        in_specs=[hbm] * 7 + [pl.BlockSpec(memory_space=pltpu.SMEM)],
-        out_specs=[hbm] * 4,
-        out_shape=[shape] * 3 + [jax.ShapeDtypeStruct((2, 4 * tokens.shape[1], D), BF)],
+        in_specs=[hbm] * 8 + [pl.BlockSpec(memory_space=pltpu.VMEM), pl.BlockSpec(memory_space=pltpu.SMEM)],
+        out_specs=[hbm] * 4 + [pl.BlockSpec(memory_space=pltpu.VMEM)],
+        out_shape=[shape] * 3
+        + [jax.ShapeDtypeStruct((2, 4 * tokens.shape[1], D), BF), jax.ShapeDtypeStruct(small.shape, F32)],
         scratch_shapes=[
+            pltpu.VMEM((4,) + small.shape, F32),
+            pltpu.VMEM((8,) + small.shape, F32),
             pltpu.VMEM((count, rows, width), BF),
             pltpu.VMEM((count, rows, D), BF),
             pltpu.VMEM((count, rows, D), BF),
@@ -1849,26 +1993,12 @@
             sems(2 * count),
             sems(4 * count),
             sems(8),
+            sems(4),
+            sems(8),
         ],
         compiler_params=params(collective_id=2, has_side_effects=True),
         name="rotate_slots",
-    )(grads, base, other, first, second, master, tokens, scales)
-
-
-def row_tables(lengths, row, count):
-    everyone = jnp.stack(batch_pieces(lengths))
-    holder = (row // 2) ^ lax.axis_index("batch")
-    mine = jnp.sum(jnp.where(jnp.arange(4)[:, None, None] == holder, everyone, 0), axis=0)
-    mine = jnp.where(row % 2 == 0, mine[:1], mine[1:])
-    ends = doc_ends(mine)[0]
-    places = jnp.arange(count, dtype=jnp.int32)
-    begin = jnp.sum(jnp.where(places[:, None] >= ends[None, :], mine, 0), axis=1)
-    start = jnp.where(places >= ends[NDOC - 2], places, begin)
-    low = start.reshape(-1, TILE)[:, 0] // TILE
-    cosine, sine = turn_tables(places - begin)
-    cosine = jnp.tile(cosine, (1, 4))
-    sine = jnp.tile(jnp.concatenate([-sine, sine], axis=1), (1, 2))
-    return start, low, cosine, sine
+    )(grads, base, early, other, first, second, master, tokens, small, scales)
 
 
 def row_groups(
@@ -1893,14 +2023,15 @@
 
     place = ((unit_owner // 9) ^ me) * 9 + unit_owner % 9
     master_low = master_slots.astype(BF)
-    pieces, x_own, dy_own, base = begin(master_low, tokens, cotangent, slots(bases))
-    start, low, cosine, sine = row_tables(lengths, blk, count)
-    start = start.reshape(1, count)
+    lengths_tile = jnp.pad(lengths, ((0, 8 - lengths.shape[0]), (0, 128 - NDOC)))
+    pieces, x_own, dy_own, base, base_early, lens = begin(master_low, tokens, cotangent, slots(bases), lengths_tile)
     attn_shard, gate_up_shard, down_shard = pick_units(place, me, master_low, pieces)
-    attn, down, x, dy, other_out = gather(attn_shard, down_shard, x_own, dy_own)
+    attn, down, x, other_out, cosine, sine, start = gather(attn_shard, down_shard, x_own, lens)
+    low = start.reshape(-1, TILE)[:, 0] // TILE
     down = down.reshape(D, FQ)
     gate_up = lax.all_gather(after(gate_up_shard, attn), "blk", axis=0, tiled=True)
-    attn, x, dy = attn.reshape(D, 4 * QW), x.reshape(count, D), dy.reshape(count, D)
+    attn, x = attn.reshape(D, 4 * QW), x.reshape(count, D)
+    dy_near, dy_far = swap_core(after(dy_own, attn)), swap_y(after(dy_own, attn))
 
     gain_one = small[:D].reshape(1, D)
     gain_two = small[D : 2 * D].reshape(1, D)
@@ -1910,26 +2041,24 @@
 
     n1, q, k, v = project(x, attn, gain_one, cosine, sine)
     a_own, maps, log_mass = attend(low, lam, q, k, v, start, head_gain)
+    dy = (dy_own, dy_near, dy_far, swap_core(after(dy_far, a_own)))
     n2, x1 = middle(a_own, x, attn, other_out.reshape(3, D, QW), gain_two)
-    base_other = swap_blk(after(base, gate_up), 2)
-    dup, out_part, dx1, dx1_low, da, gain_two_grad, gate_grad, down_grad = feed(
-        n2, dy, gate_up, down, x1, dy_own, attn, gain_two
+    dup, out_part, dx1, dx1_low, da, gain_two_grad, gate_grad, down_grad, base_other = feed(
+        n2, dy, gate_up, down, x1, dy_own, attn, gain_two, base
     )
 
     down_sums = lax.psum_scatter(down_grad, "blk", scatter_dimension=0, tiled=True)
     up_grad = dot_first(n2, dup).astype(BF)
     dx1_low = dx1_low.reshape(count, D)
-    out_grad = dot_first(dx1_low, a_own).astype(BF)
-    da = after(da, (up_grad, out_grad, base_other))
+    da = after(da, up_grad)
     dq, dk, dv, head_gain_sums, mixer_sums = attend_back(
         low, lam, q, k, v, start, head_gain, maps, log_mass, da, cosine, sine
     )
     dqkv = jnp.concatenate([dq, dk, dv], axis=1)
-    qkv_grad = dot_first(n1, dqkv).astype(BF)
     dn1_part = dot_last(dqkv, attn[:, : 3 * QW]).astype(BF)
     groups = (8, 2, 2, count // 32, D)
     attn_pieces, gate_up_pieces, down_pieces, dx, block_out, gain_one_grad = collect(
-        gate_grad, up_grad, qkv_grad, out_grad, down_sums, out_part.reshape(groups), dn1_part.reshape(groups),
+        gate_grad, up_grad, n1, dqkv, dx1_low, a_own, down_sums, out_part.reshape(groups), dn1_part.reshape(groups),
         x1, dx1, x_own, gain_one,
     )
 
@@ -1937,7 +2066,7 @@
     small_local = jnp.concatenate(
         [gain_one_grad.reshape(D), gain_two_grad.reshape(D), jnp.sum(head_gain_sums, axis=(0, 2)), mixers_grad.reshape(-1)]
     )
-    small_grads = sum_everywhere(small_local)
+    small_rows = jnp.pad(small_local, (0, 32 * 128 - small_local.shape[0])).reshape(32, 128)
 
     unit_of = inverse_order(unit_owner)
     units = lax.dynamic_slice_in_dim(unit_of, me * 9, 9)
@@ -1945,9 +2074,10 @@
 
     steps_done = step_count[0].astype(F32)
     scales = jnp.stack([jnp.float32(learn_rate), 1.0 - beta_one**steps_done, 1.0 - beta_two**steps_done])
-    new_first, new_second, new_master, input_grad = rotate_slots(
-        grads, base, base_other, slots(first), slots(second), master_slots, dx, scales
-    )
+    new_first, new_second, new_master, input_grad, small_sums = rotate_slots(
+        grads, base, base_early, base_other, slots(first), slots(second), master_slots, dx, small_rows, scales
+    )
+    small_grads = small_sums.reshape(-1)[: small_local.shape[0]]
     new_small_first = beta_one * small_first + (1.0 - beta_one) * small_grads
     new_small_second = beta_two * small_second + (1.0 - beta_two) * small_grads * small_grads
     new_small = small - small_rate * adam_step(new_small_first, new_small_second, steps_done)

time: 1010 us -> 949 us (0.940)
  waiting for transfers between devices: 23.6 us -> 1.4 us
  Pallas kernels: 878 us -> 862 us
  matrix products: 38.6 us -> 23.4 us
    pallas_call x5, Pallas kernels: 730 us -> 699 us  [the longest x1 234 us: rotate_slots(): pl.pallas_call(rotate_kernel, in_specs=[hbm] * 8 + [pl.BlockSpec(memory_s...]
    ppermute x4 -> x0, waiting for transfers between devices: 18 us -> none  [the longest x1 11.4 us: swap_blk(): return lax.ppermute(piece, 'blk', [(i, i ^ bit) for i in range(8)])]
    dot_general x3 -> x1, matrix products: 28.3 us -> 11.2 us  [dot_first(): lax.dot_general(left, right, (((0,), (0,)), ((), ())), preferred_element_...]
  transfers between devices with their start and end apart: 11 -> 5, of which waited for: 6 -> 1; matrix products, arithmetic and copies ran while one was open for 6% -> 3% of each run, Pallas kernels for 47% -> 16%
where the time goes in v5:
time: 949 us; the launch traced here: 942 us
  Pallas kernels  862 us (91%)
  matrix products  23.4 us (2%)
  local copies, waits for them, and re-layouts  21 us (2%)
  between operations  18 us (2%)
  other arithmetic  12.8 us (1%)
    pallas_call x1, Pallas kernels, rotate_slots(): pl.pallas_call(rotate_kernel, in_specs=[hbm] * 8 + [pl.BlockSpec(memory_s...  234 us
    pallas_call x1, Pallas kernels, collect(): pl.pallas_call(collect_kernel, in_specs=[vmem] * 4 + [hbm] * 5 + [vmem] *...  174 us
    pallas_call x1, Pallas kernels, begin(): pl.pallas_call(begin_kernel, in_specs=[hbm] * 4 + [pl.BlockSpec(memory_sp...  100 us
    pallas_call x1, Pallas kernels, feed(): pl.pallas_call(feed_kernel, grid=(blocks + 4,), in_specs=[rows(D, 0), pl....  98 us
    pallas_call x1, Pallas kernels, gather(): pl.pallas_call(gather_kernel, in_specs=[vmem] * 4 + [pl.BlockSpec(memory_...  92.9 us
    pallas_call x1, Pallas kernels, attend_back(): pl.pallas_call(attend_back_kernel, grid=(HEADS, blocks), in_specs=[smem,...  52.9 us
    pallas_call x1, Pallas kernels, middle(): pl.pallas_call(middle_kernel, grid=(blocks + 1,), in_specs=[pl.BlockSpec(...  45 us
    pallas_call x1, Pallas kernels, attend(): pl.pallas_call(attend_kernel, grid=(HEADS, blocks), in_specs=[smem, smem,...  41.5 us
  transfers between devices with their start and end apart: 5, of which 1 were waited for; matrix products, arithmetic and copies ran while one was open for 3% of the time, Pallas kernels for 16%

profile of v5, /device:TPU:12, one launch (start us, length us, event | category | flops | bytes accessed | tf_op | source)
XLA Modules:
  0.0 941.9 jit_solution(14332941623718706620)
XLA Ops:
  7.2 0.0 all-gather.2.cloned.1.call-start
  7.3 3.4 bitcast_convert_fusion.master_ref.own
  10.7 0.6 reshape_tile.3.rate_ref
  11.3 0.6 pad.20.lengths_ref
  11.9 0.5 fusion.3.place_ref
  12.4 100.1 %begin.1 = (bf16[3,9,192,512]{3,2,1,0:T(8,128)(2,1)}, bf16[8,64,1536]{2,1,0:T(8,128)(2,1)}, bf16[8,64,1536]{2,1,0:T(8,128)(2,1)}, bf16[9,192,1536]{2,1,0:T(8,128...) custom-call(bf16[9,192,512]{2,1,0:T(8,128)(2,1)} %bitcast_convert_fusion.master_ref.own, ...), custom_call_target="tpu_custom_call" | custom-call | tf_op jit(solution)/shard_map/begin/pallas_call | solution.py:604
  112.6 0.0 copy-start.12
  112.6 0.0 copy-start.7
  112.6 3.8 pick_units.1
  116.3 92.9 %gather.1 = (bf16[8,192,1536]{2,1,0:T(8,128)(2,1)}, bf16[8,192,1024]{2,1,0:T(8,128)(2,1)}, bf16[8,4,64,1536]{3,2,1,0:T(8,128)(2,1)}, bf16[3,8,192,384]{3,2,1,0:T...) custom-call(bf16[192,1536]{1,0:T(8,128)(2,1)} %get-tuple-element.64.shard_ref, ...), custom_call_target="tpu_custom_call" | custom-call | tf_op jit(solution)/shard_map/gather/pallas_call | solution.py:767
  209.3 0.0 all-gather.2.cloned.1.call-update
  209.3 0.5 reduce-scatter.2.cloned.1.call-start
  209.8 2.4 collective-permute-start.1
  212.2 0.1 collective-permute-start
  212.3 0.0 copy-done.7
  212.3 0.6 reshape.104.gain_ref
  212.9 0.5 broadcast.55
  213.4 1.4 reduce.5
  214.8 0.1 copy.27
  214.9 0.7 multiply_reduce_fusion
  217.0 15.3 %project.1 = (bf16[2048,1536]{1,0:T(8,128)(2,1)}, bf16[2048,384]{1,0:T(8,128)(2,1)}, bf16[2048,384]{1,0:T(8,128)(2,1)}, bf16[2048,384]{1,0:T(8,128)(2,1)}) custom-call(bf16[2048,1536]{1,0:T(8,128)(2,1)} %bitcast.52, bf16[1536,1536]{1,0:T(8,128)(2,1)} %bitcast.54, f32[1,1536]{1,0:T(1,128)} %reshape.104.gain_ref, ...), custom_call_target="tpu_custom_call" | custom-call | flops 7247757312 | bytes 22413312 | tf_op jit(solution)/shard_map/project/pallas_call | solution.py:909
  232.3 0.7 copy.25.gain_ref
  233.0 0.5 and_select_fusion.low_ref
  233.5 41.5 %attend.1 = (bf16[2048,384]{1,0:T(8,128)(2,1)}, f32[3,2,128,2048]{3,2,1,0:T(8,128)}, f32[3,8,1,512]{3,2,1,0:T(1,128)}) custom-call(s32[8]{0:T(128)} %and_select_fusion.low_ref, f32[1]{0:T(128)} %bitcast.5.lam_ref, bf16[2048,384]{1,0:T(8,128)(2,1)} %get-tuple-element.73.q_ref, bf16[2048,384]{1,0:T(8,128)(2,1)} %get-tuple-element.74.k_ref, ...), custom_call_target="tpu_custom_call" | custom-call | flops 12884901888 | bytes 12582912 | tf_op jit(solution)/shard_map/attend/pallas_call | solution.py:978
  275.1 0.0 collective-permute-done.1.dy2_ref
  275.1 0.5 collective-permute-start.2
  275.6 0.6 reshape.100.gain_ref
  276.9 0.1 select_reduce_fusion
  277.1 0.7 dynamic_slice.3.unit_ref
  277.7 0.7 pad_maximum_fusion.scale_ref
  278.4 45.0 %middle.1 = (bf16[2048,1536]{1,0:T(8,128)(2,1)}, f32[8,64,1536]{2,1,0:T(8,128)}) custom-call(bf16[2048,1536]{1,0:T(8,128)(2,1)} %bitcast.53, f32[1,1536]{1,0:T(1,128)} %reshape.100.gain_ref, bf16[2048,384]{1,0:T(8,128)(2,1)} %get-tuple-element.76.a_ref.a_hbm.a_own, bf16[1536,1536]{1,0:T(8,128)(2,1)} %bitcast.55, bf16[3,1536,384]{2,1,0:T(8,128)(2,1)} %bitcast.58, ...), custom_call_target="tpu_custom_call" | custom-call | flops 9663676416 | bytes 26738688 | tf_op jit(solution)/shard_map/middle/pallas_call | solution.py:1182
  323.4 0.0 collective-permute-done.dy1_ref
  323.4 0.0 collective-permute-done.2.dy3_ref
  323.4 0.0 all-gather.2.cloned.1.call-done.w_ref
  323.4 98.0 %feed.1 = (bf16[2048,1024]{1,0:T(8,128)(2,1)}, bf16[2048,1536]{1,0:T(8,128)(2,1)}, f32[8,64,1536]{2,1,0:T(8,128)}, bf16[8,4,64,1536]{3,2,1,0:T(8,128)(2,1)}, f32...) custom-call(bf16[2048,1536]{1,0:T(8,128)(2,1)} %get-tuple-element.78, ...), custom_call_target="tpu_custom_call" | custom-call | flops 38654705664 | bytes 47185920 | tf_op jit(solution)/shard_map/feed/pallas_call | solution.py:1375
  421.4 11.2 %convolution_convert_fusion.1.up = bf16[1536,1024]{1,0:T(8,128)(2,1)} fusion(bf16[2048,1536]{1,0:T(8,128)(2,1)} %get-tuple-element.78.n_ref, bf16[2048,1024]{1,0:T(8,128)(2,1)} %get-tuple-element.88), kind=kOutput, calls=%fused_computation.1 | convolution fusion | flops 6444023808 | bytes 13631488 | tf_op jit(solution)/shard_map/dot_general | solution.py:360
  432.7 0.0 reduce-scatter.2.cloned.1.call-update
  432.7 52.9 %attend_back.1 = (bf16[2048,384]{1,0:T(8,128)(2,1)}, bf16[2048,384]{1,0:T(8,128)(2,1)}, bf16[2048,384]{1,0:T(8,128)(2,1)}, f32[3,128,256]{2,1,0:T(8,128)}, f32[3,1,256]{2,1,0:T(1,128)}) custom-call(s32[8]{0:T(128)} %and_select_fusion.low_ref, f32[1]{0:T(128)} %bitcast.5.lam_ref, bf16[2048,384]{1,0:T(8,128)(2,1)} %get-tuple-element.73.q_ref, ...), custom_call_target="tpu_custom_call" | custom-call | flops 32212254720 | bytes 18874368 | tf_op jit(solution)/shard_map/attend_back/pallas_call | solution.py:1077
  485.6 1.4 reduce_sum.49
  488.4 0.1 multiply_bitcast_fusion.3
  488.5 0.1 reshape.113
  488.6 1.1 reduce_sum.48
  489.7 1.6 constant_dynamic-update-slice_fusion.2
  491.3 0.0 copy-done.5
  491.3 0.3 constant_dynamic-update-slice_fusion.1
  491.6 0.3 constant_dynamic-update-slice_fusion.dqkv
  492.0 2.2 copy-done.6
  494.1 12.1 %convolution_convert_fusion = bf16[2048,1536]{1,0:T(8,128)(2,1)} fusion(bf16[2048,1152]{1,0:T(8,128)(2,1)S(1)} %constant_dynamic-update-slice_fusion.dqkv, bf16[1536,1536]{1,0:T(8,128)(2,1)} %bitcast.57), kind=kOutput, calls=%fused_computation | convolution fusion | flops 7250903040 | bytes 14548992 | tf_op jit(solution)/shard_map/dot_general | solution.py:356
  506.3 1.3 reduce-scatter.2.cloned.1.call-done.down_ref
  507.6 174.1 %collect.1 = (bf16[4,192,1536]{2,1,0:T(8,128)(2,1)}, bf16[4,192,2048]{2,1,0:T(8,128)(2,1)}, bf16[4,192,1024]{2,1,0:T(8,128)(2,1)}, bf16[8,64,1536]{2,1,0:T(8,128...) custom-call(bf16[1536,1024]{1,0:T(8,128)(2,1)} %get-tuple-element.87.gate, ...), custom_call_target="tpu_custom_call" | custom-call | flops 99999997952 | bytes 33554432 | tf_op jit(solution)/shard_map/collect/pallas_call | solution.py:1669
  681.8 0.7 reduce.1
  682.5 0.6 fusion.2.small_ref
  683.1 3.8 place_units.1.g_ref
  686.9 0.0 copy-start.8
  686.9 0.0 copy-start.9
  687.0 234.2 %rotate_slots.1 = (f32[9,192,512]{2,1,0:T(8,128)}, f32[9,192,512]{2,1,0:T(8,128)}, f32[9,192,512]{2,1,0:T(8,128)}, bf16[2,256,1536]{2,1,0:T(8,128)(2,1)}, f32[32,128]{1,0:T(8,128)}) custom-call(bf16[9,192,512]{2,1,0:T(8,128)(2,1)} %place_units.1.g_ref, bf16[9,192,1536]{2,1,0:T(8,128)(2,1)} %get-tuple-element.86.base_ref, ...), custom_call_target="tpu_custom_call" | custom-call | tf_op jit(solution)/shard_map/rotate_slots/pallas_call | solution.py:1958
  921.2 1.5 divide_subtract_fusion
  922.7 1.1 copy.36
  923.9 2.7 copy.37
  926.5 1.8 copy.38
  928.3 1.5 copy-done.1
  929.8 1.8 copy.39
  931.6 1.5 copy-done
  933.1 1.8 copy.40
  (27 shorter events, 0.1 us)
Async XLA Ops:
  7.2 4.1 copy-start.11
  7.2 4.7 copy-start.13
  7.2 316.2 %all-gather.2.cloned.1.call-start = ((), (), s32[]{:S(2)}) async-start(), calls=%async_computation.1 | async-start | bytes 7077888 | tf_op jit(solution)/shard_map/all_gather | solution.py:2032
  112.6 97.3 %copy-start.12 = (bf16[8,64,1536]{2,1,0:T(8,128)(2,1)S(1)}, bf16[8,64,1536]{2,1,0:T(8,128)(2,1)}, u32[]{:S(2)}) copy-start(bf16[8,64,1536]{2,1,0:T(8,128)(2,1)} %get-tuple-element.80.dy0_ref.dyo_ref) | copy-start | bytes 4718596
  112.6 99.7 %copy-start.7 = (f32[3456]{0:T(1024)S(1)}, f32[3456]{0:T(1024)}, u32[]{:S(2)}) copy-start(f32[3456]{0:T(1024)} %param.21) | copy-start | bytes 41476
  209.3 298.3 %reduce-scatter.2.cloned.1.call-start = ((), (), s32[]{:S(2)}) async-start(), calls=%async_computation.2 | async-start | bytes 3538944 | tf_op jit(solution)/shard_map/reduce_scatter | solution.py:2050
  209.8 65.2 %collective-permute-start.1 = (bf16[8,64,1536]{2,1,0:T(8,128)(2,1)S(1)}, bf16[8,64,1536]{2,1,0:T(8,128)(2,1)}, u32[]{:S(2)}, u32[]{:S(2)}) collective-permute-start(bf16[8,64,1536]{2,1,0:T(8,128)(2,1)S(1)} %copy-done.12), channel_id=1, source_target_pairs={{0,16},{8,24},{16,0},{24,8},{1,17},{9,25},{17,1},{25,9},{2,18},{10... | collective-permute-start | bytes 4718600 | tf_op jit(solution)/shard_map/ppermute | solution.py:372
  212.2 111.1 %collective-permute-start = (bf16[8,64,1536]{2,1,0:T(8,128)(2,1)S(1)}, bf16[8,64,1536]{2,1,0:T(8,128)(2,1)}, u32[]{:S(2)}, u32[]{:S(2)}) collective-permute-start(bf16[8,64,1536]{2,1,0:T(8,128)(2,1)S(1)} %copy-done.12), channel_id=1, source_target_pairs={{0,8},{8,0},{16,24},{24,16},{1,9},{9,1},{17,25},{25,17},{2,10},{10... | collective-permute-start | bytes 4718600 | tf_op jit(solution)/shard_map/ppermute | solution.py:368
  275.1 48.3 %collective-permute-start.2 = (bf16[8,64,1536]{2,1,0:T(8,128)(2,1)}, bf16[8,64,1536]{2,1,0:T(8,128)(2,1)}, u32[]{:S(2)}, u32[]{:S(2)}) collective-permute-start(bf16[8,64,1536]{2,1,0:T(8,128)(2,1)} %collective-permute-done.1.dy2_ref), channel_id=1, source_target_pairs={{0,8},{8,0},{16,24},{24,16},{1,9},{9,1},{17,25},{25,17},{2,10},{10... | collective-permute-start | bytes 4718600 | tf_op jit(solution)/shard_map/ppermute | solution.py:368
  432.7 57.0 %copy-start.10 = (f32[1,1536]{1,0:T(1,128)S(1)}, f32[1,1536]{1,0:T(1,128)}, u32[]{:S(2)}) copy-start(f32[1,1536]{1,0:T(1,128)} %get-tuple-element.109) | copy-start | bytes 18436
  485.6 5.7 copy-start.5
  485.6 6.0 copy-start.4
  491.9 2.2 copy-start.6
  686.9 234.3 %copy-start.8 = (f32[3456]{0:T(1024)S(1)}, f32[3456]{0:T(1024)}, u32[]{:S(2)}) copy-start(f32[3456]{0:T(1024)} %param.23) | copy-start | bytes 41476
  686.9 234.3 %copy-start.9 = (f32[3456]{0:T(1024)S(1)}, f32[3456]{0:T(1024)}, u32[]{:S(2)}) copy-start(f32[3456]{0:T(1024)} %param.22) | copy-start | bytes 41476
  687.0 235.8 %copy-start.3 = (bf16[2,256,1536]{2,1,0:T(8,128)(2,1)S(1)}, bf16[2,256,1536]{2,1,0:T(8,128)(2,1)}, u32[]{:S(2)}) copy-start(bf16[2,256,1536]{2,1,0:T(8,128)(2,1)} %get-tuple-element.138) | copy-start | bytes 4718596
  921.2 5.3 copy-start.2
  926.5 3.3 copy-start.1
  929.8 3.3 copy-start
Sparse Core Ops, SparseCore 0:
  209.4 97.8 all-gather.1
  432.8 74.7 reduce-scatter.1

commit v6 on v5

--- a/solution.py
+++ b/solution.py
@@ -677,28 +677,29 @@
         pltpu.make_async_copy(down_ref, downs_ref.at[blk], s_local.at[2]),
     ]
 
-    def tables():
-        lens = [lens_ref[blk // 2, blk % 2, j] for j in range(NDOC)]
-        ends = [lens[0]]
-        for j in range(1, NDOC):
-            ends.append(ends[-1] + lens[j])
-
-        def first_of(places):
-            first = jnp.zeros_like(places)
-            for j in range(NDOC):
-                first += jnp.where(places >= ends[j], lens[j], 0)
-            return first
-
+    lens = [lens_ref[blk // 2, blk % 2, j] for j in range(NDOC)]
+    ends = [lens[0]]
+    for j in range(1, NDOC):
+        ends.append(ends[-1] + lens[j])
+
+    def first_of(places):
+        first = jnp.zeros_like(places)
+        for j in range(NDOC):
+            first += jnp.where(places >= ends[j], lens[j], 0)
+        return first
+
+    def starts():
         places = lax.broadcasted_iota(jnp.int32, start_ref.shape, 1)
         start_ref[...] = jnp.where(places >= ends[NDOC - 2], places, first_of(places))
+
+    def table(b):
         lane = lax.broadcasted_iota(jnp.int32, (TILE, VD), 1)
-        for b in range(cos_ref.shape[0] // TILE):
-            places = b * TILE + lax.broadcasted_iota(jnp.int32, (TILE, VD), 0)
-            angle = (places - first_of(places)).astype(F32) * rate_ref[...]
-            sine = jnp.sin(angle)
-            at = slice(b * TILE, (b + 1) * TILE)
-            cos_ref[at, :] = jnp.cos(angle)
-            sin_ref[at, :] = jnp.where(lane % HD < HD // 2, -sine, sine)
+        places = b * TILE + lax.broadcasted_iota(jnp.int32, (TILE, VD), 0)
+        angle = (places - first_of(places)).astype(F32) * rate_ref[...]
+        sine = jnp.sin(angle)
+        at = slice(b * TILE, (b + 1) * TILE)
+        cos_ref[at, :] = jnp.cos(angle)
+        sin_ref[at, :] = jnp.where(lane % HD < HD // 2, -sine, sine)
 
     greet((to_core, to_y, after_me, before_me))
     for part in range(2):
@@ -715,12 +716,13 @@
         copies[1]().wait_recv()
         copies[2]().start()
 
-    tables()
+    starts()
     for t in range(1, 7):
         for part in range(2):
             for up in (True, False):
                 ring(t - 1, up, part).wait_recv()
                 ring(t, up, part).start()
+        table(t - 1)
     for part in range(2):
         for up in (True, False):
             ring(0, up, part, True).start()
@@ -735,6 +737,8 @@
                 ring(t, up, part, True).start()
         if t in (3, 4):
             relay(t - 3)
+        if t in (1, 2):
+            table(t + 5)
     for part in range(2):
         for up in (True, False):
             ring(6, up, part, True).wait_recv()
@@ -926,11 +930,18 @@
     return jnp.concatenate([jnp.where(lane < HD, q, zero), jnp.where(lane >= HD, q, zero)], axis=0)
 
 
-def block_mask(j, i, start):
-    key = j * TILE + lax.broadcasted_iota(jnp.int32, (TILE, 2 * TILE), 0)
-    query = i * TILE + lax.broadcasted_iota(jnp.int32, (TILE, TILE), 1)
+def block_mask(j, n, i, start):
+    key = j * TILE + lax.broadcasted_iota(jnp.int32, (n * TILE, 2 * TILE), 0)
+    query = i * TILE + lax.broadcasted_iota(jnp.int32, (n * TILE, TILE), 1)
     query = jnp.concatenate([query, query], axis=1)
     return (key >= start) & (key <= query)
+
+
+def over_blocks(low, high, step, carry):
+    odd = (high - low) % 2
+    carry = lax.fori_loop(low, low + odd, lambda j, c: step(j, 1, c), carry)
+    pairs = (high - low) // 2
+    return lax.fori_loop(0, pairs, lambda p, c: step(low + odd + 2 * p, 2, c), carry)
 
 
 def attend_kernel(low_ref, lam_ref, q_ref, k_ref, v_ref, start_ref, gain_ref, a_ref, maps_ref, log_ref, vt_ref):
@@ -944,15 +955,18 @@
     q = split_halves(q_ref[...])
     start = jnp.concatenate([start_ref[...], start_ref[...]], axis=1)
 
-    def step(j, carry):
+    def step(j, n, carry):
         top, mass, total = carry
-        keys = k_ref[pl.ds(pl.multiple_of(j * TILE, TILE), TILE), :]
-        scores = jnp.where(block_mask(j, i, start), dot_last(keys, q), masked_fill)
+        keys = k_ref[pl.ds(pl.multiple_of(j * TILE, TILE), n * TILE), :]
+        scores = jnp.where(block_mask(j, n, i, start), dot_last(keys, q), masked_fill)
         new = jnp.maximum(top, jnp.max(scores, axis=0, keepdims=True))
         shares = jnp.exp(scores - new)
         keep = jnp.exp(top - new)
         mass = mass * keep + jnp.sum(shares, axis=0, keepdims=True)
-        total = total * keep + dot_plain(vt_ref[j], shares.astype(BF))
+        low_shares = shares.astype(BF)
+        total = total * keep
+        for b in range(n):
+            total += dot_plain(vt_ref[j + b], low_shares[b * TILE : (b + 1) * TILE])
         return new, mass, total
 
     first = (
@@ -960,7 +974,7 @@
         jnp.zeros((1, 2 * TILE), F32),
         jnp.zeros((VD, 2 * TILE), F32),
     )
-    top, mass, total = lax.fori_loop(low_ref[i], i + 1, step, first)
+    top, mass, total = over_blocks(low_ref[i], i + 1, step, first)
     maps = total / mass
     one, two = maps[:, :TILE], maps[:, TILE:]
     maps_ref[0, 0] = one
@@ -1040,19 +1054,22 @@
     offset = jnp.sum(dmaps.astype(F32) * maps, axis=0, keepdims=True)
     dq_sum[...] = jnp.zeros_like(dq_sum)
 
-    def step(j, carry):
-        at = pl.ds(pl.multiple_of(j * TILE, TILE), TILE)
+    def step(j, n, carry):
+        at = pl.ds(pl.multiple_of(j * TILE, TILE), n * TILE)
         keys, values = k_ref[at, :], v_ref[at, :]
         scores = dot_last(keys, q)
-        shares = jnp.where(block_mask(j, i, start), jnp.exp(scores - log_mass), 0.0)
+        shares = jnp.where(block_mask(j, n, i, start), jnp.exp(scores - log_mass), 0.0)
         dshares = dot_plain(values, dmaps)
         dscores = (shares * (dshares - offset)).astype(BF)
         dv_sum[at, :] += dot_last(shares.astype(BF), dmaps)
         dk_sum[at, :] += dot_plain(dscores, q)
-        dq_sum[...] += dot_plain(kt_ref[j], dscores)
+        dq = dot_plain(kt_ref[j], dscores[:TILE])
+        for b in range(1, n):
+            dq += dot_plain(kt_ref[j + b], dscores[b * TILE : (b + 1) * TILE])
+        dq_sum[...] += dq
         return carry
 
-    lax.fori_loop(low_ref[i], i + 1, step, 0)
+    over_blocks(low_ref[i], i + 1, step, 0)
     lane = lax.broadcasted_iota(jnp.int32, (TILE, VD), 1)
     dq = jnp.concatenate([dq_sum[:HD, :TILE], dq_sum[HD:, TILE:]], axis=0).T * HD**-0.5
     dq_ref[...] = turn(dq, cosq_ref[...], -sinq_ref[...], lane).astype(BF)
@@ -1770,10 +1787,10 @@
             loading(i, s).start()
     rows_start, rows_finish = return_rows_copies(rows_ref, rows_out_ref, s_rows, lax.axis_index("batch"), blk)
     greet_all()
+    rows_start()
     for s in range(count):
         loading(0, s).wait()
         send_g(s).start()
-    rows_start()
     me = lax.axis_index("batch")
     group_small[me] = small_ref[...]
 
@@ -2048,12 +2065,11 @@
     )
 
     down_sums = lax.psum_scatter(down_grad, "blk", scatter_dimension=0, tiled=True)
-    up_grad = dot_first(n2, dup).astype(BF)
     dx1_low = dx1_low.reshape(count, D)
-    da = after(da, up_grad)
     dq, dk, dv, head_gain_sums, mixer_sums = attend_back(
         low, lam, q, k, v, start, head_gain, maps, log_mass, da, cosine, sine
     )
+    up_grad = dot_first(n2, after(dup, dq)).astype(BF)
     dqkv = jnp.concatenate([dq, dk, dv], axis=1)
     dn1_part = dot_last(dqkv, attn[:, : 3 * QW]).astype(BF)
     groups = (8, 2, 2, count // 32, D)

time: 949 us -> 946 us (level)
  transfers between devices with their start and end apart: 5 -> 5, of which waited for: 1 -> 0; matrix products, arithmetic and copies ran while one was open for 3% -> 4% of each run, Pallas kernels for 16% -> 15%
where the time goes in v6:
time: 946 us; the launch traced here: 940 us
  Pallas kernels  863 us (91%)
  matrix products  22.4 us (2%)
  local copies, waits for them, and re-layouts  20.4 us (2%)
  between operations  18.3 us (2%)
  other arithmetic  12.7 us (1%)
    pallas_call x1, Pallas kernels, rotate_slots(): pl.pallas_call(rotate_kernel, in_specs=[hbm] * 8 + [pl.BlockSpec(memory_s...  241 us
    pallas_call x1, Pallas kernels, collect(): pl.pallas_call(collect_kernel, in_specs=[vmem] * 4 + [hbm] * 5 + [vmem] *...  178 us
    pallas_call x1, Pallas kernels, begin(): pl.pallas_call(begin_kernel, in_specs=[hbm] * 4 + [pl.BlockSpec(memory_sp...  100 us
    pallas_call x1, Pallas kernels, feed(): pl.pallas_call(feed_kernel, grid=(blocks + 4,), in_specs=[rows(D, 0), pl....  99.1 us
    pallas_call x1, Pallas kernels, gather(): pl.pallas_call(gather_kernel, in_specs=[vmem] * 4 + [pl.BlockSpec(memory_...  92.9 us
    pallas_call x1, Pallas kernels, attend_back(): pl.pallas_call(attend_back_kernel, grid=(HEADS, blocks), in_specs=[smem,...  49.3 us
    pallas_call x1, Pallas kernels, middle(): pl.pallas_call(middle_kernel, grid=(blocks + 1,), in_specs=[pl.BlockSpec(...  45.1 us
    pallas_call x1, Pallas kernels, attend(): pl.pallas_call(attend_kernel, grid=(HEADS, blocks), in_specs=[smem, smem,...  33.8 us
  transfers between devices with their start and end apart: 5, of which 0 were waited for; matrix products, arithmetic and copies ran while one was open for 4% of the time, Pallas kernels for 15%

profile of v6, /device:TPU:12, one launch (start us, length us, event | category | flops | bytes accessed | tf_op | source)
XLA Modules:
  0.0 940.1 jit_solution(14976111785175208442)
XLA Ops:
  7.2 0.0 all-gather.2.cloned.1.call-start
  7.3 3.4 bitcast_convert_fusion.master_ref.own
  10.7 0.6 reshape_tile.3.rate_ref
  11.3 0.6 pad.20.lengths_ref
  11.9 0.5 fusion.3.place_ref
  12.4 100.1 %begin.1 = (bf16[3,9,192,512]{3,2,1,0:T(8,128)(2,1)}, bf16[8,64,1536]{2,1,0:T(8,128)(2,1)}, bf16[8,64,1536]{2,1,0:T(8,128)(2,1)}, bf16[9,192,1536]{2,1,0:T(8,128...) custom-call(bf16[9,192,512]{2,1,0:T(8,128)(2,1)} %bitcast_convert_fusion.master_ref.own, ...), custom_call_target="tpu_custom_call" | custom-call | tf_op jit(solution)/shard_map/begin/pallas_call | solution.py:604
  112.6 0.0 copy-start.7
  112.6 3.8 pick_units.1
  116.3 92.9 %gather.1 = (bf16[8,192,1536]{2,1,0:T(8,128)(2,1)}, bf16[8,192,1024]{2,1,0:T(8,128)(2,1)}, bf16[8,4,64,1536]{3,2,1,0:T(8,128)(2,1)}, bf16[3,8,192,384]{3,2,1,0:T...) custom-call(bf16[192,1536]{1,0:T(8,128)(2,1)} %get-tuple-element.64.shard_ref, ...), custom_call_target="tpu_custom_call" | custom-call | tf_op jit(solution)/shard_map/gather/pallas_call | solution.py:771
  209.3 0.0 all-gather.2.cloned.1.call-update
  209.3 0.5 reduce-scatter.2.cloned.1.call-start
  209.8 0.0 copy-done.12
  209.8 2.4 collective-permute-start.1
  212.2 0.1 collective-permute-start
  212.3 0.6 reshape.104.gain_ref
  212.9 0.5 broadcast.55
  213.4 1.4 reduce.5
  214.8 0.1 copy.27
  214.9 0.7 multiply_reduce_fusion
  217.0 15.3 %project.1 = (bf16[2048,1536]{1,0:T(8,128)(2,1)}, bf16[2048,384]{1,0:T(8,128)(2,1)}, bf16[2048,384]{1,0:T(8,128)(2,1)}, bf16[2048,384]{1,0:T(8,128)(2,1)}) custom-call(bf16[2048,1536]{1,0:T(8,128)(2,1)} %bitcast.52, bf16[1536,1536]{1,0:T(8,128)(2,1)} %bitcast.54, f32[1,1536]{1,0:T(1,128)} %reshape.104.gain_ref, ...), custom_call_target="tpu_custom_call" | custom-call | flops 7247757312 | bytes 22413312 | tf_op jit(solution)/shard_map/project/pallas_call | solution.py:913
  232.3 0.7 copy.25.gain_ref
  233.0 0.5 and_select_fusion.low_ref
  233.5 33.8 %attend.1 = (bf16[2048,384]{1,0:T(8,128)(2,1)}, f32[3,2,128,2048]{3,2,1,0:T(8,128)}, f32[3,8,1,512]{3,2,1,0:T(1,128)}) custom-call(s32[8]{0:T(128)} %and_select_fusion.low_ref, f32[1]{0:T(128)} %bitcast.5.lam_ref, bf16[2048,384]{1,0:T(8,128)(2,1)} %get-tuple-element.73.q_ref, bf16[2048,384]{1,0:T(8,128)(2,1)} %get-tuple-element.74.k_ref, ...), custom_call_target="tpu_custom_call" | custom-call | flops 12884901888 | bytes 12582912 | tf_op jit(solution)/shard_map/attend/pallas_call | solution.py:992
  267.3 0.0 collective-permute-done.1.dy2_ref
  267.4 0.5 collective-permute-start.2
  267.9 0.6 reshape.100.gain_ref
  269.2 0.1 select_reduce_fusion
  269.3 0.7 dynamic_slice.3.unit_ref
  270.0 0.6 pad_maximum_fusion.scale_ref
  270.6 45.1 %middle.1 = (bf16[2048,1536]{1,0:T(8,128)(2,1)}, f32[8,64,1536]{2,1,0:T(8,128)}) custom-call(bf16[2048,1536]{1,0:T(8,128)(2,1)} %bitcast.53, f32[1,1536]{1,0:T(1,128)} %reshape.100.gain_ref, bf16[2048,384]{1,0:T(8,128)(2,1)} %get-tuple-element.76.a_ref.a_hbm.a_own, bf16[1536,1536]{1,0:T(8,128)(2,1)} %bitcast.55, bf16[3,1536,384]{2,1,0:T(8,128)(2,1)} %bitcast.60, ...), custom_call_target="tpu_custom_call" | custom-call | flops 9663676416 | bytes 26738688 | tf_op jit(solution)/shard_map/middle/pallas_call | solution.py:1199
  315.7 0.0 collective-permute-done.dy1_ref
  315.7 0.0 collective-permute-done.2.dy3_ref
  315.7 0.0 all-gather.2.cloned.1.call-done.w_ref
  315.7 99.1 %feed.1 = (bf16[2048,1024]{1,0:T(8,128)(2,1)}, bf16[2048,1536]{1,0:T(8,128)(2,1)}, f32[8,64,1536]{2,1,0:T(8,128)}, bf16[8,4,64,1536]{3,2,1,0:T(8,128)(2,1)}, f32...) custom-call(bf16[2048,1536]{1,0:T(8,128)(2,1)} %get-tuple-element.78, ...), custom_call_target="tpu_custom_call" | custom-call | flops 38654705664 | bytes 47185920 | tf_op jit(solution)/shard_map/feed/pallas_call | solution.py:1392
  414.8 0.0 reduce-scatter.2.cloned.1.call-update
  414.8 49.3 %attend_back.1 = (bf16[2048,384]{1,0:T(8,128)(2,1)}, bf16[2048,384]{1,0:T(8,128)(2,1)}, bf16[2048,384]{1,0:T(8,128)(2,1)}, f32[3,128,256]{2,1,0:T(8,128)}, f32[3,1,256]{2,1,0:T(1,128)}) custom-call(s32[8]{0:T(128)} %and_select_fusion.low_ref, f32[1]{0:T(128)} %bitcast.5.lam_ref, bf16[2048,384]{1,0:T(8,128)(2,1)} %get-tuple-element.73.q_ref, ...), custom_call_target="tpu_custom_call" | custom-call | flops 32212254720 | bytes 18874368 | tf_op jit(solution)/shard_map/attend_back/pallas_call | solution.py:1094
  464.1 1.4 reduce_sum.49
  466.8 0.1 multiply_bitcast_fusion.3
  466.9 0.1 reshape.113
  467.0 1.1 reduce_sum.48
  468.2 1.6 constant_dynamic-update-slice_fusion.2
  469.7 0.0 copy-start.14
  469.7 0.0 copy-done.5
  469.8 0.0 slice-start
  469.8 0.3 constant_dynamic-update-slice_fusion.1
  470.1 0.3 constant_dynamic-update-slice_fusion.dqkv
  470.4 1.5 copy-done.14
  471.9 12.0 %convolution_convert_fusion.1.up = bf16[1536,1024]{1,0:T(8,128)(2,1)} fusion(bf16[2048,1536]{1,0:T(8,128)(2,1)} %get-tuple-element.78.n_ref, bf16[2048,1024]{1,0:T(8,128)(2,1)S(1)} %copy-done.14), kind=kOutput, calls=%fused_computation.1 | convolution fusion | flops 6444023808 | bytes 13631488 | tf_op jit(solution)/shard_map/dot_general | solution.py:360
  483.9 10.4 %convolution_convert_fusion = bf16[2048,1536]{1,0:T(8,128)(2,1)} fusion(bf16[2048,1152]{1,0:T(8,128)(2,1)S(1)} %constant_dynamic-update-slice_fusion.dqkv, bf16[1536,1536]{1,0:T(8,128)(2,1)S(1)} %bitcast.59), kind=kOutput, calls=%fused_computation | convolution fusion | flops 7250903040 | bytes 14548992 | tf_op jit(solution)/shard_map/dot_general | solution.py:356
  494.4 178.4 %collect.1 = (bf16[4,192,1536]{2,1,0:T(8,128)(2,1)}, bf16[4,192,2048]{2,1,0:T(8,128)(2,1)}, bf16[4,192,1024]{2,1,0:T(8,128)(2,1)}, bf16[8,64,1536]{2,1,0:T(8,128...) custom-call(bf16[1536,1024]{1,0:T(8,128)(2,1)} %get-tuple-element.87.gate, ...), custom_call_target="tpu_custom_call" | custom-call | flops 99999997952 | bytes 33554432 | tf_op jit(solution)/shard_map/collect/pallas_call | solution.py:1686
  672.7 0.7 reduce.1
  673.5 0.6 fusion.2.small_ref
  674.1 3.8 place_units.1.g_ref
  677.9 0.0 copy-start.8
  677.9 0.0 copy-start.9
  678.0 241.2 %rotate_slots.1 = (f32[9,192,512]{2,1,0:T(8,128)}, f32[9,192,512]{2,1,0:T(8,128)}, f32[9,192,512]{2,1,0:T(8,128)}, bf16[2,256,1536]{2,1,0:T(8,128)(2,1)}, f32[32,128]{1,0:T(8,128)}) custom-call(bf16[9,192,512]{2,1,0:T(8,128)(2,1)} %place_units.1.g_ref, bf16[9,192,1536]{2,1,0:T(8,128)(2,1)} %get-tuple-element.86.base_ref, ...), custom_call_target="tpu_custom_call" | custom-call | tf_op jit(solution)/shard_map/rotate_slots/pallas_call | solution.py:1975
  919.2 1.5 divide_subtract_fusion
  920.7 1.1 copy.36
  921.9 2.7 copy.37
  924.5 1.8 copy.38
  926.3 1.5 copy-done.1
  927.8 1.8 copy.39
  929.6 1.5 copy-done
  931.1 1.8 copy.40
  (34 shorter events, 0.1 us)
Async XLA Ops:
  7.2 4.1 copy-start.11
  7.2 4.7 copy-start.13
  7.2 308.5 %all-gather.2.cloned.1.call-start = ((), (), s32[]{:S(2)}) async-start(), calls=%async_computation.1 | async-start | bytes 7077888 | tf_op jit(solution)/shard_map/all_gather | solution.py:2049
  112.6 97.3 %copy-start.12 = (bf16[8,64,1536]{2,1,0:T(8,128)(2,1)S(1)}, bf16[8,64,1536]{2,1,0:T(8,128)(2,1)}, u32[]{:S(2)}) copy-start(bf16[8,64,1536]{2,1,0:T(8,128)(2,1)} %get-tuple-element.80.dy0_ref.dyo_ref) | copy-start | bytes 4718596
  112.6 99.7 %copy-start.7 = (f32[3456]{0:T(1024)S(1)}, f32[3456]{0:T(1024)}, u32[]{:S(2)}) copy-start(f32[3456]{0:T(1024)} %param.21) | copy-start | bytes 41476
  209.3 285.0 %reduce-scatter.2.cloned.1.call-start = ((), (), s32[]{:S(2)}) async-start(), calls=%async_computation.2 | async-start | bytes 3538944 | tf_op jit(solution)/shard_map/reduce_scatter | solution.py:2067
  209.8 57.5 %collective-permute-start.1 = (bf16[8,64,1536]{2,1,0:T(8,128)(2,1)S(1)}, bf16[8,64,1536]{2,1,0:T(8,128)(2,1)}, u32[]{:S(2)}, u32[]{:S(2)}) collective-permute-start(bf16[8,64,1536]{2,1,0:T(8,128)(2,1)S(1)} %copy-done.12), channel_id=1, source_target_pairs={{0,16},{8,24},{16,0},{24,8},{1,17},{9,25},{17,1},{25,9},{2,18},{10... | collective-permute-start | bytes 4718600 | tf_op jit(solution)/shard_map/ppermute | solution.py:372
  212.2 103.4 %collective-permute-start = (bf16[8,64,1536]{2,1,0:T(8,128)(2,1)S(1)}, bf16[8,64,1536]{2,1,0:T(8,128)(2,1)}, u32[]{:S(2)}, u32[]{:S(2)}) collective-permute-start(bf16[8,64,1536]{2,1,0:T(8,128)(2,1)S(1)} %copy-done.12), channel_id=1, source_target_pairs={{0,8},{8,0},{16,24},{24,16},{1,9},{9,1},{17,25},{25,17},{2,10},{10... | collective-permute-start | bytes 4718600 | tf_op jit(solution)/shard_map/ppermute | solution.py:368
  267.4 48.3 %collective-permute-start.2 = (bf16[8,64,1536]{2,1,0:T(8,128)(2,1)}, bf16[8,64,1536]{2,1,0:T(8,128)(2,1)}, u32[]{:S(2)}, u32[]{:S(2)}) collective-permute-start(bf16[8,64,1536]{2,1,0:T(8,128)(2,1)} %collective-permute-done.1.dy2_ref), channel_id=1, source_target_pairs={{0,8},{8,0},{16,24},{24,16},{1,9},{9,1},{17,25},{25,17},{2,10},{10... | collective-permute-start | bytes 4718600 | tf_op jit(solution)/shard_map/ppermute | solution.py:368
  414.8 53.3 %copy-start.10 = (f32[1,1536]{1,0:T(1,128)S(1)}, f32[1,1536]{1,0:T(1,128)}, u32[]{:S(2)}) copy-start(f32[1,1536]{1,0:T(1,128)} %get-tuple-element.109) | copy-start | bytes 18436
  464.1 5.7 copy-start.5
  464.1 6.0 copy-start.4
  469.7 2.2 copy-start.14
  469.8 14.2 %slice-start = ((s8[4718592]{0:T(1024)(128)(4,1)}), s8[4194304]{0:T(1024)(128)(4,1)S(1)}, s32[]{:S(2)}) async-start(s8[4718592]{0:T(1024)(128)(4,1)} %bitcast.57), calls=%async_computation.3 | async-start | bytes 8388608
  471.9 12.0 %copy-start.6 = (bf16[2048,1152]{1,0:T(8,128)(2,1)}, bf16[2048,1152]{1,0:T(8,128)(2,1)S(1)}, u32[]{:S(2)}) copy-start(bf16[2048,1152]{1,0:T(8,128)(2,1)S(1)} %constant_dynamic-update-slice_fusion.dqkv) | copy-start | bytes 14155780
  471.9 12.0 %slice-start.1 = ((s8[4718592]{0:T(1024)(128)(4,1)}), s8[524288]{0:T(1024)(128)(4,1)S(1)}, s32[]{:S(2)}) async-start(s8[4718592]{0:T(1024)(128)(4,1)} %bitcast.57), calls=%async_computation.4 | async-start | bytes 1048576
  677.9 241.3 %copy-start.8 = (f32[3456]{0:T(1024)S(1)}, f32[3456]{0:T(1024)}, u32[]{:S(2)}) copy-start(f32[3456]{0:T(1024)} %param.23) | copy-start | bytes 41476
  677.9 241.3 %copy-start.9 = (f32[3456]{0:T(1024)S(1)}, f32[3456]{0:T(1024)}, u32[]{:S(2)}) copy-start(f32[3456]{0:T(1024)} %param.22) | copy-start | bytes 41476
  677.9 242.8 %copy-start.3 = (bf16[2,256,1536]{2,1,0:T(8,128)(2,1)S(1)}, bf16[2,256,1536]{2,1,0:T(8,128)(2,1)}, u32[]{:S(2)}) copy-start(bf16[2,256,1536]{2,1,0:T(8,128)(2,1)} %get-tuple-element.138) | copy-start | bytes 4718596
  919.2 5.3 copy-start.2
  924.5 3.3 copy-start.1
  927.8 3.3 copy-start
Sparse Core Ops, SparseCore 0:
  209.4 97.8 all-gather.1
  414.9 74.5 reduce-scatter.1

commit v7 on v6

--- a/solution.py
+++ b/solution.py
@@ -344,7 +344,7 @@
 HEADS = 3
 QW = HEADS * VD
 FQ = FF // 4
-EARLY = 2
+EARLY = 3
 VMEM_LIMIT = 56 * 2**20
 
 
@@ -538,14 +538,16 @@
 
     def cast(n):
         load(n).wait()
-        if n >= 2:
+        if n - 2 >= EARLY:
             store(n - 2).wait()
-            if n - 2 < EARLY:
-                share(n - 2).start()
         narrow[n % 2] = wide[n % 2].astype(BF)
         store(n).start()
         if n + 2 < slots:
             load(n + 2).start()
+
+    def share_now(n):
+        store(n).wait()
+        share(n).start()
 
     def copies(c):
         at = pl.ds(3 * c, 3)
@@ -571,9 +573,13 @@
     dy_group()
     for c in range(3):
         copies(c)[0]().start()
+    share_now(0)
+    share_now(1)
+    cast(2)
+    share_now(2)
     for n in (1, 2, 3):
         x_blk(n)
-    for n in range(2, slots):
+    for n in range(3, slots):
         cast(n)
     store(slots - 2).wait()
     store(slots - 1).wait()

time: 946 us -> 938 us (level)
  Pallas kernels: 863 us -> 850 us
where the time goes in v7:
time: 938 us; the launch traced here: 929 us
  Pallas kernels  850 us (91%)
  matrix products  22.5 us (2%)
  local copies, waits for them, and re-layouts  20.4 us (2%)
  between operations  18.2 us (2%)
  other arithmetic  12.7 us (1%)
    pallas_call x1, Pallas kernels, rotate_slots(): pl.pallas_call(rotate_kernel, in_specs=[hbm] * 8 + [pl.BlockSpec(memory_s...  240 us
    pallas_call x1, Pallas kernels, collect(): pl.pallas_call(collect_kernel, in_specs=[vmem] * 4 + [hbm] * 5 + [vmem] *...  175 us
    pallas_call x1, Pallas kernels, begin(): pl.pallas_call(begin_kernel, in_specs=[hbm] * 4 + [pl.BlockSpec(memory_sp...  100 us
    pallas_call x1, Pallas kernels, feed(): pl.pallas_call(feed_kernel, grid=(blocks + 4,), in_specs=[rows(D, 0), pl....  93.4 us
    pallas_call x1, Pallas kernels, gather(): pl.pallas_call(gather_kernel, in_specs=[vmem] * 4 + [pl.BlockSpec(memory_...  91.4 us
    pallas_call x1, Pallas kernels, attend_back(): pl.pallas_call(attend_back_kernel, grid=(HEADS, blocks), in_specs=[smem,...  48.2 us
    pallas_call x1, Pallas kernels, middle(): pl.pallas_call(middle_kernel, grid=(blocks + 1,), in_specs=[pl.BlockSpec(...  45.1 us
    pallas_call x1, Pallas kernels, attend(): pl.pallas_call(attend_kernel, grid=(HEADS, blocks), in_specs=[smem, smem,...  33.6 us
  transfers between devices with their start and end apart: 5, of which 0 were waited for; matrix products, arithmetic and copies ran while one was open for 4% of the time, Pallas kernels for 15%

profile of v7, /device:TPU:12, one launch (start us, length us, event | category | flops | bytes accessed | tf_op | source)
XLA Modules:
  0.0 929.4 jit_solution(8261484011963005552)
XLA Ops:
  7.2 0.0 all-gather.2.cloned.1.call-start
  7.3 3.4 bitcast_convert_fusion.master_ref.own
  10.7 0.6 reshape_tile.3.rate_ref
  11.3 0.6 pad.20.lengths_ref
  11.9 0.5 fusion.3.place_ref
  12.4 100.3 %begin.1 = (bf16[3,9,192,512]{3,2,1,0:T(8,128)(2,1)}, bf16[8,64,1536]{2,1,0:T(8,128)(2,1)}, bf16[8,64,1536]{2,1,0:T(8,128)(2,1)}, bf16[9,192,1536]{2,1,0:T(8,128...) custom-call(bf16[9,192,512]{2,1,0:T(8,128)(2,1)} %bitcast_convert_fusion.master_ref.own, ...), custom_call_target="tpu_custom_call" | custom-call | tf_op jit(solution)/shard_map/begin/pallas_call | solution.py:610
  112.7 0.0 copy-start.7
  112.7 3.8 pick_units.1
  116.5 91.4 %gather.1 = (bf16[8,192,1536]{2,1,0:T(8,128)(2,1)}, bf16[8,192,1024]{2,1,0:T(8,128)(2,1)}, bf16[8,4,64,1536]{3,2,1,0:T(8,128)(2,1)}, bf16[3,8,192,384]{3,2,1,0:T...) custom-call(bf16[192,1536]{1,0:T(8,128)(2,1)} %get-tuple-element.64.shard_ref, ...), custom_call_target="tpu_custom_call" | custom-call | tf_op jit(solution)/shard_map/gather/pallas_call | solution.py:777
  207.9 0.0 all-gather.2.cloned.1.call-update
  207.9 0.5 reduce-scatter.2.cloned.1.call-start
  208.5 4.0 collective-permute-start.1
  212.4 0.1 collective-permute-start
  212.5 0.0 copy-done.7
  212.5 0.6 reshape.104.gain_ref
  213.1 0.5 broadcast.55
  213.6 1.4 reduce.5
  215.0 0.1 copy.27
  215.1 0.7 multiply_reduce_fusion
  217.2 15.4 %project.1 = (bf16[2048,1536]{1,0:T(8,128)(2,1)}, bf16[2048,384]{1,0:T(8,128)(2,1)}, bf16[2048,384]{1,0:T(8,128)(2,1)}, bf16[2048,384]{1,0:T(8,128)(2,1)}) custom-call(bf16[2048,1536]{1,0:T(8,128)(2,1)} %bitcast.52, bf16[1536,1536]{1,0:T(8,128)(2,1)} %bitcast.54, f32[1,1536]{1,0:T(1,128)} %reshape.104.gain_ref, ...), custom_call_target="tpu_custom_call" | custom-call | flops 7247757312 | bytes 22413312 | tf_op jit(solution)/shard_map/project/pallas_call | solution.py:919
  232.5 0.7 copy.25.gain_ref
  233.3 0.5 and_select_fusion.low_ref
  233.8 33.6 %attend.1 = (bf16[2048,384]{1,0:T(8,128)(2,1)}, f32[3,2,128,2048]{3,2,1,0:T(8,128)}, f32[3,8,1,512]{3,2,1,0:T(1,128)}) custom-call(s32[8]{0:T(128)} %and_select_fusion.low_ref, f32[1]{0:T(128)} %bitcast.5.lam_ref, bf16[2048,384]{1,0:T(8,128)(2,1)} %get-tuple-element.73.q_ref, bf16[2048,384]{1,0:T(8,128)(2,1)} %get-tuple-element.74.k_ref, ...), custom_call_target="tpu_custom_call" | custom-call | flops 12884901888 | bytes 12582912 | tf_op jit(solution)/shard_map/attend/pallas_call | solution.py:998
  267.4 0.0 collective-permute-done.1.dy2_ref
  267.4 0.5 collective-permute-start.2
  267.9 0.6 reshape.100.gain_ref
  269.2 0.1 select_reduce_fusion
  269.3 0.7 dynamic_slice.3.unit_ref
  270.0 0.6 pad_maximum_fusion.scale_ref
  270.6 45.1 %middle.1 = (bf16[2048,1536]{1,0:T(8,128)(2,1)}, f32[8,64,1536]{2,1,0:T(8,128)}) custom-call(bf16[2048,1536]{1,0:T(8,128)(2,1)} %bitcast.53, f32[1,1536]{1,0:T(1,128)} %reshape.100.gain_ref, bf16[2048,384]{1,0:T(8,128)(2,1)} %get-tuple-element.76.a_ref.a_hbm.a_own, bf16[1536,1536]{1,0:T(8,128)(2,1)} %bitcast.55, bf16[3,1536,384]{2,1,0:T(8,128)(2,1)} %bitcast.60, ...), custom_call_target="tpu_custom_call" | custom-call | flops 9663676416 | bytes 26738688 | tf_op jit(solution)/shard_map/middle/pallas_call | solution.py:1205
  315.7 0.0 collective-permute-done.dy1_ref
  315.7 0.0 collective-permute-done.2.dy3_ref
  315.7 0.0 all-gather.2.cloned.1.call-done.w_ref
  315.7 93.4 %feed.1 = (bf16[2048,1024]{1,0:T(8,128)(2,1)}, bf16[2048,1536]{1,0:T(8,128)(2,1)}, f32[8,64,1536]{2,1,0:T(8,128)}, bf16[8,4,64,1536]{3,2,1,0:T(8,128)(2,1)}, f32...) custom-call(bf16[2048,1536]{1,0:T(8,128)(2,1)} %get-tuple-element.78, ...), custom_call_target="tpu_custom_call" | custom-call | flops 38654705664 | bytes 47185920 | tf_op jit(solution)/shard_map/feed/pallas_call | solution.py:1398
  409.1 0.0 reduce-scatter.2.cloned.1.call-update
  409.2 0.0 copy-start.10
  409.2 48.2 %attend_back.1 = (bf16[2048,384]{1,0:T(8,128)(2,1)}, bf16[2048,384]{1,0:T(8,128)(2,1)}, bf16[2048,384]{1,0:T(8,128)(2,1)}, f32[3,128,256]{2,1,0:T(8,128)}, f32[3,1,256]{2,1,0:T(1,128)}) custom-call(s32[8]{0:T(128)} %and_select_fusion.low_ref, f32[1]{0:T(128)} %bitcast.5.lam_ref, bf16[2048,384]{1,0:T(8,128)(2,1)} %get-tuple-element.73.q_ref, ...), custom_call_target="tpu_custom_call" | custom-call | flops 32212254720 | bytes 18874368 | tf_op jit(solution)/shard_map/attend_back/pallas_call | solution.py:1100
  457.4 0.0 copy-start.5
  457.4 1.4 reduce_sum.49
  460.1 0.1 multiply_bitcast_fusion.3
  460.2 0.1 reshape.113
  460.3 1.1 reduce_sum.48
  461.5 1.6 constant_dynamic-update-slice_fusion.2
  463.1 0.0 slice-start
  463.1 0.3 constant_dynamic-update-slice_fusion.1
  463.4 0.3 constant_dynamic-update-slice_fusion.dqkv
  463.7 1.5 copy-done.14
  465.2 12.1 %convolution_convert_fusion.1.up = bf16[1536,1024]{1,0:T(8,128)(2,1)} fusion(bf16[2048,1536]{1,0:T(8,128)(2,1)} %get-tuple-element.78.n_ref, bf16[2048,1024]{1,0:T(8,128)(2,1)S(1)} %copy-done.14), kind=kOutput, calls=%fused_computation.1 | convolution fusion | flops 6444023808 | bytes 13631488 | tf_op jit(solution)/shard_map/dot_general | solution.py:360
  477.3 10.4 %convolution_convert_fusion = bf16[2048,1536]{1,0:T(8,128)(2,1)} fusion(bf16[2048,1152]{1,0:T(8,128)(2,1)S(1)} %constant_dynamic-update-slice_fusion.dqkv, bf16[1536,1536]{1,0:T(8,128)(2,1)S(1)} %bitcast.59), kind=kOutput, calls=%fused_computation | convolution fusion | flops 7250903040 | bytes 14548992 | tf_op jit(solution)/shard_map/dot_general | solution.py:356
  487.8 175.3 %collect.1 = (bf16[4,192,1536]{2,1,0:T(8,128)(2,1)}, bf16[4,192,2048]{2,1,0:T(8,128)(2,1)}, bf16[4,192,1024]{2,1,0:T(8,128)(2,1)}, bf16[8,64,1536]{2,1,0:T(8,128...) custom-call(bf16[1536,1024]{1,0:T(8,128)(2,1)} %get-tuple-element.87.gate, ...), custom_call_target="tpu_custom_call" | custom-call | flops 99999997952 | bytes 33554432 | tf_op jit(solution)/shard_map/collect/pallas_call | solution.py:1692
  663.0 0.7 reduce.1
  663.7 0.6 fusion.2.small_ref
  664.4 3.8 place_units.1.g_ref
  668.2 0.0 copy-start.8
  668.2 0.0 copy-start.9
  668.2 240.2 %rotate_slots.1 = (f32[9,192,512]{2,1,0:T(8,128)}, f32[9,192,512]{2,1,0:T(8,128)}, f32[9,192,512]{2,1,0:T(8,128)}, bf16[2,256,1536]{2,1,0:T(8,128)(2,1)}, f32[32,128]{1,0:T(8,128)}) custom-call(bf16[9,192,512]{2,1,0:T(8,128)(2,1)} %place_units.1.g_ref, bf16[9,192,1536]{2,1,0:T(8,128)(2,1)} %get-tuple-element.86.base_ref, ...), custom_call_target="tpu_custom_call" | custom-call | tf_op jit(solution)/shard_map/rotate_slots/pallas_call | solution.py:1981
  908.5 1.5 divide_subtract_fusion
  910.0 1.1 copy.36
  911.1 2.7 copy.37
  913.8 1.8 copy.38
  915.6 1.5 copy-done.1
  917.1 1.8 copy.39
  918.9 1.5 copy-done
  920.4 1.8 copy.40
  (34 shorter events, 0.1 us)
Async XLA Ops:
  7.2 4.1 copy-start.11
  7.2 4.7 copy-start.13
  7.2 308.5 %all-gather.2.cloned.1.call-start = ((), (), s32[]{:S(2)}) async-start(), calls=%async_computation.1 | async-start | bytes 7077888 | tf_op jit(solution)/shard_map/all_gather | solution.py:2055
  112.7 95.7 %copy-start.12 = (bf16[8,64,1536]{2,1,0:T(8,128)(2,1)S(1)}, bf16[8,64,1536]{2,1,0:T(8,128)(2,1)}, u32[]{:S(2)}) copy-start(bf16[8,64,1536]{2,1,0:T(8,128)(2,1)} %get-tuple-element.80.dy0_ref.dyo_ref) | copy-start | bytes 4718596
  112.7 99.8 %copy-start.7 = (f32[3456]{0:T(1024)S(1)}, f32[3456]{0:T(1024)}, u32[]{:S(2)}) copy-start(f32[3456]{0:T(1024)} %param.21) | copy-start | bytes 41476
  207.9 279.8 %reduce-scatter.2.cloned.1.call-start = ((), (), s32[]{:S(2)}) async-start(), calls=%async_computation.2 | async-start | bytes 3538944 | tf_op jit(solution)/shard_map/reduce_scatter | solution.py:2073
  208.5 59.0 %collective-permute-start.1 = (bf16[8,64,1536]{2,1,0:T(8,128)(2,1)S(1)}, bf16[8,64,1536]{2,1,0:T(8,128)(2,1)}, u32[]{:S(2)}, u32[]{:S(2)}) collective-permute-start(bf16[8,64,1536]{2,1,0:T(8,128)(2,1)S(1)} %copy-done.12), channel_id=1, source_target_pairs={{0,16},{8,24},{16,0},{24,8},{1,17},{9,25},{17,1},{25,9},{2,18},{10... | collective-permute-start | bytes 4718600 | tf_op jit(solution)/shard_map/ppermute | solution.py:372
  212.4 103.2 %collective-permute-start = (bf16[8,64,1536]{2,1,0:T(8,128)(2,1)S(1)}, bf16[8,64,1536]{2,1,0:T(8,128)(2,1)}, u32[]{:S(2)}, u32[]{:S(2)}) collective-permute-start(bf16[8,64,1536]{2,1,0:T(8,128)(2,1)S(1)} %copy-done.12), channel_id=1, source_target_pairs={{0,8},{8,0},{16,24},{24,16},{1,9},{9,1},{17,25},{25,17},{2,10},{10... | collective-permute-start | bytes 4718600 | tf_op jit(solution)/shard_map/ppermute | solution.py:368
  267.4 48.3 %collective-permute-start.2 = (bf16[8,64,1536]{2,1,0:T(8,128)(2,1)}, bf16[8,64,1536]{2,1,0:T(8,128)(2,1)}, u32[]{:S(2)}, u32[]{:S(2)}) collective-permute-start(bf16[8,64,1536]{2,1,0:T(8,128)(2,1)} %collective-permute-done.1.dy2_ref), channel_id=1, source_target_pairs={{0,8},{8,0},{16,24},{24,16},{1,9},{9,1},{17,25},{25,17},{2,10},{10... | collective-permute-start | bytes 4718600 | tf_op jit(solution)/shard_map/ppermute | solution.py:368
  409.2 52.3 %copy-start.10 = (f32[1,1536]{1,0:T(1,128)S(1)}, f32[1,1536]{1,0:T(1,128)}, u32[]{:S(2)}) copy-start(f32[1,1536]{1,0:T(1,128)} %get-tuple-element.109) | copy-start | bytes 18436
  457.4 5.7 copy-start.5
  457.4 6.0 copy-start.4
  463.0 2.2 copy-start.14
  463.1 14.3 %slice-start = ((s8[4718592]{0:T(1024)(128)(4,1)}), s8[4194304]{0:T(1024)(128)(4,1)S(1)}, s32[]{:S(2)}) async-start(s8[4718592]{0:T(1024)(128)(4,1)} %bitcast.57), calls=%async_computation.3 | async-start | bytes 8388608
  465.2 12.1 %copy-start.6 = (bf16[2048,1152]{1,0:T(8,128)(2,1)}, bf16[2048,1152]{1,0:T(8,128)(2,1)S(1)}, u32[]{:S(2)}) copy-start(bf16[2048,1152]{1,0:T(8,128)(2,1)S(1)} %constant_dynamic-update-slice_fusion.dqkv) | copy-start | bytes 14155780
  465.2 12.1 %slice-start.1 = ((s8[4718592]{0:T(1024)(128)(4,1)}), s8[524288]{0:T(1024)(128)(4,1)S(1)}, s32[]{:S(2)}) async-start(s8[4718592]{0:T(1024)(128)(4,1)} %bitcast.57), calls=%async_computation.4 | async-start | bytes 1048576
  668.2 240.3 %copy-start.8 = (f32[3456]{0:T(1024)S(1)}, f32[3456]{0:T(1024)}, u32[]{:S(2)}) copy-start(f32[3456]{0:T(1024)} %param.23) | copy-start | bytes 41476
  668.2 240.3 %copy-start.9 = (f32[3456]{0:T(1024)S(1)}, f32[3456]{0:T(1024)}, u32[]{:S(2)}) copy-start(f32[3456]{0:T(1024)} %param.22) | copy-start | bytes 41476
  668.2 241.8 %copy-start.3 = (bf16[2,256,1536]{2,1,0:T(8,128)(2,1)S(1)}, bf16[2,256,1536]{2,1,0:T(8,128)(2,1)}, u32[]{:S(2)}) copy-start(bf16[2,256,1536]{2,1,0:T(8,128)(2,1)} %get-tuple-element.138) | copy-start | bytes 4718596
  908.5 5.3 copy-start.2
  913.8 3.3 copy-start.1
  917.1 3.3 copy-start
Sparse Core Ops, SparseCore 0:
  208.1 99.7 all-gather.1
  409.3 74.8 reduce-scatter.1

commit v8 on v7

--- a/solution.py
+++ b/solution.py
@@ -397,17 +397,25 @@
     pl.semaphore_wait(barrier, len(devices))
 
 
-def greet_all():
+def greet_and_rows(devices):
     barrier = pltpu.get_barrier_semaphore()
     me, blk = lax.axis_index("batch"), lax.axis_index("blk")
-
-    def signal(n, carry):
-        at = (me * 8 + blk + n) % 32
-        pl.semaphore_signal(barrier, inc=1, device_id=(at // 8, at % 8), device_id_type=MESH)
-        return carry
-
-    lax.fori_loop(1, 32, signal, 0)
-    pl.semaphore_wait(barrier, 31)
+    for device in devices:
+        pl.semaphore_signal(barrier, inc=1, device_id=device, device_id_type=MESH)
+    for i in range(2):
+        for other in range(4):
+
+            @pl.when((me != other) | (blk != 2 * me + i))
+            def signal():
+                pl.semaphore_signal(barrier, inc=1, device_id=(other, 2 * me + i), device_id_type=MESH)
+
+    @pl.when(me == blk // 2)
+    def seven():
+        pl.semaphore_wait(barrier, len(devices) + 7)
+
+    @pl.when(me != blk // 2)
+    def eight():
+        pl.semaphore_wait(barrier, len(devices) + 8)
 
 
 def remote(source, target, sems, at, device):
@@ -1635,7 +1643,7 @@
 
     back_start, back_finish = return_rows_copies(out_rows, back_ref, s_back, me, blk)
     dgain_ref[...] = jnp.zeros_like(dgain_ref)
-    greet_all()
+    greet_and_rows((to_core, to_y, after_me, before_me))
     ring_start(0)
     for j in range(2 * blocks):
         own_copy(j).start()
@@ -1652,12 +1660,13 @@
             near_step(g)
         if 3 <= g < 2 * blocks + 3:
             far_step(g - 3)
+        if g == blocks + 3:
+            back_start()
         if (r, t, p) == (0, 6, 1):
             ring_start(1)
             relay(0)
         if (r, t, p) == (0, 7, 1):
             spread(1)
-            back_start()
         if (r, t, p) == (1, 5, 0):
             relay(1)
         if (r, t) == (1, 7):
@@ -1792,7 +1801,8 @@
         for s in range(count):
             loading(i, s).start()
     rows_start, rows_finish = return_rows_copies(rows_ref, rows_out_ref, s_rows, lax.axis_index("batch"), blk)
-    greet_all()
+    group = [{"batch": (lax.axis_index("batch") + n) % 4} for n in (1, 2, 3)]
+    greet_and_rows(group + [{"blk": (blk + n) % 8} for n in range(1, 8)])
     rows_start()
     for s in range(count):
         loading(0, s).wait()

time: 938 us -> 938 us (level)
  transfers between devices with their start and end apart: 5 -> 5, of which waited for: 0 -> 0; matrix products, arithmetic and copies ran while one was open for 4% -> 4% of each run, Pallas kernels for 15% -> 14%
where the time goes in v8:
time: 938 us; the launch traced here: 930 us
  Pallas kernels  851 us (91%)
  matrix products  22.4 us (2%)
  local copies, waits for them, and re-layouts  20.4 us (2%)
  between operations  18.2 us (2%)
  other arithmetic  12.7 us (1%)
    pallas_call x1, Pallas kernels, rotate_slots(): pl.pallas_call(rotate_kernel, in_specs=[hbm] * 8 + [pl.BlockSpec(memory_s...  244 us
    pallas_call x1, Pallas kernels, collect(): pl.pallas_call(collect_kernel, in_specs=[vmem] * 4 + [hbm] * 5 + [vmem] *...  177 us
    pallas_call x1, Pallas kernels, begin(): pl.pallas_call(begin_kernel, in_specs=[hbm] * 4 + [pl.BlockSpec(memory_sp...  100 us
    pallas_call x1, Pallas kernels, feed(): pl.pallas_call(feed_kernel, grid=(blocks + 4,), in_specs=[rows(D, 0), pl....  98.4 us
    pallas_call x1, Pallas kernels, gather(): pl.pallas_call(gather_kernel, in_specs=[vmem] * 4 + [pl.BlockSpec(memory_...  91.4 us
    pallas_call x1, Pallas kernels, middle(): pl.pallas_call(middle_kernel, grid=(blocks + 1,), in_specs=[pl.BlockSpec(...  45.1 us
    pallas_call x1, Pallas kernels, attend_back(): pl.pallas_call(attend_back_kernel, grid=(HEADS, blocks), in_specs=[smem,...  42.9 us
    pallas_call x1, Pallas kernels, attend(): pl.pallas_call(attend_kernel, grid=(HEADS, blocks), in_specs=[smem, smem,...  29.8 us
  transfers between devices with their start and end apart: 5, of which 0 were waited for; matrix products, arithmetic and copies ran while one was open for 4% of the time, Pallas kernels for 14%

profile of v8, /device:TPU:12, one launch (start us, length us, event | category | flops | bytes accessed | tf_op | source)
XLA Modules:
  0.0 929.9 jit_solution(18414127056965867852)
XLA Ops:
  7.2 0.0 all-gather.2.cloned.1.call-start
  7.3 3.4 bitcast_convert_fusion.master_ref.own
  10.7 0.6 reshape_tile.3.rate_ref
  11.3 0.6 pad.20.lengths_ref
  11.9 0.5 fusion.3.place_ref
  12.4 100.3 %begin.1 = (bf16[3,9,192,512]{3,2,1,0:T(8,128)(2,1)}, bf16[8,64,1536]{2,1,0:T(8,128)(2,1)}, bf16[8,64,1536]{2,1,0:T(8,128)(2,1)}, bf16[9,192,1536]{2,1,0:T(8,128...) custom-call(bf16[9,192,512]{2,1,0:T(8,128)(2,1)} %bitcast_convert_fusion.master_ref.own, ...), custom_call_target="tpu_custom_call" | custom-call | tf_op jit(solution)/shard_map/begin/pallas_call | solution.py:618
  112.7 0.0 copy-start.7
  112.7 3.8 pick_units.1
  116.5 91.4 %gather.1 = (bf16[8,192,1536]{2,1,0:T(8,128)(2,1)}, bf16[8,192,1024]{2,1,0:T(8,128)(2,1)}, bf16[8,4,64,1536]{3,2,1,0:T(8,128)(2,1)}, bf16[3,8,192,384]{3,2,1,0:T...) custom-call(bf16[192,1536]{1,0:T(8,128)(2,1)} %get-tuple-element.64.shard_ref, ...), custom_call_target="tpu_custom_call" | custom-call | tf_op jit(solution)/shard_map/gather/pallas_call | solution.py:785
  207.9 0.0 all-gather.2.cloned.1.call-update
  207.9 0.5 reduce-scatter.2.cloned.1.call-start
  208.5 4.0 collective-permute-start.1
  212.4 0.1 collective-permute-start
  212.5 0.6 reshape.104.gain_ref
  213.1 0.5 broadcast.55
  213.6 1.4 reduce.5
  215.0 0.1 copy.27
  215.1 0.7 multiply_reduce_fusion
  217.2 15.4 %project.1 = (bf16[2048,1536]{1,0:T(8,128)(2,1)}, bf16[2048,384]{1,0:T(8,128)(2,1)}, bf16[2048,384]{1,0:T(8,128)(2,1)}, bf16[2048,384]{1,0:T(8,128)(2,1)}) custom-call(bf16[2048,1536]{1,0:T(8,128)(2,1)} %bitcast.52, bf16[1536,1536]{1,0:T(8,128)(2,1)} %bitcast.54, f32[1,1536]{1,0:T(1,128)} %reshape.104.gain_ref, ...), custom_call_target="tpu_custom_call" | custom-call | flops 7247757312 | bytes 22413312 | tf_op jit(solution)/shard_map/project/pallas_call | solution.py:927
  232.5 0.7 copy.25.gain_ref
  233.3 0.5 and_select_fusion.low_ref
  233.8 29.8 %attend.1 = (bf16[2048,384]{1,0:T(8,128)(2,1)}, f32[3,2,128,2048]{3,2,1,0:T(8,128)}, f32[3,8,1,512]{3,2,1,0:T(1,128)}) custom-call(s32[8]{0:T(128)} %and_select_fusion.low_ref, f32[1]{0:T(128)} %bitcast.5.lam_ref, bf16[2048,384]{1,0:T(8,128)(2,1)} %get-tuple-element.73.q_ref, bf16[2048,384]{1,0:T(8,128)(2,1)} %get-tuple-element.74.k_ref, ...), custom_call_target="tpu_custom_call" | custom-call | flops 12884901888 | bytes 12582912 | tf_op jit(solution)/shard_map/attend/pallas_call | solution.py:1006
  263.6 0.0 collective-permute-done.1.dy2_ref
  263.6 0.4 collective-permute-start.2
  264.0 0.6 reshape.100.gain_ref
  265.4 0.1 select_reduce_fusion
  265.5 0.7 dynamic_slice.3.unit_ref
  266.1 0.6 pad_maximum_fusion.scale_ref
  266.7 45.1 %middle.1 = (bf16[2048,1536]{1,0:T(8,128)(2,1)}, f32[8,64,1536]{2,1,0:T(8,128)}) custom-call(bf16[2048,1536]{1,0:T(8,128)(2,1)} %bitcast.53, f32[1,1536]{1,0:T(1,128)} %reshape.100.gain_ref, bf16[2048,384]{1,0:T(8,128)(2,1)} %get-tuple-element.76.a_ref.a_hbm.a_own, bf16[1536,1536]{1,0:T(8,128)(2,1)} %bitcast.55, bf16[3,1536,384]{2,1,0:T(8,128)(2,1)} %bitcast.60, ...), custom_call_target="tpu_custom_call" | custom-call | flops 9663676416 | bytes 26738688 | tf_op jit(solution)/shard_map/middle/pallas_call | solution.py:1213
  311.8 0.0 collective-permute-done.dy1_ref
  311.8 0.0 collective-permute-done.2.dy3_ref
  311.8 0.0 all-gather.2.cloned.1.call-done.w_ref
  311.9 98.4 %feed.1 = (bf16[2048,1024]{1,0:T(8,128)(2,1)}, bf16[2048,1536]{1,0:T(8,128)(2,1)}, f32[8,64,1536]{2,1,0:T(8,128)}, bf16[8,4,64,1536]{3,2,1,0:T(8,128)(2,1)}, f32...) custom-call(bf16[2048,1536]{1,0:T(8,128)(2,1)} %get-tuple-element.78, ...), custom_call_target="tpu_custom_call" | custom-call | flops 38654705664 | bytes 47185920 | tf_op jit(solution)/shard_map/feed/pallas_call | solution.py:1406
  410.3 0.0 reduce-scatter.2.cloned.1.call-update
  410.3 42.9 %attend_back.1 = (bf16[2048,384]{1,0:T(8,128)(2,1)}, bf16[2048,384]{1,0:T(8,128)(2,1)}, bf16[2048,384]{1,0:T(8,128)(2,1)}, f32[3,128,256]{2,1,0:T(8,128)}, f32[3,1,256]{2,1,0:T(1,128)}) custom-call(s32[8]{0:T(128)} %and_select_fusion.low_ref, f32[1]{0:T(128)} %bitcast.5.lam_ref, bf16[2048,384]{1,0:T(8,128)(2,1)} %get-tuple-element.73.q_ref, ...), custom_call_target="tpu_custom_call" | custom-call | flops 32212254720 | bytes 18874368 | tf_op jit(solution)/shard_map/attend_back/pallas_call | solution.py:1108
  453.2 1.4 reduce_sum.49
  456.0 0.1 multiply_bitcast_fusion.3
  456.1 0.1 reshape.113
  456.1 1.1 reduce_sum.48
  457.3 1.6 constant_dynamic-update-slice_fusion.2
  458.9 0.0 slice-start
  458.9 0.3 constant_dynamic-update-slice_fusion.1
  459.3 0.3 constant_dynamic-update-slice_fusion.dqkv
  459.6 1.5 copy-done.14
  461.1 11.9 %convolution_convert_fusion.1.up = bf16[1536,1024]{1,0:T(8,128)(2,1)} fusion(bf16[2048,1536]{1,0:T(8,128)(2,1)} %get-tuple-element.78.n_ref, bf16[2048,1024]{1,0:T(8,128)(2,1)S(1)} %copy-done.14), kind=kOutput, calls=%fused_computation.1 | convolution fusion | flops 6444023808 | bytes 13631488 | tf_op jit(solution)/shard_map/dot_general | solution.py:360
  473.0 0.0 copy-done.6
  473.1 10.4 %convolution_convert_fusion = bf16[2048,1536]{1,0:T(8,128)(2,1)} fusion(bf16[2048,1152]{1,0:T(8,128)(2,1)S(1)} %constant_dynamic-update-slice_fusion.dqkv, bf16[1536,1536]{1,0:T(8,128)(2,1)S(1)} %bitcast.59), kind=kOutput, calls=%fused_computation | convolution fusion | flops 7250903040 | bytes 14548992 | tf_op jit(solution)/shard_map/dot_general | solution.py:356
  483.5 176.6 %collect.1 = (bf16[4,192,1536]{2,1,0:T(8,128)(2,1)}, bf16[4,192,2048]{2,1,0:T(8,128)(2,1)}, bf16[4,192,1024]{2,1,0:T(8,128)(2,1)}, bf16[8,64,1536]{2,1,0:T(8,128...) custom-call(bf16[1536,1024]{1,0:T(8,128)(2,1)} %get-tuple-element.87.gate, ...), custom_call_target="tpu_custom_call" | custom-call | flops 99999997952 | bytes 33554432 | tf_op jit(solution)/shard_map/collect/pallas_call | solution.py:1701
  660.1 0.7 reduce.1
  660.8 0.6 fusion.2.small_ref
  661.4 3.8 place_units.1.g_ref
  665.2 0.0 copy-start.8
  665.2 0.0 copy-start.9
  665.3 0.0 copy-start.3
  665.3 243.6 %rotate_slots.1 = (f32[9,192,512]{2,1,0:T(8,128)}, f32[9,192,512]{2,1,0:T(8,128)}, f32[9,192,512]{2,1,0:T(8,128)}, bf16[2,256,1536]{2,1,0:T(8,128)(2,1)}, f32[32,128]{1,0:T(8,128)}) custom-call(bf16[9,192,512]{2,1,0:T(8,128)(2,1)} %place_units.1.g_ref, bf16[9,192,1536]{2,1,0:T(8,128)(2,1)} %get-tuple-element.86.base_ref, ...), custom_call_target="tpu_custom_call" | custom-call | tf_op jit(solution)/shard_map/rotate_slots/pallas_call | solution.py:1991
  908.9 0.0 copy-start.2
  908.9 1.5 divide_subtract_fusion
  910.4 1.1 copy.36
  911.6 2.7 copy.37
  914.2 1.8 copy.38
  916.0 1.5 copy-done.1
  917.5 1.8 copy.39
  919.3 1.5 copy-done
  920.8 1.8 copy.40
  (34 shorter events, 0.1 us)
Async XLA Ops:
  7.2 4.1 copy-start.11
  7.2 4.7 copy-start.13
  7.2 304.7 %all-gather.2.cloned.1.call-start = ((), (), s32[]{:S(2)}) async-start(), calls=%async_computation.1 | async-start | bytes 7077888 | tf_op jit(solution)/shard_map/all_gather | solution.py:2065
  112.7 95.7 %copy-start.12 = (bf16[8,64,1536]{2,1,0:T(8,128)(2,1)S(1)}, bf16[8,64,1536]{2,1,0:T(8,128)(2,1)}, u32[]{:S(2)}) copy-start(bf16[8,64,1536]{2,1,0:T(8,128)(2,1)} %get-tuple-element.80.dy0_ref.dyo_ref) | copy-start | bytes 4718596
  112.7 99.8 %copy-start.7 = (f32[3456]{0:T(1024)S(1)}, f32[3456]{0:T(1024)}, u32[]{:S(2)}) copy-start(f32[3456]{0:T(1024)} %param.21) | copy-start | bytes 41476
  207.9 275.6 %reduce-scatter.2.cloned.1.call-start = ((), (), s32[]{:S(2)}) async-start(), calls=%async_computation.2 | async-start | bytes 3538944 | tf_op jit(solution)/shard_map/reduce_scatter | solution.py:2083
  208.5 55.1 %collective-permute-start.1 = (bf16[8,64,1536]{2,1,0:T(8,128)(2,1)S(1)}, bf16[8,64,1536]{2,1,0:T(8,128)(2,1)}, u32[]{:S(2)}, u32[]{:S(2)}) collective-permute-start(bf16[8,64,1536]{2,1,0:T(8,128)(2,1)S(1)} %copy-done.12), channel_id=1, source_target_pairs={{0,16},{8,24},{16,0},{24,8},{1,17},{9,25},{17,1},{25,9},{2,18},{10... | collective-permute-start | bytes 4718600 | tf_op jit(solution)/shard_map/ppermute | solution.py:372
  212.4 99.4 %collective-permute-start = (bf16[8,64,1536]{2,1,0:T(8,128)(2,1)S(1)}, bf16[8,64,1536]{2,1,0:T(8,128)(2,1)}, u32[]{:S(2)}, u32[]{:S(2)}) collective-permute-start(bf16[8,64,1536]{2,1,0:T(8,128)(2,1)S(1)} %copy-done.12), channel_id=1, source_target_pairs={{0,8},{8,0},{16,24},{24,16},{1,9},{9,1},{17,25},{25,17},{2,10},{10... | collective-permute-start | bytes 4718600 | tf_op jit(solution)/shard_map/ppermute | solution.py:368
  263.6 48.2 %collective-permute-start.2 = (bf16[8,64,1536]{2,1,0:T(8,128)(2,1)}, bf16[8,64,1536]{2,1,0:T(8,128)(2,1)}, u32[]{:S(2)}, u32[]{:S(2)}) collective-permute-start(bf16[8,64,1536]{2,1,0:T(8,128)(2,1)} %collective-permute-done.1.dy2_ref), channel_id=1, source_target_pairs={{0,8},{8,0},{16,24},{24,16},{1,9},{9,1},{17,25},{25,17},{2,10},{10... | collective-permute-start | bytes 4718600 | tf_op jit(solution)/shard_map/ppermute | solution.py:368
  410.3 46.9 %copy-start.10 = (f32[1,1536]{1,0:T(1,128)S(1)}, f32[1,1536]{1,0:T(1,128)}, u32[]{:S(2)}) copy-start(f32[1,1536]{1,0:T(1,128)} %get-tuple-element.109) | copy-start | bytes 18436
  453.2 5.7 copy-start.5
  453.2 6.0 copy-start.4
  458.9 2.2 copy-start.14
  458.9 14.1 %slice-start = ((s8[4718592]{0:T(1024)(128)(4,1)}), s8[4194304]{0:T(1024)(128)(4,1)S(1)}, s32[]{:S(2)}) async-start(s8[4718592]{0:T(1024)(128)(4,1)} %bitcast.57), calls=%async_computation.3 | async-start | bytes 8388608
  461.1 12.0 %copy-start.6 = (bf16[2048,1152]{1,0:T(8,128)(2,1)}, bf16[2048,1152]{1,0:T(8,128)(2,1)S(1)}, u32[]{:S(2)}) copy-start(bf16[2048,1152]{1,0:T(8,128)(2,1)S(1)} %constant_dynamic-update-slice_fusion.dqkv) | copy-start | bytes 14155780
  461.1 12.0 %slice-start.1 = ((s8[4718592]{0:T(1024)(128)(4,1)}), s8[524288]{0:T(1024)(128)(4,1)S(1)}, s32[]{:S(2)}) async-start(s8[4718592]{0:T(1024)(128)(4,1)} %bitcast.57), calls=%async_computation.4 | async-start | bytes 1048576
  665.2 243.7 %copy-start.8 = (f32[3456]{0:T(1024)S(1)}, f32[3456]{0:T(1024)}, u32[]{:S(2)}) copy-start(f32[3456]{0:T(1024)} %param.23) | copy-start | bytes 41476
  665.2 243.7 %copy-start.9 = (f32[3456]{0:T(1024)S(1)}, f32[3456]{0:T(1024)}, u32[]{:S(2)}) copy-start(f32[3456]{0:T(1024)} %param.22) | copy-start | bytes 41476
  665.3 245.2 %copy-start.3 = (bf16[2,256,1536]{2,1,0:T(8,128)(2,1)S(1)}, bf16[2,256,1536]{2,1,0:T(8,128)(2,1)}, u32[]{:S(2)}) copy-start(bf16[2,256,1536]{2,1,0:T(8,128)(2,1)} %get-tuple-element.138) | copy-start | bytes 4718596
  908.9 5.3 copy-start.2
  914.2 3.3 copy-start.1
  917.5 3.3 copy-start
Sparse Core Ops, SparseCore 0:
  208.1 99.7 all-gather.1
  410.4 72.7 reduce-scatter.1
